TPU v7x, 32 devices: a whole 2x2x4 slice. The times are simulated.
32 devices in a mesh: group: 2 (over y), row: 4 (over z), col: 4 (over x, core).
Axes of the slice: x: 2, y: 2, z: 4, core: 2. Of those that a mesh axis runs over, the one named last changes fastest.
Arguments:
- atom_acts: bfloat16 [65536, 128], P(('group', 'row', 'col')), parts along dimension 0, may hold values from -6 to 6
- first_gain: float32 [128], replicated, may hold values from 0.25 to 1.75
- first_qkv: bfloat16 [128, 384], replicated, may hold values from -0.5 to 0.5
- first_out: bfloat16 [128, 128], replicated, may hold values from -0.5 to 0.5
- second_gain: float32 [128], replicated, may hold values from 0.25 to 1.75
- second_qkv: bfloat16 [128, 384], replicated, may hold values from -0.5 to 0.5
- second_out: bfloat16 [128, 128], replicated, may hold values from -0.5 to 0.5
- atom_bias: bfloat16 [4, 65536, 128], P(None, ('group', 'row', 'col')), parts along dimension 1, may hold values from -4 to 320
- window_start: int32 [2048], P(('group', 'row', 'col')), parts along dimension 0, may hold values from 0 to 32640, as said below
- atom_token: int32 [65536], P(('group', 'row', 'col')), parts along dimension 0, may hold values from 0 to 1023, as said below
- up_weight: bfloat16 [128, 768], replicated, may hold values from -0.5 to 0.5
- token_gain: float32 [768], replicated, may hold values from 0.25 to 1.75
- token_weight: bfloat16 [768, 3072], replicated, may hold values from -0.21875 to 0.21875
- token_out: bfloat16 [768, 768], replicated, may hold values from -0.21875 to 0.21875
- down_weight: bfloat16 [768, 128], replicated, may hold values from -0.21875 to 0.21875
- pair_bias: bfloat16 [16, 2048, 1024], P(None, ('group', 'row'), 'col'), parts along dimension 1, may hold values from -4 to 320
Outputs:
- atom_result: bfloat16 [65536, 128], P(('group', 'row', 'col')), parts along dimension 0
There are 2 independent parts, one for each index of `group`. A program takes and returns all parts, laid end to end along the dimension named above; an argument that names none is the same for every part. Nothing has to cross between parts.
Inputs may be any that keep to these rules, and one draw needn't show every extreme that they name: `atom_token`: nondecreasing along the atoms; every token has one atom or more; the tokens r * 256 to (r + 1) * 256 - 1 own exactly the atoms r * 8192 to (r + 1) * 8192 - 1; in each such block the first 128 tokens hold one atom each, the others share the rest unevenly. `window_start`: entry b is max(0, min(32640, b * 32 + d)) with d from -64 to 32 - 64; both ends of that range occur.
All inputs are finite; a program needn't handle non-finite values.
Results may differ from a plain program's by a relative error of at most 0.011.
Values may be sent and summed in bfloat16 or wider, within the bound.
No kernel may reach another device: no remote copies, remote signals or barrier semaphores. Data moves between devices by JAX's collectives and lax.ppermute only.
A program may use at most 128 MiB of HBM per device.

v0:
```python
import math

import jax
import jax.numpy as jnp
from jax import lax
from jax.sharding import PartitionSpec as P


def padded(cells, sides, width):
    for axis, dim in sides:
        count = lax.axis_size(axis)
        ends = count - 1
        head = lax.slice_in_dim(cells, 0, width, axis=dim)
        tail = lax.slice_in_dim(cells, cells.shape[dim] - width, cells.shape[dim], axis=dim)
        cells = jnp.concatenate(
            [
                lax.ppermute(tail, axis, [(i, (i + 1) % count) for i in range(ends)]),
                cells,
                lax.ppermute(head, axis, [((i + 1) % count, i) for i in range(ends)]),
            ],
            axis=dim,
        )
    return cells


def merged(part, axis, combine):
    gathered = jax.tree.map(lambda a: lax.all_gather(a, axis), part)

    def take(source):
        return jax.tree.map(lambda a: lax.dynamic_index_in_dim(a, source, 0, False), gathered)

    return lax.fori_loop(
        1, lax.axis_size(axis), lambda source, state: combine(state, take(source)), take(0)
    )


def layer_norm(values, gain_vec):
    values = values.astype(jnp.float32)
    center = values - jnp.mean(values, axis=-1, keepdims=True)
    spread = jnp.mean(center * center, axis=-1, keepdims=True)
    return center * lax.rsqrt(spread + 1e-05) * gain_vec


def window_block(atom_acts, gain_vec, qkv_weight, out_weight, atom_bias, window_start):
    atom_rows, channels = atom_acts.shape
    head_count = atom_bias.shape[0]
    key_span = atom_bias.shape[2]
    windows = window_start.shape[0]
    query_rows = atom_rows // windows
    head_size = channels // head_count
    rim_width = key_span // 2
    score_scale = 1.0 / math.sqrt(head_size)
    normed = layer_norm(atom_acts, gain_vec).astype(jnp.bfloat16)
    packed = jnp.dot(normed, qkv_weight, preferred_element_type=jnp.float32).astype(jnp.bfloat16)
    queries = packed[:, :channels]
    key_values = padded(packed[:, channels:], ((("row", "col"), 0),), rim_width)
    first_atom = lax.axis_index(("row", "col")) * atom_rows
    offsets = window_start - first_atom + rim_width
    key_index = offsets[:, None] + jnp.arange(key_span, dtype=jnp.int32)[None, :]
    beside_all = key_values[key_index]
    key_heads = beside_all[:, :, :channels].reshape(windows, key_span, head_count, head_size)
    value_heads = beside_all[:, :, channels:].reshape(windows, key_span, head_count, head_size)
    query_heads = queries.reshape(windows, query_rows, head_count, head_size)
    bias_tile = atom_bias.reshape(head_count, windows, query_rows, key_span).astype(jnp.float32)
    scores = (
        jnp.einsum("bqhd,bkhd->hbqk", query_heads, key_heads, preferred_element_type=jnp.float32)
        * score_scale
        + bias_tile
    )
    weights = jax.nn.softmax(scores, axis=-1).astype(jnp.bfloat16)
    mixed = jnp.einsum("hbqk,bkhd->bqhd", weights, value_heads, preferred_element_type=jnp.float32)
    mixed = mixed.astype(jnp.bfloat16).reshape(atom_rows, channels)
    return (
        atom_acts.astype(jnp.float32)
        + jnp.dot(mixed, out_weight, preferred_element_type=jnp.float32)
    ).astype(jnp.bfloat16)


def heads_scaled(weighted, factor):
    head_count, token_rows = factor.shape
    return (weighted.reshape(token_rows, head_count, -1) * factor.T[:, :, None]).reshape(
        token_rows, -1
    )


def join_parts(former, latter):
    row_top = jnp.maximum(former[0], latter[0])
    keep_former = jnp.exp(former[0] - row_top)
    keep_latter = jnp.exp(latter[0] - row_top)
    row_total = former[1] * keep_former + latter[1] * keep_latter
    weighted = heads_scaled(former[2], keep_former) + heads_scaled(latter[2], keep_latter)
    return (row_top, row_total, weighted)


def finish_rows(tok_mixed, gate_raw, token_act, token_out, down_weight):
    gated = (tok_mixed * jax.nn.sigmoid(gate_raw.astype(jnp.float32))).astype(jnp.bfloat16)
    tok_result = (
        token_act.astype(jnp.float32)
        + jnp.dot(gated, token_out, preferred_element_type=jnp.float32)
    ).astype(jnp.bfloat16)
    return jnp.dot(tok_result, down_weight, preferred_element_type=jnp.float32).astype(jnp.bfloat16)


def body(
    atom_acts,
    first_gain,
    first_qkv,
    first_out,
    second_gain,
    second_qkv,
    second_out,
    atom_bias,
    window_start,
    atom_token,
    up_weight,
    token_gain,
    token_weight,
    token_out,
    down_weight,
    pair_bias,
):
    atoms1 = window_block(atom_acts, first_gain, first_qkv, first_out, atom_bias, window_start)
    head_count, tok_rows, key_slots = pair_bias.shape
    channels = token_weight.shape[0]
    head_size = channels // head_count
    score_scale = 1.0 / math.sqrt(head_size)
    slot_ids = atom_token - lax.axis_index("row") * tok_rows
    member = (jnp.arange(tok_rows, dtype=jnp.int32)[:, None] == slot_ids[None, :]).astype(
        jnp.bfloat16
    )
    atom_feat = jax.nn.relu(jnp.dot(atoms1, up_weight, preferred_element_type=jnp.float32)).astype(
        jnp.bfloat16
    )
    token_sum = jnp.dot(member, atom_feat, preferred_element_type=jnp.float32)
    atom_count = jnp.sum(member.astype(jnp.float32), axis=1)
    part_sum, part_count = (
        lax.psum_scatter(token_sum, "col", scatter_dimension=0, tiled=True),
        lax.psum_scatter(atom_count, "col", scatter_dimension=0, tiled=True),
    )
    part_act = (part_sum / part_count[:, None]).astype(jnp.bfloat16)
    part_normed = layer_norm(part_act, token_gain).astype(jnp.bfloat16)
    part_proj = jnp.dot(part_normed, token_weight, preferred_element_type=jnp.float32).astype(
        jnp.bfloat16
    )
    key_values = part_proj[:, channels : 3 * channels]
    own_rows = jnp.concatenate(
        [part_proj[:, :channels], part_proj[:, 3 * channels :], part_act], axis=1
    )
    gathered = lax.all_gather(own_rows, "col", axis=0, tiled=True)
    queries = gathered[:, :channels]
    gate_raw = gathered[:, channels : 2 * channels]
    token_act = gathered[:, 2 * channels :]
    query_heads = queries.reshape(tok_rows, head_count, head_size)
    key_piece = lax.all_gather(key_values, "row", axis=0, tiled=True)
    row_top = jnp.full((head_count, tok_rows), -1e30, jnp.float32)
    weighted = jnp.zeros((tok_rows, channels), jnp.float32)
    piece_rows = key_piece.shape[0]
    key_heads = key_piece[:, :channels].reshape(piece_rows, head_count, head_size)
    value_heads = key_piece[:, channels:].reshape(piece_rows, head_count, head_size)
    bias_tile = pair_bias.astype(jnp.float32)
    scores = (
        jnp.einsum("qhd,khd->hqk", query_heads, key_heads, preferred_element_type=jnp.float32)
        * score_scale
        + bias_tile
    )
    new_top = jnp.maximum(row_top, jnp.max(scores, axis=-1))
    fading = jnp.exp(row_top - new_top)
    exp_scores = jnp.exp(scores - new_top[:, :, None])
    row_total = jnp.sum(exp_scores, axis=-1)
    piece_sum = jnp.einsum(
        "hqk,khd->qhd",
        exp_scores.astype(jnp.bfloat16),
        value_heads,
        preferred_element_type=jnp.float32,
    )
    row_top, row_total, weighted = merged(
        (
            new_top,
            row_total,
            heads_scaled(weighted, fading) + piece_sum.reshape(tok_rows, channels),
        ),
        "col",
        join_parts,
    )
    tok_mixed = heads_scaled(weighted, 1.0 / row_total)
    back_proj = finish_rows(tok_mixed, gate_raw, token_act, token_out, down_weight)
    spread_back = jnp.einsum("ta,tc->ac", member, back_proj, preferred_element_type=jnp.float32)
    atoms2 = (atoms1.astype(jnp.float32) + spread_back).astype(jnp.bfloat16)
    return window_block(atoms2, second_gain, second_qkv, second_out, atom_bias, window_start)


def solution(mesh):
    in_specs = (
        P(("group", "row", "col"), None),
        P(),
        P(),
        P(),
        P(),
        P(),
        P(),
        P(None, ("group", "row", "col"), None),
        P(("group", "row", "col")),
        P(("group", "row", "col")),
        P(),
        P(),
        P(),
        P(),
        P(),
        P(None, ("group", "row"), "col"),
    )
    out_specs = P(("group", "row", "col"), None)
    return jax.shard_map(body, mesh=mesh, in_specs=in_specs, out_specs=out_specs, check_vma=False)
```

profile of v0, /device:TPU:1, one launch (start us, length us, event | category | flops | bytes accessed | tf_op | source)
XLA Modules:
  0.0 284.6 jit_solution(14413112343181943544)
XLA Ops:
  6.6 1.3 copy.86
  8.9 4.5 %collective-permute-start = (bf16[64,256]{1,0:T(8,128)(2,1)S(1)}, bf16[64,256]{1,0:T(8,128)(2,1)S(1)}, u32[]{:S(2)}, u32[]{:S(2)}) collective-permute-start(bf16[64,256]{1,0:T(8,128)(2,1)S(1)} %get-tuple-element.224), channel_id=1, source_target_pairs={{0,1},{1,2},{2,3},{3,4},{4,5},{5,6},{6,7},{7,8},{8,9},{9,10},{10,1... | collective-permute-start | bytes 98312 | tf_op jit(solution)/shard_map/ppermute | solution.py:17
  13.5 1.9 collective-permute-start.1
  17.4 4.0 %reshape.236 = bf16[64,32,4,32]{3,2,1,0:T(4,128)(2,1)} reshape(bf16[2048,128]{1,0:T(8,128)(2,1)} %slice.97) | data formatting | bytes 1048576 | tf_op jit(solution)/shard_map/reshape | solution.py:63
  21.4 1.3 pad_maximum_fusion
  22.7 33.1 %gather_fusion = bf16[8192,256]{1,0:T(8,128)(2,1)} fusion(bf16[2176,256]{1,0:T(8,128)(2,1)S(1)} %pad_maximum_fusion, s32[8192]{0:T(1024)S(1)} %fusion.75), kind=kCustom, calls=%fused_computation | custom fusion | bytes 8421376 | tf_op jit(solution)/shard_map/gather | solution.py:60
  55.7 4.8 %fusion.82 = (bf16[64,128,128]{2,1,0:T(8,128)(2,1)}, bf16[64,128,128]{2,1,0:T(8,128)(2,1)}) fusion(bf16[64,128,256]{2,1,0:T(8,128)(2,1)} %bitcast.100), kind=kLoop, calls=%fused_computation.121 | loop fusion | bytes 8388608 | tf_op jit(solution)/shard_map/slice | solution.py:61
  60.6 4.1 %copy.121 = bf16[64,128,128]{1,2,0:T(8,128)(2,1)} copy(bf16[64,128,128]{2,1,0:T(8,128)(2,1)} %get-tuple-element.220) | data formatting | bytes 4194304
  64.7 4.1 %copy.120 = bf16[64,128,128]{1,2,0:T(8,128)(2,1)} copy(bf16[64,128,128]{2,1,0:T(8,128)(2,1)} %get-tuple-element.221) | data formatting | bytes 4194304
  68.7 6.2 %fusion.87 = (f32[4,64,32]{2,1,0:T(8,128)S(1)}, f32[4,64,32,128]{3,2,1,0:T(8,128)}) fusion(bf16[4,64,32,128]{3,2,1,0:T(8,128)(2,1)} %bitcast.112, bf16[64,32,4,32]{3,2,1,0:T(4,128)(2,1)} %reshape.236, bf16[64,128,4,32]{1,3,2,0:T(8,128)(2,1)} %bitcast.103), kind=kOutput, calls=%fused_computation.126 | convolution fusion | flops 72351872 | bytes 8945664 | tf_op jit(solution)/shard_map/sub | solution.py:70
  74.9 4.2 %convert_bitcast_fusion.1 = bf16[64,32,4,32]{1,3,2,0:T(8,128)(2,1)S(1)} fusion(bf16[64,128,4,32]{1,3,2,0:T(8,128)(2,1)} %bitcast.104, f32[4,64,32,128]{3,2,1,0:T(8,128)} %get-tuple-element.233, f32[4,64,32]{2,1,0:T(8,128)S(1)} %get-tuple-element.232), kind=kOutput, calls=%fused_computation.56 | convolution fusion | flops 69468160 | bytes 6848512 | tf_op jit(solution)/shard_map/hbqk,bkhd->bqhd/dot_general | solution.py:71
  79.1 2.7 copy.93
  81.8 3.5 %reshape.202 = bf16[2048,128]{0,1:T(8,128)(2,1)S(1)} reshape(bf16[64,32,4,32]{1,0,3,2:T(8,128)(2,1)} %copy.93) | data formatting | bytes 1048576 | tf_op jit(solution)/shard_map/reshape | solution.py:72
  85.7 2.7 fusion.29
  90.1 5.7 %all-reduce = f32[256]{0:T(256)S(1)} all-reduce(f32[256]{0:T(256)S(1)} %convert_reduce_fusion), channel_id=5, replica_groups=mesh['group'=2,'row'=4,'col'=4] {'col'}, use_global_device_ids=true, to_apply=%region_6.7.clone | all-reduce | flops 256 | bytes 2048
  95.8 17.3 %reduce-scatter.2.cloned.1.call-done = f32[64,768]{1,0:T(8,128)} async-done(((f32[256,768]{1,0:T(8,128)}), f32[64,768]{1,0:T(8,128)}) %reduce-scatter.2.cloned.1.call-update) | async-done | bytes 196624 | tf_op jit(solution)/shard_map/reduce_scatter | solution.py:137
  114.4 3.3 %convolution_convert_fusion = bf16[64,3072]{1,0:T(8,128)(2,1)S(1)} fusion(bf16[768,3072]{1,0:T(8,128)(2,1)} %param.30, bf16[64,768]{1,0:T(8,128)(2,1)S(1)} %get-tuple-element.215, f32[768]{0:T(1024)S(1)} %copy-done.21, f32[64]{0:T(128)S(1)} %add_rsqrt_fusion.2, f32[64]{0:T(128)S(1)} %broadcast_multiply_fusion.2), kind=kOutput, calls=%fused_computation.27 | convolution fusion | flops 302432256 | bytes 5213696 | tf_op jit(solution)/shard_map/dot_general | solution.py:142
  119.4 2.9 %copy.96 = bf16[16,256,256]{1,2,0:T(8,128)(2,1)S(1)} copy(bf16[16,256,256]{2,1,0:T(8,128)(2,1)} %param.33) | data formatting | bytes 4194304 | tf_op args[15]
  122.3 16.9 %all_gather.21 = bf16[256,1536]{1,0:T(8,128)(2,1)S(1)} all-gather(bf16[64,1536]{1,0:T(8,128)(2,1)S(1)} %slice-done), channel_id=1, replica_groups=mesh['group'=2,'row'=4,'col'=4] {'row'}, dimensions={0}, use_global_device_ids=true | all-gather | bytes 983040 | tf_op jit(solution)/shard_map/all_gather | solution.py:154
  140.2 1.9 copy.95
  142.1 1.9 copy.97
  144.0 1.8 slice.102
  145.8 1.9 copy.94
  147.8 2.1 fusion.88
  151.8 1.2 copy.99
  153.0 2.8 fusion.8
  155.8 8.4 %all-gather.1 = f32[64,256]{1,0:T(8,128)S(1)} all-gather(f32[16,256]{1,0:T(8,128)S(1)} %fusion.8), channel_id=3, replica_groups=mesh['group'=2,'row'=4,'col'=4] {'col'}, dimensions={0}, use_global_device_ids=true | all-gather | bytes 81920 | tf_op jit(solution)/shard_map/all_gather | solution.py:27
  164.2 5.5 %all-gather = f32[64,256]{1,0:T(8,128)S(1)} all-gather(f32[16,256]{1,0:T(8,128)S(1)} %get-tuple-element.231), channel_id=2, replica_groups=mesh['group'=2,'row'=4,'col'=4] {'col'}, dimensions={0}, use_global_device_ids=true | all-gather | bytes 81920 | tf_op jit(solution)/shard_map/all_gather | solution.py:27
  169.8 13.8 %all-gather.7.cloned.1.call-done = f32[4,256,768]{2,1,0:T(8,128)} async-done(((f32[1,256,768]{2,1,0:T(8,128)}), f32[4,256,768]{2,1,0:T(8,128)}) %all-gather.7.cloned.1.call-update) | async-done | bytes 3145744 | tf_op jit(solution)/shard_map/all_gather | solution.py:27
  183.6 1.2 slice_bitcast_fusion
  185.0 13.6 %while.19 = (s32[]{:T(128)}, f32[16,256]{1,0:T(8,128)S(1)}, f32[16,256]{1,0:T(8,128)S(1)}, f32[256,768]{0,1:T(8,128)S(1)}, f32[4,16,256]{2,1,0:T(8,128)S(1)}, /*...) while((s32[]{:T(128)}, f32[16,256]{1,0:T(8,128)S(1)}, ...), condition=%wide.region_12.13_spmd, body=%wide.region_11.12_spmd.sunk | while | flops 618501 | bytes 6930755 | solution.py:32
  186.9 1.2 constant_dynamic-slice_fusion.2
  191.5 1.2 constant_dynamic-slice_fusion.2
  196.0 1.2 constant_dynamic-slice_fusion.2
  200.1 2.8 fusion.46
  203.0 1.4 fusion.89
  205.3 2.1 collective-permute-start.2
  207.4 2.4 collective-permute-start.3
  210.9 1.8 reshape.237
  212.8 1.3 pad_maximum_fusion.1
  214.1 33.1 %gather_fusion.1 = bf16[8192,256]{1,0:T(8,128)(2,1)} fusion(bf16[2176,256]{1,0:T(8,128)(2,1)S(1)} %pad_maximum_fusion.1, s32[8192]{0:T(1024)S(1)} %copy-done.13), kind=kCustom, calls=%fused_computation.1 | custom fusion | bytes 8421376 | tf_op jit(solution)/shard_map/gather | solution.py:60
  247.2 4.8 %fusion.81 = (bf16[64,128,128]{2,1,0:T(8,128)(2,1)}, bf16[64,128,128]{2,1,0:T(8,128)(2,1)}) fusion(bf16[64,128,256]{2,1,0:T(8,128)(2,1)} %bitcast.99), kind=kLoop, calls=%fused_computation.120 | loop fusion | bytes 8388608 | tf_op jit(solution)/shard_map/slice | solution.py:61
  252.0 4.1 %copy.123 = bf16[64,128,128]{1,2,0:T(8,128)(2,1)} copy(bf16[64,128,128]{2,1,0:T(8,128)(2,1)} %get-tuple-element.218) | data formatting | bytes 4194304
  256.1 4.1 %copy.122 = bf16[64,128,128]{1,2,0:T(8,128)(2,1)} copy(bf16[64,128,128]{2,1,0:T(8,128)(2,1)} %get-tuple-element.219) | data formatting | bytes 4194304
  260.2 6.2 %fusion.90 = (f32[4,64,32]{2,1,0:T(8,128)S(1)}, f32[4,64,32,128]{3,2,1,0:T(8,128)}) fusion(bf16[4,64,32,128]{3,2,1,0:T(8,128)(2,1)} %bitcast.113, bf16[64,32,4,32]{3,2,1,0:T(4,128)(2,1)} %reshape.237, bf16[64,128,4,32]{1,3,2,0:T(8,128)(2,1)} %bitcast.105), kind=kOutput, calls=%fused_computation.129 | convolution fusion | flops 72351872 | bytes 8945664 | tf_op jit(solution)/shard_map/sub | solution.py:70
  266.3 4.2 %convert_bitcast_fusion = bf16[64,32,4,32]{1,3,2,0:T(8,128)(2,1)S(1)} fusion(bf16[64,128,4,32]{1,3,2,0:T(8,128)(2,1)} %bitcast.106, f32[4,64,32,128]{3,2,1,0:T(8,128)} %get-tuple-element.239, f32[4,64,32]{2,1,0:T(8,128)S(1)} %get-tuple-element.238), kind=kOutput, calls=%fused_computation.50 | convolution fusion | flops 69468160 | bytes 6848512 | tf_op jit(solution)/shard_map/hbqk,bkhd->bqhd/dot_general | solution.py:71
  270.5 2.7 copy.110
  273.2 3.5 %reshape.210 = bf16[2048,128]{0,1:T(8,128)(2,1)S(1)} reshape(bf16[64,32,4,32]{1,0,3,2:T(8,128)(2,1)} %copy.110) | data formatting | bytes 1048576 | tf_op jit(solution)/shard_map/reshape | solution.py:72
  (146 shorter events, 24.9 us)
Async XLA Ops:
  6.5 193.6 %copy-start = (bf16[768,768]{1,0:T(8,128)(2,1)S(1)}, bf16[768,768]{1,0:T(8,128)(2,1)}, u32[]{:S(2)}) copy-start(bf16[768,768]{1,0:T(8,128)(2,1)} %param.31) | copy-start | bytes 3538948
  6.5 1.7 copy-start.22
  6.5 1.7 copy-start.14
  6.5 8.9 %copy-start.25 = (s32[64]{0:T(128)S(1)}, s32[64]{0:T(128)}, u32[]{:S(2)}) copy-start(s32[64]{0:T(128)} %param.26) | copy-start | bytes 772
  6.5 9.0 %copy-start.20 = (s32[2048]{0:T(1024)S(1)}, s32[2048]{0:T(1024)}, u32[]{:S(2)}) copy-start(s32[2048]{0:T(1024)} %param.27) | copy-start | bytes 24580
  6.5 106.5 %reduce-scatter.2.cloned.1.call-start = ((), (), s32[]{:S(2)}) async-start(), calls=%async_computation.1 | async-start | bytes 983040 | tf_op jit(solution)/shard_map/reduce_scatter | solution.py:137
  8.9 12.4 %collective-permute-start = (bf16[64,256]{1,0:T(8,128)(2,1)S(1)}, bf16[64,256]{1,0:T(8,128)(2,1)S(1)}, u32[]{:S(2)}, u32[]{:S(2)}) collective-permute-start(bf16[64,256]{1,0:T(8,128)(2,1)S(1)} %get-tuple-element.224), channel_id=1, source_target_pairs={{0,1},{1,2},{2,3},{3,4},{4,5},{5,6},{6,7},{7,8},{8,9},{9,10},{10,1... | collective-permute-start | bytes 98312 | tf_op jit(solution)/shard_map/ppermute | solution.py:17
  13.5 7.9 %collective-permute-start.1 = (bf16[64,256]{1,0:T(8,128)(2,1)S(1)}, bf16[64,256]{1,0:T(8,128)(2,1)S(1)}, u32[]{:S(2)}, u32[]{:S(2)}) collective-permute-start(bf16[64,256]{1,0:T(8,128)(2,1)S(1)} %get-tuple-element.225), channel_id=1, source_target_pairs={{1,0},{2,1},{3,2},{4,3},{5,4},{6,5},{7,6},{8,7},{9,8},{10,9},{11,1... | collective-permute-start | bytes 98312 | tf_op jit(solution)/shard_map/ppermute | solution.py:19
  15.5 7.2 %copy-start.12 = (s32[8192]{0:T(1024)}, s32[8192]{0:T(1024)S(1)}, u32[]{:S(2)}) copy-start(s32[8192]{0:T(1024)S(1)} %fusion.75) | copy-start | bytes 98308
  15.5 74.2 %copy-start.16 = (s32[2048]{0:T(1024)}, s32[2048]{0:T(1024)S(1)}, u32[]{:S(2)}) copy-start(s32[2048]{0:T(1024)S(1)} %broadcast_subtract_fusion) | copy-start | bytes 24580
  81.8 3.5 %copy-start.19 = (bf16[128,128]{1,0:T(8,128)(2,1)S(1)}, bf16[128,128]{1,0:T(8,128)(2,1)}, u32[]{:S(2)}) copy-start(bf16[128,128]{1,0:T(8,128)(2,1)} %param.21) | copy-start | bytes 98308
  81.8 3.9 %copy-start.24 = (bf16[128,768]{1,0:T(8,128)(2,1)S(1)}, bf16[128,768]{1,0:T(8,128)(2,1)}, u32[]{:S(2)}) copy-start(bf16[128,768]{1,0:T(8,128)(2,1)} %param.28) | copy-start | bytes 589828
  85.7 2.7 copy-start.2
  85.7 2.8 copy-start.26
  85.7 28.7 %copy-start.21 = (f32[768]{0:T(1024)S(1)}, f32[768]{0:T(1024)}, u32[]{:S(2)}) copy-start(f32[768]{0:T(1024)} %param.29) | copy-start | bytes 9220
  88.5 55.6 %all-gather.5.cloned.1.call-start = ((), (), s32[]{:S(2)}) async-start(), calls=%async_computation.2 | async-start | bytes 1474560 | tf_op jit(solution)/shard_map/all_gather | solution.py:149
  117.8 0.7 copy-start.4
  119.3 3.0 %slice-start = ((bf16[64,3072]{1,0:T(8,128)(2,1)}), bf16[64,1536]{1,0:T(8,128)(2,1)S(1)}, s32[]{:S(2)}) async-start(bf16[64,3072]{1,0:T(8,128)(2,1)} %copy-done.4), calls=%async_computation.4 | async-start | bytes 393216 | tf_op jit(solution)/shard_map/slice | solution.py:145
  119.3 64.3 %all-gather.7.cloned.1.call-start = ((), (), s32[]{:S(2)}) async-start(), calls=%async_computation.3 | async-start | bytes 3932160 | tf_op jit(solution)/shard_map/all_gather | solution.py:27
  147.8 2.1 copy-start.5
  149.8 2.0 copy-start.1
  185.1 1.3 copy-start.6
  185.1 1.3 copy-start.10
  186.3 0.6 copy-start.8
  188.4 1.1 copy-start.7
  188.4 1.1 copy-start.9
  188.4 1.1 copy-start.11
  189.6 1.3 copy-start.6
  189.6 1.3 copy-start.10
  190.9 0.6 copy-start.8
  192.9 1.1 copy-start.7
  192.9 1.1 copy-start.9
  192.9 1.1 copy-start.11
  194.1 1.3 copy-start.6
  194.1 1.3 copy-start.10
  195.4 0.6 copy-start.8
  197.4 1.1 copy-start.7
  197.4 1.1 copy-start.9
  197.5 1.1 copy-start.11
  200.1 2.8 copy-start.3
  200.1 2.8 copy-start.17
  203.0 1.6 copy-start.15
  203.0 1.6 copy-start.23
  205.3 7.5 %collective-permute-start.2 = (bf16[64,256]{1,0:T(8,128)(2,1)S(1)}, bf16[64,256]{1,0:T(8,128)(2,1)S(1)}, u32[]{:S(2)}, u32[]{:S(2)}) collective-permute-start(bf16[64,256]{1,0:T(8,128)(2,1)S(1)} %get-tuple-element.222), channel_id=1, source_target_pairs={{0,1},{1,2},{2,3},{3,4},{4,5},{5,6},{6,7},{7,8},{8,9},{9,10},{10,1... | collective-permute-start | bytes 98312 | tf_op jit(solution)/shard_map/ppermute | solution.py:17
  207.4 5.4 %collective-permute-start.3 = (bf16[64,256]{1,0:T(8,128)(2,1)S(1)}, bf16[64,256]{1,0:T(8,128)(2,1)S(1)}, u32[]{:S(2)}, u32[]{:S(2)}) collective-permute-start(bf16[64,256]{1,0:T(8,128)(2,1)S(1)} %get-tuple-element.223), channel_id=1, source_target_pairs={{1,0},{2,1},{3,2},{4,3},{5,4},{6,5},{7,6},{8,7},{9,8},{10,9},{11,1... | collective-permute-start | bytes 98312 | tf_op jit(solution)/shard_map/ppermute | solution.py:19
  210.9 3.2 %copy-start.13 = (s32[8192]{0:T(1024)S(1)}, s32[8192]{0:T(1024)}, u32[]{:S(2)}) copy-start(s32[8192]{0:T(1024)} %copy-done.12) | copy-start | bytes 98308
  273.2 3.5 %copy-start.18 = (bf16[128,128]{1,0:T(8,128)(2,1)S(1)}, bf16[128,128]{1,0:T(8,128)(2,1)}, u32[]{:S(2)}) copy-start(bf16[128,128]{1,0:T(8,128)(2,1)} %param.24) | copy-start | bytes 98308
Sparse Core Ops, SparseCore 0:
  88.6 24.4 reduce-scatter.1
  119.4 17.8 all-gather.4
  153.2 30.3 all-gather.6
where the time goes:
time: 287 us; the launch traced here: 285 us
  local copies, waits for them, and re-layouts  140 us (49%)
  blocking collectives  36.6 us (13%)
  matrix products  35.8 us (12%)
  waiting for transfers between devices  31.2 us (11%)
  other arithmetic  15.3 us (5%)
  between operations  14.3 us (5%)
  starting transfers between devices  11.1 us (4%)
    gather x2, local copies, waits for them, and re-layouts, window_block(): beside_all = key_values[key_index]  66.1 us
    unnamed x50, local copies, waits for them, and re-layouts  23.2 us
    reduce_scatter x1, waiting for transfers between devices, body(): lax.psum_scatter(token_sum, 'col', scatter_dimension=0, tiled=True)  17.3 us
    all_gather x1, blocking collectives, body(): key_piece = lax.all_gather(key_values, 'row', axis=0, tiled=True)  16.9 us
    all_gather x2, blocking collectives, merged(): gathered = jax.tree.map(lambda a: lax.all_gather(a, axis), part)  13.9 us
    all_gather x1, waiting for transfers between devices, merged(): gathered = jax.tree.map(lambda a: lax.all_gather(a, axis), part)  13.8 us
    sub x2, matrix products, window_block(): weights = jax.nn.softmax(scores, axis=-1).astype(jnp.bfloat16)  12.4 us
    slice x2, local copies, waits for them, and re-layouts, window_block(): beside_all[:, :, :channels]  9.62 us
  transfers between devices with their start and end apart: 7, of which 2 were waited for; matrix products, arithmetic and copies ran while one was open for 7% of the time, Pallas kernels for 0%

commit v1 on v0

v1 whole, which is shorter than its diff:
```python
import functools
import math

import jax
import jax.numpy as jnp
from jax import lax
from jax.experimental import pallas as pl
from jax.experimental.pallas import tpu as pltpu
from jax.sharding import PartitionSpec as P

BF = jnp.bfloat16
F32 = jnp.float32
RIM = 64
LANES = 128
VMEM = pl.BlockSpec(memory_space=pltpu.VMEM)
SMEM = pl.BlockSpec(memory_space=pltpu.SMEM)


def dot(a, b):
    return jnp.dot(a, b, preferred_element_type=F32)


def dot_nt(a, b):
    return lax.dot_general(a, b, (((1,), (1,)), ((), ())), preferred_element_type=F32)


def dot_tn(a, b):
    return lax.dot_general(a, b, (((0,), (0,)), ((), ())), preferred_element_type=F32)


def norm_rows(values, gain):
    center = values - jnp.mean(values, axis=-1, keepdims=True)
    spread = jnp.mean(center * center, axis=-1, keepdims=True)
    return center * lax.rsqrt(spread + 1e-05) * gain


def token_of(count, share, first_parity):
    half = count // 2
    row = lax.broadcasted_iota(jnp.int32, (count, 1), 0)
    second = (row >= half).astype(jnp.int32)
    inner = row - second * half
    shift = share.bit_length() - 1
    share_pair = inner >> shift
    inside = inner & (share - 1)
    parity = first_parity + second - 2 * first_parity * second
    return (2 * share_pair + parity) * share + inside


def one_hot(table_ids, atom_ids):
    return jnp.where(table_ids == atom_ids, 1.0, 0.0).astype(BF)


def project(rows, gain, qkv, q, k, v, at):
    channels = rows.shape[1]
    packed = dot(norm_rows(rows.astype(F32), gain).astype(BF), qkv).astype(BF)
    place = slice(RIM + at, RIM + at + rows.shape[0])
    q[at : at + rows.shape[0], :] = packed[:, :channels]
    k[place, :] = packed[:, channels : 2 * channels].astype(F32)
    v[place, :] = packed[:, 2 * channels :].astype(F32)


def project_rim(rows, gain, qkv, k, v, at):
    channels = rows.shape[1]
    normed = norm_rows(rows.astype(F32), gain).astype(BF)
    packed = dot(normed, qkv[:, channels:]).astype(BF).astype(F32)
    place = pl.ds(pl.multiple_of(at, RIM), RIM)
    k[place, :] = packed[:, :channels]
    v[place, :] = packed[:, channels:]


def attend_windows(offsets, bias, q, k, v, mixed):
    heads, atom_rows, span = bias.shape
    windows = offsets.shape[0]
    block = atom_rows // windows
    channels = q.shape[1]
    size = channels // heads
    scale = 1.0 / math.sqrt(size)
    stacked = heads * block
    head_row = lax.broadcasted_iota(jnp.int32, (heads, block, channels), 0).reshape(stacked, channels)
    head_lane = lax.broadcasted_iota(jnp.int32, (stacked, channels), 1) // size
    own_head = jnp.where(head_row == head_lane, 1.0, 0.0).astype(BF)
    lane_head = lax.broadcasted_iota(jnp.int32, (block, channels), 1) // size

    def one_window(window, carry):
        begin = offsets[window]
        anchor = pl.multiple_of(window * block, block)
        keys = k[pl.ds(begin, span), :].astype(BF)
        values = v[pl.ds(begin, span), :].astype(BF)
        query = q[pl.ds(anchor, block), :]
        spread = jnp.concatenate([query] * heads, axis=0) * own_head
        tile = bias[:, pl.ds(anchor, block), :].reshape(stacked, span).astype(F32)
        scores = dot_nt(spread, keys) * scale + tile
        top = jnp.max(scores, axis=-1, keepdims=True)
        raised = jnp.exp(scores - top)
        weights = (raised / jnp.sum(raised, axis=-1, keepdims=True)).astype(BF)
        out = dot(weights, values)
        picked = out[:block]
        for head in range(1, heads):
            picked = jnp.where(lane_head == head, out[head * block : (head + 1) * block], picked)
        mixed[pl.ds(anchor, block), :] = picked.astype(BF)
        return carry

    lax.fori_loop(0, windows, one_window, 0, unroll=4)


def first_block(
    info, offsets, ids, acts, near, far, gain, qkv, out_weight, bias, up, atoms, send, keep, q, k, v, mixed, *, share
):
    side = info[0]
    rows, channels = acts.shape
    gain_row = gain[...]
    weight = qkv[...]
    end = RIM + rows
    project_rim(near[:RIM, :], gain_row, weight, k, v, jnp.where(side == 0, end, 0))
    project_rim(far[:RIM, :], gain_row, weight, k, v, jnp.where(side == 0, 0, end))
    step = 256
    for at in range(0, rows, step):
        project(acts[at : at + step, :], gain_row, weight, q, k, v, at)
    attend_windows(offsets, bias, q, k, v, mixed)
    for at in range(0, rows, step):
        part = acts[at : at + step, :].astype(F32) + dot(mixed[at : at + step, :], out_weight[...])
        atoms[at : at + step, :] = part.astype(BF)
    tokens = 2 * send.shape[0]
    half = tokens // 2
    member = one_hot(token_of(tokens, share, 1 - side), ids[...])
    wide = up.shape[1]
    atom_rows = atoms[...]
    for at in range(0, wide, step):
        feat = jnp.maximum(dot(atom_rows, up[:, at : at + step]), 0.0).astype(BF)
        sums = dot(member, feat).astype(BF)
        send[:, at : at + step] = sums[:half]
        keep[:, at : at + step] = sums[half:]
    count = dot(member, jnp.ones((rows, LANES), BF))
    high = jnp.floor(count * (1.0 / 64.0))
    low = count - 64.0 * high
    lane = lax.broadcasted_iota(jnp.int32, (tokens, LANES), 1)
    pieces = jnp.where(lane == 0, high, jnp.where(lane == 1, low, 0.0)).astype(BF)
    send[:, wide:] = pieces[:half]
    keep[:, wide:] = pieces[half:]


def mean_tokens(*refs, count):
    parts, gain, act, normed = refs[:count], refs[count], refs[count + 1], refs[count + 2]
    total = parts[0][...].astype(F32)
    for part in parts[1:]:
        total = total + part[...].astype(F32)
    wide = act.shape[1]
    atoms = total[:, wide : wide + 1] * 64.0 + total[:, wide + 1 : wide + 2]
    rounded = (total[:, :wide] / atoms).astype(BF)
    act[...] = rounded
    normed[...] = norm_rows(rounded.astype(F32), gain[...]).astype(BF)


def query_tokens(info, weight, gain, own_act, *refs, others):
    other_acts, act, queries, gates = refs[:others], refs[others], refs[others + 1], refs[others + 2]
    share, wide = own_act.shape
    pairs = others + 1
    place = info[2]
    act[pl.ds(pl.multiple_of(place * share, share), share), :] = own_act[...]
    for step in range(1, pairs):
        at = lax.rem(place - step + pairs, pairs) * share
        act[pl.ds(pl.multiple_of(at, share), share), :] = other_acts[step - 1][...]
    normed = norm_rows(act[...].astype(F32), gain[...]).astype(BF)
    queries[...] = dot(normed, weight[:, :wide]).astype(BF)
    raw = dot(normed, weight[:, 3 * wide :]).astype(BF).astype(F32)
    gates[...] = jax.nn.sigmoid(raw)


def attend_tokens(info, weight, queries, bias_own, bias_near, *refs, rows_count):
    own, near = refs[:rows_count], refs[rows_count : 2 * rows_count]
    out, tokens, keys_values = refs[2 * rows_count], refs[2 * rows_count + 1], refs[2 * rows_count + 2]
    share, wide = own[0].shape
    side, row = info[0], info[1]
    keys = rows_count * share
    for step in range(rows_count):
        at = lax.rem(row - step + rows_count, rows_count) * share
        tokens[pl.ds(pl.multiple_of(at, share), share), :] = own[step][...]
        tokens[pl.ds(pl.multiple_of(at + keys, share), share), :] = near[step][...]
    keys_values[...] = dot(tokens[...], weight[:, wide : 3 * wide]).astype(BF)
    count = queries.shape[0]
    pairs = count // share
    heads = bias_own.shape[0]
    size = wide // heads
    scale = 1.0 / math.sqrt(size)
    lane = lax.broadcasted_iota(jnp.int32, (count, LANES), 1)
    blocks = [None] * (wide // LANES)
    logs = jnp.zeros((count, LANES), F32)
    for head in range(heads):
        first, last = head * size, (head + 1) * size
        low, high = first // LANES, -(-last // LANES)
        chunk = slice(low * LANES, high * LANES)
        chunk_lane = lax.broadcasted_iota(jnp.int32, (count, (high - low) * LANES), 1) + low * LANES
        inside = (chunk_lane >= first) & (chunk_lane < last)
        query = jnp.where(inside, queries[:, chunk].astype(F32), 0.0).astype(BF)
        own_rows = [
            bias_own[head, pl.ds(pl.multiple_of((2 * pair + side) * share, share), share), :] for pair in range(pairs)
        ]
        own_tile = jnp.concatenate(own_rows, axis=0).astype(F32)
        scores_own = dot_nt(query, keys_values[:keys, chunk]) * scale + own_tile
        scores_near = dot_nt(query, keys_values[keys:, chunk]) * scale + bias_near[head].astype(F32)
        top = jnp.maximum(
            jnp.max(scores_own, axis=-1, keepdims=True), jnp.max(scores_near, axis=-1, keepdims=True)
        )
        raised_own = jnp.exp(scores_own - top)
        raised_near = jnp.exp(scores_near - top)
        total = jnp.sum(raised_own, axis=-1, keepdims=True) + jnp.sum(raised_near, axis=-1, keepdims=True)
        values = slice(wide + chunk.start, wide + chunk.stop)
        mixed = dot(raised_own.astype(BF), keys_values[:keys, values]) + dot(
            raised_near.astype(BF), keys_values[keys:, values]
        )
        mixed = mixed / total
        logs = jnp.where(lane == head, top + jnp.log(total), logs)
        for block in range(low, high):
            piece = mixed[:, (block - low) * LANES : (block - low + 1) * LANES]
            if blocks[block] is None:
                blocks[block] = piece
            else:
                blocks[block] = jnp.where(lane + block * LANES >= first, piece, blocks[block])
    for block, piece in enumerate(blocks):
        out[:, block * LANES : (block + 1) * LANES] = piece.astype(BF)
    top_piece = logs.astype(BF).astype(F32)
    rest = logs - top_piece
    middle = rest.astype(BF).astype(F32)
    rest = rest - middle
    out[:, wide:] = (top_piece + pltpu.roll(middle, heads, 1) + pltpu.roll(rest, 2 * heads, 1)).astype(BF)


def finish_tokens(act, gates, token_out, down, *refs, parts_count):
    parts, back = refs[:parts_count], refs[parts_count]
    count, wide = act.shape
    heads = 16
    size = wide // heads
    logs = []
    for part in parts:
        packed = part[:, wide:].astype(F32)
        logs.append(
            packed + pltpu.roll(packed, LANES - heads, 1) + pltpu.roll(packed, LANES - 2 * heads, 1)
        )
    top = functools.reduce(jnp.maximum, logs)
    weights = [jnp.exp(log - top) for log in logs]
    total = functools.reduce(jnp.add, weights)
    head = lax.broadcasted_iota(jnp.int32, (LANES, wide), 0)
    feature = lax.broadcasted_iota(jnp.int32, (LANES, wide), 1)
    expand = jnp.where((feature >= head * size) & (feature < (head + 1) * size), 1.0, 0.0).astype(BF)
    mixed = jnp.zeros((count, wide), F32)
    for part, weight in zip(parts, weights):
        factor = weight / total
        coarse = factor.astype(BF)
        fine = (factor - coarse.astype(F32)).astype(BF)
        mixed = mixed + (dot(coarse, expand) + dot(fine, expand)) * part[:, :wide].astype(F32)
    gated = (mixed * gates[...]).astype(BF)
    result = (act[...].astype(F32) + dot(gated, token_out[...])).astype(BF)
    back[...] = dot(result, down[...]).astype(BF)


def second_block(
    info, offsets, ids, atoms1, near, far, near_ids, far_ids, own_back, near_back, far_back,
    gain, qkv, out_weight, bias, result, q, k, v, mixed, table, atoms2, *, share, columns
):
    side, column = info[0], info[3]
    rows, channels = atoms1.shape
    gain_row = gain[...]
    weight = qkv[...]
    half = own_back.shape[0]
    tokens = 2 * half
    table[:half, :] = own_back[...]
    table[half:, :] = near_back[...]
    table_ids = token_of(tokens, share, side)
    end = RIM + rows
    first_token = (info[1] * tokens).astype(F32)

    def rim_ids(message):
        packed = message[RIM : RIM + 16, :].astype(F32)
        return (packed[0:1, :RIM] * 64.0 + packed[1:2, :RIM] - first_token).astype(jnp.int32)

    near_rows = near[...].astype(F32) + dot_tn(one_hot(table_ids, rim_ids(near_ids)), table[...])
    project_rim(near_rows.astype(BF), gain_row, weight, k, v, jnp.where(side == 0, end, 0))
    far_token = rim_ids(far_ids)
    beyond = lax.broadcasted_iota(jnp.int32, (RIM, 1), 0) + jnp.where(
        column == 0, -RIM, jnp.where(column == columns - 1, tokens, 4 * tokens)
    )
    far_rows = (
        far[...].astype(F32)
        + dot_tn(one_hot(table_ids, far_token), table[...])
        + dot_tn(one_hot(beyond, far_token), far_back[...])
    )
    project_rim(far_rows.astype(BF), gain_row, weight, k, v, jnp.where(side == 0, 0, end))
    step = 256
    for at in range(0, rows, step):
        member = one_hot(table_ids, ids[:, at : at + step])
        moved = (atoms1[at : at + step, :].astype(F32) + dot_tn(member, table[...])).astype(BF)
        atoms2[at : at + step, :] = moved
        project(moved, gain_row, weight, q, k, v, at)
    attend_windows(offsets, bias, q, k, v, mixed)
    for at in range(0, rows, step):
        part = atoms2[at : at + step, :].astype(F32) + dot(mixed[at : at + step, :], out_weight[...])
        result[at : at + step, :] = part.astype(BF)


def call(kernel, outs, scratch, specs, flops, limit=40):
    return pl.pallas_call(
        kernel,
        out_shape=outs,
        in_specs=specs,
        out_specs=jax.tree.map(lambda _: VMEM, outs),
        scratch_shapes=scratch,
        compiler_params=pltpu.CompilerParams(vmem_limit_bytes=limit * 1024 * 1024),
        cost_estimate=pl.CostEstimate(flops=flops, bytes_accessed=4_000_000, transcendentals=1_000_000),
    )


def body(
    atom_acts, first_gain, first_qkv, first_out, second_gain, second_qkv, second_out, atom_bias, window_start,
    atom_token, up_weight, token_gain, token_weight, token_out, down_weight, pair_bias,
):
    rows, channels = atom_acts.shape
    heads, tok_rows, slots = pair_bias.shape
    wide = token_weight.shape[0]
    row_count, col_count = lax.axis_size("row"), lax.axis_size("col")
    pairs = col_count // 2
    share = tok_rows // col_count
    half = tok_rows // 2
    row, col = lax.axis_index("row"), lax.axis_index("col")
    side, pair = col % 2, col // 2
    info = jnp.stack([side, row, pair, col]).astype(jnp.int32)
    devices = row_count * col_count

    def to_near(x):
        return lax.ppermute(x, "col", [(i, i ^ 1) for i in range(col_count)])

    def to_far(x):
        swap = [(i, (i + 1) % devices if i % 2 else (i - 1) % devices) for i in range(devices)]
        return lax.ppermute(x, ("row", "col"), swap)

    def along_pairs(x, step):
        return lax.ppermute(
            x, "col", [(2 * i + k, 2 * ((i + step) % pairs) + k) for i in range(pairs) for k in range(2)]
        )

    def along_rows(x, step):
        return lax.ppermute(x, "row", [(i, (i + step) % row_count) for i in range(row_count)])

    def rim_of(x, last):
        return lax.dynamic_slice_in_dim(x, jnp.where(last, rows - RIM, 0), RIM, axis=0)

    def message(last):
        acts = rim_of(atom_acts, last)
        ids = rim_of(atom_token, last)
        coded = jnp.stack([ids >> 6, ids & 63]).astype(BF)
        coded = jnp.pad(coded, ((0, 14), (0, channels - RIM)))
        return jnp.concatenate([acts, coded], axis=0)

    near_acts = to_near(message(side == 0))
    far_acts = to_far(message(side == 1))
    split_bias = pair_bias.reshape(heads, pairs, 2, share, slots)
    bias_near = to_near(lax.dynamic_index_in_dim(split_bias, 1 - side, 2, False).reshape(heads, half, slots))

    offsets = window_start - (row * col_count + col) * rows + RIM
    ids = (atom_token - row * tok_rows).reshape(1, rows)
    window_scratch = [
        pltpu.VMEM((rows, channels), BF),
        pltpu.VMEM((rows + 2 * RIM, channels), F32),
        pltpu.VMEM((rows + 2 * RIM, channels), F32),
        pltpu.VMEM((rows, channels), BF),
    ]
    packed_shape = jax.ShapeDtypeStruct((half, wide + LANES), BF)
    atoms1, send, keep = call(
        functools.partial(first_block, share=share),
        [jax.ShapeDtypeStruct((rows, channels), BF), packed_shape, packed_shape],
        window_scratch,
        [SMEM, SMEM] + [VMEM] * 9,
        3_000_000_000,
    )(
        info, offsets, ids, atom_acts, near_acts, far_acts, first_gain.reshape(1, -1), first_qkv, first_out,
        atom_bias, up_weight,
    )

    chip_sum = (keep.astype(F32) + to_near(send).astype(F32)).astype(BF)
    sums = [lax.dynamic_slice_in_dim(chip_sum, pair * share, share, axis=0)]
    for step in range(1, pairs):
        piece = lax.dynamic_slice_in_dim(chip_sum, (pair + step) % pairs * share, share, axis=0)
        sums.append(along_pairs(piece, step))
    share_shape = jax.ShapeDtypeStruct((share, wide), BF)
    gain_row = token_gain.reshape(1, -1)
    act, normed = call(
        functools.partial(mean_tokens, count=len(sums)), [share_shape] * 2, [], [VMEM] * (len(sums) + 1), 1_000_000
    )(*sums, gain_row)

    own_keys = [normed] + [along_rows(normed, step) for step in range(1, row_count)]
    near_keys = [to_near(x) for x in own_keys]
    other_acts = [along_pairs(act, step) for step in range(1, pairs)]
    half_shape = jax.ShapeDtypeStruct((half, wide), BF)
    act_rows, queries, gates = call(
        functools.partial(query_tokens, others=len(other_acts)),
        [half_shape, half_shape, jax.ShapeDtypeStruct((half, wide), F32)],
        [],
        [SMEM] + [VMEM] * (3 + len(other_acts)),
        300_000_000,
    )(info, token_weight, gain_row, act, *other_acts)

    near_atoms = to_near(rim_of(atoms1, side == 0))
    far_atoms = to_far(rim_of(atoms1, side == 1))

    part = call(
        functools.partial(attend_tokens, rows_count=row_count),
        packed_shape,
        [pltpu.VMEM((2 * slots, wide), BF), pltpu.VMEM((2 * slots, 2 * wide), BF)],
        [SMEM] + [VMEM] * (4 + 2 * row_count),
        2_000_000_000,
    )(info, token_weight, queries, pair_bias, bias_near, *own_keys, *near_keys)

    parts = [part] + [along_pairs(part, step) for step in range(1, pairs)]
    own_back = call(
        functools.partial(finish_tokens, parts_count=pairs),
        jax.ShapeDtypeStruct((half, channels), BF),
        [],
        [VMEM] * (4 + pairs),
        200_000_000,
    )(act_rows, gates, token_out, down_weight, *parts)

    near_back = to_near(own_back)
    if share >= RIM:
        last_rows = own_back[half - RIM :]
        first_rows = own_back[:RIM]
    else:
        both = jnp.where(side == 0, jnp.stack([own_back, near_back]), jnp.stack([near_back, own_back]))
        both = both.reshape(2, pairs, share, channels).transpose(1, 0, 2, 3).reshape(tok_rows, channels)
        last_rows = both[tok_rows - RIM :]
        first_rows = both[:RIM]
    far_back = to_far(jnp.where(side == 1, last_rows, first_rows))

    return call(
        functools.partial(second_block, share=share, columns=col_count),
        jax.ShapeDtypeStruct((rows, channels), BF),
        window_scratch + [pltpu.VMEM((tok_rows, channels), BF), pltpu.VMEM((rows, channels), BF)],
        [SMEM, SMEM] + [VMEM] * 13,
        1_500_000_000,
    )(
        info, offsets, ids, atoms1, near_atoms, far_atoms, near_acts, far_acts, own_back, near_back, far_back,
        second_gain.reshape(1, -1), second_qkv, second_out, atom_bias,
    )


def solution(mesh):
    atoms = P(("group", "row", "col"))
    in_specs = (
        P(("group", "row", "col"), None),
        P(), P(), P(), P(), P(), P(),
        P(None, ("group", "row", "col"), None),
        atoms,
        atoms,
        P(), P(), P(), P(), P(),
        P(None, ("group", "row"), "col"),
    )
    out_specs = P(("group", "row", "col"), None)
    return jax.shard_map(body, mesh=mesh, in_specs=in_specs, out_specs=out_specs, check_vma=False)
```

time: 287 us -> 113 us (0.39)
  the two profiles are of different devices: /device:TPU:1 before, /device:TPU:0 now
where the time goes in v1:
time: 113 us; the launch traced here: 112 us
  Pallas kernels  62.8 us (56%)
  waiting for transfers between devices  19.4 us (17%)
  starting transfers between devices  19.3 us (17%)
  local copies, waits for them, and re-layouts  9.43 us (8%)
    pallas_call x1, Pallas kernels, body(): call(functools.partial(second_block, share=share, columns=col_count), jax...  28.1 us
    pallas_call x1, Pallas kernels, body(): call(functools.partial(first_block, share=share), [jax.ShapeDtypeStruct((...  26.6 us
    ppermute x3, starting transfers between devices, to_far(): return lax.ppermute(x, ('row', 'col'), swap)  11.7 us
    ppermute x3, waiting for transfers between devices, along_pairs(): lax.ppermute(x, 'col', [(2 * i + k, 2 * ((i + step) % pairs) + k) for i i...  9.42 us
    unnamed x36, local copies, waits for them, and re-layouts  6.32 us
    ppermute x3, waiting for transfers between devices, along_rows(): lax.ppermute(x, 'row', [(i, (i + step) % row_count) for i in range(row_co...  6.31 us
    pallas_call x1, Pallas kernels, body(): call(functools.partial(attend_tokens, rows_count=row_count), packed_shape...  5.65 us
    ppermute x3, starting transfers between devices, along_rows(): lax.ppermute(x, 'row', [(i, (i + step) % row_count) for i in range(row_co...  4.18 us
  transfers between devices with their start and end apart: 18, of which 8 were waited for; matrix products, arithmetic and copies ran while one was open for 2% of the time, Pallas kernels for 26%

profile of v1, /device:TPU:0, one launch (start us, length us, event | category | flops | bytes accessed | tf_op | source)
XLA Modules:
  0.0 112.3 jit_solution(16704984944451409871)
XLA Ops:
  0.1 0.9 convert_bitcast_fusion.1
  0.9 0.7 constant_dynamic-slice_fusion.5
  1.7 0.5 collective-permute-start
  2.2 5.7 %collective-permute-start.1 = (bf16[80,128]{1,0:T(8,128)(2,1)S(1)}, bf16[80,128]{1,0:T(8,128)(2,1)S(1)}, u32[]{:S(2)}, u32[]{:S(2)}) collective-permute-start(bf16[80,128]{1,0:T(8,128)(2,1)S(1)} %pad_maximum_fusion.1), channel_id=1, source_target_pairs={{0,15},{1,2},{2,1},{3,4},{4,3},{5,6},{6,5},{7,8},{8,7},{9,10},{10,... | collective-permute-start | bytes 61448 | tf_op jit(solution)/shard_map/ppermute | solution.py:333
  7.9 2.3 %constant_dynamic-slice_fusion = bf16[16,2,1,64,256]{4,3,2,1,0:T(8,128)(2,1)} fusion(bf16[16,2,2,64,256]{4,3,2,1,0:T(8,128)(2,1)} %bitcast.19, s32[]{:T(128)S(6)} %select_n.57), kind=kLoop, calls=%fused_computation.18 | loop fusion | bytes 2097156 | tf_op jit(solution)/shard_map/jit(dynamic_index_in_dim)/dynamic_slice | solution.py:356
  10.3 0.0 collective-permute-start.7
  10.3 0.1 pad_add_fusion.info
  10.4 0.0 collective-permute-done.near.near_ids
  10.4 0.0 collective-permute-done.1.far.far_ids
  10.5 0.0 copy-start.6
  10.5 1.6 %copy-done.6 = bf16[4,2048,128]{2,1,0:T(8,128)(2,1)S(1)} copy-done((bf16[4,2048,128]{2,1,0:T(8,128)(2,1)S(1)}, bf16[4,2048,128]{2,1,0:T(8,128)(2,1)}, u32[]{:S(2)}) %copy-start.6) | copy-done | bytes 2097176
  12.1 26.6 %shard_map.154 = (bf16[2048,128]{1,0:T(8,128)(2,1)S(1)}, bf16[128,896]{1,0:T(8,128)(2,1)S(1)}, bf16[128,896]{1,0:T(8,128)(2,1)S(1)}) custom-call(s32[4]{0:T(128)S(1)} %pad_add_fusion.info, s32[64]{0:T(128)S(1)} %subtract_add_fusion.offsets, s32[1,2048]{1,0:T(1,128)S(1)} %bitcast.20, bf16[2048,128]{1,0:T(8,128)(2,1)S(1)} %copy-done.5, ...), custom_call_target="tpu_custom_call" | custom-call | flops 3000000000 | bytes 4000000 | tf_op jit(solution)/shard_map/pallas_call | solution.py:367
  38.7 0.5 collective-permute-start.4
  39.2 1.1 collective-permute-done.4
  40.4 0.1 add_convert_fusion
  40.4 0.0 copy-start.2
  40.5 0.1 collective-permute-start.5
  40.6 5.4 %collective-permute-done.5.refs_1_ = bf16[64,896]{1,0:T(8,128)(2,1)S(1)} collective-permute-done((bf16[64,896]{1,0:T(8,128)(2,1)S(1)}, bf16[64,896]{1,0:T(8,128)(2,1)S(1)}, u32[]{:S(2)}, u32[]{:S(2)}) %collective-permute-start.5) | collective-permute-done | bytes 114720 | tf_op jit(solution)/shard_map/ppermute | solution.py:336
  46.0 0.3 shard_map.155
  46.3 0.4 collective-permute-start.6
  46.7 0.0 collective-permute-start.8
  46.7 4.2 %collective-permute-start.9 = (bf16[64,768]{1,0:T(8,128)(2,1)S(1)}, bf16[64,768]{1,0:T(8,128)(2,1)S(1)}, u32[]{:S(2)}, u32[]{:S(2)}) collective-permute-start(bf16[64,768]{1,0:T(8,128)(2,1)S(1)} %get-tuple-element.20.refs_0_), channel_id=1, source_target_pairs={{0,8},{4,12},{8,0},{12,4},{1,9},{5,13},{9,1},{13,5},{2,10},{6,14},... | collective-permute-start | bytes 294920 | tf_op jit(solution)/shard_map/ppermute | solution.py:341
  50.8 0.0 collective-permute-start.10
  50.9 0.1 collective-permute-done.6.refs_0_
  51.0 3.3 %collective-permute-done.8.refs_1_ = bf16[64,768]{1,0:T(8,128)(2,1)S(1)} collective-permute-done((bf16[64,768]{1,0:T(8,128)(2,1)S(1)}, bf16[64,768]{1,0:T(8,128)(2,1)S(1)}, u32[]{:S(2)}, u32[]{:S(2)}) %collective-permute-start.8) | collective-permute-done | bytes 98336 | tf_op jit(solution)/shard_map/ppermute | solution.py:341
  54.3 0.0 collective-permute-start.12
  54.3 2.7 %collective-permute-done.9.refs_2_ = bf16[64,768]{1,0:T(8,128)(2,1)S(1)} collective-permute-done((bf16[64,768]{1,0:T(8,128)(2,1)S(1)}, bf16[64,768]{1,0:T(8,128)(2,1)S(1)}, u32[]{:S(2)}, u32[]{:S(2)}) %collective-permute-start.9) | collective-permute-done | bytes 98336 | tf_op jit(solution)/shard_map/ppermute | solution.py:341
  57.0 0.0 collective-permute-start.13
  57.0 0.3 collective-permute-done.10.refs_3_
  57.3 0.2 collective-permute-start.14
  57.5 2.3 %copy-done = bf16[768,3072]{1,0:T(8,128)(2,1)S(1)} copy-done((bf16[768,3072]{1,0:T(8,128)(2,1)S(1)}, bf16[768,3072]{1,0:T(8,128)(2,1)}, u32[]{:S(2)}) %copy-start) | copy-done | bytes 4718616
  59.9 1.2 %shard_map.156 = (bf16[128,768]{1,0:T(8,128)(2,1)S(1)}, bf16[128,768]{1,0:T(8,128)(2,1)S(1)}, f32[128,768]{1,0:T(8,128)S(1)}) custom-call(s32[4]{0:T(128)S(1)} %pad_add_fusion.info, bf16[768,3072]{1,0:T(8,128)(2,1)S(1)} %copy-done, f32[1,768]{1,0:T(1,128)S(1)} %reshape.21.refs_2_.gain, bf16[64,768]{1,0:T(8,128)(2,1)S(1)} %get-tuple-element.16.own_act, ...), custom_call_target="tpu_custom_call" | custom-call | flops 300000000 | bytes 4000000 | tf_op jit(solution)/shard_map/pallas_call | solution.py:393
  61.1 0.0 collective-permute-done.12.refs_5_
  61.1 0.0 copy-start.1
  61.1 2.3 %copy-done.1 = bf16[768,3072]{1,0:T(8,128)(2,1)S(1)} copy-done((bf16[768,3072]{1,0:T(8,128)(2,1)S(1)}, bf16[768,3072]{1,0:T(8,128)(2,1)}, u32[]{:S(2)}) %copy-start.1) | copy-done | bytes 4718616
  63.5 5.6 %shard_map.157.refs_0_ = bf16[128,896]{1,0:T(8,128)(2,1)S(1)} custom-call(s32[4]{0:T(128)S(1)} %pad_add_fusion.info, bf16[768,3072]{1,0:T(8,128)(2,1)S(1)} %copy-done.1, bf16[128,768]{1,0:T(8,128)(2,1)S(1)} %get-tuple-element.19.queries, bf16[16,256,256]{2,1,0:T(8,128)(2,1)S(1)} %copy-done.2, bf16[16,128,256]{2,1,0:T(8,128)(2,1)S(1)} %collective-permute-done.7.bias_near, ...), custom_call_target="tpu_custom_call" | custom-call | flops 2000000000 | bytes 4000000 | tf_op jit(solution)/shard_map/pallas_call | solution.py:404
  69.1 0.0 copy-start.7
  69.1 0.0 copy-start.10
  69.2 0.0 copy-start.12
  69.2 0.0 copy-start.14
  69.2 1.6 %collective-permute-start.15 = (bf16[128,896]{1,0:T(8,128)(2,1)S(1)}, bf16[128,896]{1,0:T(8,128)(2,1)S(1)}, u32[]{:S(2)}, u32[]{:S(2)}) collective-permute-start(bf16[128,896]{1,0:T(8,128)(2,1)S(1)} %shard_map.157.refs_0_), channel_id=1, source_target_pairs={{0,2},{1,3},{2,0},{3,1},{4,6},{5,7},{6,4},{7,5},{8,10},{9,11},{10,... | collective-permute-start | bytes 688136 | tf_op jit(solution)/shard_map/ppermute | solution.py:336
  70.8 2.6 %collective-permute-start.3 = (bf16[64,128]{1,0:T(8,128)(2,1)S(1)}, bf16[64,128]{1,0:T(8,128)(2,1)S(1)}, u32[]{:S(2)}, u32[]{:S(2)}) collective-permute-start(bf16[64,128]{1,0:T(8,128)(2,1)S(1)} %get-tuple-element.21), channel_id=1, source_target_pairs={{0,15},{1,2},{2,1},{3,4},{4,3},{5,6},{6,5},{7,8},{8,7},{9,10},{10,... | collective-permute-start | bytes 49160 | tf_op jit(solution)/shard_map/ppermute | solution.py:333
  73.4 3.9 %collective-permute-done.15.refs_1_ = bf16[128,896]{1,0:T(8,128)(2,1)S(1)} collective-permute-done((bf16[128,896]{1,0:T(8,128)(2,1)S(1)}, bf16[128,896]{1,0:T(8,128)(2,1)S(1)}, u32[]{:S(2)}, u32[]{:S(2)}) %collective-permute-start.15) | collective-permute-done | bytes 229408 | tf_op jit(solution)/shard_map/ppermute | solution.py:336
  77.3 0.9 shard_map.158.own_back
  78.2 0.1 collective-permute-start.16
  78.3 3.4 %collective-permute-start.17 = (bf16[64,128]{1,0:T(8,128)(2,1)S(1)}, bf16[64,128]{1,0:T(8,128)(2,1)S(1)}, u32[]{:S(2)}, u32[]{:S(2)}) collective-permute-start(bf16[64,128]{1,0:T(8,128)(2,1)S(1)} %slice_select_fusion), channel_id=1, source_target_pairs={{0,15},{1,2},{2,1},{3,4},{4,3},{5,6},{6,5},{7,8},{8,7},{9,10},{10,... | collective-permute-start | bytes 49160 | tf_op jit(solution)/shard_map/ppermute | solution.py:333
  81.7 2.5 %collective-permute-done.17.far_back = bf16[64,128]{1,0:T(8,128)(2,1)S(1)} collective-permute-done((bf16[64,128]{1,0:T(8,128)(2,1)S(1)}, bf16[64,128]{1,0:T(8,128)(2,1)S(1)}, u32[]{:S(2)}, u32[]{:S(2)}) %collective-permute-start.17) | collective-permute-done | bytes 16416 | tf_op jit(solution)/shard_map/ppermute | solution.py:333
  84.2 28.1 %shard_map.159 = bf16[2048,128]{1,0:T(8,128)(2,1)} custom-call(s32[4]{0:T(128)S(1)} %pad_add_fusion.info, s32[64]{0:T(128)S(1)} %subtract_add_fusion.offsets, s32[1,2048]{1,0:T(1,128)S(1)} %bitcast.21, bf16[2048,128]{1,0:T(8,128)(2,1)S(1)} %get-tuple-element.13.atoms1, bf16[64,128]{1,0:T(8,128)(2,1)S(1)} %collective-permute-done.2.near, ...), custom_call_target="tpu_custom_call" | custom-call | flops 1500000000 | bytes 4000000 | tf_op jit(solution)/shard_map/pallas_call | solution.py:432
  (45 shorter events, 0.2 us)
Async XLA Ops:
  0.0 10.3 %copy-start.15 = (s32[2048]{0:T(1024)S(1)}, s32[2048]{0:T(1024)}, u32[]{:S(2)}) copy-start(s32[2048]{0:T(1024)} %param.25) | copy-start | bytes 24580
  0.0 10.4 %copy-start.5 = (bf16[2048,128]{1,0:T(8,128)(2,1)S(1)}, bf16[2048,128]{1,0:T(8,128)(2,1)}, u32[]{:S(2)}) copy-start(bf16[2048,128]{1,0:T(8,128)(2,1)} %acts.1) | copy-start | bytes 1572868
  0.0 10.3 %copy-start.17 = (s32[64]{0:T(128)S(1)}, s32[64]{0:T(128)}, u32[]{:S(2)}) copy-start(s32[64]{0:T(128)} %param.24) | copy-start | bytes 772
  0.0 10.4 %copy-start.13 = (f32[128]{0:T(128)S(1)}, f32[128]{0:T(128)}, u32[]{:S(2)}) copy-start(f32[128]{0:T(128)} %param.17) | copy-start | bytes 1540
  0.0 10.4 %copy-start.9 = (bf16[128,384]{1,0:T(8,128)(2,1)S(1)}, bf16[128,384]{1,0:T(8,128)(2,1)}, u32[]{:S(2)}) copy-start(bf16[128,384]{1,0:T(8,128)(2,1)} %qkv.2) | copy-start | bytes 294916
  0.0 10.4 %copy-start.11 = (bf16[128,128]{1,0:T(8,128)(2,1)S(1)}, bf16[128,128]{1,0:T(8,128)(2,1)}, u32[]{:S(2)}) copy-start(bf16[128,128]{1,0:T(8,128)(2,1)} %out_weight.2) | copy-start | bytes 98308
  0.0 10.4 %copy-start.8 = (bf16[128,768]{1,0:T(8,128)(2,1)S(1)}, bf16[128,768]{1,0:T(8,128)(2,1)}, u32[]{:S(2)}) copy-start(bf16[128,768]{1,0:T(8,128)(2,1)} %up.1) | copy-start | bytes 589828
  1.7 8.7 %collective-permute-start = (bf16[80,128]{1,0:T(8,128)(2,1)S(1)}, bf16[80,128]{1,0:T(8,128)(2,1)S(1)}, u32[]{:S(2)}, u32[]{:S(2)}) collective-permute-start(bf16[80,128]{1,0:T(8,128)(2,1)S(1)} %pad_maximum_fusion), channel_id=1, source_target_pairs={{0,1},{1,0},{2,3},{3,2},{4,5},{5,4},{6,7},{7,6},{8,9},{9,8},{10,11... | collective-permute-start | bytes 61448 | tf_op jit(solution)/shard_map/ppermute | solution.py:329
  2.2 8.2 %collective-permute-start.1 = (bf16[80,128]{1,0:T(8,128)(2,1)S(1)}, bf16[80,128]{1,0:T(8,128)(2,1)S(1)}, u32[]{:S(2)}, u32[]{:S(2)}) collective-permute-start(bf16[80,128]{1,0:T(8,128)(2,1)S(1)} %pad_maximum_fusion.1), channel_id=1, source_target_pairs={{0,15},{1,2},{2,1},{3,4},{4,3},{5,6},{6,5},{7,8},{8,7},{9,10},{10,... | collective-permute-start | bytes 61448 | tf_op jit(solution)/shard_map/ppermute | solution.py:333
  10.3 50.8 %collective-permute-start.7 = (bf16[16,128,256]{2,1,0:T(8,128)(2,1)}, bf16[16,128,256]{2,1,0:T(8,128)(2,1)S(1)}, u32[]{:S(2)}, u32[]{:S(2)}) collective-permute-start(bf16[16,128,256]{2,1,0:T(8,128)(2,1)} %bitcast.11), channel_id=1, source_target_pairs={{0,1},{1,0},{2,3},{3,2},{4,5},{5,4},{6,7},{7,6},{8,9},{9,8},{10,11... | collective-permute-start | bytes 3145736 | tf_op jit(solution)/shard_map/ppermute | solution.py:329
  10.5 1.6 %copy-start.6 = (bf16[4,2048,128]{2,1,0:T(8,128)(2,1)S(1)}, bf16[4,2048,128]{2,1,0:T(8,128)(2,1)}, u32[]{:S(2)}) copy-start(bf16[4,2048,128]{2,1,0:T(8,128)(2,1)} %bias.3) | copy-start | bytes 6291460
  12.0 28.5 %copy-start.16 = (f32[768]{0:T(1024)S(1)}, f32[768]{0:T(1024)}, u32[]{:S(2)}) copy-start(f32[768]{0:T(1024)} %param.27) | copy-start | bytes 9220
  38.7 1.7 %collective-permute-start.4 = (bf16[128,896]{1,0:T(8,128)(2,1)S(1)}, bf16[128,896]{1,0:T(8,128)(2,1)S(1)}, u32[]{:S(2)}, u32[]{:S(2)}) collective-permute-start(bf16[128,896]{1,0:T(8,128)(2,1)S(1)} %get-tuple-element.15), channel_id=1, source_target_pairs={{0,1},{1,0},{2,3},{3,2},{4,5},{5,4},{6,7},{7,6},{8,9},{9,8},{10,11... | collective-permute-start | bytes 688136 | tf_op jit(solution)/shard_map/ppermute | solution.py:329
  40.4 20.7 %copy-start.2 = (bf16[16,256,256]{2,1,0:T(8,128)(2,1)S(1)}, bf16[16,256,256]{2,1,0:T(8,128)(2,1)}, u32[]{:S(2)}) copy-start(bf16[16,256,256]{2,1,0:T(8,128)(2,1)} %bias_own.1) | copy-start | bytes 6291460
  40.5 5.5 %collective-permute-start.5 = (bf16[64,896]{1,0:T(8,128)(2,1)S(1)}, bf16[64,896]{1,0:T(8,128)(2,1)S(1)}, u32[]{:S(2)}, u32[]{:S(2)}) collective-permute-start(bf16[64,896]{1,0:T(8,128)(2,1)S(1)} %get-tuple-element.25), channel_id=1, source_target_pairs={{0,2},{1,3},{2,0},{3,1},{4,6},{5,7},{6,4},{7,5},{8,10},{9,11},{10,... | collective-permute-start | bytes 344072 | tf_op jit(solution)/shard_map/ppermute | solution.py:336
  46.3 4.7 %collective-permute-start.6 = (bf16[64,768]{1,0:T(8,128)(2,1)S(1)}, bf16[64,768]{1,0:T(8,128)(2,1)S(1)}, u32[]{:S(2)}, u32[]{:S(2)}) collective-permute-start(bf16[64,768]{1,0:T(8,128)(2,1)S(1)} %get-tuple-element.16.own_act), channel_id=1, source_target_pairs={{0,2},{1,3},{2,0},{3,1},{4,6},{5,7},{6,4},{7,5},{8,10},{9,11},{10,... | collective-permute-start | bytes 294920 | tf_op jit(solution)/shard_map/ppermute | solution.py:336
  46.7 7.7 %collective-permute-start.8 = (bf16[64,768]{1,0:T(8,128)(2,1)S(1)}, bf16[64,768]{1,0:T(8,128)(2,1)S(1)}, u32[]{:S(2)}, u32[]{:S(2)}) collective-permute-start(bf16[64,768]{1,0:T(8,128)(2,1)S(1)} %get-tuple-element.20.refs_0_), channel_id=1, source_target_pairs={{0,4},{4,8},{8,12},{12,0},{1,5},{5,9},{9,13},{13,1},{2,6},{6,10},{... | collective-permute-start | bytes 294920 | tf_op jit(solution)/shard_map/ppermute | solution.py:341
  46.7 10.3 %collective-permute-start.9 = (bf16[64,768]{1,0:T(8,128)(2,1)S(1)}, bf16[64,768]{1,0:T(8,128)(2,1)S(1)}, u32[]{:S(2)}, u32[]{:S(2)}) collective-permute-start(bf16[64,768]{1,0:T(8,128)(2,1)S(1)} %get-tuple-element.20.refs_0_), channel_id=1, source_target_pairs={{0,8},{4,12},{8,0},{12,4},{1,9},{5,13},{9,1},{13,5},{2,10},{6,14},... | collective-permute-start | bytes 294920 | tf_op jit(solution)/shard_map/ppermute | solution.py:341
  50.8 6.5 %collective-permute-start.10 = (bf16[64,768]{1,0:T(8,128)(2,1)S(1)}, bf16[64,768]{1,0:T(8,128)(2,1)S(1)}, u32[]{:S(2)}, u32[]{:S(2)}) collective-permute-start(bf16[64,768]{1,0:T(8,128)(2,1)S(1)} %get-tuple-element.20.refs_0_), channel_id=1, source_target_pairs={{0,12},{4,0},{8,4},{12,8},{1,13},{5,1},{9,5},{13,9},{2,14},{6,2},{... | collective-permute-start | bytes 294920 | tf_op jit(solution)/shard_map/ppermute | solution.py:341
  51.0 10.1 %collective-permute-start.11 = (bf16[64,768]{1,0:T(8,128)(2,1)S(1)}, bf16[64,768]{1,0:T(8,128)(2,1)S(1)}, u32[]{:S(2)}, u32[]{:S(2)}) collective-permute-start(bf16[64,768]{1,0:T(8,128)(2,1)S(1)} %get-tuple-element.20.refs_0_), channel_id=1, source_target_pairs={{0,1},{1,0},{2,3},{3,2},{4,5},{5,4},{6,7},{7,6},{8,9},{9,8},{10,11... | collective-permute-start | bytes 294920 | tf_op jit(solution)/shard_map/ppermute | solution.py:329
  54.3 6.7 %collective-permute-start.12 = (bf16[64,768]{1,0:T(8,128)(2,1)S(1)}, bf16[64,768]{1,0:T(8,128)(2,1)S(1)}, u32[]{:S(2)}, u32[]{:S(2)}) collective-permute-start(bf16[64,768]{1,0:T(8,128)(2,1)S(1)} %collective-permute-done.8.refs_1_), channel_id=1, source_target_pairs={{0,1},{1,0},{2,3},{3,2},{4,5},{5,4},{6,7},{7,6},{8,9},{9,8},{10,11... | collective-permute-start | bytes 294920 | tf_op jit(solution)/shard_map/ppermute | solution.py:329
  57.0 4.1 %collective-permute-start.13 = (bf16[64,768]{1,0:T(8,128)(2,1)S(1)}, bf16[64,768]{1,0:T(8,128)(2,1)S(1)}, u32[]{:S(2)}, u32[]{:S(2)}) collective-permute-start(bf16[64,768]{1,0:T(8,128)(2,1)S(1)} %collective-permute-done.9.refs_2_), channel_id=1, source_target_pairs={{0,1},{1,0},{2,3},{3,2},{4,5},{5,4},{6,7},{7,6},{8,9},{9,8},{10,11... | collective-permute-start | bytes 294920 | tf_op jit(solution)/shard_map/ppermute | solution.py:329
  57.3 3.8 %collective-permute-start.14 = (bf16[64,768]{1,0:T(8,128)(2,1)S(1)}, bf16[64,768]{1,0:T(8,128)(2,1)S(1)}, u32[]{:S(2)}, u32[]{:S(2)}) collective-permute-start(bf16[64,768]{1,0:T(8,128)(2,1)S(1)} %collective-permute-done.10.refs_3_), channel_id=1, source_target_pairs={{0,1},{1,0},{2,3},{3,2},{4,5},{5,4},{6,7},{7,6},{8,9},{9,8},{10,11... | collective-permute-start | bytes 294920 | tf_op jit(solution)/shard_map/ppermute | solution.py:329
  57.5 2.3 %copy-start = (bf16[768,3072]{1,0:T(8,128)(2,1)S(1)}, bf16[768,3072]{1,0:T(8,128)(2,1)}, u32[]{:S(2)}) copy-start(bf16[768,3072]{1,0:T(8,128)(2,1)} %weight.3) | copy-start | bytes 14155780
  61.1 2.3 %copy-start.1 = (bf16[768,3072]{1,0:T(8,128)(2,1)S(1)}, bf16[768,3072]{1,0:T(8,128)(2,1)}, u32[]{:S(2)}) copy-start(bf16[768,3072]{1,0:T(8,128)(2,1)} %weight.3) | copy-start | bytes 14155780
  63.5 13.8 %copy-start.3 = (bf16[768,768]{1,0:T(8,128)(2,1)S(1)}, bf16[768,768]{1,0:T(8,128)(2,1)}, u32[]{:S(2)}) copy-start(bf16[768,768]{1,0:T(8,128)(2,1)} %token_out.1) | copy-start | bytes 3538948
  63.5 13.8 %copy-start.4 = (bf16[768,128]{1,0:T(8,128)(2,1)S(1)}, bf16[768,128]{1,0:T(8,128)(2,1)}, u32[]{:S(2)}) copy-start(bf16[768,128]{1,0:T(8,128)(2,1)} %down.1) | copy-start | bytes 589828
  69.1 15.1 %copy-start.7 = (bf16[4,2048,128]{2,1,0:T(8,128)(2,1)S(1)}, bf16[4,2048,128]{2,1,0:T(8,128)(2,1)}, u32[]{:S(2)}) copy-start(bf16[4,2048,128]{2,1,0:T(8,128)(2,1)} %bias.3) | copy-start | bytes 6291460
  69.1 15.0 %copy-start.10 = (bf16[128,384]{1,0:T(8,128)(2,1)S(1)}, bf16[128,384]{1,0:T(8,128)(2,1)}, u32[]{:S(2)}) copy-start(bf16[128,384]{1,0:T(8,128)(2,1)} %qkv.3) | copy-start | bytes 294916
  69.2 15.0 %copy-start.12 = (bf16[128,128]{1,0:T(8,128)(2,1)S(1)}, bf16[128,128]{1,0:T(8,128)(2,1)}, u32[]{:S(2)}) copy-start(bf16[128,128]{1,0:T(8,128)(2,1)} %out_weight.3) | copy-start | bytes 98308
  69.2 15.0 %copy-start.14 = (f32[128]{0:T(128)S(1)}, f32[128]{0:T(128)}, u32[]{:S(2)}) copy-start(f32[128]{0:T(128)} %param.20) | copy-start | bytes 1540
  69.2 8.1 %collective-permute-start.15 = (bf16[128,896]{1,0:T(8,128)(2,1)S(1)}, bf16[128,896]{1,0:T(8,128)(2,1)S(1)}, u32[]{:S(2)}, u32[]{:S(2)}) collective-permute-start(bf16[128,896]{1,0:T(8,128)(2,1)S(1)} %shard_map.157.refs_0_), channel_id=1, source_target_pairs={{0,2},{1,3},{2,0},{3,1},{4,6},{5,7},{6,4},{7,5},{8,10},{9,11},{10,... | collective-permute-start | bytes 688136 | tf_op jit(solution)/shard_map/ppermute | solution.py:336
  70.8 10.9 %collective-permute-start.2 = (bf16[64,128]{1,0:T(8,128)(2,1)S(1)}, bf16[64,128]{1,0:T(8,128)(2,1)S(1)}, u32[]{:S(2)}, u32[]{:S(2)}) collective-permute-start(bf16[64,128]{1,0:T(8,128)(2,1)S(1)} %get-tuple-element.22), channel_id=1, source_target_pairs={{0,1},{1,0},{2,3},{3,2},{4,5},{5,4},{6,7},{7,6},{8,9},{9,8},{10,11... | collective-permute-start | bytes 49160 | tf_op jit(solution)/shard_map/ppermute | solution.py:329
  70.8 10.9 %collective-permute-start.3 = (bf16[64,128]{1,0:T(8,128)(2,1)S(1)}, bf16[64,128]{1,0:T(8,128)(2,1)S(1)}, u32[]{:S(2)}, u32[]{:S(2)}) collective-permute-start(bf16[64,128]{1,0:T(8,128)(2,1)S(1)} %get-tuple-element.21), channel_id=1, source_target_pairs={{0,15},{1,2},{2,1},{3,4},{4,3},{5,6},{6,5},{7,8},{8,7},{9,10},{10,... | collective-permute-start | bytes 49160 | tf_op jit(solution)/shard_map/ppermute | solution.py:333
  78.2 6.0 %collective-permute-start.16 = (bf16[128,128]{1,0:T(8,128)(2,1)S(1)}, bf16[128,128]{1,0:T(8,128)(2,1)S(1)}, u32[]{:S(2)}, u32[]{:S(2)}) collective-permute-start(bf16[128,128]{1,0:T(8,128)(2,1)S(1)} %shard_map.158.own_back), channel_id=1, source_target_pairs={{0,1},{1,0},{2,3},{3,2},{4,5},{5,4},{6,7},{7,6},{8,9},{9,8},{10,11... | collective-permute-start | bytes 98312 | tf_op jit(solution)/shard_map/ppermute | solution.py:329
  78.3 5.9 %collective-permute-start.17 = (bf16[64,128]{1,0:T(8,128)(2,1)S(1)}, bf16[64,128]{1,0:T(8,128)(2,1)S(1)}, u32[]{:S(2)}, u32[]{:S(2)}) collective-permute-start(bf16[64,128]{1,0:T(8,128)(2,1)S(1)} %slice_select_fusion), channel_id=1, source_target_pairs={{0,15},{1,2},{2,1},{3,4},{4,3},{5,6},{6,5},{7,8},{8,7},{9,10},{10,... | collective-permute-start | bytes 49160 | tf_op jit(solution)/shard_map/ppermute | solution.py:333

commit v2 on v1

--- a/solution.py
+++ b/solution.py
@@ -53,26 +53,16 @@
 def project(rows, gain, qkv, q, k, v, at):
     channels = rows.shape[1]
     packed = dot(norm_rows(rows.astype(F32), gain).astype(BF), qkv).astype(BF)
-    place = slice(RIM + at, RIM + at + rows.shape[0])
-    q[at : at + rows.shape[0], :] = packed[:, :channels]
+    place = slice(at, at + rows.shape[0])
+    q[place, :] = packed[:, :channels]
     k[place, :] = packed[:, channels : 2 * channels].astype(F32)
     v[place, :] = packed[:, 2 * channels :].astype(F32)
 
 
-def project_rim(rows, gain, qkv, k, v, at):
-    channels = rows.shape[1]
-    normed = norm_rows(rows.astype(F32), gain).astype(BF)
-    packed = dot(normed, qkv[:, channels:]).astype(BF).astype(F32)
-    place = pl.ds(pl.multiple_of(at, RIM), RIM)
-    k[place, :] = packed[:, :channels]
-    v[place, :] = packed[:, channels:]
-
-
-def attend_windows(offsets, bias, q, k, v, mixed):
-    heads, atom_rows, span = bias.shape
-    windows = offsets.shape[0]
-    block = atom_rows // windows
+def attend_windows(places, bias, q, k, v, mixed):
+    heads, _, span = bias.shape
     channels = q.shape[1]
+    block = span - 3 * RIM // 2
     size = channels // heads
     scale = 1.0 / math.sqrt(size)
     stacked = heads * block
@@ -80,46 +70,97 @@
     head_lane = lax.broadcasted_iota(jnp.int32, (stacked, channels), 1) // size
     own_head = jnp.where(head_row == head_lane, 1.0, 0.0).astype(BF)
     lane_head = lax.broadcasted_iota(jnp.int32, (block, channels), 1) // size
-
-    def one_window(window, carry):
-        begin = offsets[window]
-        anchor = pl.multiple_of(window * block, block)
-        keys = k[pl.ds(begin, span), :].astype(BF)
-        values = v[pl.ds(begin, span), :].astype(BF)
-        query = q[pl.ds(anchor, block), :]
-        spread = jnp.concatenate([query] * heads, axis=0) * own_head
-        tile = bias[:, pl.ds(anchor, block), :].reshape(stacked, span).astype(F32)
-        scores = dot_nt(spread, keys) * scale + tile
-        top = jnp.max(scores, axis=-1, keepdims=True)
-        raised = jnp.exp(scores - top)
-        weights = (raised / jnp.sum(raised, axis=-1, keepdims=True)).astype(BF)
+    ones = jnp.ones((span, channels), BF)
+
+    def picked(stack):
+        out = stack[:block]
+        for head in range(1, heads):
+            out = jnp.where(lane_head == head, stack[head * block : (head + 1) * block], out)
+        return out
+
+    scores = []
+    for query_at, _, key_at in places:
+        spread = jnp.concatenate([q[pl.ds(query_at, block), :]] * heads, axis=0) * own_head
+        scores.append(dot_nt(spread, k[pl.ds(key_at, span), :].astype(BF)))
+    raised = []
+    for (_, bias_at, _), score in zip(places, scores):
+        tile = bias[:, pl.ds(bias_at, block), :].reshape(stacked, span).astype(F32)
+        score = score * scale + tile
+        raised.append(jnp.exp(score - jnp.max(score, axis=-1, keepdims=True)).astype(BF))
+    for (query_at, _, key_at), weights in zip(places, raised):
+        values = jnp.concatenate([v[pl.ds(key_at, span), :].astype(BF), ones], axis=1)
         out = dot(weights, values)
-        picked = out[:block]
-        for head in range(1, heads):
-            picked = jnp.where(lane_head == head, out[head * block : (head + 1) * block], picked)
-        mixed[pl.ds(anchor, block), :] = picked.astype(BF)
+        mixed[pl.ds(query_at, block), :] = (picked(out[:, :channels]) / picked(out[:, channels:])).astype(BF)
+
+
+def inner_windows(offsets, bias, q, k, v, mixed, edge_q, edge_k, edge_v):
+    windows = offsets.shape[0]
+    rows = q.shape[0]
+    block = rows // windows
+    edge = RIM // block
+    group = next(size for size in (15, 12, 10, 6, 5, 4, 3, 2, 1) if (windows - 2 * edge) % size == 0)
+
+    def one_group(step, carry):
+        places = []
+        for member in range(group):
+            window = edge + step * group + member
+            at = pl.multiple_of(window * block, block)
+            places.append((at, at, offsets[window] - RIM))
+        attend_windows(places, bias, q, k, v, mixed)
         return carry
 
-    lax.fori_loop(0, windows, one_window, 0, unroll=4)
-
-
-def first_block(
-    info, offsets, ids, acts, near, far, gain, qkv, out_weight, bias, up, atoms, send, keep, q, k, v, mixed, *, share
+    lax.fori_loop(0, (windows - 2 * edge) // group, one_group, 0)
+    edge_q[:RIM, :] = q[:RIM, :]
+    edge_q[RIM:, :] = q[rows - RIM :, :]
+    for source, target in ((k, edge_k), (v, edge_v)):
+        target[: 2 * RIM, :] = source[: 2 * RIM, :]
+        target[2 * RIM :, :] = source[rows - 2 * RIM :, :]
+
+
+def edge_windows(offsets, bias, gain, qkv, near, far, side, edge_q, edge_k, edge_v, k, v, mixed):
+    windows = offsets.shape[0]
+    rows = bias.shape[1]
+    channels = edge_q.shape[1]
+    block = rows // windows
+    edge = RIM // block
+    for source, target in ((edge_k, k), (edge_v, v)):
+        target[RIM : 3 * RIM, :] = source[: 2 * RIM, :]
+        target[3 * RIM : 5 * RIM, :] = source[2 * RIM :, :]
+    normed = norm_rows(jnp.concatenate([near, far], axis=0), gain).astype(BF)
+    packed = dot(normed, qkv[:, channels:]).astype(BF).astype(F32)
+    near_at = pl.multiple_of(jnp.where(side == 0, 5 * RIM, 0), RIM)
+    far_at = pl.multiple_of(5 * RIM - near_at, RIM)
+    for at, part in ((near_at, packed[:RIM]), (far_at, packed[RIM:])):
+        k[pl.ds(at, RIM), :] = part[:, :channels]
+        v[pl.ds(at, RIM), :] = part[:, channels:]
+    places = []
+    for member in range(edge):
+        places.append((member * block, member * block, offsets[member]))
+    for member in range(edge):
+        window = windows - edge + member
+        places.append((RIM + member * block, window * block, offsets[window] - (rows - 4 * RIM)))
+    attend_windows(places, bias, edge_q, k, v, mixed)
+
+
+def first_inner(offsets, acts, gain, qkv, bias, mixed, edge_q, edge_k, edge_v, q, k, v):
+    step = 256
+    for at in range(0, acts.shape[0], step):
+        project(acts[at : at + step, :], gain[...], qkv[...], q, k, v, at)
+    inner_windows(offsets, bias, q, k, v, mixed, edge_q, edge_k, edge_v)
+
+
+def first_edge(
+    info, offsets, ids, acts, near, far, gain, qkv, out_weight, bias, up, mixed, edge_q, edge_k, edge_v,
+    atoms, send, keep, k, v, edge_mixed, *, share
 ):
     side = info[0]
-    rows, channels = acts.shape
-    gain_row = gain[...]
-    weight = qkv[...]
-    end = RIM + rows
-    project_rim(near[:RIM, :], gain_row, weight, k, v, jnp.where(side == 0, end, 0))
-    project_rim(far[:RIM, :], gain_row, weight, k, v, jnp.where(side == 0, 0, end))
+    rows = acts.shape[0]
+    edge_windows(
+        offsets, bias, gain[...], qkv[...], near[:RIM, :].astype(F32), far[:RIM, :].astype(F32), side,
+        edge_q, edge_k, edge_v, k, v, edge_mixed,
+    )
+    close_rows(acts, mixed, edge_mixed, out_weight, atoms)
     step = 256
-    for at in range(0, rows, step):
-        project(acts[at : at + step, :], gain_row, weight, q, k, v, at)
-    attend_windows(offsets, bias, q, k, v, mixed)
-    for at in range(0, rows, step):
-        part = acts[at : at + step, :].astype(F32) + dot(mixed[at : at + step, :], out_weight[...])
-        atoms[at : at + step, :] = part.astype(BF)
     tokens = 2 * send.shape[0]
     half = tokens // 2
     member = one_hot(token_of(tokens, share, 1 - side), ids[...])
@@ -137,6 +178,21 @@
     pieces = jnp.where(lane == 0, high, jnp.where(lane == 1, low, 0.0)).astype(BF)
     send[:, wide:] = pieces[:half]
     keep[:, wide:] = pieces[half:]
+
+
+def close_rows(acts, mixed, edge_mixed, out_weight, out):
+    rows = acts.shape[0]
+    weight = out_weight[...]
+    step = 256
+    for at in range(0, rows, step):
+        first, last = at, at + step
+        pieces = [mixed[max(first, RIM) : min(last, rows - RIM), :]]
+        if first == 0:
+            pieces.insert(0, edge_mixed[:RIM, :])
+        if last == rows:
+            pieces.append(edge_mixed[RIM:, :])
+        block = jnp.concatenate(pieces, axis=0)
+        out[first:last, :] = (acts[first:last, :].astype(F32) + dot(block, weight)).astype(BF)
 
 
 def mean_tokens(*refs, count):
@@ -253,51 +309,54 @@
     back[...] = dot(result, down[...]).astype(BF)
 
 
-def second_block(
-    info, offsets, ids, atoms1, near, far, near_ids, far_ids, own_back, near_back, far_back,
-    gain, qkv, out_weight, bias, result, q, k, v, mixed, table, atoms2, *, share, columns
+def second_inner(
+    info, offsets, ids, atoms1, own_back, near_back, gain, qkv, bias,
+    atoms2, mixed, edge_q, edge_k, edge_v, q, k, v, *, share
+):
+    tokens = 2 * own_back.shape[0]
+    table = jnp.concatenate([own_back[...], near_back[...]], axis=0)
+    table_ids = token_of(tokens, share, info[0])
+    step = 256
+    for at in range(0, atoms1.shape[0], step):
+        member = one_hot(table_ids, ids[:, at : at + step])
+        moved = (atoms1[at : at + step, :].astype(F32) + dot_tn(member, table)).astype(BF)
+        atoms2[at : at + step, :] = moved
+        project(moved, gain[...], qkv[...], q, k, v, at)
+    inner_windows(offsets, bias, q, k, v, mixed, edge_q, edge_k, edge_v)
+
+
+def second_edge(
+    info, offsets, atoms2, near, far, near_ids, far_ids, own_back, near_back, far_back, gain, qkv, out_weight, bias,
+    mixed, edge_q, edge_k, edge_v, result, k, v, edge_mixed, *, share, columns
 ):
     side, column = info[0], info[3]
-    rows, channels = atoms1.shape
-    gain_row = gain[...]
-    weight = qkv[...]
-    half = own_back.shape[0]
-    tokens = 2 * half
-    table[:half, :] = own_back[...]
-    table[half:, :] = near_back[...]
+    tokens = 2 * own_back.shape[0]
+    table = jnp.concatenate([own_back[...], near_back[...]], axis=0)
     table_ids = token_of(tokens, share, side)
-    end = RIM + rows
     first_token = (info[1] * tokens).astype(F32)
 
     def rim_ids(message):
         packed = message[RIM : RIM + 16, :].astype(F32)
         return (packed[0:1, :RIM] * 64.0 + packed[1:2, :RIM] - first_token).astype(jnp.int32)
 
-    near_rows = near[...].astype(F32) + dot_tn(one_hot(table_ids, rim_ids(near_ids)), table[...])
-    project_rim(near_rows.astype(BF), gain_row, weight, k, v, jnp.where(side == 0, end, 0))
+    near_rows = near[...].astype(F32) + dot_tn(one_hot(table_ids, rim_ids(near_ids)), table)
     far_token = rim_ids(far_ids)
     beyond = lax.broadcasted_iota(jnp.int32, (RIM, 1), 0) + jnp.where(
         column == 0, -RIM, jnp.where(column == columns - 1, tokens, 4 * tokens)
     )
     far_rows = (
         far[...].astype(F32)
-        + dot_tn(one_hot(table_ids, far_token), table[...])
+        + dot_tn(one_hot(table_ids, far_token), table)
         + dot_tn(one_hot(beyond, far_token), far_back[...])
     )
-    project_rim(far_rows.astype(BF), gain_row, weight, k, v, jnp.where(side == 0, 0, end))
-    step = 256
-    for at in range(0, rows, step):
-        member = one_hot(table_ids, ids[:, at : at + step])
-        moved = (atoms1[at : at + step, :].astype(F32) + dot_tn(member, table[...])).astype(BF)
-        atoms2[at : at + step, :] = moved
-        project(moved, gain_row, weight, q, k, v, at)
-    attend_windows(offsets, bias, q, k, v, mixed)
-    for at in range(0, rows, step):
-        part = atoms2[at : at + step, :].astype(F32) + dot(mixed[at : at + step, :], out_weight[...])
-        result[at : at + step, :] = part.astype(BF)
-
-
-def call(kernel, outs, scratch, specs, flops, limit=40):
+    edge_windows(
+        offsets, bias, gain[...], qkv[...], near_rows.astype(BF).astype(F32), far_rows.astype(BF).astype(F32), side,
+        edge_q, edge_k, edge_v, k, v, edge_mixed,
+    )
+    close_rows(atoms2, mixed, edge_mixed, out_weight, result)
+
+
+def call(kernel, outs, scratch, specs, flops, limit=28):
     return pl.pallas_call(
         kernel,
         out_shape=outs,
@@ -329,7 +388,8 @@
         return lax.ppermute(x, "col", [(i, i ^ 1) for i in range(col_count)])
 
     def to_far(x):
-        swap = [(i, (i + 1) % devices if i % 2 else (i - 1) % devices) for i in range(devices)]
+        swap = [(i, i + 1 if i % 2 else i - 1) for i in range(1, devices - 1)]
+        swap = [(0, 0)] + swap + [(devices - 1, devices - 1)]
         return lax.ppermute(x, ("row", "col"), swap)
 
     def along_pairs(x, step):
@@ -357,22 +417,37 @@
 
     offsets = window_start - (row * col_count + col) * rows + RIM
     ids = (atom_token - row * tok_rows).reshape(1, rows)
-    window_scratch = [
+    inner_scratch = [
         pltpu.VMEM((rows, channels), BF),
-        pltpu.VMEM((rows + 2 * RIM, channels), F32),
-        pltpu.VMEM((rows + 2 * RIM, channels), F32),
-        pltpu.VMEM((rows, channels), BF),
+        pltpu.VMEM((rows, channels), F32),
+        pltpu.VMEM((rows, channels), F32),
+    ]
+    edge_scratch = [
+        pltpu.VMEM((6 * RIM, channels), F32),
+        pltpu.VMEM((6 * RIM, channels), F32),
+        pltpu.VMEM((2 * RIM, channels), BF),
+    ]
+    atom_shape = jax.ShapeDtypeStruct((rows, channels), BF)
+    edge_shapes = [
+        jax.ShapeDtypeStruct((2 * RIM, channels), BF),
+        jax.ShapeDtypeStruct((4 * RIM, channels), F32),
+        jax.ShapeDtypeStruct((4 * RIM, channels), F32),
     ]
     packed_shape = jax.ShapeDtypeStruct((half, wide + LANES), BF)
+    first_gain, second_gain = first_gain.reshape(1, -1), second_gain.reshape(1, -1)
+    mixed1 = call(
+        first_inner, [atom_shape] + edge_shapes, inner_scratch, [SMEM] + [VMEM] * 4, 1_500_000_000, 24
+    )(offsets, atom_acts, first_gain, first_qkv, atom_bias)
     atoms1, send, keep = call(
-        functools.partial(first_block, share=share),
-        [jax.ShapeDtypeStruct((rows, channels), BF), packed_shape, packed_shape],
-        window_scratch,
-        [SMEM, SMEM] + [VMEM] * 9,
-        3_000_000_000,
+        functools.partial(first_edge, share=share),
+        [atom_shape, packed_shape, packed_shape],
+        edge_scratch,
+        [SMEM, SMEM] + [VMEM] * 13,
+        2_000_000_000,
+        24,
     )(
-        info, offsets, ids, atom_acts, near_acts, far_acts, first_gain.reshape(1, -1), first_qkv, first_out,
-        atom_bias, up_weight,
+        info, offsets, ids, atom_acts, near_acts, far_acts, first_gain, first_qkv, first_out,
+        atom_bias, up_weight, *mixed1,
     )
 
     chip_sum = (keep.astype(F32) + to_near(send).astype(F32)).astype(BF)
@@ -429,15 +504,24 @@
         first_rows = both[:RIM]
     far_back = to_far(jnp.where(side == 1, last_rows, first_rows))
 
+    atoms2, *mixed2 = call(
+        functools.partial(second_inner, share=share),
+        [atom_shape, atom_shape] + edge_shapes,
+        inner_scratch,
+        [SMEM, SMEM] + [VMEM] * 7,
+        1_500_000_000,
+        24,
+    )(info, offsets, ids, atoms1, own_back, near_back, second_gain, second_qkv, atom_bias)
     return call(
-        functools.partial(second_block, share=share, columns=col_count),
-        jax.ShapeDtypeStruct((rows, channels), BF),
-        window_scratch + [pltpu.VMEM((tok_rows, channels), BF), pltpu.VMEM((rows, channels), BF)],
-        [SMEM, SMEM] + [VMEM] * 13,
-        1_500_000_000,
+        functools.partial(second_edge, share=share, columns=col_count),
+        atom_shape,
+        edge_scratch,
+        [SMEM, SMEM] + [VMEM] * 16,
+        300_000_000,
+        24,
     )(
-        info, offsets, ids, atoms1, near_atoms, far_atoms, near_acts, far_acts, own_back, near_back, far_back,
-        second_gain.reshape(1, -1), second_qkv, second_out, atom_bias,
+        info, offsets, atoms2, near_atoms, far_atoms, near_acts, far_acts, own_back, near_back, far_back,
+        second_gain, second_qkv, second_out, atom_bias, *mixed2,
     )
 
 

time: 113 us -> 75 us (0.66)
  the two profiles are of different devices: /device:TPU:0 before, /device:TPU:1 now
where the time goes in v2:
time: 75 us; the launch traced here: 74.3 us
  Pallas kernels  27.1 us (36%)
  starting transfers between devices  26.4 us (35%)
  local copies, waits for them, and re-layouts  9.68 us (13%)
  waiting for transfers between devices  8.69 us (12%)
  other arithmetic  2.05 us (3%)
    ppermute x3, starting transfers between devices, to_far(): return lax.ppermute(x, ('row', 'col'), swap)  10.2 us
    ppermute x9, starting transfers between devices, to_near(): return lax.ppermute(x, 'col', [(i, i ^ 1) for i in range(col_count)])  8.07 us
    pallas_call x1, Pallas kernels, body(): call(functools.partial(second_inner, share=share), [atom_shape, atom_shap...  7.26 us
    unnamed x38, local copies, waits for them, and re-layouts  6.56 us
    pallas_call x1, Pallas kernels, body(): call(functools.partial(attend_tokens, rows_count=row_count), packed_shape...  5.65 us
    ppermute x3, waiting for transfers between devices, along_pairs(): lax.ppermute(x, 'col', [(2 * i + k, 2 * ((i + step) % pairs) + k) for i i...  5.63 us
    pallas_call x1, Pallas kernels, body(): call(first_inner, [atom_shape] + edge_shapes, inner_scratch, [SMEM] + [VM...  4.8 us
    ppermute x3, starting transfers between devices, along_rows(): lax.ppermute(x, 'row', [(i, (i + step) % row_count) for i in range(row_co...  4.65 us
  transfers between devices with their start and end apart: 18, of which 4 were waited for; matrix products, arithmetic and copies ran while one was open for 5% of the time, Pallas kernels for 25%

profile of v2, /device:TPU:1, one launch (start us, length us, event | category | flops | bytes accessed | tf_op | source)
XLA Modules:
  0.0 74.3 jit_solution(8987964540819660140)
XLA Ops:
  0.1 0.9 %convert_bitcast_fusion.1 = (bf16[1,64]{1,0:T(2,128)(2,1)S(1)}, bf16[1,64]{1,0:T(2,128)(2,1)S(1)}, bf16[1,64]{1,0:T(2,128)(2,1)S(1)}, bf16[1,64]{1,0:T(2,128)(2,1)S(1)}) fusion(s32[2048]{0:T(1024)} %param.25, s32[]{:T(128)S(6)} %select_n.53, s32[]{:T(128)S(6)} %select_n.52), kind=kLoop, calls=%fused_computation.27 | loop fusion | flops 512 | bytes 1032 | tf_op jit(solution)/shard_map/stack | solution.py:409
  1.0 0.7 constant_dynamic-slice_fusion.5
  1.8 0.1 collective-permute-start
  1.9 4.5 %collective-permute-start.1 = (bf16[80,128]{1,0:T(8,128)(2,1)S(1)}, bf16[80,128]{1,0:T(8,128)(2,1)S(1)}, u32[]{:S(2)}, u32[]{:S(2)}) collective-permute-start(bf16[80,128]{1,0:T(8,128)(2,1)S(1)} %pad_maximum_fusion.1), channel_id=1, source_target_pairs={{0,0},{1,2},{2,1},{3,4},{4,3},{5,6},{6,5},{7,8},{8,7},{9,10},{10,9... | collective-permute-start | bytes 61448 | tf_op jit(solution)/shard_map/ppermute | solution.py:393
  6.4 2.3 %constant_dynamic-slice_fusion.2 = bf16[16,2,1,64,256]{4,3,2,1,0:T(8,128)(2,1)} fusion(bf16[16,2,2,64,256]{4,3,2,1,0:T(8,128)(2,1)} %bitcast.19, s32[]{:T(128)S(6)} %select_n.57), kind=kLoop, calls=%fused_computation.20 | loop fusion | bytes 2097156 | tf_op jit(solution)/shard_map/jit(dynamic_index_in_dim)/dynamic_slice | solution.py:416
  8.8 0.0 copy-start.8
  8.8 1.0 %copy-done.8 = bf16[2048,128]{1,0:T(8,128)(2,1)S(1)} copy-done((bf16[2048,128]{1,0:T(8,128)(2,1)S(1)}, bf16[2048,128]{1,0:T(8,128)(2,1)}, u32[]{:S(2)}) %copy-start.8) | copy-done | bytes 524312
  9.9 4.8 %shard_map.154 = (bf16[2048,128]{1,0:T(8,128)(2,1)S(1)}, bf16[128,128]{1,0:T(8,128)(2,1)S(1)}, f32[256,128]{1,0:T(8,128)S(1)}, f32[256,128]{1,0:T(8,128)S(1)}) custom-call(s32[64]{0:T(128)S(1)} %subtract_add_fusion.offsets, bf16[2048,128]{1,0:T(8,128)(2,1)S(1)} %copy-done.8, f32[1,128]{1,0:T(1,128)S(1)} %bitcast.24, bf16[128,384]{1,0:T(8,128)(2,1)S(1)} %copy-done.13, ...), custom_call_target="tpu_custom_call" | custom-call | flops 1500000000 | bytes 4000000 | tf_op jit(solution)/shard_map/pallas_call | solution.py:438
  14.7 0.1 pad_add_fusion.info
  14.7 0.0 collective-permute-done.near.near_ids
  14.8 0.0 collective-permute-done.1.far.far_ids
  14.8 0.0 copy-start.17
  14.8 4.3 %shard_map.155 = (bf16[2048,128]{1,0:T(8,128)(2,1)S(1)}, bf16[128,896]{1,0:T(8,128)(2,1)}, bf16[128,896]{1,0:T(8,128)(2,1)S(1)}) custom-call(s32[4]{0:T(128)S(1)} %pad_add_fusion.info, s32[64]{0:T(128)S(1)} %subtract_add_fusion.offsets, s32[1,2048]{1,0:T(1,128)S(1)} %bitcast.20, bf16[2048,128]{1,0:T(8,128)(2,1)S(1)} %copy-done.8, ...), custom_call_target="tpu_custom_call" | custom-call | flops 2000000000 | bytes 4000000 | tf_op jit(solution)/shard_map/pallas_call | solution.py:441
  19.1 0.8 %copy-done.9 = bf16[2048,128]{1,0:T(8,128)(2,1)} copy-done((bf16[2048,128]{1,0:T(8,128)(2,1)}, bf16[2048,128]{1,0:T(8,128)(2,1)S(1)}, u32[]{:S(2)}) %copy-start.9) | copy-done | bytes 524312
  19.9 0.5 collective-permute-start.2
  20.4 1.5 %collective-permute-done.2 = bf16[128,896]{1,0:T(8,128)(2,1)} collective-permute-done((bf16[128,896]{1,0:T(8,128)(2,1)}, bf16[128,896]{1,0:T(8,128)(2,1)}, u32[]{:S(2)}, u32[]{:S(2)}) %collective-permute-start.2) | collective-permute-done | bytes 229408 | tf_op jit(solution)/shard_map/ppermute | solution.py:388
  21.8 1.0 %add_convert_fusion = bf16[128,896]{1,0:T(8,128)(2,1)S(1)} fusion(bf16[128,896]{1,0:T(8,128)(2,1)} %collective-permute-done.2, bf16[128,896]{1,0:T(8,128)(2,1)S(1)} %get-tuple-element.27), kind=kLoop, calls=%fused_computation | loop fusion | flops 458752 | bytes 688128 | tf_op jit(solution)/shard_map/convert_element_type | solution.py:453
  22.8 0.0 copy-start.2
  22.9 1.4 %collective-permute-start.3 = (bf16[64,896]{1,0:T(8,128)(2,1)S(1)}, bf16[64,896]{1,0:T(8,128)(2,1)S(1)}, u32[]{:S(2)}, u32[]{:S(2)}) collective-permute-start(bf16[64,896]{1,0:T(8,128)(2,1)S(1)} %get-tuple-element.43), channel_id=1, source_target_pairs={{0,2},{1,3},{2,0},{3,1},{4,6},{5,7},{6,4},{7,5},{8,10},{9,11},{10,... | collective-permute-start | bytes 344072 | tf_op jit(solution)/shard_map/ppermute | solution.py:396
  24.3 3.0 %collective-permute-done.3.refs_1_ = bf16[64,896]{1,0:T(8,128)(2,1)S(1)} collective-permute-done((bf16[64,896]{1,0:T(8,128)(2,1)S(1)}, bf16[64,896]{1,0:T(8,128)(2,1)S(1)}, u32[]{:S(2)}, u32[]{:S(2)}) %collective-permute-start.3) | collective-permute-done | bytes 114720 | tf_op jit(solution)/shard_map/ppermute | solution.py:396
  27.3 0.3 shard_map.156
  27.7 1.4 %collective-permute-start.4 = (bf16[64,768]{1,0:T(8,128)(2,1)S(1)}, bf16[64,768]{1,0:T(8,128)(2,1)S(1)}, u32[]{:S(2)}, u32[]{:S(2)}) collective-permute-start(bf16[64,768]{1,0:T(8,128)(2,1)S(1)} %get-tuple-element.29.own_act), channel_id=1, source_target_pairs={{0,2},{1,3},{2,0},{3,1},{4,6},{5,7},{6,4},{7,5},{8,10},{9,11},{10,... | collective-permute-start | bytes 294920 | tf_op jit(solution)/shard_map/ppermute | solution.py:396
  29.0 1.2 %collective-permute-start.6 = (bf16[64,768]{1,0:T(8,128)(2,1)S(1)}, bf16[64,768]{1,0:T(8,128)(2,1)S(1)}, u32[]{:S(2)}, u32[]{:S(2)}) collective-permute-start(bf16[64,768]{1,0:T(8,128)(2,1)S(1)} %get-tuple-element.33.refs_0_), channel_id=1, source_target_pairs={{0,4},{4,8},{8,12},{12,0},{1,5},{5,9},{9,13},{13,1},{2,6},{6,10},{... | collective-permute-start | bytes 294920 | tf_op jit(solution)/shard_map/ppermute | solution.py:401
  30.3 1.9 %collective-permute-start.7 = (bf16[64,768]{1,0:T(8,128)(2,1)S(1)}, bf16[64,768]{1,0:T(8,128)(2,1)S(1)}, u32[]{:S(2)}, u32[]{:S(2)}) collective-permute-start(bf16[64,768]{1,0:T(8,128)(2,1)S(1)} %get-tuple-element.33.refs_0_), channel_id=1, source_target_pairs={{0,8},{4,12},{8,0},{12,4},{1,9},{5,13},{9,1},{13,5},{2,10},{6,14},... | collective-permute-start | bytes 294920 | tf_op jit(solution)/shard_map/ppermute | solution.py:401
  32.2 1.5 %collective-permute-start.8 = (bf16[64,768]{1,0:T(8,128)(2,1)S(1)}, bf16[64,768]{1,0:T(8,128)(2,1)S(1)}, u32[]{:S(2)}, u32[]{:S(2)}) collective-permute-start(bf16[64,768]{1,0:T(8,128)(2,1)S(1)} %get-tuple-element.33.refs_0_), channel_id=1, source_target_pairs={{0,12},{4,0},{8,4},{12,8},{1,13},{5,1},{9,5},{13,9},{2,14},{6,2},{... | collective-permute-start | bytes 294920 | tf_op jit(solution)/shard_map/ppermute | solution.py:401
  33.7 0.0 collective-permute-done.4.refs_0_
  33.7 2.3 %collective-permute-start.9 = (bf16[64,768]{1,0:T(8,128)(2,1)S(1)}, bf16[64,768]{1,0:T(8,128)(2,1)S(1)}, u32[]{:S(2)}, u32[]{:S(2)}) collective-permute-start(bf16[64,768]{1,0:T(8,128)(2,1)S(1)} %get-tuple-element.33.refs_0_), channel_id=1, source_target_pairs={{0,1},{1,0},{2,3},{3,2},{4,5},{5,4},{6,7},{7,6},{8,9},{9,8},{10,11... | collective-permute-start | bytes 294920 | tf_op jit(solution)/shard_map/ppermute | solution.py:388
  36.0 1.9 %collective-permute-start.10 = (bf16[64,768]{1,0:T(8,128)(2,1)S(1)}, bf16[64,768]{1,0:T(8,128)(2,1)S(1)}, u32[]{:S(2)}, u32[]{:S(2)}) collective-permute-start(bf16[64,768]{1,0:T(8,128)(2,1)S(1)} %collective-permute-done.6.refs_1_), channel_id=1, source_target_pairs={{0,1},{1,0},{2,3},{3,2},{4,5},{5,4},{6,7},{7,6},{8,9},{9,8},{10,11... | collective-permute-start | bytes 294920 | tf_op jit(solution)/shard_map/ppermute | solution.py:388
  38.0 1.6 %collective-permute-done.7.refs_2_ = bf16[64,768]{1,0:T(8,128)(2,1)S(1)} collective-permute-done((bf16[64,768]{1,0:T(8,128)(2,1)S(1)}, bf16[64,768]{1,0:T(8,128)(2,1)S(1)}, u32[]{:S(2)}, u32[]{:S(2)}) %collective-permute-start.7) | collective-permute-done | bytes 98336 | tf_op jit(solution)/shard_map/ppermute | solution.py:401
  39.5 1.1 %collective-permute-start.11 = (bf16[64,768]{1,0:T(8,128)(2,1)S(1)}, bf16[64,768]{1,0:T(8,128)(2,1)S(1)}, u32[]{:S(2)}, u32[]{:S(2)}) collective-permute-start(bf16[64,768]{1,0:T(8,128)(2,1)S(1)} %collective-permute-done.7.refs_2_), channel_id=1, source_target_pairs={{0,1},{1,0},{2,3},{3,2},{4,5},{5,4},{6,7},{7,6},{8,9},{9,8},{10,11... | collective-permute-start | bytes 294920 | tf_op jit(solution)/shard_map/ppermute | solution.py:388
  40.6 0.0 collective-permute-start.12
  40.6 2.3 %copy-done = bf16[768,3072]{1,0:T(8,128)(2,1)S(1)} copy-done((bf16[768,3072]{1,0:T(8,128)(2,1)S(1)}, bf16[768,3072]{1,0:T(8,128)(2,1)}, u32[]{:S(2)}) %copy-start) | copy-done | bytes 4718616
  42.9 1.2 %shard_map.157 = (bf16[128,768]{1,0:T(8,128)(2,1)S(1)}, bf16[128,768]{1,0:T(8,128)(2,1)S(1)}, f32[128,768]{1,0:T(8,128)S(1)}) custom-call(s32[4]{0:T(128)S(1)} %pad_add_fusion.info, bf16[768,3072]{1,0:T(8,128)(2,1)S(1)} %copy-done, f32[1,768]{1,0:T(1,128)S(1)} %reshape.21.refs_2_.gain, bf16[64,768]{1,0:T(8,128)(2,1)S(1)} %get-tuple-element.29.own_act, ...), custom_call_target="tpu_custom_call" | custom-call | flops 300000000 | bytes 4000000 | tf_op jit(solution)/shard_map/pallas_call | solution.py:468
  44.2 0.0 copy-start.1
  44.2 2.3 %copy-done.1 = bf16[768,3072]{1,0:T(8,128)(2,1)S(1)} copy-done((bf16[768,3072]{1,0:T(8,128)(2,1)S(1)}, bf16[768,3072]{1,0:T(8,128)(2,1)}, u32[]{:S(2)}) %copy-start.1) | copy-done | bytes 4718616
  46.6 5.6 %shard_map.158.refs_0_ = bf16[128,896]{1,0:T(8,128)(2,1)S(1)} custom-call(s32[4]{0:T(128)S(1)} %pad_add_fusion.info, bf16[768,3072]{1,0:T(8,128)(2,1)S(1)} %copy-done.1, bf16[128,768]{1,0:T(8,128)(2,1)S(1)} %get-tuple-element.32.queries, bf16[16,256,256]{2,1,0:T(8,128)(2,1)S(1)} %copy-done.2, bf16[16,128,256]{2,1,0:T(8,128)(2,1)S(1)} %collective-permute-done.5.bias_near, ...), custom_call_target="tpu_custom_call" | custom-call | flops 2000000000 | bytes 4000000 | tf_op jit(solution)/shard_map/pallas_call | solution.py:479
  52.2 0.0 copy-start.6
  52.2 0.0 copy-start.11
  52.2 0.8 %collective-permute-start.13 = (bf16[128,896]{1,0:T(8,128)(2,1)S(1)}, bf16[128,896]{1,0:T(8,128)(2,1)S(1)}, u32[]{:S(2)}, u32[]{:S(2)}) collective-permute-start(bf16[128,896]{1,0:T(8,128)(2,1)S(1)} %shard_map.158.refs_0_), channel_id=1, source_target_pairs={{0,2},{1,3},{2,0},{3,1},{4,6},{5,7},{6,4},{7,5},{8,10},{9,11},{10,... | collective-permute-start | bytes 688136 | tf_op jit(solution)/shard_map/ppermute | solution.py:396
  53.0 0.7 collective-permute-start.15
  53.7 2.6 %collective-permute-start.16 = (bf16[64,128]{1,0:T(8,128)(2,1)S(1)}, bf16[64,128]{1,0:T(8,128)(2,1)S(1)}, u32[]{:S(2)}, u32[]{:S(2)}) collective-permute-start(bf16[64,128]{1,0:T(8,128)(2,1)S(1)} %get-tuple-element.39), channel_id=1, source_target_pairs={{0,0},{1,2},{2,1},{3,4},{4,3},{5,6},{6,5},{7,8},{8,7},{9,10},{10,9... | collective-permute-start | bytes 49160 | tf_op jit(solution)/shard_map/ppermute | solution.py:393
  56.4 2.6 %collective-permute-done.13.refs_1_ = bf16[128,896]{1,0:T(8,128)(2,1)S(1)} collective-permute-done((bf16[128,896]{1,0:T(8,128)(2,1)S(1)}, bf16[128,896]{1,0:T(8,128)(2,1)S(1)}, u32[]{:S(2)}, u32[]{:S(2)}) %collective-permute-start.13) | collective-permute-done | bytes 229408 | tf_op jit(solution)/shard_map/ppermute | solution.py:396
  59.0 0.9 %shard_map.159.own_back = bf16[128,128]{1,0:T(8,128)(2,1)S(1)} custom-call(bf16[128,768]{1,0:T(8,128)(2,1)S(1)} %get-tuple-element.30.act, f32[128,768]{1,0:T(8,128)S(1)} %get-tuple-element.31.gates, bf16[768,768]{1,0:T(8,128)(2,1)S(1)} %copy-done.4, bf16[768,128]{1,0:T(8,128)(2,1)S(1)} %copy-done.5, bf16[128,896]{1,0:T(8,128)(2,1)S(1)} %shard_map.158.refs_0_, ...), custom_call_target="tpu_custom_call" | custom-call | flops 200000000 | bytes 4000000 | tf_op jit(solution)/shard_map/pallas_call | solution.py:488
  59.9 1.4 %collective-permute-start.14 = (bf16[128,128]{1,0:T(8,128)(2,1)S(1)}, bf16[128,128]{1,0:T(8,128)(2,1)S(1)}, u32[]{:S(2)}, u32[]{:S(2)}) collective-permute-start(bf16[128,128]{1,0:T(8,128)(2,1)S(1)} %shard_map.159.own_back), channel_id=1, source_target_pairs={{0,1},{1,0},{2,3},{3,2},{4,5},{5,4},{6,7},{7,6},{8,9},{9,8},{10,11... | collective-permute-start | bytes 98312 | tf_op jit(solution)/shard_map/ppermute | solution.py:388
  61.3 3.0 %collective-permute-start.17 = (bf16[64,128]{1,0:T(8,128)(2,1)S(1)}, bf16[64,128]{1,0:T(8,128)(2,1)S(1)}, u32[]{:S(2)}, u32[]{:S(2)}) collective-permute-start(bf16[64,128]{1,0:T(8,128)(2,1)S(1)} %slice_select_fusion), channel_id=1, source_target_pairs={{0,0},{1,2},{2,1},{3,4},{4,3},{5,6},{6,5},{7,8},{8,7},{9,10},{10,9... | collective-permute-start | bytes 49160 | tf_op jit(solution)/shard_map/ppermute | solution.py:393
  64.4 0.0 copy-start.7
  64.4 7.3 %shard_map.160 = (bf16[2048,128]{1,0:T(8,128)(2,1)S(1)}, bf16[2048,128]{1,0:T(8,128)(2,1)S(1)}, bf16[128,128]{1,0:T(8,128)(2,1)S(1)}, f32[256,128]{1,0:T(8,128)S(1)}, f32[256,128]{1,0:T(8,128)S(1)}) custom-call(s32[4]{0:T(128)S(1)} %pad_add_fusion.info, s32[64]{0:T(128)S(1)} %subtract_add_fusion.offsets, s32[1,2048]{1,0:T(1,128)S(1)} %bitcast.21, ...), custom_call_target="tpu_custom_call" | custom-call | flops 1500000000 | bytes 4000000 | tf_op jit(solution)/shard_map/pallas_call | solution.py:507
  71.7 2.6 %shard_map.161 = bf16[2048,128]{1,0:T(8,128)(2,1)} custom-call(s32[4]{0:T(128)S(1)} %pad_add_fusion.info, s32[64]{0:T(128)S(1)} %subtract_add_fusion.offsets, bf16[2048,128]{1,0:T(8,128)(2,1)S(1)} %get-tuple-element.34.atoms2, bf16[64,128]{1,0:T(8,128)(2,1)S(1)} %collective-permute-done.15.near, bf16[64,128]{1,0:T(8,128)(2,1)S(1)} %collective-permute-done.16.far, ...), custom_call_target="tpu_custom_call" | custom-call | flops 300000000 | bytes 4000000 | tf_op jit(solution)/shard_map/pallas_call | solution.py:515
  (49 shorter events, 0.2 us)
Async XLA Ops:
  0.0 8.7 %copy-start.16 = (s32[2048]{0:T(1024)S(1)}, s32[2048]{0:T(1024)}, u32[]{:S(2)}) copy-start(s32[2048]{0:T(1024)} %param.25) | copy-start | bytes 24580
  0.0 8.8 %copy-start.18 = (s32[64]{0:T(128)S(1)}, s32[64]{0:T(128)}, u32[]{:S(2)}) copy-start(s32[64]{0:T(128)} %param.24) | copy-start | bytes 772
  0.0 8.8 %copy-start.15 = (f32[128]{0:T(128)S(1)}, f32[128]{0:T(128)}, u32[]{:S(2)}) copy-start(f32[128]{0:T(128)} %param.17) | copy-start | bytes 1540
  0.0 8.8 %copy-start.13 = (bf16[128,384]{1,0:T(8,128)(2,1)S(1)}, bf16[128,384]{1,0:T(8,128)(2,1)}, u32[]{:S(2)}) copy-start(bf16[128,384]{1,0:T(8,128)(2,1)} %qkv.5) | copy-start | bytes 294916
  0.0 8.8 %copy-start.3 = (bf16[4,2048,128]{2,1,0:T(8,128)(2,1)S(1)}, bf16[4,2048,128]{2,1,0:T(8,128)(2,1)}, u32[]{:S(2)}) copy-start(bf16[4,2048,128]{2,1,0:T(8,128)(2,1)} %bias.7) | copy-start | bytes 6291460
  1.8 13.0 %collective-permute-start = (bf16[80,128]{1,0:T(8,128)(2,1)S(1)}, bf16[80,128]{1,0:T(8,128)(2,1)S(1)}, u32[]{:S(2)}, u32[]{:S(2)}) collective-permute-start(bf16[80,128]{1,0:T(8,128)(2,1)S(1)} %pad_maximum_fusion), channel_id=1, source_target_pairs={{0,1},{1,0},{2,3},{3,2},{4,5},{5,4},{6,7},{7,6},{8,9},{9,8},{10,11... | collective-permute-start | bytes 61448 | tf_op jit(solution)/shard_map/ppermute | solution.py:388
  1.9 12.9 %collective-permute-start.1 = (bf16[80,128]{1,0:T(8,128)(2,1)S(1)}, bf16[80,128]{1,0:T(8,128)(2,1)S(1)}, u32[]{:S(2)}, u32[]{:S(2)}) collective-permute-start(bf16[80,128]{1,0:T(8,128)(2,1)S(1)} %pad_maximum_fusion.1), channel_id=1, source_target_pairs={{0,0},{1,2},{2,1},{3,4},{4,3},{5,6},{6,5},{7,8},{8,7},{9,10},{10,9... | collective-permute-start | bytes 61448 | tf_op jit(solution)/shard_map/ppermute | solution.py:393
  8.7 35.5 %collective-permute-start.5 = (bf16[16,128,256]{2,1,0:T(8,128)(2,1)}, bf16[16,128,256]{2,1,0:T(8,128)(2,1)S(1)}, u32[]{:S(2)}, u32[]{:S(2)}) collective-permute-start(bf16[16,128,256]{2,1,0:T(8,128)(2,1)} %bitcast.11), channel_id=1, source_target_pairs={{0,1},{1,0},{2,3},{3,2},{4,5},{5,4},{6,7},{7,6},{8,9},{9,8},{10,11... | collective-permute-start | bytes 3145736 | tf_op jit(solution)/shard_map/ppermute | solution.py:388
  8.8 1.0 %copy-start.8 = (bf16[2048,128]{1,0:T(8,128)(2,1)S(1)}, bf16[2048,128]{1,0:T(8,128)(2,1)}, u32[]{:S(2)}) copy-start(bf16[2048,128]{1,0:T(8,128)(2,1)} %acts.3) | copy-start | bytes 1572868
  9.9 4.9 %copy-start.12 = (bf16[128,768]{1,0:T(8,128)(2,1)S(1)}, bf16[128,768]{1,0:T(8,128)(2,1)}, u32[]{:S(2)}) copy-start(bf16[128,768]{1,0:T(8,128)(2,1)} %up.1) | copy-start | bytes 589828
  9.9 4.9 %copy-start.14 = (bf16[128,128]{1,0:T(8,128)(2,1)S(1)}, bf16[128,128]{1,0:T(8,128)(2,1)}, u32[]{:S(2)}) copy-start(bf16[128,128]{1,0:T(8,128)(2,1)} %out_weight.2) | copy-start | bytes 98308
  14.8 9.5 %copy-start.17 = (f32[768]{0:T(1024)S(1)}, f32[768]{0:T(1024)}, u32[]{:S(2)}) copy-start(f32[768]{0:T(1024)} %param.27) | copy-start | bytes 9220
  19.1 0.8 %copy-start.9 = (bf16[2048,128]{1,0:T(8,128)(2,1)}, bf16[2048,128]{1,0:T(8,128)(2,1)S(1)}, u32[]{:S(2)}) copy-start(bf16[2048,128]{1,0:T(8,128)(2,1)S(1)} %get-tuple-element.26.atoms1) | copy-start | bytes 1572868
  19.9 1.9 %collective-permute-start.2 = (bf16[128,896]{1,0:T(8,128)(2,1)}, bf16[128,896]{1,0:T(8,128)(2,1)}, u32[]{:S(2)}, u32[]{:S(2)}) collective-permute-start(bf16[128,896]{1,0:T(8,128)(2,1)} %get-tuple-element.28), channel_id=1, source_target_pairs={{0,1},{1,0},{2,3},{3,2},{4,5},{5,4},{6,7},{7,6},{8,9},{9,8},{10,11... | collective-permute-start | bytes 688136 | tf_op jit(solution)/shard_map/ppermute | solution.py:388
  22.8 21.4 %copy-start.2 = (bf16[16,256,256]{2,1,0:T(8,128)(2,1)S(1)}, bf16[16,256,256]{2,1,0:T(8,128)(2,1)}, u32[]{:S(2)}) copy-start(bf16[16,256,256]{2,1,0:T(8,128)(2,1)} %bias_own.1) | copy-start | bytes 6291460
  22.9 4.4 %collective-permute-start.3 = (bf16[64,896]{1,0:T(8,128)(2,1)S(1)}, bf16[64,896]{1,0:T(8,128)(2,1)S(1)}, u32[]{:S(2)}, u32[]{:S(2)}) collective-permute-start(bf16[64,896]{1,0:T(8,128)(2,1)S(1)} %get-tuple-element.43), channel_id=1, source_target_pairs={{0,2},{1,3},{2,0},{3,1},{4,6},{5,7},{6,4},{7,5},{8,10},{9,11},{10,... | collective-permute-start | bytes 344072 | tf_op jit(solution)/shard_map/ppermute | solution.py:396
  27.7 6.0 %collective-permute-start.4 = (bf16[64,768]{1,0:T(8,128)(2,1)S(1)}, bf16[64,768]{1,0:T(8,128)(2,1)S(1)}, u32[]{:S(2)}, u32[]{:S(2)}) collective-permute-start(bf16[64,768]{1,0:T(8,128)(2,1)S(1)} %get-tuple-element.29.own_act), channel_id=1, source_target_pairs={{0,2},{1,3},{2,0},{3,1},{4,6},{5,7},{6,4},{7,5},{8,10},{9,11},{10,... | collective-permute-start | bytes 294920 | tf_op jit(solution)/shard_map/ppermute | solution.py:396
  29.0 7.0 %collective-permute-start.6 = (bf16[64,768]{1,0:T(8,128)(2,1)S(1)}, bf16[64,768]{1,0:T(8,128)(2,1)S(1)}, u32[]{:S(2)}, u32[]{:S(2)}) collective-permute-start(bf16[64,768]{1,0:T(8,128)(2,1)S(1)} %get-tuple-element.33.refs_0_), channel_id=1, source_target_pairs={{0,4},{4,8},{8,12},{12,0},{1,5},{5,9},{9,13},{13,1},{2,6},{6,10},{... | collective-permute-start | bytes 294920 | tf_op jit(solution)/shard_map/ppermute | solution.py:401
  30.3 9.2 %collective-permute-start.7 = (bf16[64,768]{1,0:T(8,128)(2,1)S(1)}, bf16[64,768]{1,0:T(8,128)(2,1)S(1)}, u32[]{:S(2)}, u32[]{:S(2)}) collective-permute-start(bf16[64,768]{1,0:T(8,128)(2,1)S(1)} %get-tuple-element.33.refs_0_), channel_id=1, source_target_pairs={{0,8},{4,12},{8,0},{12,4},{1,9},{5,13},{9,1},{13,5},{2,10},{6,14},... | collective-permute-start | bytes 294920 | tf_op jit(solution)/shard_map/ppermute | solution.py:401
  32.2 8.4 %collective-permute-start.8 = (bf16[64,768]{1,0:T(8,128)(2,1)S(1)}, bf16[64,768]{1,0:T(8,128)(2,1)S(1)}, u32[]{:S(2)}, u32[]{:S(2)}) collective-permute-start(bf16[64,768]{1,0:T(8,128)(2,1)S(1)} %get-tuple-element.33.refs_0_), channel_id=1, source_target_pairs={{0,12},{4,0},{8,4},{12,8},{1,13},{5,1},{9,5},{13,9},{2,14},{6,2},{... | collective-permute-start | bytes 294920 | tf_op jit(solution)/shard_map/ppermute | solution.py:401
  33.7 10.5 %collective-permute-start.9 = (bf16[64,768]{1,0:T(8,128)(2,1)S(1)}, bf16[64,768]{1,0:T(8,128)(2,1)S(1)}, u32[]{:S(2)}, u32[]{:S(2)}) collective-permute-start(bf16[64,768]{1,0:T(8,128)(2,1)S(1)} %get-tuple-element.33.refs_0_), channel_id=1, source_target_pairs={{0,1},{1,0},{2,3},{3,2},{4,5},{5,4},{6,7},{7,6},{8,9},{9,8},{10,11... | collective-permute-start | bytes 294920 | tf_op jit(solution)/shard_map/ppermute | solution.py:388
  36.0 8.1 %collective-permute-start.10 = (bf16[64,768]{1,0:T(8,128)(2,1)S(1)}, bf16[64,768]{1,0:T(8,128)(2,1)S(1)}, u32[]{:S(2)}, u32[]{:S(2)}) collective-permute-start(bf16[64,768]{1,0:T(8,128)(2,1)S(1)} %collective-permute-done.6.refs_1_), channel_id=1, source_target_pairs={{0,1},{1,0},{2,3},{3,2},{4,5},{5,4},{6,7},{7,6},{8,9},{9,8},{10,11... | collective-permute-start | bytes 294920 | tf_op jit(solution)/shard_map/ppermute | solution.py:388
  39.5 4.6 %collective-permute-start.11 = (bf16[64,768]{1,0:T(8,128)(2,1)S(1)}, bf16[64,768]{1,0:T(8,128)(2,1)S(1)}, u32[]{:S(2)}, u32[]{:S(2)}) collective-permute-start(bf16[64,768]{1,0:T(8,128)(2,1)S(1)} %collective-permute-done.7.refs_2_), channel_id=1, source_target_pairs={{0,1},{1,0},{2,3},{3,2},{4,5},{5,4},{6,7},{7,6},{8,9},{9,8},{10,11... | collective-permute-start | bytes 294920 | tf_op jit(solution)/shard_map/ppermute | solution.py:388
  40.6 3.6 %collective-permute-start.12 = (bf16[64,768]{1,0:T(8,128)(2,1)S(1)}, bf16[64,768]{1,0:T(8,128)(2,1)S(1)}, u32[]{:S(2)}, u32[]{:S(2)}) collective-permute-start(bf16[64,768]{1,0:T(8,128)(2,1)S(1)} %collective-permute-done.8.refs_3_), channel_id=1, source_target_pairs={{0,1},{1,0},{2,3},{3,2},{4,5},{5,4},{6,7},{7,6},{8,9},{9,8},{10,11... | collective-permute-start | bytes 294920 | tf_op jit(solution)/shard_map/ppermute | solution.py:388
  40.6 2.3 %copy-start = (bf16[768,3072]{1,0:T(8,128)(2,1)S(1)}, bf16[768,3072]{1,0:T(8,128)(2,1)}, u32[]{:S(2)}) copy-start(bf16[768,3072]{1,0:T(8,128)(2,1)} %weight.3) | copy-start | bytes 14155780
  44.2 2.3 %copy-start.1 = (bf16[768,3072]{1,0:T(8,128)(2,1)S(1)}, bf16[768,3072]{1,0:T(8,128)(2,1)}, u32[]{:S(2)}) copy-start(bf16[768,3072]{1,0:T(8,128)(2,1)} %weight.3) | copy-start | bytes 14155780
  46.5 6.4 %copy-start.10 = (bf16[2048,128]{1,0:T(8,128)(2,1)S(1)}, bf16[2048,128]{1,0:T(8,128)(2,1)}, u32[]{:S(2)}) copy-start(bf16[2048,128]{1,0:T(8,128)(2,1)} %copy-done.9) | copy-start | bytes 1572868
  46.6 12.4 %copy-start.4 = (bf16[768,768]{1,0:T(8,128)(2,1)S(1)}, bf16[768,768]{1,0:T(8,128)(2,1)}, u32[]{:S(2)}) copy-start(bf16[768,768]{1,0:T(8,128)(2,1)} %token_out.1) | copy-start | bytes 3538948
  46.6 12.4 %copy-start.5 = (bf16[768,128]{1,0:T(8,128)(2,1)S(1)}, bf16[768,128]{1,0:T(8,128)(2,1)}, u32[]{:S(2)}) copy-start(bf16[768,128]{1,0:T(8,128)(2,1)} %down.1) | copy-start | bytes 589828
  52.2 12.2 %copy-start.6 = (bf16[128,384]{1,0:T(8,128)(2,1)S(1)}, bf16[128,384]{1,0:T(8,128)(2,1)}, u32[]{:S(2)}) copy-start(bf16[128,384]{1,0:T(8,128)(2,1)} %qkv.7) | copy-start | bytes 294916
  52.2 12.2 %copy-start.11 = (f32[128]{0:T(128)S(1)}, f32[128]{0:T(128)}, u32[]{:S(2)}) copy-start(f32[128]{0:T(128)} %param.20) | copy-start | bytes 1540
  52.2 6.7 %collective-permute-start.13 = (bf16[128,896]{1,0:T(8,128)(2,1)S(1)}, bf16[128,896]{1,0:T(8,128)(2,1)S(1)}, u32[]{:S(2)}, u32[]{:S(2)}) collective-permute-start(bf16[128,896]{1,0:T(8,128)(2,1)S(1)} %shard_map.158.refs_0_), channel_id=1, source_target_pairs={{0,2},{1,3},{2,0},{3,1},{4,6},{5,7},{6,4},{7,5},{8,10},{9,11},{10,... | collective-permute-start | bytes 688136 | tf_op jit(solution)/shard_map/ppermute | solution.py:396
  53.0 18.7 %collective-permute-start.15 = (bf16[64,128]{1,0:T(8,128)(2,1)S(1)}, bf16[64,128]{1,0:T(8,128)(2,1)S(1)}, u32[]{:S(2)}, u32[]{:S(2)}) collective-permute-start(bf16[64,128]{1,0:T(8,128)(2,1)S(1)} %get-tuple-element.40), channel_id=1, source_target_pairs={{0,1},{1,0},{2,3},{3,2},{4,5},{5,4},{6,7},{7,6},{8,9},{9,8},{10,11... | collective-permute-start | bytes 49160 | tf_op jit(solution)/shard_map/ppermute | solution.py:388
  53.7 18.0 %collective-permute-start.16 = (bf16[64,128]{1,0:T(8,128)(2,1)S(1)}, bf16[64,128]{1,0:T(8,128)(2,1)S(1)}, u32[]{:S(2)}, u32[]{:S(2)}) collective-permute-start(bf16[64,128]{1,0:T(8,128)(2,1)S(1)} %get-tuple-element.39), channel_id=1, source_target_pairs={{0,0},{1,2},{2,1},{3,4},{4,3},{5,6},{6,5},{7,8},{8,7},{9,10},{10,9... | collective-permute-start | bytes 49160 | tf_op jit(solution)/shard_map/ppermute | solution.py:393
  59.9 4.5 %collective-permute-start.14 = (bf16[128,128]{1,0:T(8,128)(2,1)S(1)}, bf16[128,128]{1,0:T(8,128)(2,1)S(1)}, u32[]{:S(2)}, u32[]{:S(2)}) collective-permute-start(bf16[128,128]{1,0:T(8,128)(2,1)S(1)} %shard_map.159.own_back), channel_id=1, source_target_pairs={{0,1},{1,0},{2,3},{3,2},{4,5},{5,4},{6,7},{7,6},{8,9},{9,8},{10,11... | collective-permute-start | bytes 98312 | tf_op jit(solution)/shard_map/ppermute | solution.py:388
  61.3 10.4 %collective-permute-start.17 = (bf16[64,128]{1,0:T(8,128)(2,1)S(1)}, bf16[64,128]{1,0:T(8,128)(2,1)S(1)}, u32[]{:S(2)}, u32[]{:S(2)}) collective-permute-start(bf16[64,128]{1,0:T(8,128)(2,1)S(1)} %slice_select_fusion), channel_id=1, source_target_pairs={{0,0},{1,2},{2,1},{3,4},{4,3},{5,6},{6,5},{7,8},{8,7},{9,10},{10,9... | collective-permute-start | bytes 49160 | tf_op jit(solution)/shard_map/ppermute | solution.py:393
  64.4 7.3 %copy-start.7 = (bf16[128,128]{1,0:T(8,128)(2,1)S(1)}, bf16[128,128]{1,0:T(8,128)(2,1)}, u32[]{:S(2)}) copy-start(bf16[128,128]{1,0:T(8,128)(2,1)} %out_weight.3) | copy-start | bytes 98308

commit v3 on v2

--- a/solution.py
+++ b/solution.py
@@ -14,6 +14,7 @@
 LANES = 128
 VMEM = pl.BlockSpec(memory_space=pltpu.VMEM)
 SMEM = pl.BlockSpec(memory_space=pltpu.SMEM)
+HBM = pl.BlockSpec(memory_space=pltpu.HBM)
 
 
 def dot(a, b):
@@ -34,9 +35,9 @@
     return center * lax.rsqrt(spread + 1e-05) * gain
 
 
-def token_of(count, share, first_parity):
+def token_of(count, share, first_parity, dim=0):
     half = count // 2
-    row = lax.broadcasted_iota(jnp.int32, (count, 1), 0)
+    row = lax.broadcasted_iota(jnp.int32, (count, 1) if dim == 0 else (1, count), dim)
     second = (row >= half).astype(jnp.int32)
     inner = row - second * half
     shift = share.bit_length() - 1
@@ -93,6 +94,14 @@
         mixed[pl.ds(query_at, block), :] = (picked(out[:, :channels]) / picked(out[:, channels:])).astype(BF)
 
 
+class starts_from:
+    def __init__(self, starts, base):
+        self.starts, self.base, self.shape = starts, base, starts.shape
+
+    def __getitem__(self, window):
+        return self.starts[window] - self.base
+
+
 def inner_windows(offsets, bias, q, k, v, mixed, edge_q, edge_k, edge_v):
     windows = offsets.shape[0]
     rows = q.shape[0]
@@ -105,7 +114,7 @@
         for member in range(group):
             window = edge + step * group + member
             at = pl.multiple_of(window * block, block)
-            places.append((at, at, offsets[window] - RIM))
+            places.append((at, at, offsets[window]))
         attend_windows(places, bias, q, k, v, mixed)
         return carry
 
@@ -142,28 +151,60 @@
     attend_windows(places, bias, edge_q, k, v, mixed)
 
 
-def first_inner(offsets, acts, gain, qkv, bias, mixed, edge_q, edge_k, edge_v, q, k, v):
+def fetches(sources, targets, sems, first=0):
+    return [
+        pltpu.make_async_copy(source, target, sems.at[first + index])
+        for index, (source, target) in enumerate(zip(sources, targets))
+    ]
+
+
+def first_inner(
+    info, acts_far, gain_far, qkv_far, bias_far, starts_far, mixed, edge_q, edge_k, edge_v,
+    q, k, v, acts, gain, qkv, bias, starts, sems, *, pieces
+):
+    rows = acts.shape[0]
+    part = rows // pieces
+    cuts = [pl.ds(index * part, part) for index in range(pieces)]
+    small = fetches([gain_far, qkv_far], [gain, qkv], sems)
+    moving = fetches([acts_far.at[cut, :] for cut in cuts], [acts.at[cut, :] for cut in cuts], sems, 2)
+    late = fetches([starts_far, bias_far], [starts, bias], sems, 2 + pieces)
+    for copy in moving[:1] + small + moving[1:] + late:
+        copy.start()
+    for copy in small:
+        copy.wait()
     step = 256
-    for at in range(0, acts.shape[0], step):
+    for at in range(0, rows, step):
+        if at % part == 0:
+            moving[at // part].wait()
         project(acts[at : at + step, :], gain[...], qkv[...], q, k, v, at)
-    inner_windows(offsets, bias, q, k, v, mixed, edge_q, edge_k, edge_v)
+    for copy in late:
+        copy.wait()
+    inner_windows(starts_from(starts, info[4]), bias, q, k, v, mixed, edge_q, edge_k, edge_v)
 
 
 def first_edge(
     info, offsets, ids, acts, near, far, gain, qkv, out_weight, bias, up, mixed, edge_q, edge_k, edge_v,
-    atoms, send, keep, k, v, edge_mixed, *, share
+    atoms, send, keep, near_message, far_message, k, v, edge_mixed, *, share
 ):
     side = info[0]
     rows = acts.shape[0]
     edge_windows(
-        offsets, bias, gain[...], qkv[...], near[:RIM, :].astype(F32), far[:RIM, :].astype(F32), side,
+        starts_from(offsets, info[4] - RIM), bias, gain[...], qkv[...], near[...].astype(F32), far[...].astype(F32), side,
         edge_q, edge_k, edge_v, k, v, edge_mixed,
     )
     close_rows(acts, mixed, edge_mixed, out_weight, atoms)
     step = 256
     tokens = 2 * send.shape[0]
     half = tokens // 2
-    member = one_hot(token_of(tokens, share, 1 - side), ids[...])
+    head_ids = ids[:, :RIM]
+    tail_ids = ids[:, rows - RIM :]
+    for message, last in ((near_message, 1 - side), (far_message, side)):
+        at = pl.multiple_of(last * (rows - RIM), RIM)
+        message[:RIM, :] = atoms[pl.ds(at, RIM), :]
+        sent = head_ids + last * (tail_ids - head_ids)
+        coded = jnp.concatenate([sent >> 6, sent & 63], axis=1).astype(F32)
+        message[RIM:, :] = jnp.broadcast_to(coded, (16, 2 * RIM)).astype(BF)
+    member = one_hot(token_of(tokens, share, 1 - side) + info[1] * tokens, ids[...])
     wide = up.shape[1]
     atom_rows = atoms[...]
     for at in range(0, wide, step):
@@ -207,9 +248,15 @@
     normed[...] = norm_rows(rounded.astype(F32), gain[...]).astype(BF)
 
 
-def query_tokens(info, weight, gain, own_act, *refs, others):
-    other_acts, act, queries, gates = refs[:others], refs[others], refs[others + 1], refs[others + 2]
+def query_tokens(info, weight_far, gain, own_act, *refs, others):
+    other_acts = refs[:others]
+    act, queries, gates, query_weight, gate_weight, sems = refs[others:]
     share, wide = own_act.shape
+    copies = fetches(
+        [weight_far.at[:, pl.ds(0, wide)], weight_far.at[:, pl.ds(3 * wide, wide)]], [query_weight, gate_weight], sems
+    )
+    for copy in copies:
+        copy.start()
     pairs = others + 1
     place = info[2]
     act[pl.ds(pl.multiple_of(place * share, share), share), :] = own_act[...]
@@ -217,68 +264,140 @@
         at = lax.rem(place - step + pairs, pairs) * share
         act[pl.ds(pl.multiple_of(at, share), share), :] = other_acts[step - 1][...]
     normed = norm_rows(act[...].astype(F32), gain[...]).astype(BF)
-    queries[...] = dot(normed, weight[:, :wide]).astype(BF)
-    raw = dot(normed, weight[:, 3 * wide :]).astype(BF).astype(F32)
+    copies[0].wait()
+    queries[...] = dot(normed, query_weight[...]).astype(BF)
+    copies[1].wait()
+    raw = dot(normed, gate_weight[...]).astype(BF).astype(F32)
     gates[...] = jax.nn.sigmoid(raw)
 
 
-def attend_tokens(info, weight, queries, bias_own, bias_near, *refs, rows_count):
-    own, near = refs[:rows_count], refs[rows_count : 2 * rows_count]
-    out, tokens, keys_values = refs[2 * rows_count], refs[2 * rows_count + 1], refs[2 * rows_count + 2]
-    share, wide = own[0].shape
+def place_keys(info, own, near, tokens):
+    share = own[0].shape[0]
+    group = LANES // share
+    place = info[1] & (group - 1)
+    for index, (own_rows, near_rows) in enumerate(zip(own, near)):
+        at = index // group * 2 * LANES + (place ^ (index % group)) * share
+        tokens[pl.ds(pl.multiple_of(at, share), share), :] = own_rows[...]
+        tokens[pl.ds(pl.multiple_of(at + LANES, share), share), :] = near_rows[...]
+
+
+def bias_pieces(info, biases_far, first, tile, share):
+    count, blocks = tile.shape[1], tile.shape[2] // (2 * LANES)
+    group = LANES // share
     side, row = info[0], info[1]
-    keys = rows_count * share
-    for step in range(rows_count):
-        at = lax.rem(row - step + rows_count, rows_count) * share
-        tokens[pl.ds(pl.multiple_of(at, share), share), :] = own[step][...]
-        tokens[pl.ds(pl.multiple_of(at + keys, share), share), :] = near[step][...]
-    keys_values[...] = dot(tokens[...], weight[:, wide : 3 * wide]).astype(BF)
-    count = queries.shape[0]
-    pairs = count // share
-    heads = bias_own.shape[0]
+    sources, targets = [], []
+    for block in range(blocks):
+        slot = pl.multiple_of(((row // group) ^ (first + block)) * LANES, LANES)
+        for half, bias_far in enumerate(biases_far):
+            for pair in range(count // share):
+                at = pl.multiple_of((2 * pair + side) * share, share)
+                sources.append(bias_far.at[:, pl.ds(at, share), pl.ds(slot, LANES)])
+                targets.append(tile.at[:, pl.ds(pair * share, share), pl.ds((2 * block + half) * LANES, LANES)])
+    return sources, targets
+
+
+def attend_heads(queries, bias, keys, values, previous, keep):
+    count, wide = queries.shape
+    heads = bias.shape[0]
     size = wide // heads
     scale = 1.0 / math.sqrt(size)
+    span = keys.shape[0] // LANES
     lane = lax.broadcasted_iota(jnp.int32, (count, LANES), 1)
-    blocks = [None] * (wide // LANES)
-    logs = jnp.zeros((count, LANES), F32)
-    for head in range(heads):
-        first, last = head * size, (head + 1) * size
-        low, high = first // LANES, -(-last // LANES)
-        chunk = slice(low * LANES, high * LANES)
-        chunk_lane = lax.broadcasted_iota(jnp.int32, (count, (high - low) * LANES), 1) + low * LANES
-        inside = (chunk_lane >= first) & (chunk_lane < last)
-        query = jnp.where(inside, queries[:, chunk].astype(F32), 0.0).astype(BF)
-        own_rows = [
-            bias_own[head, pl.ds(pl.multiple_of((2 * pair + side) * share, share), share), :] for pair in range(pairs)
-        ]
-        own_tile = jnp.concatenate(own_rows, axis=0).astype(F32)
-        scores_own = dot_nt(query, keys_values[:keys, chunk]) * scale + own_tile
-        scores_near = dot_nt(query, keys_values[keys:, chunk]) * scale + bias_near[head].astype(F32)
-        top = jnp.maximum(
-            jnp.max(scores_own, axis=-1, keepdims=True), jnp.max(scores_near, axis=-1, keepdims=True)
-        )
-        raised_own = jnp.exp(scores_own - top)
-        raised_near = jnp.exp(scores_near - top)
-        total = jnp.sum(raised_own, axis=-1, keepdims=True) + jnp.sum(raised_near, axis=-1, keepdims=True)
-        values = slice(wide + chunk.start, wide + chunk.stop)
-        mixed = dot(raised_own.astype(BF), keys_values[:keys, values]) + dot(
-            raised_near.astype(BF), keys_values[keys:, values]
-        )
-        mixed = mixed / total
-        logs = jnp.where(lane == head, top + jnp.log(total), logs)
-        for block in range(low, high):
-            piece = mixed[:, (block - low) * LANES : (block - low + 1) * LANES]
-            if blocks[block] is None:
-                blocks[block] = piece
-            else:
-                blocks[block] = jnp.where(lane + block * LANES >= first, piece, blocks[block])
-    for block, piece in enumerate(blocks):
-        out[:, block * LANES : (block + 1) * LANES] = piece.astype(BF)
-    top_piece = logs.astype(BF).astype(F32)
-    rest = logs - top_piece
-    middle = rest.astype(BF).astype(F32)
-    rest = rest - middle
-    out[:, wide:] = (top_piece + pltpu.roll(middle, heads, 1) + pltpu.roll(rest, 2 * heads, 1)).astype(BF)
+    out = [None] * (wide // LANES)
+    together = 4
+    for start in range(0, heads, together):
+        members = []
+        for head in range(start, start + together):
+            first, last = head * size, (head + 1) * size
+            low, high = first // LANES, -(-last // LANES)
+            chunk = slice(low * LANES, high * LANES)
+            chunk_lane = lax.broadcasted_iota(jnp.int32, (count, (high - low) * LANES), 1) + low * LANES
+            inside = (chunk_lane >= first) & (chunk_lane < last)
+            query = jnp.where(inside, queries[:, chunk].astype(F32), 0.0).astype(BF)
+            members.append((head, first, low, high, dot_nt(query, keys[:, chunk])))
+        raised = []
+        for head, first, low, high, score in members:
+            score = score * scale + bias[head].astype(F32)
+            top = jnp.broadcast_to(jnp.max(score, axis=-1, keepdims=True), (count, LANES))
+            if previous is not None:
+                former = previous[1][head]
+                top = jnp.maximum(top, former)
+            weights = jnp.exp(score - jnp.concatenate([top] * span, axis=1))
+            total = jnp.broadcast_to(jnp.sum(weights, axis=-1, keepdims=True), (count, LANES))
+            fade = None
+            if previous is not None:
+                fade = jnp.exp(former - top)
+                total = total + fade * previous[2][head]
+            keep(head, top, total)
+            raised.append((weights.astype(BF), fade, total))
+        for (head, first, low, high, _), (weights, fade, total) in zip(members, raised):
+            mixed = dot(weights, values[:, low * LANES : high * LANES])
+            if previous is not None:
+                inverse = 1.0 / total
+            for block in range(low, high):
+                piece = mixed[:, (block - low) * LANES : (block - low + 1) * LANES]
+                if previous is not None:
+                    piece = (piece + fade * previous[0][:, block * LANES : (block + 1) * LANES]) * inverse
+                if out[block] is not None:
+                    piece = jnp.where(lane + block * LANES >= first, piece, out[block])
+                out[block] = piece
+    return out
+
+
+def attend_first(info, weight_far, queries, own_far, near_far, *refs, rows_count):
+    own, near = refs[:rows_count], refs[rows_count : 2 * rows_count]
+    key_weight, value_weight, rest_bias, mixed, tops, totals, tokens, keys, values, bias, sems = refs[2 * rows_count :]
+    share, wide = own[0].shape
+    weights = fetches(
+        [weight_far.at[:, pl.ds(wide, wide)], weight_far.at[:, pl.ds(2 * wide, wide)]], [key_weight, value_weight], sems
+    )
+    now = fetches(*bias_pieces(info, (own_far, near_far), 0, bias, share), sems, 2)
+    later = fetches(*bias_pieces(info, (own_far, near_far), 1, rest_bias, share), sems, 2 + len(now))
+    for copy in weights + now + later:
+        copy.start()
+    place_keys(info, own, near, tokens)
+    weights[0].wait()
+    keys[...] = dot(tokens[...], key_weight[...]).astype(BF)
+    weights[1].wait()
+    values[...] = dot(tokens[...], value_weight[...]).astype(BF)
+    for copy in now:
+        copy.wait()
+
+    def keep(head, top, total):
+        tops[head] = top
+        totals[head] = total
+
+    out = attend_heads(queries, bias, keys, values, None, keep)
+    for block, piece in enumerate(out):
+        mixed[:, block * LANES : (block + 1) * LANES] = piece
+    for copy in later:
+        copy.wait()
+
+
+def attend_rest(queries, key_weight, value_weight, bias, info, former, former_top, former_total, *refs, rows_count):
+    own, near = refs[:rows_count], refs[rows_count : 2 * rows_count]
+    packed, tokens, keys, values = refs[2 * rows_count :]
+    heads = bias.shape[0]
+    count, wide = queries.shape
+    place_keys(info, own, near, tokens)
+    keys[...] = dot(tokens[...], key_weight[...]).astype(BF)
+    values[...] = dot(tokens[...], value_weight[...]).astype(BF)
+    lane = lax.broadcasted_iota(jnp.int32, (count, LANES), 1)
+    ends = [jnp.zeros((count, LANES), F32), jnp.ones((count, LANES), F32)]
+
+    def keep(head, top, total):
+        ends[0] = jnp.where(lane == head, top, ends[0])
+        ends[1] = jnp.where(lane == head, total, ends[1])
+
+    out = attend_heads(queries, bias, keys, values, (former, former_top, former_total), keep)
+    for block, piece in enumerate(out):
+        packed[:, block * LANES : (block + 1) * LANES] = piece.astype(BF)
+    logs = ends[0] + jnp.log(ends[1])
+    first = logs.astype(BF).astype(F32)
+    rest = logs - first
+    second = rest.astype(BF).astype(F32)
+    rest = rest - second
+    packed[:, wide:] = (first + pltpu.roll(second, heads, 1) + pltpu.roll(rest, 2 * heads, 1)).astype(BF)
 
 
 def finish_tokens(act, gates, token_out, down, *refs, parts_count):
@@ -315,18 +434,26 @@
 ):
     tokens = 2 * own_back.shape[0]
     table = jnp.concatenate([own_back[...], near_back[...]], axis=0)
-    table_ids = token_of(tokens, share, info[0])
+    table_ids = (token_of(tokens, share, info[0], 1) + info[1] * tokens).astype(F32)
     step = 256
     for at in range(0, atoms1.shape[0], step):
-        member = one_hot(table_ids, ids[:, at : at + step])
-        moved = (atoms1[at : at + step, :].astype(F32) + dot_tn(member, table)).astype(BF)
+        members = []
+        for first in range(at, at + step, LANES):
+            atom_ids = jnp.broadcast_to(ids[:, first : first + LANES].astype(F32), (LANES, LANES)).T
+            members.append(
+                jnp.concatenate(
+                    [one_hot(table_ids[:, t : t + LANES], atom_ids) for t in range(0, tokens, LANES)], axis=1
+                )
+            )
+        member = jnp.concatenate(members, axis=0)
+        moved = (atoms1[at : at + step, :].astype(F32) + dot(member, table)).astype(BF)
         atoms2[at : at + step, :] = moved
         project(moved, gain[...], qkv[...], q, k, v, at)
-    inner_windows(offsets, bias, q, k, v, mixed, edge_q, edge_k, edge_v)
+    inner_windows(starts_from(offsets, info[4]), bias, q, k, v, mixed, edge_q, edge_k, edge_v)
 
 
 def second_edge(
-    info, offsets, atoms2, near, far, near_ids, far_ids, own_back, near_back, far_back, gain, qkv, out_weight, bias,
+    info, offsets, atoms2, near, far, own_back, near_back, far_back, gain, qkv, out_weight, bias,
     mixed, edge_q, edge_k, edge_v, result, k, v, edge_mixed, *, share, columns
 ):
     side, column = info[0], info[3]
@@ -336,27 +463,31 @@
     first_token = (info[1] * tokens).astype(F32)
 
     def rim_ids(message):
-        packed = message[RIM : RIM + 16, :].astype(F32)
-        return (packed[0:1, :RIM] * 64.0 + packed[1:2, :RIM] - first_token).astype(jnp.int32)
-
-    near_rows = near[...].astype(F32) + dot_tn(one_hot(table_ids, rim_ids(near_ids)), table)
-    far_token = rim_ids(far_ids)
+        packed = message[RIM:, :].astype(F32)
+        return (packed[0:1, :RIM] * 64.0 + packed[0:1, RIM:] - first_token).astype(jnp.int32)
+
+    near_rows = near[:RIM, :].astype(F32) + dot_tn(one_hot(table_ids, rim_ids(near)), table)
+    far_token = rim_ids(far)
     beyond = lax.broadcasted_iota(jnp.int32, (RIM, 1), 0) + jnp.where(
         column == 0, -RIM, jnp.where(column == columns - 1, tokens, 4 * tokens)
     )
     far_rows = (
-        far[...].astype(F32)
+        far[:RIM, :].astype(F32)
         + dot_tn(one_hot(table_ids, far_token), table)
         + dot_tn(one_hot(beyond, far_token), far_back[...])
     )
     edge_windows(
-        offsets, bias, gain[...], qkv[...], near_rows.astype(BF).astype(F32), far_rows.astype(BF).astype(F32), side,
+        starts_from(offsets, info[4] - RIM), bias, gain[...], qkv[...], near_rows.astype(BF).astype(F32), far_rows.astype(BF).astype(F32), side,
         edge_q, edge_k, edge_v, k, v, edge_mixed,
     )
     close_rows(atoms2, mixed, edge_mixed, out_weight, result)
 
 
-def call(kernel, outs, scratch, specs, flops, limit=28):
+def stay(x):
+    return pltpu.with_memory_space_constraint(x, pltpu.HBM)
+
+
+def call(kernel, outs, scratch, specs, flops, limit=20):
     return pl.pallas_call(
         kernel,
         out_shape=outs,
@@ -364,7 +495,7 @@
         out_specs=jax.tree.map(lambda _: VMEM, outs),
         scratch_shapes=scratch,
         compiler_params=pltpu.CompilerParams(vmem_limit_bytes=limit * 1024 * 1024),
-        cost_estimate=pl.CostEstimate(flops=flops, bytes_accessed=4_000_000, transcendentals=1_000_000),
+        cost_estimate=pl.CostEstimate(flops=flops, bytes_accessed=1_000, transcendentals=1_000),
     )
 
 
@@ -381,7 +512,7 @@
     half = tok_rows // 2
     row, col = lax.axis_index("row"), lax.axis_index("col")
     side, pair = col % 2, col // 2
-    info = jnp.stack([side, row, pair, col]).astype(jnp.int32)
+    info = jnp.stack([side, row, pair, col, (row * col_count + col) * rows]).astype(jnp.int32)
     devices = row_count * col_count
 
     def to_near(x):
@@ -398,25 +529,15 @@
         )
 
     def along_rows(x, step):
-        return lax.ppermute(x, "row", [(i, (i + step) % row_count) for i in range(row_count)])
+        return lax.ppermute(x, "row", [(i, i ^ step) for i in range(row_count)])
 
     def rim_of(x, last):
         return lax.dynamic_slice_in_dim(x, jnp.where(last, rows - RIM, 0), RIM, axis=0)
 
-    def message(last):
-        acts = rim_of(atom_acts, last)
-        ids = rim_of(atom_token, last)
-        coded = jnp.stack([ids >> 6, ids & 63]).astype(BF)
-        coded = jnp.pad(coded, ((0, 14), (0, channels - RIM)))
-        return jnp.concatenate([acts, coded], axis=0)
-
-    near_acts = to_near(message(side == 0))
-    far_acts = to_far(message(side == 1))
-    split_bias = pair_bias.reshape(heads, pairs, 2, share, slots)
-    bias_near = to_near(lax.dynamic_index_in_dim(split_bias, 1 - side, 2, False).reshape(heads, half, slots))
-
-    offsets = window_start - (row * col_count + col) * rows + RIM
-    ids = (atom_token - row * tok_rows).reshape(1, rows)
+    near_acts = to_near(rim_of(atom_acts, side == 0))
+    far_acts = to_far(rim_of(atom_acts, side == 1))
+
+    ids = atom_token.reshape(1, rows)
     inner_scratch = [
         pltpu.VMEM((rows, channels), BF),
         pltpu.VMEM((rows, channels), F32),
@@ -435,22 +556,34 @@
     ]
     packed_shape = jax.ShapeDtypeStruct((half, wide + LANES), BF)
     first_gain, second_gain = first_gain.reshape(1, -1), second_gain.reshape(1, -1)
+    pieces = 4
+    first_args = [atom_acts, first_gain, first_qkv, atom_bias]
     mixed1 = call(
-        first_inner, [atom_shape] + edge_shapes, inner_scratch, [SMEM] + [VMEM] * 4, 1_500_000_000, 24
-    )(offsets, atom_acts, first_gain, first_qkv, atom_bias)
-    atoms1, send, keep = call(
+        functools.partial(first_inner, pieces=pieces),
+        [atom_shape] + edge_shapes,
+        inner_scratch
+        + [pltpu.VMEM(x.shape, x.dtype) for x in first_args]
+        + [pltpu.SMEM(window_start.shape, jnp.int32), pltpu.SemaphoreType.DMA((4 + pieces,))],
+        [SMEM] + [HBM] * 5,
+        1_500_000_000,
+        16,
+    )(info, *map(stay, first_args), stay(window_start))
+    message_shape = jax.ShapeDtypeStruct((RIM + 16, channels), BF)
+    atoms1, send, keep, near_message, far_message = call(
         functools.partial(first_edge, share=share),
-        [atom_shape, packed_shape, packed_shape],
+        [atom_shape, packed_shape, packed_shape, message_shape, message_shape],
         edge_scratch,
         [SMEM, SMEM] + [VMEM] * 13,
         2_000_000_000,
-        24,
+        16,
     )(
-        info, offsets, ids, atom_acts, near_acts, far_acts, first_gain, first_qkv, first_out,
+        info, window_start, ids, atom_acts, near_acts, far_acts, first_gain, first_qkv, first_out,
         atom_bias, up_weight, *mixed1,
     )
 
     chip_sum = (keep.astype(F32) + to_near(send).astype(F32)).astype(BF)
+    chip_sum, near_bias = lax.optimization_barrier((chip_sum, pair_bias))
+    bias_near = to_near(near_bias)
     sums = [lax.dynamic_slice_in_dim(chip_sum, pair * share, share, axis=0)]
     for step in range(1, pairs):
         piece = lax.dynamic_slice_in_dim(chip_sum, (pair + step) % pairs * share, share, axis=0)
@@ -461,30 +594,53 @@
         functools.partial(mean_tokens, count=len(sums)), [share_shape] * 2, [], [VMEM] * (len(sums) + 1), 1_000_000
     )(*sums, gain_row)
 
+    group = LANES // share
     own_keys = [normed] + [along_rows(normed, step) for step in range(1, row_count)]
-    near_keys = [to_near(x) for x in own_keys]
+    near_keys = [to_near(x) for x in own_keys[:group]]
     other_acts = [along_pairs(act, step) for step in range(1, pairs)]
     half_shape = jax.ShapeDtypeStruct((half, wide), BF)
+    wide_shape = jax.ShapeDtypeStruct((half, wide), F32)
     act_rows, queries, gates = call(
         functools.partial(query_tokens, others=len(other_acts)),
-        [half_shape, half_shape, jax.ShapeDtypeStruct((half, wide), F32)],
-        [],
-        [SMEM] + [VMEM] * (3 + len(other_acts)),
-        300_000_000,
-    )(info, token_weight, gain_row, act, *other_acts)
-
-    near_atoms = to_near(rim_of(atoms1, side == 0))
-    far_atoms = to_far(rim_of(atoms1, side == 1))
-
+        [half_shape, half_shape, wide_shape],
+        [pltpu.VMEM((wide, wide), BF)] * 2 + [pltpu.SemaphoreType.DMA((2,))],
+        [SMEM, HBM] + [VMEM] * (2 + len(other_acts)),
+        1_000,
+    )(info, stay(token_weight), gain_row, act, *other_acts)
+
+    rest = row_count - group
+
+    def key_scratch(count):
+        keys = 2 * count * share
+        return [pltpu.VMEM((keys, wide), BF)] * 3
+
+    head_shape = jax.ShapeDtypeStruct((heads, half, LANES), F32)
+    weight_shape = jax.ShapeDtypeStruct((wide, wide), BF)
+    pieces = 2 * pairs * (row_count // group)
+    *held, mixed, tops, totals = call(
+        functools.partial(attend_first, rows_count=group),
+        [weight_shape, weight_shape, jax.ShapeDtypeStruct((heads, half, 2 * rest * share), BF)]
+        + [wide_shape, head_shape, head_shape],
+        key_scratch(group) + [pltpu.VMEM((heads, half, 2 * LANES), BF), pltpu.SemaphoreType.DMA((2 + pieces,))],
+        [SMEM, HBM, VMEM, HBM, HBM] + [VMEM] * (2 * group),
+        1_000,
+    )(info, stay(token_weight), queries, stay(pair_bias), stay(bias_near), *own_keys[:group], *near_keys)
+    rest_keys, mixed = lax.optimization_barrier((own_keys[group:], mixed))
+    rest_near = [to_near(x) for x in rest_keys]
     part = call(
-        functools.partial(attend_tokens, rows_count=row_count),
+        functools.partial(attend_rest, rows_count=rest),
         packed_shape,
-        [pltpu.VMEM((2 * slots, wide), BF), pltpu.VMEM((2 * slots, 2 * wide), BF)],
-        [SMEM] + [VMEM] * (4 + 2 * row_count),
+        key_scratch(rest),
+        [VMEM] * 4 + [SMEM] + [VMEM] * (3 + 2 * rest),
         2_000_000_000,
-    )(info, token_weight, queries, pair_bias, bias_near, *own_keys, *near_keys)
-
-    parts = [part] + [along_pairs(part, step) for step in range(1, pairs)]
+    )(queries, *held, info, mixed, tops, totals, *rest_keys, *rest_near)
+
+    near_message, far_message, part = lax.optimization_barrier((near_message, far_message, part))
+    parts = [along_pairs(part, step) for step in range(1, pairs)]
+    near_message, far_message, parts = lax.optimization_barrier(
+        (to_near(near_message), to_far(far_message), parts)
+    )
+    parts = [part] + parts
     own_back = call(
         functools.partial(finish_tokens, parts_count=pairs),
         jax.ShapeDtypeStruct((half, channels), BF),
@@ -510,17 +666,17 @@
         inner_scratch,
         [SMEM, SMEM] + [VMEM] * 7,
         1_500_000_000,
-        24,
-    )(info, offsets, ids, atoms1, own_back, near_back, second_gain, second_qkv, atom_bias)
+        16,
+    )(info, window_start, ids, atoms1, own_back, near_back, second_gain, second_qkv, atom_bias)
     return call(
         functools.partial(second_edge, share=share, columns=col_count),
         atom_shape,
         edge_scratch,
-        [SMEM, SMEM] + [VMEM] * 16,
+        [SMEM, SMEM] + [VMEM] * 14,
         300_000_000,
-        24,
+        16,
     )(
-        info, offsets, atoms2, near_atoms, far_atoms, near_acts, far_acts, own_back, near_back, far_back,
+        info, window_start, atoms2, near_message, far_message, own_back, near_back, far_back,
         second_gain, second_qkv, second_out, atom_bias, *mixed2,
     )
 

time: 75 us -> 67.7 us (0.903)
  local copies, waits for them, and re-layouts: 9.68 us -> 0.92 us
  Pallas kernels: 27.1 us -> 31.8 us
  starting transfers between devices: 26.4 us -> 24.1 us
  other arithmetic: 2.05 us -> 0.06 us
  waiting for transfers between devices: 8.69 us -> 9.67 us
    unnamed x38 -> x28, local copies, waits for them, and re-layouts: 6.56 us -> 0.07 us
    pallas_call x2 -> x3, Pallas kernels: 10.4 us -> 14.4 us  [the longest x1 6.87 us: body(): call(functools.partial(first_inner, pieces=pieces), [atom_shape] + edge_s...]
    ppermute x3, waiting for transfers between devices: 0.01 us -> 3.85 us  [to_far(): return lax.ppermute(x, ('row', 'col'), swap)]
    ppermute x9, starting transfers between devices: 8.07 us -> 5.31 us  [to_near(): return lax.ppermute(x, 'col', [(i, i ^ 1) for i in range(col_count)])]
    ppermute x3, waiting for transfers between devices: 5.63 us -> 3.09 us  [along_pairs(): lax.ppermute(x, 'col', [(2 * i + k, 2 * ((i + step) % pairs) + k) for i i...]
    dynamic_slice x1 -> x0, local copies, waits for them, and re-layouts: 2.35 us -> none  [body(): lax.dynamic_index_in_dim(split_bias, 1 - side, 2, False)]
    ppermute x3, waiting for transfers between devices: 1.57 us -> 0.01 us  [along_rows(): return lax.ppermute(x, 'row', [(i, i ^ step) for i in range(row_count)])]
    pallas_call x1, Pallas kernels: 1.21 us -> 2.63 us  [body(): call(functools.partial(query_tokens, others=len(other_acts)), [half_shape...]
  transfers between devices with their start and end apart: 18 -> 18, of which waited for: 4 -> 5; matrix products, arithmetic and copies ran while one was open for 5% -> 0% of each run, Pallas kernels for 25% -> 32%
where the time goes in v3:
time: 67.7 us; the launch traced here: 67 us
  Pallas kernels  31.8 us (47%)
  starting transfers between devices  24.1 us (36%)
  waiting for transfers between devices  9.67 us (14%)
  local copies, waits for them, and re-layouts  0.92 us (1%)
    ppermute x3, starting transfers between devices, to_far(): return lax.ppermute(x, ('row', 'col'), swap)  10.2 us
    pallas_call x1, Pallas kernels, body(): call(functools.partial(second_inner, share=share), [atom_shape, atom_shap...  7.24 us
    pallas_call x1, Pallas kernels, body(): call(functools.partial(first_inner, pieces=pieces), [atom_shape] + edge_s...  6.87 us
    ppermute x3, starting transfers between devices, along_rows(): return lax.ppermute(x, 'row', [(i, i ^ step) for i in range(row_count)])  5.51 us
    ppermute x9, starting transfers between devices, to_near(): return lax.ppermute(x, 'col', [(i, i ^ 1) for i in range(col_count)])  5.31 us
    pallas_call x1, Pallas kernels, body(): call(functools.partial(attend_first, rows_count=group), [weight_shape, we...  4.52 us
    ppermute x3, waiting for transfers between devices, to_far(): return lax.ppermute(x, ('row', 'col'), swap)  3.85 us
    pallas_call x1, Pallas kernels, body(): call(functools.partial(first_edge, share=share), [atom_shape, packed_shap...  3.67 us
  transfers between devices with their start and end apart: 18, of which 5 were waited for; matrix products, arithmetic and copies ran while one was open for 0% of the time, Pallas kernels for 32%

profile of v3, /device:TPU:1, one launch (start us, length us, event | category | flops | bytes accessed | tf_op | source)
XLA Modules:
  0.0 67.0 jit_solution(2725797579462723077)
XLA Ops:
  0.0 0.7 %constant_dynamic-slice_fusion.2 = (bf16[64,128]{1,0:T(8,128)(2,1)S(1)}, bf16[64,128]{1,0:T(8,128)(2,1)S(1)}) fusion(bf16[2048,128]{1,0:T(8,128)(2,1)} %acts.1, s32[]{:T(128)S(6)} %select_n.41, s32[]{:T(128)S(6)} %select_n.40), kind=kLoop, calls=%fused_computation.4 | loop fusion | bytes 65544 | tf_op jit(solution)/shard_map/dynamic_slice | solution.py:535
  0.7 0.1 collective-permute-start
  0.8 4.4 %collective-permute-start.1 = (bf16[64,128]{1,0:T(8,128)(2,1)S(1)}, bf16[64,128]{1,0:T(8,128)(2,1)S(1)}, u32[]{:S(2)}, u32[]{:S(2)}) collective-permute-start(bf16[64,128]{1,0:T(8,128)(2,1)S(1)} %get-tuple-element.77), channel_id=1, source_target_pairs={{0,0},{1,2},{2,1},{3,4},{4,3},{5,6},{6,5},{7,8},{8,7},{9,10},{10,9... | collective-permute-start | bytes 49160 | tf_op jit(solution)/shard_map/ppermute | solution.py:524
  5.3 0.1 stack.23.info
  5.4 0.0 copy-start.9
  5.4 0.0 copy-start.10
  5.4 0.0 copy-start.11
  5.4 0.0 copy-start.12
  5.4 6.9 %shard_map.154 = (bf16[2048,128]{1,0:T(8,128)(2,1)S(1)}, bf16[128,128]{1,0:T(8,128)(2,1)S(1)}, f32[256,128]{1,0:T(8,128)S(1)}, f32[256,128]{1,0:T(8,128)S(1)}) custom-call(s32[5]{0:T(128)S(1)} %stack.23.info, bf16[2048,128]{1,0:T(8,128)(2,1)} %acts.1, f32[1,128]{1,0:T(1,128)} %bitcast.12, bf16[128,384]{1,0:T(8,128)(2,1)} %qkv.3, bf16[4,2048,128]{2,1,0:T(8,128)(2,1)} %bias.5, ...), custom_call_target="tpu_custom_call" | custom-call | flops 1500000000 | bytes 1000 | tf_op jit(solution)/shard_map/pallas_call | solution.py:561
  12.3 0.0 collective-permute-done.near
  12.4 0.0 copy-start.13
  12.4 3.7 %shard_map.155 = (bf16[2048,128]{1,0:T(8,128)(2,1)S(1)}, bf16[128,896]{1,0:T(8,128)(2,1)S(1)}, bf16[128,896]{1,0:T(8,128)(2,1)S(1)}, bf16[80,128]{1,0:T(8,128)(2,1)S(1)}, bf16[80,128]{1,0:T(8,128)(2,1)S(1)}) custom-call(s32[5]{0:T(128)S(1)} %stack.23.info, s32[64]{0:T(128)S(1)} %copy-done.6, s32[1,2048]{1,0:T(1,128)S(1)} %bitcast.10, ...), custom_call_target="tpu_custom_call" | custom-call | flops 2000000000 | bytes 1000 | tf_op jit(solution)/shard_map/pallas_call | solution.py:572
  16.1 0.1 collective-permute-start.2
  16.2 1.5 %collective-permute-done.2 = bf16[128,896]{1,0:T(8,128)(2,1)S(1)} collective-permute-done((bf16[128,896]{1,0:T(8,128)(2,1)S(1)}, bf16[128,896]{1,0:T(8,128)(2,1)S(1)}, u32[]{:S(2)}, u32[]{:S(2)}) %collective-permute-start.2) | collective-permute-done | bytes 229408 | tf_op jit(solution)/shard_map/ppermute | solution.py:519
  17.6 0.1 add_convert_fusion
  17.7 0.2 collective-permute-start.5
  17.9 1.3 %collective-permute-start.3 = (bf16[64,896]{1,0:T(8,128)(2,1)S(1)}, bf16[64,896]{1,0:T(8,128)(2,1)S(1)}, u32[]{:S(2)}, u32[]{:S(2)}) collective-permute-start(bf16[64,896]{1,0:T(8,128)(2,1)S(1)} %get-tuple-element.79), channel_id=1, source_target_pairs={{0,2},{1,3},{2,0},{3,1},{4,6},{5,7},{6,4},{7,5},{8,10},{9,11},{10,... | collective-permute-start | bytes 344072 | tf_op jit(solution)/shard_map/ppermute | solution.py:527
  19.3 3.1 %collective-permute-done.3.refs_1_ = bf16[64,896]{1,0:T(8,128)(2,1)S(1)} collective-permute-done((bf16[64,896]{1,0:T(8,128)(2,1)S(1)}, bf16[64,896]{1,0:T(8,128)(2,1)S(1)}, u32[]{:S(2)}, u32[]{:S(2)}) %collective-permute-start.3) | collective-permute-done | bytes 114720 | tf_op jit(solution)/shard_map/ppermute | solution.py:527
  22.4 0.3 shard_map.156
  22.7 1.9 %collective-permute-start.6 = (bf16[64,768]{1,0:T(8,128)(2,1)S(1)}, bf16[64,768]{1,0:T(8,128)(2,1)S(1)}, u32[]{:S(2)}, u32[]{:S(2)}) collective-permute-start(bf16[64,768]{1,0:T(8,128)(2,1)S(1)} %get-tuple-element.56.refs_0_), channel_id=1, source_target_pairs={{0,4},{4,0},{8,12},{12,8},{1,5},{5,1},{9,13},{13,9},{2,6},{6,2},{1... | collective-permute-start | bytes 294920 | tf_op jit(solution)/shard_map/ppermute | solution.py:532
  24.6 0.7 %collective-permute-start.4 = (bf16[64,768]{1,0:T(8,128)(2,1)S(1)}, bf16[64,768]{1,0:T(8,128)(2,1)S(1)}, u32[]{:S(2)}, u32[]{:S(2)}) collective-permute-start(bf16[64,768]{1,0:T(8,128)(2,1)S(1)} %get-tuple-element.49.own_act), channel_id=1, source_target_pairs={{0,2},{1,3},{2,0},{3,1},{4,6},{5,7},{6,4},{7,5},{8,10},{9,11},{10,... | collective-permute-start | bytes 294920 | tf_op jit(solution)/shard_map/ppermute | solution.py:527
  25.3 1.8 %collective-permute-start.7 = (bf16[64,768]{1,0:T(8,128)(2,1)S(1)}, bf16[64,768]{1,0:T(8,128)(2,1)S(1)}, u32[]{:S(2)}, u32[]{:S(2)}) collective-permute-start(bf16[64,768]{1,0:T(8,128)(2,1)S(1)} %get-tuple-element.56.refs_0_), channel_id=1, source_target_pairs={{0,1},{1,0},{2,3},{3,2},{4,5},{5,4},{6,7},{7,6},{8,9},{9,8},{10,11... | collective-permute-start | bytes 294920 | tf_op jit(solution)/shard_map/ppermute | solution.py:519
  27.1 1.5 %collective-permute-start.8 = (bf16[64,768]{1,0:T(8,128)(2,1)S(1)}, bf16[64,768]{1,0:T(8,128)(2,1)S(1)}, u32[]{:S(2)}, u32[]{:S(2)}) collective-permute-start(bf16[64,768]{1,0:T(8,128)(2,1)S(1)} %collective-permute-done.6.refs_1_), channel_id=1, source_target_pairs={{0,1},{1,0},{2,3},{3,2},{4,5},{5,4},{6,7},{7,6},{8,9},{9,8},{10,11... | collective-permute-start | bytes 294920 | tf_op jit(solution)/shard_map/ppermute | solution.py:519
  28.6 2.6 %collective-permute-start.9 = (bf16[64,768]{1,0:T(8,128)(2,1)S(1)}, bf16[64,768]{1,0:T(8,128)(2,1)S(1)}, u32[]{:S(2)}, u32[]{:S(2)}) collective-permute-start(bf16[64,768]{1,0:T(8,128)(2,1)S(1)} %get-tuple-element.56.refs_0_), channel_id=1, source_target_pairs={{0,8},{4,12},{8,0},{12,4},{1,9},{5,13},{9,1},{13,5},{2,10},{6,14},... | collective-permute-start | bytes 294920 | tf_op jit(solution)/shard_map/ppermute | solution.py:532
  31.2 1.1 %collective-permute-start.10 = (bf16[64,768]{1,0:T(8,128)(2,1)S(1)}, bf16[64,768]{1,0:T(8,128)(2,1)S(1)}, u32[]{:S(2)}, u32[]{:S(2)}) collective-permute-start(bf16[64,768]{1,0:T(8,128)(2,1)S(1)} %get-tuple-element.56.refs_0_), channel_id=1, source_target_pairs={{0,12},{4,8},{8,4},{12,0},{1,13},{5,9},{9,5},{13,1},{2,14},{6,10},... | collective-permute-start | bytes 294920 | tf_op jit(solution)/shard_map/ppermute | solution.py:532
  32.2 2.6 %shard_map.157 = (bf16[128,768]{1,0:T(8,128)(2,1)S(1)}, bf16[128,768]{1,0:T(8,128)(2,1)S(1)}, f32[128,768]{1,0:T(8,128)S(1)}) custom-call(s32[5]{0:T(128)S(1)} %stack.23.info, bf16[768,3072]{1,0:T(8,128)(2,1)} %weight_far.3, f32[1,768]{1,0:T(1,128)S(1)} %reshape.14.refs_2_.gain, bf16[64,768]{1,0:T(8,128)(2,1)S(1)} %get-tuple-element.49.own_act, ...), custom_call_target="tpu_custom_call" | custom-call | flops 1000 | bytes 1000 | tf_op jit(solution)/shard_map/pallas_call | solution.py:603
  34.9 0.0 collective-permute-done.7.refs_2_
  34.9 4.5 %shard_map.158 = (bf16[768,768]{1,0:T(8,128)(2,1)S(1)}, bf16[768,768]{1,0:T(8,128)(2,1)S(1)}, bf16[16,128,256]{2,1,0:T(8,128)(2,1)S(1)}, f32[128,768]{1,0:T(8,12...) custom-call(s32[5]{0:T(128)S(1)} %stack.23.info, bf16[768,3072]{1,0:T(8,128)(2,1)} %weight_far.3, ...), custom_call_target="tpu_custom_call" | custom-call | flops 1000 | bytes 1000 | tf_op jit(solution)/shard_map/pallas_call | solution.py:620
  39.4 0.0 collective-permute-done.9.refs_0_
  39.4 0.0 collective-permute-done.10.refs_1_
  39.5 0.7 %collective-permute-start.11 = (bf16[64,768]{1,0:T(8,128)(2,1)S(1)}, bf16[64,768]{1,0:T(8,128)(2,1)S(1)}, u32[]{:S(2)}, u32[]{:S(2)}) collective-permute-start(bf16[64,768]{1,0:T(8,128)(2,1)S(1)} %collective-permute-done.9.refs_0_), channel_id=1, source_target_pairs={{0,1},{1,0},{2,3},{3,2},{4,5},{5,4},{6,7},{7,6},{8,9},{9,8},{10,11... | collective-permute-start | bytes 294920 | tf_op jit(solution)/shard_map/ppermute | solution.py:519
  40.2 0.1 collective-permute-start.12
  40.3 0.9 %collective-permute-done.11.refs_2_ = bf16[64,768]{1,0:T(8,128)(2,1)S(1)} collective-permute-done((bf16[64,768]{1,0:T(8,128)(2,1)S(1)}, bf16[64,768]{1,0:T(8,128)(2,1)S(1)}, u32[]{:S(2)}, u32[]{:S(2)}) %collective-permute-start.11) | collective-permute-done | bytes 98336 | tf_op jit(solution)/shard_map/ppermute | solution.py:519
  41.1 0.4 collective-permute-done.12.refs_3_
  41.5 3.0 %shard_map.159.refs_0_ = bf16[128,896]{1,0:T(8,128)(2,1)S(1)} custom-call(bf16[128,768]{1,0:T(8,128)(2,1)S(1)} %get-tuple-element.54.queries, bf16[768,768]{1,0:T(8,128)(2,1)S(1)} %get-tuple-element.57.key_weight, bf16[768,768]{1,0:T(8,128)(2,1)S(1)} %get-tuple-element.58.value_weight, bf16[16,128,256]{2,1,0:T(8,128)(2,1)S(1)} %get-tuple-element.59.bias, ...), custom_call_target="tpu_custom_call" | custom-call | flops 2000000000 | bytes 1000 | tf_op jit(solution)/shard_map/pallas_call | solution.py:630
  44.5 0.0 copy-start.3
  44.5 0.0 copy-start.7
  44.5 1.1 %collective-permute-start.15 = (bf16[128,896]{1,0:T(8,128)(2,1)S(1)}, bf16[128,896]{1,0:T(8,128)(2,1)S(1)}, u32[]{:S(2)}, u32[]{:S(2)}) collective-permute-start(bf16[128,896]{1,0:T(8,128)(2,1)S(1)} %shard_map.159.refs_0_), channel_id=1, source_target_pairs={{0,2},{1,3},{2,0},{3,1},{4,6},{5,7},{6,4},{7,5},{8,10},{9,11},{10,... | collective-permute-start | bytes 688136 | tf_op jit(solution)/shard_map/ppermute | solution.py:527
  45.6 0.4 collective-permute-start.13
  46.0 2.3 %collective-permute-start.14 = (bf16[80,128]{1,0:T(8,128)(2,1)S(1)}, bf16[80,128]{1,0:T(8,128)(2,1)S(1)}, u32[]{:S(2)}, u32[]{:S(2)}) collective-permute-start(bf16[80,128]{1,0:T(8,128)(2,1)S(1)} %get-tuple-element.68), channel_id=1, source_target_pairs={{0,0},{1,2},{2,1},{3,4},{4,3},{5,6},{6,5},{7,8},{8,7},{9,10},{10,9... | collective-permute-start | bytes 61448 | tf_op jit(solution)/shard_map/ppermute | solution.py:524
  48.3 0.0 collective-permute-done.13.near
  48.3 3.8 %collective-permute-done.14.far = bf16[80,128]{1,0:T(8,128)(2,1)S(1)} collective-permute-done((bf16[80,128]{1,0:T(8,128)(2,1)S(1)}, bf16[80,128]{1,0:T(8,128)(2,1)S(1)}, u32[]{:S(2)}, u32[]{:S(2)}) %collective-permute-start.14) | collective-permute-done | bytes 20512 | tf_op jit(solution)/shard_map/ppermute | solution.py:524
  52.2 0.9 %shard_map.160.own_back = bf16[128,128]{1,0:T(8,128)(2,1)S(1)} custom-call(bf16[128,768]{1,0:T(8,128)(2,1)S(1)} %get-tuple-element.50.act, f32[128,768]{1,0:T(8,128)S(1)} %get-tuple-element.51.gates, bf16[768,768]{1,0:T(8,128)(2,1)S(1)} %copy-done.1, bf16[768,128]{1,0:T(8,128)(2,1)S(1)} %copy-done.2, bf16[128,896]{1,0:T(8,128)(2,1)S(1)} %shard_map.159.refs_0_, ...), custom_call_target="tpu_custom_call" | custom-call | flops 200000000 | bytes 1000 | tf_op jit(solution)/shard_map/pallas_call | solution.py:644
  53.1 0.5 collective-permute-start.16
  53.6 3.4 %collective-permute-start.17 = (bf16[64,128]{1,0:T(8,128)(2,1)S(1)}, bf16[64,128]{1,0:T(8,128)(2,1)S(1)}, u32[]{:S(2)}, u32[]{:S(2)}) collective-permute-start(bf16[64,128]{1,0:T(8,128)(2,1)S(1)} %slice_select_fusion), channel_id=1, source_target_pairs={{0,0},{1,2},{2,1},{3,4},{4,3},{5,6},{6,5},{7,8},{8,7},{9,10},{10,9... | collective-permute-start | bytes 49160 | tf_op jit(solution)/shard_map/ppermute | solution.py:524
  57.0 0.0 copy-start.4
  57.1 7.2 %shard_map.161 = (bf16[2048,128]{1,0:T(8,128)(2,1)S(1)}, bf16[2048,128]{1,0:T(8,128)(2,1)S(1)}, bf16[128,128]{1,0:T(8,128)(2,1)S(1)}, f32[256,128]{1,0:T(8,128)S(1)}, f32[256,128]{1,0:T(8,128)S(1)}) custom-call(s32[5]{0:T(128)S(1)} %stack.23.info, s32[64]{0:T(128)S(1)} %copy-done.6, s32[1,2048]{1,0:T(1,128)S(1)} %bitcast.11, ...), custom_call_target="tpu_custom_call" | custom-call | flops 1500000000 | bytes 1000 | tf_op jit(solution)/shard_map/pallas_call | solution.py:663
  64.3 2.6 %shard_map.162 = bf16[2048,128]{1,0:T(8,128)(2,1)} custom-call(s32[5]{0:T(128)S(1)} %stack.23.info, s32[64]{0:T(128)S(1)} %copy-done.6, bf16[2048,128]{1,0:T(8,128)(2,1)S(1)} %get-tuple-element.70.atoms2, bf16[80,128]{1,0:T(8,128)(2,1)S(1)} %collective-permute-done.13.near, bf16[80,128]{1,0:T(8,128)(2,1)S(1)} %collective-permute-done.14.far, ...), custom_call_target="tpu_custom_call" | custom-call | flops 300000000 | bytes 1000 | tf_op jit(solution)/shard_map/pallas_call | solution.py:671
  (31 shorter events, 0.1 us)
Async XLA Ops:
  0.7 11.6 %collective-permute-start = (bf16[64,128]{1,0:T(8,128)(2,1)S(1)}, bf16[64,128]{1,0:T(8,128)(2,1)S(1)}, u32[]{:S(2)}, u32[]{:S(2)}) collective-permute-start(bf16[64,128]{1,0:T(8,128)(2,1)S(1)} %get-tuple-element.78), channel_id=1, source_target_pairs={{0,1},{1,0},{2,3},{3,2},{4,5},{5,4},{6,7},{7,6},{8,9},{9,8},{10,11... | collective-permute-start | bytes 49160 | tf_op jit(solution)/shard_map/ppermute | solution.py:519
  0.8 11.5 %collective-permute-start.1 = (bf16[64,128]{1,0:T(8,128)(2,1)S(1)}, bf16[64,128]{1,0:T(8,128)(2,1)S(1)}, u32[]{:S(2)}, u32[]{:S(2)}) collective-permute-start(bf16[64,128]{1,0:T(8,128)(2,1)S(1)} %get-tuple-element.77), channel_id=1, source_target_pairs={{0,0},{1,2},{2,1},{3,4},{4,3},{5,6},{6,5},{7,8},{8,7},{9,10},{10,9... | collective-permute-start | bytes 49160 | tf_op jit(solution)/shard_map/ppermute | solution.py:524
  5.4 7.0 %copy-start = (bf16[4,2048,128]{2,1,0:T(8,128)(2,1)S(1)}, bf16[4,2048,128]{2,1,0:T(8,128)(2,1)}, u32[]{:S(2)}) copy-start(bf16[4,2048,128]{2,1,0:T(8,128)(2,1)} %bias.5) | copy-start | bytes 6291460
  5.4 7.0 %copy-start.5 = (bf16[2048,128]{1,0:T(8,128)(2,1)S(1)}, bf16[2048,128]{1,0:T(8,128)(2,1)}, u32[]{:S(2)}) copy-start(bf16[2048,128]{1,0:T(8,128)(2,1)} %acts.1) | copy-start | bytes 1572868
  5.4 7.0 %copy-start.6 = (s32[64]{0:T(128)S(1)}, s32[64]{0:T(128)}, u32[]{:S(2)}) copy-start(s32[64]{0:T(128)} %offsets.5) | copy-start | bytes 772
  5.4 7.0 %copy-start.8 = (bf16[128,768]{1,0:T(8,128)(2,1)S(1)}, bf16[128,768]{1,0:T(8,128)(2,1)}, u32[]{:S(2)}) copy-start(bf16[128,768]{1,0:T(8,128)(2,1)} %up.1) | copy-start | bytes 589828
  5.4 7.0 %copy-start.9 = (bf16[128,384]{1,0:T(8,128)(2,1)S(1)}, bf16[128,384]{1,0:T(8,128)(2,1)}, u32[]{:S(2)}) copy-start(bf16[128,384]{1,0:T(8,128)(2,1)} %qkv.3) | copy-start | bytes 294916
  5.4 7.0 %copy-start.10 = (bf16[128,128]{1,0:T(8,128)(2,1)S(1)}, bf16[128,128]{1,0:T(8,128)(2,1)}, u32[]{:S(2)}) copy-start(bf16[128,128]{1,0:T(8,128)(2,1)} %out_weight.2) | copy-start | bytes 98308
  5.4 7.0 %copy-start.11 = (s32[2048]{0:T(1024)S(1)}, s32[2048]{0:T(1024)}, u32[]{:S(2)}) copy-start(s32[2048]{0:T(1024)} %param.25) | copy-start | bytes 24580
  5.4 7.0 %copy-start.12 = (f32[128]{0:T(128)S(1)}, f32[128]{0:T(128)}, u32[]{:S(2)}) copy-start(f32[128]{0:T(128)} %param.17) | copy-start | bytes 1540
  12.4 6.9 %copy-start.13 = (f32[768]{0:T(1024)S(1)}, f32[768]{0:T(1024)}, u32[]{:S(2)}) copy-start(f32[768]{0:T(1024)} %param.27) | copy-start | bytes 9220
  16.1 1.6 %collective-permute-start.2 = (bf16[128,896]{1,0:T(8,128)(2,1)S(1)}, bf16[128,896]{1,0:T(8,128)(2,1)S(1)}, u32[]{:S(2)}, u32[]{:S(2)}) collective-permute-start(bf16[128,896]{1,0:T(8,128)(2,1)S(1)} %get-tuple-element.47), channel_id=1, source_target_pairs={{0,1},{1,0},{2,3},{3,2},{4,5},{5,4},{6,7},{7,6},{8,9},{9,8},{10,11... | collective-permute-start | bytes 688136 | tf_op jit(solution)/shard_map/ppermute | solution.py:519
  17.7 17.2 %collective-permute-start.5 = (bf16[16,256,256]{2,1,0:T(8,128)(2,1)}, bf16[16,256,256]{2,1,0:T(8,128)(2,1)}, u32[]{:S(2)}, u32[]{:S(2)}) collective-permute-start(bf16[16,256,256]{2,1,0:T(8,128)(2,1)} %own_far.1), channel_id=1, source_target_pairs={{0,1},{1,0},{2,3},{3,2},{4,5},{5,4},{6,7},{7,6},{8,9},{9,8},{10,11... | collective-permute-start | bytes 6291464 | tf_op jit(solution)/shard_map/ppermute | solution.py:519
  17.9 4.4 %collective-permute-start.3 = (bf16[64,896]{1,0:T(8,128)(2,1)S(1)}, bf16[64,896]{1,0:T(8,128)(2,1)S(1)}, u32[]{:S(2)}, u32[]{:S(2)}) collective-permute-start(bf16[64,896]{1,0:T(8,128)(2,1)S(1)} %get-tuple-element.79), channel_id=1, source_target_pairs={{0,2},{1,3},{2,0},{3,1},{4,6},{5,7},{6,4},{7,5},{8,10},{9,11},{10,... | collective-permute-start | bytes 344072 | tf_op jit(solution)/shard_map/ppermute | solution.py:527
  22.7 4.4 %collective-permute-start.6 = (bf16[64,768]{1,0:T(8,128)(2,1)S(1)}, bf16[64,768]{1,0:T(8,128)(2,1)S(1)}, u32[]{:S(2)}, u32[]{:S(2)}) collective-permute-start(bf16[64,768]{1,0:T(8,128)(2,1)S(1)} %get-tuple-element.56.refs_0_), channel_id=1, source_target_pairs={{0,4},{4,0},{8,12},{12,8},{1,5},{5,1},{9,13},{13,9},{2,6},{6,2},{1... | collective-permute-start | bytes 294920 | tf_op jit(solution)/shard_map/ppermute | solution.py:532
  24.6 6.6 %collective-permute-start.4 = (bf16[64,768]{1,0:T(8,128)(2,1)S(1)}, bf16[64,768]{1,0:T(8,128)(2,1)S(1)}, u32[]{:S(2)}, u32[]{:S(2)}) collective-permute-start(bf16[64,768]{1,0:T(8,128)(2,1)S(1)} %get-tuple-element.49.own_act), channel_id=1, source_target_pairs={{0,2},{1,3},{2,0},{3,1},{4,6},{5,7},{6,4},{7,5},{8,10},{9,11},{10,... | collective-permute-start | bytes 294920 | tf_op jit(solution)/shard_map/ppermute | solution.py:527
  25.3 9.6 %collective-permute-start.7 = (bf16[64,768]{1,0:T(8,128)(2,1)S(1)}, bf16[64,768]{1,0:T(8,128)(2,1)S(1)}, u32[]{:S(2)}, u32[]{:S(2)}) collective-permute-start(bf16[64,768]{1,0:T(8,128)(2,1)S(1)} %get-tuple-element.56.refs_0_), channel_id=1, source_target_pairs={{0,1},{1,0},{2,3},{3,2},{4,5},{5,4},{6,7},{7,6},{8,9},{9,8},{10,11... | collective-permute-start | bytes 294920 | tf_op jit(solution)/shard_map/ppermute | solution.py:519
  27.1 7.8 %collective-permute-start.8 = (bf16[64,768]{1,0:T(8,128)(2,1)S(1)}, bf16[64,768]{1,0:T(8,128)(2,1)S(1)}, u32[]{:S(2)}, u32[]{:S(2)}) collective-permute-start(bf16[64,768]{1,0:T(8,128)(2,1)S(1)} %collective-permute-done.6.refs_1_), channel_id=1, source_target_pairs={{0,1},{1,0},{2,3},{3,2},{4,5},{5,4},{6,7},{7,6},{8,9},{9,8},{10,11... | collective-permute-start | bytes 294920 | tf_op jit(solution)/shard_map/ppermute | solution.py:519
  28.6 10.8 %collective-permute-start.9 = (bf16[64,768]{1,0:T(8,128)(2,1)S(1)}, bf16[64,768]{1,0:T(8,128)(2,1)S(1)}, u32[]{:S(2)}, u32[]{:S(2)}) collective-permute-start(bf16[64,768]{1,0:T(8,128)(2,1)S(1)} %get-tuple-element.56.refs_0_), channel_id=1, source_target_pairs={{0,8},{4,12},{8,0},{12,4},{1,9},{5,13},{9,1},{13,5},{2,10},{6,14},... | collective-permute-start | bytes 294920 | tf_op jit(solution)/shard_map/ppermute | solution.py:532
  31.2 8.3 %collective-permute-start.10 = (bf16[64,768]{1,0:T(8,128)(2,1)S(1)}, bf16[64,768]{1,0:T(8,128)(2,1)S(1)}, u32[]{:S(2)}, u32[]{:S(2)}) collective-permute-start(bf16[64,768]{1,0:T(8,128)(2,1)S(1)} %get-tuple-element.56.refs_0_), channel_id=1, source_target_pairs={{0,12},{4,8},{8,4},{12,0},{1,13},{5,9},{9,5},{13,1},{2,14},{6,10},... | collective-permute-start | bytes 294920 | tf_op jit(solution)/shard_map/ppermute | solution.py:532
  39.5 1.7 %collective-permute-start.11 = (bf16[64,768]{1,0:T(8,128)(2,1)S(1)}, bf16[64,768]{1,0:T(8,128)(2,1)S(1)}, u32[]{:S(2)}, u32[]{:S(2)}) collective-permute-start(bf16[64,768]{1,0:T(8,128)(2,1)S(1)} %collective-permute-done.9.refs_0_), channel_id=1, source_target_pairs={{0,1},{1,0},{2,3},{3,2},{4,5},{5,4},{6,7},{7,6},{8,9},{9,8},{10,11... | collective-permute-start | bytes 294920 | tf_op jit(solution)/shard_map/ppermute | solution.py:519
  40.2 1.3 %collective-permute-start.12 = (bf16[64,768]{1,0:T(8,128)(2,1)S(1)}, bf16[64,768]{1,0:T(8,128)(2,1)S(1)}, u32[]{:S(2)}, u32[]{:S(2)}) collective-permute-start(bf16[64,768]{1,0:T(8,128)(2,1)S(1)} %collective-permute-done.10.refs_1_), channel_id=1, source_target_pairs={{0,1},{1,0},{2,3},{3,2},{4,5},{5,4},{6,7},{7,6},{8,9},{9,8},{10,11... | collective-permute-start | bytes 294920 | tf_op jit(solution)/shard_map/ppermute | solution.py:519
  41.5 10.7 %copy-start.1 = (bf16[768,768]{1,0:T(8,128)(2,1)S(1)}, bf16[768,768]{1,0:T(8,128)(2,1)}, u32[]{:S(2)}) copy-start(bf16[768,768]{1,0:T(8,128)(2,1)} %token_out.1) | copy-start | bytes 3538948
  41.5 10.7 %copy-start.2 = (bf16[768,128]{1,0:T(8,128)(2,1)S(1)}, bf16[768,128]{1,0:T(8,128)(2,1)}, u32[]{:S(2)}) copy-start(bf16[768,128]{1,0:T(8,128)(2,1)} %down.1) | copy-start | bytes 589828
  44.5 12.5 %copy-start.3 = (bf16[128,384]{1,0:T(8,128)(2,1)S(1)}, bf16[128,384]{1,0:T(8,128)(2,1)}, u32[]{:S(2)}) copy-start(bf16[128,384]{1,0:T(8,128)(2,1)} %qkv.5) | copy-start | bytes 294916
  44.5 12.5 %copy-start.7 = (f32[128]{0:T(128)S(1)}, f32[128]{0:T(128)}, u32[]{:S(2)}) copy-start(f32[128]{0:T(128)} %param.20) | copy-start | bytes 1540
  44.5 7.7 %collective-permute-start.15 = (bf16[128,896]{1,0:T(8,128)(2,1)S(1)}, bf16[128,896]{1,0:T(8,128)(2,1)S(1)}, u32[]{:S(2)}, u32[]{:S(2)}) collective-permute-start(bf16[128,896]{1,0:T(8,128)(2,1)S(1)} %shard_map.159.refs_0_), channel_id=1, source_target_pairs={{0,2},{1,3},{2,0},{3,1},{4,6},{5,7},{6,4},{7,5},{8,10},{9,11},{10,... | collective-permute-start | bytes 688136 | tf_op jit(solution)/shard_map/ppermute | solution.py:527
  45.6 2.8 %collective-permute-start.13 = (bf16[80,128]{1,0:T(8,128)(2,1)S(1)}, bf16[80,128]{1,0:T(8,128)(2,1)S(1)}, u32[]{:S(2)}, u32[]{:S(2)}) collective-permute-start(bf16[80,128]{1,0:T(8,128)(2,1)S(1)} %get-tuple-element.67), channel_id=1, source_target_pairs={{0,1},{1,0},{2,3},{3,2},{4,5},{5,4},{6,7},{7,6},{8,9},{9,8},{10,11... | collective-permute-start | bytes 61448 | tf_op jit(solution)/shard_map/ppermute | solution.py:519
  46.0 6.2 %collective-permute-start.14 = (bf16[80,128]{1,0:T(8,128)(2,1)S(1)}, bf16[80,128]{1,0:T(8,128)(2,1)S(1)}, u32[]{:S(2)}, u32[]{:S(2)}) collective-permute-start(bf16[80,128]{1,0:T(8,128)(2,1)S(1)} %get-tuple-element.68), channel_id=1, source_target_pairs={{0,0},{1,2},{2,1},{3,4},{4,3},{5,6},{6,5},{7,8},{8,7},{9,10},{10,9... | collective-permute-start | bytes 61448 | tf_op jit(solution)/shard_map/ppermute | solution.py:524
  53.1 3.9 %collective-permute-start.16 = (bf16[128,128]{1,0:T(8,128)(2,1)S(1)}, bf16[128,128]{1,0:T(8,128)(2,1)S(1)}, u32[]{:S(2)}, u32[]{:S(2)}) collective-permute-start(bf16[128,128]{1,0:T(8,128)(2,1)S(1)} %shard_map.160.own_back), channel_id=1, source_target_pairs={{0,1},{1,0},{2,3},{3,2},{4,5},{5,4},{6,7},{7,6},{8,9},{9,8},{10,11... | collective-permute-start | bytes 98312 | tf_op jit(solution)/shard_map/ppermute | solution.py:519
  53.6 10.7 %collective-permute-start.17 = (bf16[64,128]{1,0:T(8,128)(2,1)S(1)}, bf16[64,128]{1,0:T(8,128)(2,1)S(1)}, u32[]{:S(2)}, u32[]{:S(2)}) collective-permute-start(bf16[64,128]{1,0:T(8,128)(2,1)S(1)} %slice_select_fusion), channel_id=1, source_target_pairs={{0,0},{1,2},{2,1},{3,4},{4,3},{5,6},{6,5},{7,8},{8,7},{9,10},{10,9... | collective-permute-start | bytes 49160 | tf_op jit(solution)/shard_map/ppermute | solution.py:524
  57.0 7.3 %copy-start.4 = (bf16[128,128]{1,0:T(8,128)(2,1)S(1)}, bf16[128,128]{1,0:T(8,128)(2,1)}, u32[]{:S(2)}) copy-start(bf16[128,128]{1,0:T(8,128)(2,1)} %out_weight.3) | copy-start | bytes 98308

commit v4 on v3

--- a/solution.py
+++ b/solution.py
@@ -102,14 +102,20 @@
         return self.starts[window] - self.base
 
 
-def inner_windows(offsets, bias, q, k, v, mixed, edge_q, edge_k, edge_v):
+def window_group(windows, edge):
+    return next(size for size in (15, 12, 10, 6, 5, 4, 3, 2, 1) if (windows - 2 * edge) % size == 0)
+
+
+def inner_windows(offsets, bias, q, k, v, mixed, edge_q, edge_k, edge_v, ready=None):
     windows = offsets.shape[0]
     rows = q.shape[0]
     block = rows // windows
     edge = RIM // block
-    group = next(size for size in (15, 12, 10, 6, 5, 4, 3, 2, 1) if (windows - 2 * edge) % size == 0)
+    group = window_group(windows, edge)
 
     def one_group(step, carry):
+        if ready is not None:
+            ready(step)
         places = []
         for member in range(group):
             window = edge + step * group + member
@@ -128,9 +134,9 @@
 
 def edge_windows(offsets, bias, gain, qkv, near, far, side, edge_q, edge_k, edge_v, k, v, mixed):
     windows = offsets.shape[0]
-    rows = bias.shape[1]
     channels = edge_q.shape[1]
-    block = rows // windows
+    block = bias.shape[2] - 3 * RIM // 2
+    rows = windows * block
     edge = RIM // block
     for source, target in ((edge_k, k), (edge_v, v)):
         target[RIM : 3 * RIM, :] = source[: 2 * RIM, :]
@@ -147,7 +153,8 @@
         places.append((member * block, member * block, offsets[member]))
     for member in range(edge):
         window = windows - edge + member
-        places.append((RIM + member * block, window * block, offsets[window] - (rows - 4 * RIM)))
+        at = RIM + member * block
+        places.append((at, at, offsets[window] - (rows - 4 * RIM)))
     attend_windows(places, bias, edge_q, k, v, mixed)
 
 
@@ -159,40 +166,61 @@
 
 
 def first_inner(
-    info, acts_far, gain_far, qkv_far, bias_far, starts_far, mixed, edge_q, edge_k, edge_v,
-    q, k, v, acts, gain, qkv, bias, starts, sems, *, pieces
+    info, acts_far, gain_far, qkv_far, starts_far, bias_far, mixed, edge_q, edge_k, edge_v, edge_bias,
+    q, k, v, acts, gain, qkv, starts, bias, sems, bias_sems, *, pieces
 ):
     rows = acts.shape[0]
+    windows = starts.shape[0]
+    block = rows // windows
+    span = window_group(windows, RIM // block) * block
     part = rows // pieces
     cuts = [pl.ds(index * part, part) for index in range(pieces)]
-    small = fetches([gain_far, qkv_far], [gain, qkv], sems)
-    moving = fetches([acts_far.at[cut, :] for cut in cuts], [acts.at[cut, :] for cut in cuts], sems, 2)
-    late = fetches([starts_far, bias_far], [starts, bias], sems, 2 + pieces)
-    for copy in moving[:1] + small + moving[1:] + late:
+    small = fetches([gain_far, qkv_far, starts_far], [gain, qkv, starts], sems)
+    moving = fetches([acts_far.at[cut, :] for cut in cuts], [acts.at[cut, :] for cut in cuts], sems, 3)
+    ends = fetches(
+        [bias_far.at[:, pl.ds(at, RIM), :] for at in (0, rows - RIM)],
+        [edge_bias.at[:, pl.ds(at, RIM), :] for at in (0, RIM)],
+        sems,
+        3 + pieces,
+    )
+
+    def tile(step):
+        place = pl.ds(pl.multiple_of(RIM + step * span, block), span)
+        return pltpu.make_async_copy(bias_far.at[:, place, :], bias.at[:, place, :], bias_sems.at[step])
+
+    for copy in moving[:1] + small + moving[1:]:
         copy.start()
     for copy in small:
         copy.wait()
     step = 256
-    for at in range(0, rows, step):
-        if at % part == 0:
-            moving[at // part].wait()
-        project(acts[at : at + step, :], gain[...], qkv[...], q, k, v, at)
-    for copy in late:
+    for index, copy in enumerate(moving):
         copy.wait()
-    inner_windows(starts_from(starts, info[4]), bias, q, k, v, mixed, edge_q, edge_k, edge_v)
+        if index == 0:
+            for group in range(bias_sems.shape[0]):
+                tile(group).start()
+            for end in ends:
+                end.start()
+        for at in range(index * part, (index + 1) * part, step):
+            project(acts[at : at + step, :], gain[...], qkv[...], q, k, v, at)
+    inner_windows(
+        starts_from(starts, info[4]), bias, q, k, v, mixed, edge_q, edge_k, edge_v, lambda index: tile(index).wait()
+    )
+    for end in ends:
+        end.wait()
 
 
 def first_edge(
-    info, offsets, ids, acts, near, far, gain, qkv, out_weight, bias, up, mixed, edge_q, edge_k, edge_v,
+    info, offsets, ids, acts, near, far, gain, qkv, out_weight, up, mixed, edge_q, edge_k, edge_v, bias,
     atoms, send, keep, near_message, far_message, k, v, edge_mixed, *, share
 ):
     side = info[0]
     rows = acts.shape[0]
+    close_inner(acts, mixed, out_weight, atoms)
     edge_windows(
         starts_from(offsets, info[4] - RIM), bias, gain[...], qkv[...], near[...].astype(F32), far[...].astype(F32), side,
         edge_q, edge_k, edge_v, k, v, edge_mixed,
     )
-    close_rows(acts, mixed, edge_mixed, out_weight, atoms)
+    close_edge(acts, edge_mixed, out_weight, atoms)
     step = 256
     tokens = 2 * send.shape[0]
     half = tokens // 2
@@ -221,19 +249,20 @@
     keep[:, wide:] = pieces[half:]
 
 
-def close_rows(acts, mixed, edge_mixed, out_weight, out):
+def close_inner(acts, mixed, out_weight, out):
     rows = acts.shape[0]
-    weight = out_weight[...]
     step = 256
     for at in range(0, rows, step):
-        first, last = at, at + step
-        pieces = [mixed[max(first, RIM) : min(last, rows - RIM), :]]
-        if first == 0:
-            pieces.insert(0, edge_mixed[:RIM, :])
-        if last == rows:
-            pieces.append(edge_mixed[RIM:, :])
-        block = jnp.concatenate(pieces, axis=0)
-        out[first:last, :] = (acts[first:last, :].astype(F32) + dot(block, weight)).astype(BF)
+        first, last = max(at, RIM), min(at + step, rows - RIM)
+        part = acts[first:last, :].astype(F32) + dot(mixed[first:last, :], out_weight[...])
+        out[first:last, :] = part.astype(BF)
+
+
+def close_edge(acts, mixed, out_weight, out):
+    rows = acts.shape[0]
+    moved = dot(mixed[...], out_weight[...])
+    out[:RIM, :] = (acts[:RIM, :].astype(F32) + moved[:RIM]).astype(BF)
+    out[rows - RIM :, :] = (acts[rows - RIM :, :].astype(F32) + moved[RIM:]).astype(BF)
 
 
 def mean_tokens(*refs, count):
@@ -271,29 +300,46 @@
     gates[...] = jax.nn.sigmoid(raw)
 
 
-def place_keys(info, own, near, tokens):
+def place_keys(info, own, near, tokens, steps, solo):
     share = own[0].shape[0]
     group = LANES // share
     place = info[1] & (group - 1)
-    for index, (own_rows, near_rows) in enumerate(zip(own, near)):
-        at = index // group * 2 * LANES + (place ^ (index % group)) * share
-        tokens[pl.ds(pl.multiple_of(at, share), share), :] = own_rows[...]
-        tokens[pl.ds(pl.multiple_of(at + LANES, share), share), :] = near_rows[...]
-
-
-def bias_pieces(info, biases_far, first, tile, share):
-    count, blocks = tile.shape[1], tile.shape[2] // (2 * LANES)
+    lead = 2 * share if solo else 0
+    for own_rows, near_rows, step in zip(own, near, steps):
+        if solo and step < group:
+            places = (0, share)
+        else:
+            at = lead + (step // group - (steps[0] + solo) // group) * 2 * LANES + (place ^ (step % group)) * share
+            places = (at, at + LANES)
+        for rows, at in zip((own_rows, near_rows), places):
+            tokens[pl.ds(pl.multiple_of(at, share), share), :] = rows[...]
+
+
+def bias_pieces(info, biases_far, block, targets, share):
+    count = targets[0].shape[1]
     group = LANES // share
     side, row = info[0], info[1]
-    sources, targets = [], []
-    for block in range(blocks):
-        slot = pl.multiple_of(((row // group) ^ (first + block)) * LANES, LANES)
-        for half, bias_far in enumerate(biases_far):
-            for pair in range(count // share):
-                at = pl.multiple_of((2 * pair + side) * share, share)
-                sources.append(bias_far.at[:, pl.ds(at, share), pl.ds(slot, LANES)])
-                targets.append(tile.at[:, pl.ds(pair * share, share), pl.ds((2 * block + half) * LANES, LANES)])
-    return sources, targets
+    slot = pl.multiple_of(((row // group) ^ block) * LANES, LANES)
+    sources, places = [], []
+    for bias_far, target in zip(biases_far, targets):
+        for pair in range(count // share):
+            at = pl.multiple_of((2 * pair + side) * share, share)
+            sources.append(bias_far.at[:, pl.ds(at, share), pl.ds(slot, LANES)])
+            places.append(target.at[:, pl.ds(pair * share, share), :])
+    return sources, places
+
+
+def split_bias(info, slots, bias, rest):
+    heads, count = bias.shape[0], bias.shape[1]
+    lane = lax.broadcasted_iota(jnp.int32, (count, LANES), 1)
+    lower = lane < LANES // 2
+    first = info[1] & 1
+    for head in range(heads):
+        own, near = slots[0, head].astype(F32), slots[1, head].astype(F32)
+        low = jnp.where(lower, own, pltpu.roll(near, LANES // 2, 1))
+        high = jnp.where(lower, pltpu.roll(own, LANES // 2, 1), near)
+        bias[head] = jnp.where(first == 0, low, high).astype(BF)
+        rest[head, :, :LANES] = jnp.where(first == 0, high, low).astype(BF)
 
 
 def attend_heads(queries, bias, keys, values, previous, keep):
@@ -344,24 +390,37 @@
     return out
 
 
-def attend_first(info, weight_far, queries, own_far, near_far, *refs, rows_count):
+def attend_first(info, weight_far, queries, own_far, near_far, *refs, steps, solo):
+    rows_count = len(steps)
     own, near = refs[:rows_count], refs[rows_count : 2 * rows_count]
-    key_weight, value_weight, rest_bias, mixed, tops, totals, tokens, keys, values, bias, sems = refs[2 * rows_count :]
+    key_weight, value_weight, rest_bias, mixed, tops, totals, tokens, keys, values, bias, slots, sems = refs[
+        2 * rows_count :
+    ]
     share, wide = own[0].shape
     weights = fetches(
         [weight_far.at[:, pl.ds(wide, wide)], weight_far.at[:, pl.ds(2 * wide, wide)]], [key_weight, value_weight], sems
     )
-    now = fetches(*bias_pieces(info, (own_far, near_far), 0, bias, share), sems, 2)
-    later = fetches(*bias_pieces(info, (own_far, near_far), 1, rest_bias, share), sems, 2 + len(now))
+    biases_far = (own_far, near_far)
+    targets = (slots.at[0], slots.at[1]) if solo else [bias.at[:, :, pl.ds(at, LANES)] for at in (0, LANES)]
+    now = fetches(*bias_pieces(info, biases_far, 0, targets, share), sems, 2)
+    later = []
+    lead = LANES if solo else 0
+    for block in range((rest_bias.shape[2] - lead) // (2 * LANES)):
+        first = lead + block * 2 * LANES
+        targets = [rest_bias.at[:, :, pl.ds(at, LANES)] for at in (first, first + LANES)]
+        sources, places = bias_pieces(info, biases_far, block + 1, targets, share)
+        later += fetches(sources, places, sems, 2 + len(now) + len(later))
     for copy in weights + now + later:
         copy.start()
-    place_keys(info, own, near, tokens)
+    place_keys(info, own, near, tokens, steps, solo)
     weights[0].wait()
     keys[...] = dot(tokens[...], key_weight[...]).astype(BF)
     weights[1].wait()
     values[...] = dot(tokens[...], value_weight[...]).astype(BF)
     for copy in now:
         copy.wait()
+    if solo:
+        split_bias(info, slots, bias, rest_bias)
 
     def keep(head, top, total):
         tops[head] = top
@@ -374,12 +433,13 @@
         copy.wait()
 
 
-def attend_rest(queries, key_weight, value_weight, bias, info, former, former_top, former_total, *refs, rows_count):
+def attend_rest(queries, key_weight, value_weight, bias, info, former, former_top, former_total, *refs, steps, solo):
+    rows_count = len(steps)
     own, near = refs[:rows_count], refs[rows_count : 2 * rows_count]
     packed, tokens, keys, values = refs[2 * rows_count :]
     heads = bias.shape[0]
     count, wide = queries.shape
-    place_keys(info, own, near, tokens)
+    place_keys(info, own, near, tokens, steps, solo)
     keys[...] = dot(tokens[...], key_weight[...]).astype(BF)
     values[...] = dot(tokens[...], value_weight[...]).astype(BF)
     lane = lax.broadcasted_iota(jnp.int32, (count, LANES), 1)
@@ -446,17 +506,20 @@
                 )
             )
         member = jnp.concatenate(members, axis=0)
-        moved = (atoms1[at : at + step, :].astype(F32) + dot(member, table)).astype(BF)
-        atoms2[at : at + step, :] = moved
-        project(moved, gain[...], qkv[...], q, k, v, at)
+        atoms2[at : at + step, :] = (atoms1[at : at + step, :].astype(F32) + dot(member, table)).astype(BF)
+    for at in range(0, atoms1.shape[0], step):
+        project(atoms2[at : at + step, :], gain[...], qkv[...], q, k, v, at)
     inner_windows(starts_from(offsets, info[4]), bias, q, k, v, mixed, edge_q, edge_k, edge_v)
 
 
 def second_edge(
     info, offsets, atoms2, near, far, own_back, near_back, far_back, gain, qkv, out_weight, bias,
-    mixed, edge_q, edge_k, edge_v, result, k, v, edge_mixed, *, share, columns
+    mixed, edge_q, edge_k, edge_v, result, k, v, edge_mixed, ends, *, share, columns
 ):
     side, column = info[0], info[3]
+    close_inner(atoms2, mixed, out_weight, result)
+    ends[:, :RIM, :] = bias[:, :RIM, :]
+    ends[:, RIM:, :] = bias[:, bias.shape[1] - RIM :, :]
     tokens = 2 * own_back.shape[0]
     table = jnp.concatenate([own_back[...], near_back[...]], axis=0)
     table_ids = token_of(tokens, share, side)
@@ -477,10 +540,10 @@
         + dot_tn(one_hot(beyond, far_token), far_back[...])
     )
     edge_windows(
-        starts_from(offsets, info[4] - RIM), bias, gain[...], qkv[...], near_rows.astype(BF).astype(F32), far_rows.astype(BF).astype(F32), side,
+        starts_from(offsets, info[4] - RIM), ends, gain[...], qkv[...], near_rows.astype(BF).astype(F32), far_rows.astype(BF).astype(F32), side,
         edge_q, edge_k, edge_v, k, v, edge_mixed,
     )
-    close_rows(atoms2, mixed, edge_mixed, out_weight, result)
+    close_edge(atoms2, edge_mixed, out_weight, result)
 
 
 def stay(x):
@@ -522,6 +585,14 @@
         swap = [(i, i + 1 if i % 2 else i - 1) for i in range(1, devices - 1)]
         swap = [(0, 0)] + swap + [(devices - 1, devices - 1)]
         return lax.ppermute(x, ("row", "col"), swap)
+
+    def to_beyond(x):
+        swap = {i: i for i in range(devices)}
+        for i in range(1, row_count):
+            first, last = i * col_count, i * col_count - 1
+            for one, other in ((first, first - col_count + 1), (last, last + col_count - 1)):
+                swap[one], swap[other] = other, one
+        return lax.ppermute(x, ("row", "col"), sorted(swap.items()))
 
     def along_pairs(x, step):
         return lax.ppermute(
@@ -556,18 +627,22 @@
     ]
     packed_shape = jax.ShapeDtypeStruct((half, wide + LANES), BF)
     first_gain, second_gain = first_gain.reshape(1, -1), second_gain.reshape(1, -1)
-    pieces = 4
-    first_args = [atom_acts, first_gain, first_qkv, atom_bias]
+    pieces = 2
+    windows = window_start.shape[0]
+    edge = RIM * windows // rows
+    groups = (windows - 2 * edge) // window_group(windows, edge)
+    first_args = [atom_acts, first_gain, first_qkv]
     mixed1 = call(
         functools.partial(first_inner, pieces=pieces),
-        [atom_shape] + edge_shapes,
+        [atom_shape] + edge_shapes + [jax.ShapeDtypeStruct((atom_bias.shape[0], 2 * RIM, atom_bias.shape[2]), BF)],
         inner_scratch
         + [pltpu.VMEM(x.shape, x.dtype) for x in first_args]
-        + [pltpu.SMEM(window_start.shape, jnp.int32), pltpu.SemaphoreType.DMA((4 + pieces,))],
+        + [pltpu.SMEM(window_start.shape, jnp.int32), pltpu.VMEM(atom_bias.shape, BF)]
+        + [pltpu.SemaphoreType.DMA((5 + pieces,)), pltpu.SemaphoreType.DMA((groups,))],
         [SMEM] + [HBM] * 5,
         1_500_000_000,
         16,
-    )(info, *map(stay, first_args), stay(window_start))
+    )(info, *map(stay, first_args), stay(window_start), stay(atom_bias))
     message_shape = jax.ShapeDtypeStruct((RIM + 16, channels), BF)
     atoms1, send, keep, near_message, far_message = call(
         functools.partial(first_edge, share=share),
@@ -578,7 +653,7 @@
         16,
     )(
         info, window_start, ids, atom_acts, near_acts, far_acts, first_gain, first_qkv, first_out,
-        atom_bias, up_weight, *mixed1,
+        up_weight, *mixed1,
     )
 
     chip_sum = (keep.astype(F32) + to_near(send).astype(F32)).astype(BF)
@@ -595,8 +670,10 @@
     )(*sums, gain_row)
 
     group = LANES // share
+    solo = group == 2
+    split = 1 if solo else group
     own_keys = [normed] + [along_rows(normed, step) for step in range(1, row_count)]
-    near_keys = [to_near(x) for x in own_keys[:group]]
+    near_keys = [to_near(x) for x in own_keys[:split]]
     other_acts = [along_pairs(act, step) for step in range(1, pairs)]
     half_shape = jax.ShapeDtypeStruct((half, wide), BF)
     wide_shape = jax.ShapeDtypeStruct((half, wide), F32)
@@ -608,27 +685,33 @@
         1_000,
     )(info, stay(token_weight), gain_row, act, *other_acts)
 
-    rest = row_count - group
+    rest = row_count - split
 
     def key_scratch(count):
-        keys = 2 * count * share
-        return [pltpu.VMEM((keys, wide), BF)] * 3
+        return [pltpu.VMEM((2 * count * share, wide), BF)] * 3
+
+    def bias_shape(count):
+        return jax.ShapeDtypeStruct((heads, half, 2 * count * share), BF)
 
     head_shape = jax.ShapeDtypeStruct((heads, half, LANES), F32)
     weight_shape = jax.ShapeDtypeStruct((wide, wide), BF)
-    pieces = 2 * pairs * (row_count // group)
+    copies = 2 + 2 * pairs * (row_count // group)
+    bias_scratch = [
+        pltpu.VMEM((heads, half, 2 * split * share), BF),
+        pltpu.VMEM((2, heads, half, LANES), BF),
+        pltpu.SemaphoreType.DMA((copies,)),
+    ]
     *held, mixed, tops, totals = call(
-        functools.partial(attend_first, rows_count=group),
-        [weight_shape, weight_shape, jax.ShapeDtypeStruct((heads, half, 2 * rest * share), BF)]
-        + [wide_shape, head_shape, head_shape],
-        key_scratch(group) + [pltpu.VMEM((heads, half, 2 * LANES), BF), pltpu.SemaphoreType.DMA((2 + pieces,))],
-        [SMEM, HBM, VMEM, HBM, HBM] + [VMEM] * (2 * group),
+        functools.partial(attend_first, steps=list(range(split)), solo=solo),
+        [weight_shape, weight_shape, bias_shape(rest), wide_shape, head_shape, head_shape],
+        key_scratch(split) + bias_scratch,
+        [SMEM, HBM, VMEM, HBM, HBM] + [VMEM] * (2 * split),
         1_000,
-    )(info, stay(token_weight), queries, stay(pair_bias), stay(bias_near), *own_keys[:group], *near_keys)
-    rest_keys, mixed = lax.optimization_barrier((own_keys[group:], mixed))
+    )(info, stay(token_weight), queries, stay(pair_bias), stay(bias_near), *own_keys[:split], *near_keys)
+    rest_keys, mixed = lax.optimization_barrier((own_keys[split:], mixed))
     rest_near = [to_near(x) for x in rest_keys]
     part = call(
-        functools.partial(attend_rest, rows_count=rest),
+        functools.partial(attend_rest, steps=list(range(split, row_count)), solo=solo),
         packed_shape,
         key_scratch(rest),
         [VMEM] * 4 + [SMEM] + [VMEM] * (3 + 2 * rest),
@@ -658,7 +741,7 @@
         both = both.reshape(2, pairs, share, channels).transpose(1, 0, 2, 3).reshape(tok_rows, channels)
         last_rows = both[tok_rows - RIM :]
         first_rows = both[:RIM]
-    far_back = to_far(jnp.where(side == 1, last_rows, first_rows))
+    far_back = to_beyond(jnp.where(side == 1, last_rows, first_rows))
 
     atoms2, *mixed2 = call(
         functools.partial(second_inner, share=share),
@@ -671,7 +754,7 @@
     return call(
         functools.partial(second_edge, share=share, columns=col_count),
         atom_shape,
-        edge_scratch,
+        edge_scratch + [pltpu.VMEM((atom_bias.shape[0], 2 * RIM, atom_bias.shape[2]), BF)],
         [SMEM, SMEM] + [VMEM] * 14,
         300_000_000,
         16,

time: 67.7 us -> 63.8 us (0.942)
  Pallas kernels: 31.8 us -> 29.6 us
  starting transfers between devices: 24.1 us -> 23.4 us
    ppermute x3 -> x2, starting transfers between devices: 10.2 us -> 7.46 us  [to_far(): return lax.ppermute(x, ('row', 'col'), swap)]
    ppermute x0 -> x1, starting transfers between devices: none -> 2.44 us  [to_beyond(): return lax.ppermute(x, ('row', 'col'), sorted(swap.items()))]
    pallas_call x1, Pallas kernels: 7.24 us -> 5.16 us  [body(): call(functools.partial(second_inner, share=share), [atom_shape, atom_shap...]
    ppermute x3, starting transfers between devices: 5.51 us -> 4.51 us  [along_rows(): return lax.ppermute(x, 'row', [(i, i ^ step) for i in range(row_count)])]
    pallas_call x1, Pallas kernels: 6.87 us -> 6.18 us  [body(): call(functools.partial(first_inner, pieces=pieces), [atom_shape] + edge_s...]
    ppermute x3 -> x2, waiting for transfers between devices: 3.85 us -> 3.54 us  [to_far(): return lax.ppermute(x, ('row', 'col'), swap)]
  transfers between devices with their start and end apart: 18 -> 18, of which waited for: 5 -> 6; matrix products, arithmetic and copies ran while one was open for 0% -> 0% of each run, Pallas kernels for 32% -> 29%
where the time goes in v4:
time: 63.8 us; the launch traced here: 63.4 us
  Pallas kernels  29.6 us (46%)
  starting transfers between devices  23.4 us (37%)
  waiting for transfers between devices  9.08 us (14%)
  local copies, waits for them, and re-layouts  0.92 us (1%)
    ppermute x2, starting transfers between devices, to_far(): return lax.ppermute(x, ('row', 'col'), swap)  7.46 us
    pallas_call x1, Pallas kernels, body(): call(functools.partial(first_inner, pieces=pieces), [atom_shape] + edge_s...  6.18 us
    ppermute x9, starting transfers between devices, to_near(): return lax.ppermute(x, 'col', [(i, i ^ 1) for i in range(col_count)])  5.86 us
    pallas_call x1, Pallas kernels, body(): call(functools.partial(second_inner, share=share), [atom_shape, atom_shap...  5.16 us
    ppermute x3, starting transfers between devices, along_rows(): return lax.ppermute(x, 'row', [(i, i ^ step) for i in range(row_count)])  4.51 us
    pallas_call x1, Pallas kernels, body(): call(functools.partial(attend_rest, steps=list(range(split, row_count)),...  4.07 us
    pallas_call x1, Pallas kernels, body(): call(functools.partial(attend_first, steps=list(range(split)), solo=solo)...  4.04 us
    pallas_call x1, Pallas kernels, body(): call(functools.partial(first_edge, share=share), [atom_shape, packed_shap...  3.67 us
  transfers between devices with their start and end apart: 18, of which 6 were waited for; matrix products, arithmetic and copies ran while one was open for 0% of the time, Pallas kernels for 29%

profile of v4, /device:TPU:1, one launch (start us, length us, event | category | flops | bytes accessed | tf_op | source)
XLA Modules:
  0.0 63.4 jit_solution(6387908528006462726)
XLA Ops:
  0.0 0.7 %constant_dynamic-slice_fusion.2 = (bf16[64,128]{1,0:T(8,128)(2,1)S(1)}, bf16[64,128]{1,0:T(8,128)(2,1)S(1)}) fusion(bf16[2048,128]{1,0:T(8,128)(2,1)} %acts.1, s32[]{:T(128)S(6)} %select_n.41, s32[]{:T(128)S(6)} %select_n.40), kind=kLoop, calls=%fused_computation.4 | loop fusion | bytes 65544 | tf_op jit(solution)/shard_map/dynamic_slice | solution.py:606
  0.7 0.1 collective-permute-start
  0.8 4.4 %collective-permute-start.1 = (bf16[64,128]{1,0:T(8,128)(2,1)S(1)}, bf16[64,128]{1,0:T(8,128)(2,1)S(1)}, u32[]{:S(2)}, u32[]{:S(2)}) collective-permute-start(bf16[64,128]{1,0:T(8,128)(2,1)S(1)} %get-tuple-element.81), channel_id=1, source_target_pairs={{0,0},{1,2},{2,1},{3,4},{4,3},{5,6},{6,5},{7,8},{8,7},{9,10},{10,9... | collective-permute-start | bytes 49160 | tf_op jit(solution)/shard_map/ppermute | solution.py:587
  5.3 0.1 stack.23.info
  5.4 0.0 copy-start.10
  5.4 0.0 copy-start.11
  5.4 0.0 copy-start.12
  5.4 6.2 %shard_map.154 = (bf16[2048,128]{1,0:T(8,128)(2,1)S(1)}, bf16[128,128]{1,0:T(8,128)(2,1)S(1)}, f32[256,128]{1,0:T(8,128)S(1)}, f32[256,128]{1,0:T(8,128)S(1)}, bf16[4,128,128]{2,1,0:T(8,128)(2,1)S(1)}) custom-call(s32[5]{0:T(128)S(1)} %stack.23.info, bf16[2048,128]{1,0:T(8,128)(2,1)} %acts.1, f32[1,128]{1,0:T(1,128)} %bitcast.12, bf16[128,384]{1,0:T(8,128)(2,1)} %qkv.3, ...), custom_call_target="tpu_custom_call" | custom-call | flops 1500000000 | bytes 1000 | tf_op jit(solution)/shard_map/pallas_call | solution.py:635
  11.6 0.0 collective-permute-done.near
  11.6 0.0 collective-permute-done.1.far
  11.7 0.0 copy-start.13
  11.7 0.0 copy-start.14
  11.7 3.7 %shard_map.155 = (bf16[2048,128]{1,0:T(8,128)(2,1)S(1)}, bf16[128,896]{1,0:T(8,128)(2,1)S(1)}, bf16[128,896]{1,0:T(8,128)(2,1)S(1)}, bf16[80,128]{1,0:T(8,128)(2,1)S(1)}, bf16[80,128]{1,0:T(8,128)(2,1)S(1)}) custom-call(s32[5]{0:T(128)S(1)} %stack.23.info, s32[64]{0:T(128)S(1)} %copy-done.6, s32[1,2048]{1,0:T(1,128)S(1)} %bitcast.10, ...), custom_call_target="tpu_custom_call" | custom-call | flops 2000000000 | bytes 1000 | tf_op jit(solution)/shard_map/pallas_call | solution.py:647
  15.4 0.1 collective-permute-start.2
  15.5 1.5 %collective-permute-done.2 = bf16[128,896]{1,0:T(8,128)(2,1)S(1)} collective-permute-done((bf16[128,896]{1,0:T(8,128)(2,1)S(1)}, bf16[128,896]{1,0:T(8,128)(2,1)S(1)}, u32[]{:S(2)}, u32[]{:S(2)}) %collective-permute-start.2) | collective-permute-done | bytes 229408 | tf_op jit(solution)/shard_map/ppermute | solution.py:582
  16.9 0.1 add_convert_fusion
  17.0 0.2 collective-permute-start.5
  17.2 1.3 %collective-permute-start.3 = (bf16[64,896]{1,0:T(8,128)(2,1)S(1)}, bf16[64,896]{1,0:T(8,128)(2,1)S(1)}, u32[]{:S(2)}, u32[]{:S(2)}) collective-permute-start(bf16[64,896]{1,0:T(8,128)(2,1)S(1)} %get-tuple-element.83), channel_id=1, source_target_pairs={{0,2},{1,3},{2,0},{3,1},{4,6},{5,7},{6,4},{7,5},{8,10},{9,11},{10,... | collective-permute-start | bytes 344072 | tf_op jit(solution)/shard_map/ppermute | solution.py:598
  18.6 3.1 %collective-permute-done.3.refs_1_ = bf16[64,896]{1,0:T(8,128)(2,1)S(1)} collective-permute-done((bf16[64,896]{1,0:T(8,128)(2,1)S(1)}, bf16[64,896]{1,0:T(8,128)(2,1)S(1)}, u32[]{:S(2)}, u32[]{:S(2)}) %collective-permute-start.3) | collective-permute-done | bytes 114720 | tf_op jit(solution)/shard_map/ppermute | solution.py:598
  21.7 0.3 shard_map.156
  22.0 1.3 %collective-permute-start.4 = (bf16[64,768]{1,0:T(8,128)(2,1)S(1)}, bf16[64,768]{1,0:T(8,128)(2,1)S(1)}, u32[]{:S(2)}, u32[]{:S(2)}) collective-permute-start(bf16[64,768]{1,0:T(8,128)(2,1)S(1)} %get-tuple-element.52.own_act), channel_id=1, source_target_pairs={{0,2},{1,3},{2,0},{3,1},{4,6},{5,7},{6,4},{7,5},{8,10},{9,11},{10,... | collective-permute-start | bytes 294920 | tf_op jit(solution)/shard_map/ppermute | solution.py:598
  23.3 1.5 %collective-permute-start.6 = (bf16[64,768]{1,0:T(8,128)(2,1)S(1)}, bf16[64,768]{1,0:T(8,128)(2,1)S(1)}, u32[]{:S(2)}, u32[]{:S(2)}) collective-permute-start(bf16[64,768]{1,0:T(8,128)(2,1)S(1)} %get-tuple-element.59.refs_0_), channel_id=1, source_target_pairs={{0,1},{1,0},{2,3},{3,2},{4,5},{5,4},{6,7},{7,6},{8,9},{9,8},{10,11... | collective-permute-start | bytes 294920 | tf_op jit(solution)/shard_map/ppermute | solution.py:582
  24.8 1.3 %collective-permute-start.7 = (bf16[64,768]{1,0:T(8,128)(2,1)S(1)}, bf16[64,768]{1,0:T(8,128)(2,1)S(1)}, u32[]{:S(2)}, u32[]{:S(2)}) collective-permute-start(bf16[64,768]{1,0:T(8,128)(2,1)S(1)} %get-tuple-element.59.refs_0_), channel_id=1, source_target_pairs={{0,4},{4,0},{8,12},{12,8},{1,5},{5,1},{9,13},{13,9},{2,6},{6,2},{1... | collective-permute-start | bytes 294920 | tf_op jit(solution)/shard_map/ppermute | solution.py:603
  26.1 1.7 %collective-permute-start.8 = (bf16[64,768]{1,0:T(8,128)(2,1)S(1)}, bf16[64,768]{1,0:T(8,128)(2,1)S(1)}, u32[]{:S(2)}, u32[]{:S(2)}) collective-permute-start(bf16[64,768]{1,0:T(8,128)(2,1)S(1)} %get-tuple-element.59.refs_0_), channel_id=1, source_target_pairs={{0,8},{4,12},{8,0},{12,4},{1,9},{5,13},{9,1},{13,5},{2,10},{6,14},... | collective-permute-start | bytes 294920 | tf_op jit(solution)/shard_map/ppermute | solution.py:603
  27.8 1.5 %collective-permute-start.9 = (bf16[64,768]{1,0:T(8,128)(2,1)S(1)}, bf16[64,768]{1,0:T(8,128)(2,1)S(1)}, u32[]{:S(2)}, u32[]{:S(2)}) collective-permute-start(bf16[64,768]{1,0:T(8,128)(2,1)S(1)} %get-tuple-element.59.refs_0_), channel_id=1, source_target_pairs={{0,12},{4,8},{8,4},{12,0},{1,13},{5,9},{9,5},{13,1},{2,14},{6,10},... | collective-permute-start | bytes 294920 | tf_op jit(solution)/shard_map/ppermute | solution.py:603
  29.3 2.6 %shard_map.157 = (bf16[128,768]{1,0:T(8,128)(2,1)S(1)}, bf16[128,768]{1,0:T(8,128)(2,1)S(1)}, f32[128,768]{1,0:T(8,128)S(1)}) custom-call(s32[5]{0:T(128)S(1)} %stack.23.info, bf16[768,3072]{1,0:T(8,128)(2,1)} %weight_far.3, f32[1,768]{1,0:T(1,128)S(1)} %reshape.14.refs_2_.gain, bf16[64,768]{1,0:T(8,128)(2,1)S(1)} %get-tuple-element.52.own_act, ...), custom_call_target="tpu_custom_call" | custom-call | flops 1000 | bytes 1000 | tf_op jit(solution)/shard_map/pallas_call | solution.py:680
  32.0 0.0 collective-permute-done.6.refs_1_
  32.0 4.0 %shard_map.158 = (bf16[768,768]{1,0:T(8,128)(2,1)S(1)}, bf16[768,768]{1,0:T(8,128)(2,1)S(1)}, bf16[16,128,384]{2,1,0:T(8,128)(2,1)S(1)}, f32[128,768]{1,0:T(8,12...) custom-call(s32[5]{0:T(128)S(1)} %stack.23.info, bf16[768,3072]{1,0:T(8,128)(2,1)} %weight_far.3, ...), custom_call_target="tpu_custom_call" | custom-call | flops 1000 | bytes 1000 | tf_op jit(solution)/shard_map/pallas_call | solution.py:704
  36.1 2.4 %collective-permute-start.10 = (bf16[64,768]{1,0:T(8,128)(2,1)S(1)}, bf16[64,768]{1,0:T(8,128)(2,1)S(1)}, u32[]{:S(2)}, u32[]{:S(2)}) collective-permute-start(bf16[64,768]{1,0:T(8,128)(2,1)S(1)} %collective-permute-done.7.refs_0_), channel_id=1, source_target_pairs={{0,1},{1,0},{2,3},{3,2},{4,5},{5,4},{6,7},{7,6},{8,9},{9,8},{10,11... | collective-permute-start | bytes 294920 | tf_op jit(solution)/shard_map/ppermute | solution.py:582
  38.5 0.1 collective-permute-start.11
  38.6 0.4 collective-permute-start.12
  39.0 0.4 collective-permute-done.10.refs_3_
  39.5 0.4 collective-permute-done.11.refs_4_
  39.8 0.2 collective-permute-done.12.refs_5_
  40.0 4.1 %shard_map.159.refs_0_ = bf16[128,896]{1,0:T(8,128)(2,1)S(1)} custom-call(bf16[128,768]{1,0:T(8,128)(2,1)S(1)} %get-tuple-element.57.queries, bf16[768,768]{1,0:T(8,128)(2,1)S(1)} %get-tuple-element.60.key_weight, bf16[768,768]{1,0:T(8,128)(2,1)S(1)} %get-tuple-element.61.value_weight, bf16[16,128,384]{2,1,0:T(8,128)(2,1)S(1)} %get-tuple-element.62.bias, ...), custom_call_target="tpu_custom_call" | custom-call | flops 2000000000 | bytes 1000 | tf_op jit(solution)/shard_map/pallas_call | solution.py:713
  44.1 0.0 copy-start
  44.1 0.0 copy-start.3
  44.1 0.0 copy-start.7
  44.1 0.5 collective-permute-start.15
  44.6 0.6 %collective-permute-start.13 = (bf16[80,128]{1,0:T(8,128)(2,1)S(1)}, bf16[80,128]{1,0:T(8,128)(2,1)S(1)}, u32[]{:S(2)}, u32[]{:S(2)}) collective-permute-start(bf16[80,128]{1,0:T(8,128)(2,1)S(1)} %get-tuple-element.71), channel_id=1, source_target_pairs={{0,1},{1,0},{2,3},{3,2},{4,5},{5,4},{6,7},{7,6},{8,9},{9,8},{10,11... | collective-permute-start | bytes 61448 | tf_op jit(solution)/shard_map/ppermute | solution.py:582
  45.2 3.0 %collective-permute-start.14 = (bf16[80,128]{1,0:T(8,128)(2,1)S(1)}, bf16[80,128]{1,0:T(8,128)(2,1)S(1)}, u32[]{:S(2)}, u32[]{:S(2)}) collective-permute-start(bf16[80,128]{1,0:T(8,128)(2,1)S(1)} %get-tuple-element.72), channel_id=1, source_target_pairs={{0,0},{1,2},{2,1},{3,4},{4,3},{5,6},{6,5},{7,8},{8,7},{9,10},{10,9... | collective-permute-start | bytes 61448 | tf_op jit(solution)/shard_map/ppermute | solution.py:587
  48.3 3.5 %collective-permute-done.14.far = bf16[80,128]{1,0:T(8,128)(2,1)S(1)} collective-permute-done((bf16[80,128]{1,0:T(8,128)(2,1)S(1)}, bf16[80,128]{1,0:T(8,128)(2,1)S(1)}, u32[]{:S(2)}, u32[]{:S(2)}) %collective-permute-start.14) | collective-permute-done | bytes 20512 | tf_op jit(solution)/shard_map/ppermute | solution.py:587
  51.8 0.9 %shard_map.160.own_back = bf16[128,128]{1,0:T(8,128)(2,1)S(1)} custom-call(bf16[128,768]{1,0:T(8,128)(2,1)S(1)} %get-tuple-element.53.act, f32[128,768]{1,0:T(8,128)S(1)} %get-tuple-element.54.gates, bf16[768,768]{1,0:T(8,128)(2,1)S(1)} %copy-done.1, bf16[768,128]{1,0:T(8,128)(2,1)S(1)} %copy-done.2, bf16[128,896]{1,0:T(8,128)(2,1)S(1)} %shard_map.159.refs_0_, ...), custom_call_target="tpu_custom_call" | custom-call | flops 200000000 | bytes 1000 | tf_op jit(solution)/shard_map/pallas_call | solution.py:727
  52.7 0.5 collective-permute-start.16
  53.2 2.4 %collective-permute-start.17 = (bf16[64,128]{1,0:T(8,128)(2,1)S(1)}, bf16[64,128]{1,0:T(8,128)(2,1)S(1)}, u32[]{:S(2)}, u32[]{:S(2)}) collective-permute-start(bf16[64,128]{1,0:T(8,128)(2,1)S(1)} %slice_select_fusion), channel_id=1, source_target_pairs={{0,0},{1,4},{2,2},{3,6},{4,1},{5,8},{6,3},{7,10},{8,5},{9,12},{10,... | collective-permute-start | bytes 49160 | tf_op jit(solution)/shard_map/ppermute | solution.py:595
  55.7 0.0 copy-start.4
  55.7 5.2 %shard_map.161 = (bf16[2048,128]{1,0:T(8,128)(2,1)S(1)}, bf16[2048,128]{1,0:T(8,128)(2,1)S(1)}, bf16[128,128]{1,0:T(8,128)(2,1)S(1)}, f32[256,128]{1,0:T(8,128)S(1)}, f32[256,128]{1,0:T(8,128)S(1)}) custom-call(s32[5]{0:T(128)S(1)} %stack.23.info, s32[64]{0:T(128)S(1)} %copy-done.6, s32[1,2048]{1,0:T(1,128)S(1)} %bitcast.11, ...), custom_call_target="tpu_custom_call" | custom-call | flops 1500000000 | bytes 1000 | tf_op jit(solution)/shard_map/pallas_call | solution.py:746
  60.9 2.6 %shard_map.162 = bf16[2048,128]{1,0:T(8,128)(2,1)} custom-call(s32[5]{0:T(128)S(1)} %stack.23.info, s32[64]{0:T(128)S(1)} %copy-done.6, bf16[2048,128]{1,0:T(8,128)(2,1)S(1)} %get-tuple-element.74.atoms2, bf16[80,128]{1,0:T(8,128)(2,1)S(1)} %collective-permute-done.13.near, bf16[80,128]{1,0:T(8,128)(2,1)S(1)} %collective-permute-done.14.far, ...), custom_call_target="tpu_custom_call" | custom-call | flops 300000000 | bytes 1000 | tf_op jit(solution)/shard_map/pallas_call | solution.py:754
  (33 shorter events, 0.1 us)
Async XLA Ops:
  0.7 10.9 %collective-permute-start = (bf16[64,128]{1,0:T(8,128)(2,1)S(1)}, bf16[64,128]{1,0:T(8,128)(2,1)S(1)}, u32[]{:S(2)}, u32[]{:S(2)}) collective-permute-start(bf16[64,128]{1,0:T(8,128)(2,1)S(1)} %get-tuple-element.82), channel_id=1, source_target_pairs={{0,1},{1,0},{2,3},{3,2},{4,5},{5,4},{6,7},{7,6},{8,9},{9,8},{10,11... | collective-permute-start | bytes 49160 | tf_op jit(solution)/shard_map/ppermute | solution.py:582
  0.8 10.8 %collective-permute-start.1 = (bf16[64,128]{1,0:T(8,128)(2,1)S(1)}, bf16[64,128]{1,0:T(8,128)(2,1)S(1)}, u32[]{:S(2)}, u32[]{:S(2)}) collective-permute-start(bf16[64,128]{1,0:T(8,128)(2,1)S(1)} %get-tuple-element.81), channel_id=1, source_target_pairs={{0,0},{1,2},{2,1},{3,4},{4,3},{5,6},{6,5},{7,8},{8,7},{9,10},{10,9... | collective-permute-start | bytes 49160 | tf_op jit(solution)/shard_map/ppermute | solution.py:587
  5.4 6.3 %copy-start.5 = (bf16[2048,128]{1,0:T(8,128)(2,1)S(1)}, bf16[2048,128]{1,0:T(8,128)(2,1)}, u32[]{:S(2)}) copy-start(bf16[2048,128]{1,0:T(8,128)(2,1)} %acts.1) | copy-start | bytes 1572868
  5.4 6.3 %copy-start.6 = (s32[64]{0:T(128)S(1)}, s32[64]{0:T(128)}, u32[]{:S(2)}) copy-start(s32[64]{0:T(128)} %offsets.5) | copy-start | bytes 772
  5.4 6.3 %copy-start.8 = (bf16[128,768]{1,0:T(8,128)(2,1)S(1)}, bf16[128,768]{1,0:T(8,128)(2,1)}, u32[]{:S(2)}) copy-start(bf16[128,768]{1,0:T(8,128)(2,1)} %up.1) | copy-start | bytes 589828
  5.4 6.3 %copy-start.9 = (bf16[128,384]{1,0:T(8,128)(2,1)S(1)}, bf16[128,384]{1,0:T(8,128)(2,1)}, u32[]{:S(2)}) copy-start(bf16[128,384]{1,0:T(8,128)(2,1)} %qkv.3) | copy-start | bytes 294916
  5.4 6.3 %copy-start.10 = (bf16[128,128]{1,0:T(8,128)(2,1)S(1)}, bf16[128,128]{1,0:T(8,128)(2,1)}, u32[]{:S(2)}) copy-start(bf16[128,128]{1,0:T(8,128)(2,1)} %out_weight.2) | copy-start | bytes 98308
  5.4 6.3 %copy-start.11 = (s32[2048]{0:T(1024)S(1)}, s32[2048]{0:T(1024)}, u32[]{:S(2)}) copy-start(s32[2048]{0:T(1024)} %param.25) | copy-start | bytes 24580
  5.4 6.3 %copy-start.12 = (f32[128]{0:T(128)S(1)}, f32[128]{0:T(128)}, u32[]{:S(2)}) copy-start(f32[128]{0:T(128)} %param.17) | copy-start | bytes 1540
  11.7 5.3 %copy-start.13 = (bf16[16,256,256]{2,1,0:T(8,128)(2,1)S(1)}, bf16[16,256,256]{2,1,0:T(8,128)(2,1)}, u32[]{:S(2)}) copy-start(bf16[16,256,256]{2,1,0:T(8,128)(2,1)} %own_far.1) | copy-start | bytes 6291460
  11.7 6.9 %copy-start.14 = (f32[768]{0:T(1024)S(1)}, f32[768]{0:T(1024)}, u32[]{:S(2)}) copy-start(f32[768]{0:T(1024)} %param.27) | copy-start | bytes 9220
  15.4 1.6 %collective-permute-start.2 = (bf16[128,896]{1,0:T(8,128)(2,1)S(1)}, bf16[128,896]{1,0:T(8,128)(2,1)S(1)}, u32[]{:S(2)}, u32[]{:S(2)}) collective-permute-start(bf16[128,896]{1,0:T(8,128)(2,1)S(1)} %get-tuple-element.50), channel_id=1, source_target_pairs={{0,1},{1,0},{2,3},{3,2},{4,5},{5,4},{6,7},{7,6},{8,9},{9,8},{10,11... | collective-permute-start | bytes 688136 | tf_op jit(solution)/shard_map/ppermute | solution.py:582
  17.0 15.0 %collective-permute-start.5 = (bf16[16,256,256]{2,1,0:T(8,128)(2,1)S(1)}, bf16[16,256,256]{2,1,0:T(8,128)(2,1)}, u32[]{:S(2)}, u32[]{:S(2)}) collective-permute-start(bf16[16,256,256]{2,1,0:T(8,128)(2,1)S(1)} %copy-done.13), channel_id=1, source_target_pairs={{0,1},{1,0},{2,3},{3,2},{4,5},{5,4},{6,7},{7,6},{8,9},{9,8},{10,11... | collective-permute-start | bytes 6291464 | tf_op jit(solution)/shard_map/ppermute | solution.py:582
  17.2 4.4 %collective-permute-start.3 = (bf16[64,896]{1,0:T(8,128)(2,1)S(1)}, bf16[64,896]{1,0:T(8,128)(2,1)S(1)}, u32[]{:S(2)}, u32[]{:S(2)}) collective-permute-start(bf16[64,896]{1,0:T(8,128)(2,1)S(1)} %get-tuple-element.83), channel_id=1, source_target_pairs={{0,2},{1,3},{2,0},{3,1},{4,6},{5,7},{6,4},{7,5},{8,10},{9,11},{10,... | collective-permute-start | bytes 344072 | tf_op jit(solution)/shard_map/ppermute | solution.py:598
  22.0 5.8 %collective-permute-start.4 = (bf16[64,768]{1,0:T(8,128)(2,1)S(1)}, bf16[64,768]{1,0:T(8,128)(2,1)S(1)}, u32[]{:S(2)}, u32[]{:S(2)}) collective-permute-start(bf16[64,768]{1,0:T(8,128)(2,1)S(1)} %get-tuple-element.52.own_act), channel_id=1, source_target_pairs={{0,2},{1,3},{2,0},{3,1},{4,6},{5,7},{6,4},{7,5},{8,10},{9,11},{10,... | collective-permute-start | bytes 294920 | tf_op jit(solution)/shard_map/ppermute | solution.py:598
  23.3 8.6 %collective-permute-start.6 = (bf16[64,768]{1,0:T(8,128)(2,1)S(1)}, bf16[64,768]{1,0:T(8,128)(2,1)S(1)}, u32[]{:S(2)}, u32[]{:S(2)}) collective-permute-start(bf16[64,768]{1,0:T(8,128)(2,1)S(1)} %get-tuple-element.59.refs_0_), channel_id=1, source_target_pairs={{0,1},{1,0},{2,3},{3,2},{4,5},{5,4},{6,7},{7,6},{8,9},{9,8},{10,11... | collective-permute-start | bytes 294920 | tf_op jit(solution)/shard_map/ppermute | solution.py:582
  24.8 11.2 %collective-permute-start.7 = (bf16[64,768]{1,0:T(8,128)(2,1)S(1)}, bf16[64,768]{1,0:T(8,128)(2,1)S(1)}, u32[]{:S(2)}, u32[]{:S(2)}) collective-permute-start(bf16[64,768]{1,0:T(8,128)(2,1)S(1)} %get-tuple-element.59.refs_0_), channel_id=1, source_target_pairs={{0,4},{4,0},{8,12},{12,8},{1,5},{5,1},{9,13},{13,9},{2,6},{6,2},{1... | collective-permute-start | bytes 294920 | tf_op jit(solution)/shard_map/ppermute | solution.py:603
  26.1 9.9 %collective-permute-start.8 = (bf16[64,768]{1,0:T(8,128)(2,1)S(1)}, bf16[64,768]{1,0:T(8,128)(2,1)S(1)}, u32[]{:S(2)}, u32[]{:S(2)}) collective-permute-start(bf16[64,768]{1,0:T(8,128)(2,1)S(1)} %get-tuple-element.59.refs_0_), channel_id=1, source_target_pairs={{0,8},{4,12},{8,0},{12,4},{1,9},{5,13},{9,1},{13,5},{2,10},{6,14},... | collective-permute-start | bytes 294920 | tf_op jit(solution)/shard_map/ppermute | solution.py:603
  27.8 8.3 %collective-permute-start.9 = (bf16[64,768]{1,0:T(8,128)(2,1)S(1)}, bf16[64,768]{1,0:T(8,128)(2,1)S(1)}, u32[]{:S(2)}, u32[]{:S(2)}) collective-permute-start(bf16[64,768]{1,0:T(8,128)(2,1)S(1)} %get-tuple-element.59.refs_0_), channel_id=1, source_target_pairs={{0,12},{4,8},{8,4},{12,0},{1,13},{5,9},{9,5},{13,1},{2,14},{6,10},... | collective-permute-start | bytes 294920 | tf_op jit(solution)/shard_map/ppermute | solution.py:603
  36.1 3.4 %collective-permute-start.10 = (bf16[64,768]{1,0:T(8,128)(2,1)S(1)}, bf16[64,768]{1,0:T(8,128)(2,1)S(1)}, u32[]{:S(2)}, u32[]{:S(2)}) collective-permute-start(bf16[64,768]{1,0:T(8,128)(2,1)S(1)} %collective-permute-done.7.refs_0_), channel_id=1, source_target_pairs={{0,1},{1,0},{2,3},{3,2},{4,5},{5,4},{6,7},{7,6},{8,9},{9,8},{10,11... | collective-permute-start | bytes 294920 | tf_op jit(solution)/shard_map/ppermute | solution.py:582
  38.5 1.3 %collective-permute-start.11 = (bf16[64,768]{1,0:T(8,128)(2,1)S(1)}, bf16[64,768]{1,0:T(8,128)(2,1)S(1)}, u32[]{:S(2)}, u32[]{:S(2)}) collective-permute-start(bf16[64,768]{1,0:T(8,128)(2,1)S(1)} %collective-permute-done.8.refs_1_), channel_id=1, source_target_pairs={{0,1},{1,0},{2,3},{3,2},{4,5},{5,4},{6,7},{7,6},{8,9},{9,8},{10,11... | collective-permute-start | bytes 294920 | tf_op jit(solution)/shard_map/ppermute | solution.py:582
  38.6 1.4 %collective-permute-start.12 = (bf16[64,768]{1,0:T(8,128)(2,1)S(1)}, bf16[64,768]{1,0:T(8,128)(2,1)S(1)}, u32[]{:S(2)}, u32[]{:S(2)}) collective-permute-start(bf16[64,768]{1,0:T(8,128)(2,1)S(1)} %collective-permute-done.9.refs_2_), channel_id=1, source_target_pairs={{0,1},{1,0},{2,3},{3,2},{4,5},{5,4},{6,7},{7,6},{8,9},{9,8},{10,11... | collective-permute-start | bytes 294920 | tf_op jit(solution)/shard_map/ppermute | solution.py:582
  40.0 11.8 %copy-start.1 = (bf16[768,768]{1,0:T(8,128)(2,1)S(1)}, bf16[768,768]{1,0:T(8,128)(2,1)}, u32[]{:S(2)}) copy-start(bf16[768,768]{1,0:T(8,128)(2,1)} %token_out.1) | copy-start | bytes 3538948
  40.0 11.8 %copy-start.2 = (bf16[768,128]{1,0:T(8,128)(2,1)S(1)}, bf16[768,128]{1,0:T(8,128)(2,1)}, u32[]{:S(2)}) copy-start(bf16[768,128]{1,0:T(8,128)(2,1)} %down.1) | copy-start | bytes 589828
  44.1 11.6 %copy-start = (bf16[4,2048,128]{2,1,0:T(8,128)(2,1)S(1)}, bf16[4,2048,128]{2,1,0:T(8,128)(2,1)}, u32[]{:S(2)}) copy-start(bf16[4,2048,128]{2,1,0:T(8,128)(2,1)} %bias.3) | copy-start | bytes 6291460
  44.1 11.6 %copy-start.3 = (bf16[128,384]{1,0:T(8,128)(2,1)S(1)}, bf16[128,384]{1,0:T(8,128)(2,1)}, u32[]{:S(2)}) copy-start(bf16[128,384]{1,0:T(8,128)(2,1)} %qkv.5) | copy-start | bytes 294916
  44.1 11.6 %copy-start.7 = (f32[128]{0:T(128)S(1)}, f32[128]{0:T(128)}, u32[]{:S(2)}) copy-start(f32[128]{0:T(128)} %param.20) | copy-start | bytes 1540
  44.1 7.7 %collective-permute-start.15 = (bf16[128,896]{1,0:T(8,128)(2,1)S(1)}, bf16[128,896]{1,0:T(8,128)(2,1)S(1)}, u32[]{:S(2)}, u32[]{:S(2)}) collective-permute-start(bf16[128,896]{1,0:T(8,128)(2,1)S(1)} %shard_map.159.refs_0_), channel_id=1, source_target_pairs={{0,2},{1,3},{2,0},{3,1},{4,6},{5,7},{6,4},{7,5},{8,10},{9,11},{10,... | collective-permute-start | bytes 688136 | tf_op jit(solution)/shard_map/ppermute | solution.py:598
  44.6 3.7 %collective-permute-start.13 = (bf16[80,128]{1,0:T(8,128)(2,1)S(1)}, bf16[80,128]{1,0:T(8,128)(2,1)S(1)}, u32[]{:S(2)}, u32[]{:S(2)}) collective-permute-start(bf16[80,128]{1,0:T(8,128)(2,1)S(1)} %get-tuple-element.71), channel_id=1, source_target_pairs={{0,1},{1,0},{2,3},{3,2},{4,5},{5,4},{6,7},{7,6},{8,9},{9,8},{10,11... | collective-permute-start | bytes 61448 | tf_op jit(solution)/shard_map/ppermute | solution.py:582
  45.2 6.6 %collective-permute-start.14 = (bf16[80,128]{1,0:T(8,128)(2,1)S(1)}, bf16[80,128]{1,0:T(8,128)(2,1)S(1)}, u32[]{:S(2)}, u32[]{:S(2)}) collective-permute-start(bf16[80,128]{1,0:T(8,128)(2,1)S(1)} %get-tuple-element.72), channel_id=1, source_target_pairs={{0,0},{1,2},{2,1},{3,4},{4,3},{5,6},{6,5},{7,8},{8,7},{9,10},{10,9... | collective-permute-start | bytes 61448 | tf_op jit(solution)/shard_map/ppermute | solution.py:587
  52.7 2.9 %collective-permute-start.16 = (bf16[128,128]{1,0:T(8,128)(2,1)S(1)}, bf16[128,128]{1,0:T(8,128)(2,1)S(1)}, u32[]{:S(2)}, u32[]{:S(2)}) collective-permute-start(bf16[128,128]{1,0:T(8,128)(2,1)S(1)} %shard_map.160.own_back), channel_id=1, source_target_pairs={{0,1},{1,0},{2,3},{3,2},{4,5},{5,4},{6,7},{7,6},{8,9},{9,8},{10,11... | collective-permute-start | bytes 98312 | tf_op jit(solution)/shard_map/ppermute | solution.py:582
  53.2 7.7 %collective-permute-start.17 = (bf16[64,128]{1,0:T(8,128)(2,1)S(1)}, bf16[64,128]{1,0:T(8,128)(2,1)S(1)}, u32[]{:S(2)}, u32[]{:S(2)}) collective-permute-start(bf16[64,128]{1,0:T(8,128)(2,1)S(1)} %slice_select_fusion), channel_id=1, source_target_pairs={{0,0},{1,4},{2,2},{3,6},{4,1},{5,8},{6,3},{7,10},{8,5},{9,12},{10,... | collective-permute-start | bytes 49160 | tf_op jit(solution)/shard_map/ppermute | solution.py:595
  55.7 5.2 %copy-start.4 = (bf16[128,128]{1,0:T(8,128)(2,1)S(1)}, bf16[128,128]{1,0:T(8,128)(2,1)}, u32[]{:S(2)}) copy-start(bf16[128,128]{1,0:T(8,128)(2,1)} %out_weight.3) | copy-start | bytes 98308

commit v5 on v4

--- a/solution.py
+++ b/solution.py
@@ -577,22 +577,36 @@
     side, pair = col % 2, col // 2
     info = jnp.stack([side, row, pair, col, (row * col_count + col) * rows]).astype(jnp.int32)
     devices = row_count * col_count
+    group_count = lax.axis_size("group")
 
     def to_near(x):
         return lax.ppermute(x, "col", [(i, i ^ 1) for i in range(col_count)])
 
+    def swapped(x, swap):
+        pairs_list = []
+        for i in range(group_count * devices):
+            group_at, at = divmod(i, devices)
+            if at in swap:
+                target = group_at * devices + swap[at]
+            else:
+                target = (group_at ^ 1) * devices + at if group_count % 2 == 0 else i
+            pairs_list.append((i, target))
+        return lax.ppermute(x, ("group", "row", "col"), pairs_list)
+
     def to_far(x):
-        swap = [(i, i + 1 if i % 2 else i - 1) for i in range(1, devices - 1)]
-        swap = [(0, 0)] + swap + [(devices - 1, devices - 1)]
-        return lax.ppermute(x, ("row", "col"), swap)
+        return swapped(x, {i: i + 1 if i % 2 else i - 1 for i in range(1, devices - 1)})
 
     def to_beyond(x):
-        swap = {i: i for i in range(devices)}
+        swap = {}
         for i in range(1, row_count):
             first, last = i * col_count, i * col_count - 1
             for one, other in ((first, first - col_count + 1), (last, last + col_count - 1)):
                 swap[one], swap[other] = other, one
-        return lax.ppermute(x, ("row", "col"), sorted(swap.items()))
+        if col_count > 4:
+            for i in range(devices):
+                if 2 <= i % col_count < col_count - 2:
+                    swap[i] = i ^ 1
+        return swapped(x, swap)
 
     def along_pairs(x, step):
         return lax.ppermute(
@@ -672,7 +686,8 @@
     group = LANES // share
     solo = group == 2
     split = 1 if solo else group
-    own_keys = [normed] + [along_rows(normed, step) for step in range(1, row_count)]
+    moved_keys = [along_rows(normed, step) for step in range(row_count - 1, 0, -1)]
+    own_keys = [normed] + moved_keys[::-1]
     near_keys = [to_near(x) for x in own_keys[:split]]
     other_acts = [along_pairs(act, step) for step in range(1, pairs)]
     half_shape = jax.ShapeDtypeStruct((half, wide), BF)

time: 63.8 us -> 60.9 us (0.955)
  starting transfers between devices: 23.4 us -> 17.5 us
  waiting for transfers between devices: 9.08 us -> 11.6 us
    ppermute x3, starting transfers between devices: 9.9 us -> 3.34 us  [swapped(): return lax.ppermute(x, ('group', 'row', 'col'), pairs_list)]
    ppermute x3, waiting for transfers between devices: 3.54 us -> 5.06 us  [swapped(): return lax.ppermute(x, ('group', 'row', 'col'), pairs_list)]
    ppermute x9, starting transfers between devices: 5.86 us -> 6.52 us  [to_near(): return lax.ppermute(x, 'col', [(i, i ^ 1) for i in range(col_count)])]
  transfers between devices with their start and end apart: 18 -> 18, of which waited for: 6 -> 8; matrix products, arithmetic and copies ran while one was open for 0% -> 0% of each run, Pallas kernels for 29% -> 31%
where the time goes in v5:
time: 60.9 us; the launch traced here: 59.9 us
  Pallas kernels  29.6 us (49%)
  starting transfers between devices  17.5 us (29%)
  waiting for transfers between devices  11.6 us (19%)
  local copies, waits for them, and re-layouts  0.92 us (2%)
    ppermute x9, starting transfers between devices, to_near(): return lax.ppermute(x, 'col', [(i, i ^ 1) for i in range(col_count)])  6.52 us
    pallas_call x1, Pallas kernels, body(): call(functools.partial(first_inner, pieces=pieces), [atom_shape] + edge_s...  6.17 us
    pallas_call x1, Pallas kernels, body(): call(functools.partial(second_inner, share=share), [atom_shape, atom_shap...  5.16 us
    ppermute x3, waiting for transfers between devices, swapped(): return lax.ppermute(x, ('group', 'row', 'col'), pairs_list)  5.06 us
    ppermute x3, starting transfers between devices, along_rows(): return lax.ppermute(x, 'row', [(i, i ^ step) for i in range(row_count)])  4.53 us
    pallas_call x1, Pallas kernels, body(): call(functools.partial(attend_rest, steps=list(range(split, row_count)),...  4.07 us
    pallas_call x1, Pallas kernels, body(): call(functools.partial(attend_first, steps=list(range(split)), solo=solo)...  4.04 us
    pallas_call x1, Pallas kernels, body(): call(functools.partial(first_edge, share=share), [atom_shape, packed_shap...  3.67 us
  transfers between devices with their start and end apart: 18, of which 8 were waited for; matrix products, arithmetic and copies ran while one was open for 0% of the time, Pallas kernels for 31%

profile of v5, /device:TPU:1, one launch (start us, length us, event | category | flops | bytes accessed | tf_op | source)
XLA Modules:
  0.0 59.9 jit_solution(13575613046948734851)
XLA Ops:
  0.0 0.7 %constant_dynamic-slice_fusion.2 = (bf16[64,128]{1,0:T(8,128)(2,1)S(1)}, bf16[64,128]{1,0:T(8,128)(2,1)S(1)}) fusion(bf16[2048,128]{1,0:T(8,128)(2,1)} %acts.1, s32[]{:T(128)S(6)} %select_n.41, s32[]{:T(128)S(6)} %select_n.40), kind=kLoop, calls=%fused_computation.4 | loop fusion | bytes 65544 | tf_op jit(solution)/shard_map/dynamic_slice | solution.py:620
  0.7 0.1 collective-permute-start
  0.8 2.5 %collective-permute-start.1 = (bf16[64,128]{1,0:T(8,128)(2,1)S(1)}, bf16[64,128]{1,0:T(8,128)(2,1)S(1)}, u32[]{:S(2)}, u32[]{:S(2)}) collective-permute-start(bf16[64,128]{1,0:T(8,128)(2,1)S(1)} %get-tuple-element.81), channel_id=1, source_target_pairs={{0,16},{1,2},{2,1},{3,4},{4,3},{5,6},{6,5},{7,8},{8,7},{9,10},{10,... | collective-permute-start | bytes 49160 | tf_op jit(solution)/shard_map/ppermute | solution.py:594
  3.3 0.1 stack.23.info
  3.4 0.0 copy-start.10
  3.5 0.0 copy-start.11
  3.5 0.0 copy-start.12
  3.5 6.2 %shard_map.154 = (bf16[2048,128]{1,0:T(8,128)(2,1)S(1)}, bf16[128,128]{1,0:T(8,128)(2,1)S(1)}, f32[256,128]{1,0:T(8,128)S(1)}, f32[256,128]{1,0:T(8,128)S(1)}, bf16[4,128,128]{2,1,0:T(8,128)(2,1)S(1)}) custom-call(s32[5]{0:T(128)S(1)} %stack.23.info, bf16[2048,128]{1,0:T(8,128)(2,1)} %acts.1, f32[1,128]{1,0:T(1,128)} %bitcast.12, bf16[128,384]{1,0:T(8,128)(2,1)} %qkv.3, ...), custom_call_target="tpu_custom_call" | custom-call | flops 1500000000 | bytes 1000 | tf_op jit(solution)/shard_map/pallas_call | solution.py:649
  9.7 0.0 collective-permute-done.1.far
  9.7 0.0 copy-start.13
  9.8 0.0 copy-start.14
  9.8 3.7 %shard_map.155 = (bf16[2048,128]{1,0:T(8,128)(2,1)S(1)}, bf16[128,896]{1,0:T(8,128)(2,1)S(1)}, bf16[128,896]{1,0:T(8,128)(2,1)S(1)}, bf16[80,128]{1,0:T(8,128)(2,1)S(1)}, bf16[80,128]{1,0:T(8,128)(2,1)S(1)}) custom-call(s32[5]{0:T(128)S(1)} %stack.23.info, s32[64]{0:T(128)S(1)} %copy-done.6, s32[1,2048]{1,0:T(1,128)S(1)} %bitcast.10, ...), custom_call_target="tpu_custom_call" | custom-call | flops 2000000000 | bytes 1000 | tf_op jit(solution)/shard_map/pallas_call | solution.py:661
  13.4 0.5 collective-permute-start.2
  13.9 1.1 %collective-permute-done.2 = bf16[128,896]{1,0:T(8,128)(2,1)S(1)} collective-permute-done((bf16[128,896]{1,0:T(8,128)(2,1)S(1)}, bf16[128,896]{1,0:T(8,128)(2,1)S(1)}, u32[]{:S(2)}, u32[]{:S(2)}) %collective-permute-start.2) | collective-permute-done | bytes 229408 | tf_op jit(solution)/shard_map/ppermute | solution.py:583
  15.0 0.1 add_convert_fusion
  15.1 0.4 collective-permute-start.5
  15.6 1.1 %collective-permute-start.3 = (bf16[64,896]{1,0:T(8,128)(2,1)S(1)}, bf16[64,896]{1,0:T(8,128)(2,1)S(1)}, u32[]{:S(2)}, u32[]{:S(2)}) collective-permute-start(bf16[64,896]{1,0:T(8,128)(2,1)S(1)} %get-tuple-element.83), channel_id=1, source_target_pairs={{0,2},{1,3},{2,0},{3,1},{4,6},{5,7},{6,4},{7,5},{8,10},{9,11},{10,... | collective-permute-start | bytes 344072 | tf_op jit(solution)/shard_map/ppermute | solution.py:612
  16.7 3.6 %collective-permute-done.3.refs_1_ = bf16[64,896]{1,0:T(8,128)(2,1)S(1)} collective-permute-done((bf16[64,896]{1,0:T(8,128)(2,1)S(1)}, bf16[64,896]{1,0:T(8,128)(2,1)S(1)}, u32[]{:S(2)}, u32[]{:S(2)}) %collective-permute-start.3) | collective-permute-done | bytes 114720 | tf_op jit(solution)/shard_map/ppermute | solution.py:612
  20.3 0.3 shard_map.156
  20.6 0.8 %collective-permute-start.4 = (bf16[64,768]{1,0:T(8,128)(2,1)S(1)}, bf16[64,768]{1,0:T(8,128)(2,1)S(1)}, u32[]{:S(2)}, u32[]{:S(2)}) collective-permute-start(bf16[64,768]{1,0:T(8,128)(2,1)S(1)} %get-tuple-element.52.own_act), channel_id=1, source_target_pairs={{0,2},{1,3},{2,0},{3,1},{4,6},{5,7},{6,4},{7,5},{8,10},{9,11},{10,... | collective-permute-start | bytes 294920 | tf_op jit(solution)/shard_map/ppermute | solution.py:612
  21.4 1.5 %collective-permute-start.6 = (bf16[64,768]{1,0:T(8,128)(2,1)S(1)}, bf16[64,768]{1,0:T(8,128)(2,1)S(1)}, u32[]{:S(2)}, u32[]{:S(2)}) collective-permute-start(bf16[64,768]{1,0:T(8,128)(2,1)S(1)} %get-tuple-element.59.refs_0_), channel_id=1, source_target_pairs={{0,1},{1,0},{2,3},{3,2},{4,5},{5,4},{6,7},{7,6},{8,9},{9,8},{10,11... | collective-permute-start | bytes 294920 | tf_op jit(solution)/shard_map/ppermute | solution.py:583
  22.9 1.3 %collective-permute-start.7 = (bf16[64,768]{1,0:T(8,128)(2,1)S(1)}, bf16[64,768]{1,0:T(8,128)(2,1)S(1)}, u32[]{:S(2)}, u32[]{:S(2)}) collective-permute-start(bf16[64,768]{1,0:T(8,128)(2,1)S(1)} %get-tuple-element.59.refs_0_), channel_id=1, source_target_pairs={{0,4},{4,0},{8,12},{12,8},{1,5},{5,1},{9,13},{13,9},{2,6},{6,2},{1... | collective-permute-start | bytes 294920 | tf_op jit(solution)/shard_map/ppermute | solution.py:617
  24.2 2.4 %collective-permute-start.8 = (bf16[64,768]{1,0:T(8,128)(2,1)S(1)}, bf16[64,768]{1,0:T(8,128)(2,1)S(1)}, u32[]{:S(2)}, u32[]{:S(2)}) collective-permute-start(bf16[64,768]{1,0:T(8,128)(2,1)S(1)} %get-tuple-element.59.refs_0_), channel_id=1, source_target_pairs={{0,8},{4,12},{8,0},{12,4},{1,9},{5,13},{9,1},{13,5},{2,10},{6,14},... | collective-permute-start | bytes 294920 | tf_op jit(solution)/shard_map/ppermute | solution.py:617
  26.6 0.0 collective-permute-done.4.refs_0_
  26.6 0.9 %collective-permute-start.9 = (bf16[64,768]{1,0:T(8,128)(2,1)S(1)}, bf16[64,768]{1,0:T(8,128)(2,1)S(1)}, u32[]{:S(2)}, u32[]{:S(2)}) collective-permute-start(bf16[64,768]{1,0:T(8,128)(2,1)S(1)} %get-tuple-element.59.refs_0_), channel_id=1, source_target_pairs={{0,12},{4,8},{8,4},{12,0},{1,13},{5,9},{9,5},{13,1},{2,14},{6,10},... | collective-permute-start | bytes 294920 | tf_op jit(solution)/shard_map/ppermute | solution.py:617
  27.5 2.6 %shard_map.157 = (bf16[128,768]{1,0:T(8,128)(2,1)S(1)}, bf16[128,768]{1,0:T(8,128)(2,1)S(1)}, f32[128,768]{1,0:T(8,128)S(1)}) custom-call(s32[5]{0:T(128)S(1)} %stack.23.info, bf16[768,3072]{1,0:T(8,128)(2,1)} %weight_far.3, f32[1,768]{1,0:T(1,128)S(1)} %reshape.14.refs_2_.gain, bf16[64,768]{1,0:T(8,128)(2,1)S(1)} %get-tuple-element.52.own_act, ...), custom_call_target="tpu_custom_call" | custom-call | flops 1000 | bytes 1000 | tf_op jit(solution)/shard_map/pallas_call | solution.py:695
  30.1 4.0 %shard_map.158 = (bf16[768,768]{1,0:T(8,128)(2,1)S(1)}, bf16[768,768]{1,0:T(8,128)(2,1)S(1)}, bf16[16,128,384]{2,1,0:T(8,128)(2,1)S(1)}, f32[128,768]{1,0:T(8,12...) custom-call(s32[5]{0:T(128)S(1)} %stack.23.info, bf16[768,3072]{1,0:T(8,128)(2,1)} %weight_far.3, ...), custom_call_target="tpu_custom_call" | custom-call | flops 1000 | bytes 1000 | tf_op jit(solution)/shard_map/pallas_call | solution.py:719
  34.2 2.4 %collective-permute-start.10 = (bf16[64,768]{1,0:T(8,128)(2,1)S(1)}, bf16[64,768]{1,0:T(8,128)(2,1)S(1)}, u32[]{:S(2)}, u32[]{:S(2)}) collective-permute-start(bf16[64,768]{1,0:T(8,128)(2,1)S(1)} %collective-permute-done.7.refs_0_), channel_id=1, source_target_pairs={{0,1},{1,0},{2,3},{3,2},{4,5},{5,4},{6,7},{7,6},{8,9},{9,8},{10,11... | collective-permute-start | bytes 294920 | tf_op jit(solution)/shard_map/ppermute | solution.py:583
  36.6 0.1 collective-permute-start.11
  36.7 0.4 collective-permute-start.12
  37.2 0.4 collective-permute-done.10.refs_3_
  37.6 0.4 collective-permute-done.11.refs_4_
  37.9 0.2 collective-permute-done.12.refs_5_
  38.1 4.1 %shard_map.159.refs_0_ = bf16[128,896]{1,0:T(8,128)(2,1)S(1)} custom-call(bf16[128,768]{1,0:T(8,128)(2,1)S(1)} %get-tuple-element.57.queries, bf16[768,768]{1,0:T(8,128)(2,1)S(1)} %get-tuple-element.60.key_weight, bf16[768,768]{1,0:T(8,128)(2,1)S(1)} %get-tuple-element.61.value_weight, bf16[16,128,384]{2,1,0:T(8,128)(2,1)S(1)} %get-tuple-element.62.bias, ...), custom_call_target="tpu_custom_call" | custom-call | flops 2000000000 | bytes 1000 | tf_op jit(solution)/shard_map/pallas_call | solution.py:728
  42.2 0.0 copy-start
  42.2 0.0 copy-start.3
  42.2 0.0 copy-start.7
  42.2 1.2 %collective-permute-start.15 = (bf16[128,896]{1,0:T(8,128)(2,1)S(1)}, bf16[128,896]{1,0:T(8,128)(2,1)S(1)}, u32[]{:S(2)}, u32[]{:S(2)}) collective-permute-start(bf16[128,896]{1,0:T(8,128)(2,1)S(1)} %shard_map.159.refs_0_), channel_id=1, source_target_pairs={{0,2},{1,3},{2,0},{3,1},{4,6},{5,7},{6,4},{7,5},{8,10},{9,11},{10,... | collective-permute-start | bytes 688136 | tf_op jit(solution)/shard_map/ppermute | solution.py:612
  43.4 0.6 %collective-permute-start.13 = (bf16[80,128]{1,0:T(8,128)(2,1)S(1)}, bf16[80,128]{1,0:T(8,128)(2,1)S(1)}, u32[]{:S(2)}, u32[]{:S(2)}) collective-permute-start(bf16[80,128]{1,0:T(8,128)(2,1)S(1)} %get-tuple-element.71), channel_id=1, source_target_pairs={{0,1},{1,0},{2,3},{3,2},{4,5},{5,4},{6,7},{7,6},{8,9},{9,8},{10,11... | collective-permute-start | bytes 61448 | tf_op jit(solution)/shard_map/ppermute | solution.py:583
  44.0 0.3 collective-permute-start.14
  44.3 0.6 collective-permute-done.13.near
  44.9 5.1 %collective-permute-done.14.far = bf16[80,128]{1,0:T(8,128)(2,1)S(1)} collective-permute-done((bf16[80,128]{1,0:T(8,128)(2,1)S(1)}, bf16[80,128]{1,0:T(8,128)(2,1)S(1)}, u32[]{:S(2)}, u32[]{:S(2)}) %collective-permute-start.14) | collective-permute-done | bytes 20512 | tf_op jit(solution)/shard_map/ppermute | solution.py:594
  49.9 0.9 %shard_map.160.own_back = bf16[128,128]{1,0:T(8,128)(2,1)S(1)} custom-call(bf16[128,768]{1,0:T(8,128)(2,1)S(1)} %get-tuple-element.53.act, f32[128,768]{1,0:T(8,128)S(1)} %get-tuple-element.54.gates, bf16[768,768]{1,0:T(8,128)(2,1)S(1)} %copy-done.1, bf16[768,128]{1,0:T(8,128)(2,1)S(1)} %copy-done.2, bf16[128,896]{1,0:T(8,128)(2,1)S(1)} %shard_map.159.refs_0_, ...), custom_call_target="tpu_custom_call" | custom-call | flops 200000000 | bytes 1000 | tf_op jit(solution)/shard_map/pallas_call | solution.py:742
  50.8 0.5 collective-permute-start.16
  51.3 0.5 collective-permute-start.17
  51.8 0.3 collective-permute-done.16.near_back
  52.2 5.2 %shard_map.161 = (bf16[2048,128]{1,0:T(8,128)(2,1)S(1)}, bf16[2048,128]{1,0:T(8,128)(2,1)S(1)}, bf16[128,128]{1,0:T(8,128)(2,1)S(1)}, f32[256,128]{1,0:T(8,128)S(1)}, f32[256,128]{1,0:T(8,128)S(1)}) custom-call(s32[5]{0:T(128)S(1)} %stack.23.info, s32[64]{0:T(128)S(1)} %copy-done.6, s32[1,2048]{1,0:T(1,128)S(1)} %bitcast.11, ...), custom_call_target="tpu_custom_call" | custom-call | flops 1500000000 | bytes 1000 | tf_op jit(solution)/shard_map/pallas_call | solution.py:761
  57.3 2.6 %shard_map.162 = bf16[2048,128]{1,0:T(8,128)(2,1)} custom-call(s32[5]{0:T(128)S(1)} %stack.23.info, s32[64]{0:T(128)S(1)} %copy-done.6, bf16[2048,128]{1,0:T(8,128)(2,1)S(1)} %get-tuple-element.74.atoms2, bf16[80,128]{1,0:T(8,128)(2,1)S(1)} %collective-permute-done.13.near, bf16[80,128]{1,0:T(8,128)(2,1)S(1)} %collective-permute-done.14.far, ...), custom_call_target="tpu_custom_call" | custom-call | flops 300000000 | bytes 1000 | tf_op jit(solution)/shard_map/pallas_call | solution.py:769
  (33 shorter events, 0.1 us)
Async XLA Ops:
  0.7 8.9 %collective-permute-start = (bf16[64,128]{1,0:T(8,128)(2,1)S(1)}, bf16[64,128]{1,0:T(8,128)(2,1)S(1)}, u32[]{:S(2)}, u32[]{:S(2)}) collective-permute-start(bf16[64,128]{1,0:T(8,128)(2,1)S(1)} %get-tuple-element.82), channel_id=1, source_target_pairs={{0,1},{1,0},{2,3},{3,2},{4,5},{5,4},{6,7},{7,6},{8,9},{9,8},{10,11... | collective-permute-start | bytes 49160 | tf_op jit(solution)/shard_map/ppermute | solution.py:583
  0.8 8.9 %collective-permute-start.1 = (bf16[64,128]{1,0:T(8,128)(2,1)S(1)}, bf16[64,128]{1,0:T(8,128)(2,1)S(1)}, u32[]{:S(2)}, u32[]{:S(2)}) collective-permute-start(bf16[64,128]{1,0:T(8,128)(2,1)S(1)} %get-tuple-element.81), channel_id=1, source_target_pairs={{0,16},{1,2},{2,1},{3,4},{4,3},{5,6},{6,5},{7,8},{8,7},{9,10},{10,... | collective-permute-start | bytes 49160 | tf_op jit(solution)/shard_map/ppermute | solution.py:594
  3.4 6.2 %copy-start.5 = (bf16[2048,128]{1,0:T(8,128)(2,1)S(1)}, bf16[2048,128]{1,0:T(8,128)(2,1)}, u32[]{:S(2)}) copy-start(bf16[2048,128]{1,0:T(8,128)(2,1)} %acts.1) | copy-start | bytes 1572868
  3.4 6.3 %copy-start.6 = (s32[64]{0:T(128)S(1)}, s32[64]{0:T(128)}, u32[]{:S(2)}) copy-start(s32[64]{0:T(128)} %offsets.5) | copy-start | bytes 772
  3.4 6.3 %copy-start.8 = (bf16[128,768]{1,0:T(8,128)(2,1)S(1)}, bf16[128,768]{1,0:T(8,128)(2,1)}, u32[]{:S(2)}) copy-start(bf16[128,768]{1,0:T(8,128)(2,1)} %up.1) | copy-start | bytes 589828
  3.4 6.3 %copy-start.9 = (bf16[128,384]{1,0:T(8,128)(2,1)S(1)}, bf16[128,384]{1,0:T(8,128)(2,1)}, u32[]{:S(2)}) copy-start(bf16[128,384]{1,0:T(8,128)(2,1)} %qkv.3) | copy-start | bytes 294916
  3.4 6.3 %copy-start.10 = (bf16[128,128]{1,0:T(8,128)(2,1)S(1)}, bf16[128,128]{1,0:T(8,128)(2,1)}, u32[]{:S(2)}) copy-start(bf16[128,128]{1,0:T(8,128)(2,1)} %out_weight.2) | copy-start | bytes 98308
  3.5 6.3 %copy-start.11 = (s32[2048]{0:T(1024)S(1)}, s32[2048]{0:T(1024)}, u32[]{:S(2)}) copy-start(s32[2048]{0:T(1024)} %param.25) | copy-start | bytes 24580
  3.5 6.3 %copy-start.12 = (f32[128]{0:T(128)S(1)}, f32[128]{0:T(128)}, u32[]{:S(2)}) copy-start(f32[128]{0:T(128)} %param.17) | copy-start | bytes 1540
  9.7 5.4 %copy-start.13 = (bf16[16,256,256]{2,1,0:T(8,128)(2,1)S(1)}, bf16[16,256,256]{2,1,0:T(8,128)(2,1)}, u32[]{:S(2)}) copy-start(bf16[16,256,256]{2,1,0:T(8,128)(2,1)} %own_far.1) | copy-start | bytes 6291460
  9.8 6.9 %copy-start.14 = (f32[768]{0:T(1024)S(1)}, f32[768]{0:T(1024)}, u32[]{:S(2)}) copy-start(f32[768]{0:T(1024)} %param.27) | copy-start | bytes 9220
  13.4 1.6 %collective-permute-start.2 = (bf16[128,896]{1,0:T(8,128)(2,1)S(1)}, bf16[128,896]{1,0:T(8,128)(2,1)S(1)}, u32[]{:S(2)}, u32[]{:S(2)}) collective-permute-start(bf16[128,896]{1,0:T(8,128)(2,1)S(1)} %get-tuple-element.50), channel_id=1, source_target_pairs={{0,1},{1,0},{2,3},{3,2},{4,5},{5,4},{6,7},{7,6},{8,9},{9,8},{10,11... | collective-permute-start | bytes 688136 | tf_op jit(solution)/shard_map/ppermute | solution.py:583
  15.1 15.0 %collective-permute-start.5 = (bf16[16,256,256]{2,1,0:T(8,128)(2,1)S(1)}, bf16[16,256,256]{2,1,0:T(8,128)(2,1)}, u32[]{:S(2)}, u32[]{:S(2)}) collective-permute-start(bf16[16,256,256]{2,1,0:T(8,128)(2,1)S(1)} %copy-done.13), channel_id=1, source_target_pairs={{0,1},{1,0},{2,3},{3,2},{4,5},{5,4},{6,7},{7,6},{8,9},{9,8},{10,11... | collective-permute-start | bytes 6291464 | tf_op jit(solution)/shard_map/ppermute | solution.py:583
  15.6 4.7 %collective-permute-start.3 = (bf16[64,896]{1,0:T(8,128)(2,1)S(1)}, bf16[64,896]{1,0:T(8,128)(2,1)S(1)}, u32[]{:S(2)}, u32[]{:S(2)}) collective-permute-start(bf16[64,896]{1,0:T(8,128)(2,1)S(1)} %get-tuple-element.83), channel_id=1, source_target_pairs={{0,2},{1,3},{2,0},{3,1},{4,6},{5,7},{6,4},{7,5},{8,10},{9,11},{10,... | collective-permute-start | bytes 344072 | tf_op jit(solution)/shard_map/ppermute | solution.py:612
  20.6 6.0 %collective-permute-start.4 = (bf16[64,768]{1,0:T(8,128)(2,1)S(1)}, bf16[64,768]{1,0:T(8,128)(2,1)S(1)}, u32[]{:S(2)}, u32[]{:S(2)}) collective-permute-start(bf16[64,768]{1,0:T(8,128)(2,1)S(1)} %get-tuple-element.52.own_act), channel_id=1, source_target_pairs={{0,2},{1,3},{2,0},{3,1},{4,6},{5,7},{6,4},{7,5},{8,10},{9,11},{10,... | collective-permute-start | bytes 294920 | tf_op jit(solution)/shard_map/ppermute | solution.py:612
  21.4 8.7 %collective-permute-start.6 = (bf16[64,768]{1,0:T(8,128)(2,1)S(1)}, bf16[64,768]{1,0:T(8,128)(2,1)S(1)}, u32[]{:S(2)}, u32[]{:S(2)}) collective-permute-start(bf16[64,768]{1,0:T(8,128)(2,1)S(1)} %get-tuple-element.59.refs_0_), channel_id=1, source_target_pairs={{0,1},{1,0},{2,3},{3,2},{4,5},{5,4},{6,7},{7,6},{8,9},{9,8},{10,11... | collective-permute-start | bytes 294920 | tf_op jit(solution)/shard_map/ppermute | solution.py:583
  22.9 11.2 %collective-permute-start.7 = (bf16[64,768]{1,0:T(8,128)(2,1)S(1)}, bf16[64,768]{1,0:T(8,128)(2,1)S(1)}, u32[]{:S(2)}, u32[]{:S(2)}) collective-permute-start(bf16[64,768]{1,0:T(8,128)(2,1)S(1)} %get-tuple-element.59.refs_0_), channel_id=1, source_target_pairs={{0,4},{4,0},{8,12},{12,8},{1,5},{5,1},{9,13},{13,9},{2,6},{6,2},{1... | collective-permute-start | bytes 294920 | tf_op jit(solution)/shard_map/ppermute | solution.py:617
  24.2 10.0 %collective-permute-start.8 = (bf16[64,768]{1,0:T(8,128)(2,1)S(1)}, bf16[64,768]{1,0:T(8,128)(2,1)S(1)}, u32[]{:S(2)}, u32[]{:S(2)}) collective-permute-start(bf16[64,768]{1,0:T(8,128)(2,1)S(1)} %get-tuple-element.59.refs_0_), channel_id=1, source_target_pairs={{0,8},{4,12},{8,0},{12,4},{1,9},{5,13},{9,1},{13,5},{2,10},{6,14},... | collective-permute-start | bytes 294920 | tf_op jit(solution)/shard_map/ppermute | solution.py:617
  26.6 7.6 %collective-permute-start.9 = (bf16[64,768]{1,0:T(8,128)(2,1)S(1)}, bf16[64,768]{1,0:T(8,128)(2,1)S(1)}, u32[]{:S(2)}, u32[]{:S(2)}) collective-permute-start(bf16[64,768]{1,0:T(8,128)(2,1)S(1)} %get-tuple-element.59.refs_0_), channel_id=1, source_target_pairs={{0,12},{4,8},{8,4},{12,0},{1,13},{5,9},{9,5},{13,1},{2,14},{6,10},... | collective-permute-start | bytes 294920 | tf_op jit(solution)/shard_map/ppermute | solution.py:617
  34.2 3.4 %collective-permute-start.10 = (bf16[64,768]{1,0:T(8,128)(2,1)S(1)}, bf16[64,768]{1,0:T(8,128)(2,1)S(1)}, u32[]{:S(2)}, u32[]{:S(2)}) collective-permute-start(bf16[64,768]{1,0:T(8,128)(2,1)S(1)} %collective-permute-done.7.refs_0_), channel_id=1, source_target_pairs={{0,1},{1,0},{2,3},{3,2},{4,5},{5,4},{6,7},{7,6},{8,9},{9,8},{10,11... | collective-permute-start | bytes 294920 | tf_op jit(solution)/shard_map/ppermute | solution.py:583
  36.6 1.3 %collective-permute-start.11 = (bf16[64,768]{1,0:T(8,128)(2,1)S(1)}, bf16[64,768]{1,0:T(8,128)(2,1)S(1)}, u32[]{:S(2)}, u32[]{:S(2)}) collective-permute-start(bf16[64,768]{1,0:T(8,128)(2,1)S(1)} %collective-permute-done.8.refs_1_), channel_id=1, source_target_pairs={{0,1},{1,0},{2,3},{3,2},{4,5},{5,4},{6,7},{7,6},{8,9},{9,8},{10,11... | collective-permute-start | bytes 294920 | tf_op jit(solution)/shard_map/ppermute | solution.py:583
  36.7 1.4 %collective-permute-start.12 = (bf16[64,768]{1,0:T(8,128)(2,1)S(1)}, bf16[64,768]{1,0:T(8,128)(2,1)S(1)}, u32[]{:S(2)}, u32[]{:S(2)}) collective-permute-start(bf16[64,768]{1,0:T(8,128)(2,1)S(1)} %collective-permute-done.9.refs_2_), channel_id=1, source_target_pairs={{0,1},{1,0},{2,3},{3,2},{4,5},{5,4},{6,7},{7,6},{8,9},{9,8},{10,11... | collective-permute-start | bytes 294920 | tf_op jit(solution)/shard_map/ppermute | solution.py:583
  38.1 11.8 %copy-start.1 = (bf16[768,768]{1,0:T(8,128)(2,1)S(1)}, bf16[768,768]{1,0:T(8,128)(2,1)}, u32[]{:S(2)}) copy-start(bf16[768,768]{1,0:T(8,128)(2,1)} %token_out.1) | copy-start | bytes 3538948
  38.1 11.8 %copy-start.2 = (bf16[768,128]{1,0:T(8,128)(2,1)S(1)}, bf16[768,128]{1,0:T(8,128)(2,1)}, u32[]{:S(2)}) copy-start(bf16[768,128]{1,0:T(8,128)(2,1)} %down.1) | copy-start | bytes 589828
  42.2 10.0 %copy-start = (bf16[4,2048,128]{2,1,0:T(8,128)(2,1)S(1)}, bf16[4,2048,128]{2,1,0:T(8,128)(2,1)}, u32[]{:S(2)}) copy-start(bf16[4,2048,128]{2,1,0:T(8,128)(2,1)} %bias.3) | copy-start | bytes 6291460
  42.2 10.0 %copy-start.3 = (bf16[128,384]{1,0:T(8,128)(2,1)S(1)}, bf16[128,384]{1,0:T(8,128)(2,1)}, u32[]{:S(2)}) copy-start(bf16[128,384]{1,0:T(8,128)(2,1)} %qkv.5) | copy-start | bytes 294916
  42.2 9.9 %copy-start.7 = (f32[128]{0:T(128)S(1)}, f32[128]{0:T(128)}, u32[]{:S(2)}) copy-start(f32[128]{0:T(128)} %param.20) | copy-start | bytes 1540
  42.2 7.7 %collective-permute-start.15 = (bf16[128,896]{1,0:T(8,128)(2,1)S(1)}, bf16[128,896]{1,0:T(8,128)(2,1)S(1)}, u32[]{:S(2)}, u32[]{:S(2)}) collective-permute-start(bf16[128,896]{1,0:T(8,128)(2,1)S(1)} %shard_map.159.refs_0_), channel_id=1, source_target_pairs={{0,2},{1,3},{2,0},{3,1},{4,6},{5,7},{6,4},{7,5},{8,10},{9,11},{10,... | collective-permute-start | bytes 688136 | tf_op jit(solution)/shard_map/ppermute | solution.py:612
  43.4 1.5 %collective-permute-start.13 = (bf16[80,128]{1,0:T(8,128)(2,1)S(1)}, bf16[80,128]{1,0:T(8,128)(2,1)S(1)}, u32[]{:S(2)}, u32[]{:S(2)}) collective-permute-start(bf16[80,128]{1,0:T(8,128)(2,1)S(1)} %get-tuple-element.71), channel_id=1, source_target_pairs={{0,1},{1,0},{2,3},{3,2},{4,5},{5,4},{6,7},{7,6},{8,9},{9,8},{10,11... | collective-permute-start | bytes 61448 | tf_op jit(solution)/shard_map/ppermute | solution.py:583
  44.0 5.9 %collective-permute-start.14 = (bf16[80,128]{1,0:T(8,128)(2,1)S(1)}, bf16[80,128]{1,0:T(8,128)(2,1)S(1)}, u32[]{:S(2)}, u32[]{:S(2)}) collective-permute-start(bf16[80,128]{1,0:T(8,128)(2,1)S(1)} %get-tuple-element.72), channel_id=1, source_target_pairs={{0,16},{1,2},{2,1},{3,4},{4,3},{5,6},{6,5},{7,8},{8,7},{9,10},{10,... | collective-permute-start | bytes 61448 | tf_op jit(solution)/shard_map/ppermute | solution.py:594
  50.8 1.3 %collective-permute-start.16 = (bf16[128,128]{1,0:T(8,128)(2,1)S(1)}, bf16[128,128]{1,0:T(8,128)(2,1)S(1)}, u32[]{:S(2)}, u32[]{:S(2)}) collective-permute-start(bf16[128,128]{1,0:T(8,128)(2,1)S(1)} %shard_map.160.own_back), channel_id=1, source_target_pairs={{0,1},{1,0},{2,3},{3,2},{4,5},{5,4},{6,7},{7,6},{8,9},{9,8},{10,11... | collective-permute-start | bytes 98312 | tf_op jit(solution)/shard_map/ppermute | solution.py:583
  51.3 6.0 %collective-permute-start.17 = (bf16[64,128]{1,0:T(8,128)(2,1)S(1)}, bf16[64,128]{1,0:T(8,128)(2,1)S(1)}, u32[]{:S(2)}, u32[]{:S(2)}) collective-permute-start(bf16[64,128]{1,0:T(8,128)(2,1)S(1)} %slice_select_fusion), channel_id=1, source_target_pairs={{0,16},{1,4},{2,18},{3,6},{4,1},{5,8},{6,3},{7,10},{8,5},{9,12},{1... | collective-permute-start | bytes 49160 | tf_op jit(solution)/shard_map/ppermute | solution.py:594
  52.1 5.2 %copy-start.4 = (bf16[128,128]{1,0:T(8,128)(2,1)S(1)}, bf16[128,128]{1,0:T(8,128)(2,1)}, u32[]{:S(2)}) copy-start(bf16[128,128]{1,0:T(8,128)(2,1)} %out_weight.3) | copy-start | bytes 98308

commit v6 on v5

--- a/solution.py
+++ b/solution.py
@@ -277,29 +277,6 @@
     normed[...] = norm_rows(rounded.astype(F32), gain[...]).astype(BF)
 
 
-def query_tokens(info, weight_far, gain, own_act, *refs, others):
-    other_acts = refs[:others]
-    act, queries, gates, query_weight, gate_weight, sems = refs[others:]
-    share, wide = own_act.shape
-    copies = fetches(
-        [weight_far.at[:, pl.ds(0, wide)], weight_far.at[:, pl.ds(3 * wide, wide)]], [query_weight, gate_weight], sems
-    )
-    for copy in copies:
-        copy.start()
-    pairs = others + 1
-    place = info[2]
-    act[pl.ds(pl.multiple_of(place * share, share), share), :] = own_act[...]
-    for step in range(1, pairs):
-        at = lax.rem(place - step + pairs, pairs) * share
-        act[pl.ds(pl.multiple_of(at, share), share), :] = other_acts[step - 1][...]
-    normed = norm_rows(act[...].astype(F32), gain[...]).astype(BF)
-    copies[0].wait()
-    queries[...] = dot(normed, query_weight[...]).astype(BF)
-    copies[1].wait()
-    raw = dot(normed, gate_weight[...]).astype(BF).astype(F32)
-    gates[...] = jax.nn.sigmoid(raw)
-
-
 def place_keys(info, own, near, tokens, steps, solo):
     share = own[0].shape[0]
     group = LANES // share
@@ -309,7 +286,7 @@
         if solo and step < group:
             places = (0, share)
         else:
-            at = lead + (step // group - (steps[0] + solo) // group) * 2 * LANES + (place ^ (step % group)) * share
+            at = lead + (step // group - (0 not in steps)) * 2 * LANES + (place ^ (step % group)) * share
             places = (at, at + LANES)
         for rows, at in zip((own_rows, near_rows), places):
             tokens[pl.ds(pl.multiple_of(at, share), share), :] = rows[...]
@@ -342,9 +319,9 @@
         rest[head, :, :LANES] = jnp.where(first == 0, high, low).astype(BF)
 
 
-def attend_heads(queries, bias, keys, values, previous, keep):
+def attend_heads(queries, biases, keys, values, previous, keep):
     count, wide = queries.shape
-    heads = bias.shape[0]
+    heads = biases[0].shape[0]
     size = wide // heads
     scale = 1.0 / math.sqrt(size)
     span = keys.shape[0] // LANES
@@ -363,7 +340,8 @@
             members.append((head, first, low, high, dot_nt(query, keys[:, chunk])))
         raised = []
         for head, first, low, high, score in members:
-            score = score * scale + bias[head].astype(F32)
+            tile = jnp.concatenate([bias[head] for bias in biases], axis=1)
+            score = score * scale + tile.astype(F32)
             top = jnp.broadcast_to(jnp.max(score, axis=-1, keepdims=True), (count, LANES))
             if previous is not None:
                 former = previous[1][head]
@@ -390,58 +368,75 @@
     return out
 
 
-def attend_first(info, weight_far, queries, own_far, near_far, *refs, steps, solo):
+def attend_first(info, weight_far, gain, own_act, own_far, near_far, *refs, others, steps, solo):
     rows_count = len(steps)
-    own, near = refs[:rows_count], refs[rows_count : 2 * rows_count]
-    key_weight, value_weight, rest_bias, mixed, tops, totals, tokens, keys, values, bias, slots, sems = refs[
-        2 * rows_count :
-    ]
+    other_acts, refs = refs[:others], refs[others:]
+    own, near, refs = refs[:rows_count], refs[rows_count : 2 * rows_count], refs[2 * rows_count :]
+    act, queries, gates, key_weight, value_weight, pair_bias, mixed, tops, totals = refs[:9]
+    query_weight, gate_weight, tokens, keys, values, bias, slots, sems = refs[9:]
     share, wide = own[0].shape
     weights = fetches(
-        [weight_far.at[:, pl.ds(wide, wide)], weight_far.at[:, pl.ds(2 * wide, wide)]], [key_weight, value_weight], sems
-    )
-    biases_far = (own_far, near_far)
+        [weight_far.at[:, pl.ds(part * wide, wide)] for part in range(4)],
+        [query_weight, key_weight, value_weight, gate_weight],
+        sems,
+    )
     targets = (slots.at[0], slots.at[1]) if solo else [bias.at[:, :, pl.ds(at, LANES)] for at in (0, LANES)]
-    now = fetches(*bias_pieces(info, biases_far, 0, targets, share), sems, 2)
-    later = []
-    lead = LANES if solo else 0
-    for block in range((rest_bias.shape[2] - lead) // (2 * LANES)):
-        first = lead + block * 2 * LANES
-        targets = [rest_bias.at[:, :, pl.ds(at, LANES)] for at in (first, first + LANES)]
-        sources, places = bias_pieces(info, biases_far, block + 1, targets, share)
-        later += fetches(sources, places, sems, 2 + len(now) + len(later))
-    for copy in weights + now + later:
+    tiles = fetches(*bias_pieces(info, (own_far, near_far), 0, targets, share), sems, 4)
+    for copy in weights[:3] + tiles + weights[3:]:
         copy.start()
+    pairs = others + 1
+    place = info[2]
+    act[pl.ds(pl.multiple_of(place * share, share), share), :] = own_act[...]
+    for step in range(1, pairs):
+        at = lax.rem(place - step + pairs, pairs) * share
+        act[pl.ds(pl.multiple_of(at, share), share), :] = other_acts[step - 1][...]
+    normed = norm_rows(act[...].astype(F32), gain[...]).astype(BF)
     place_keys(info, own, near, tokens, steps, solo)
     weights[0].wait()
+    queries[...] = dot(normed, query_weight[...]).astype(BF)
+    weights[1].wait()
     keys[...] = dot(tokens[...], key_weight[...]).astype(BF)
-    weights[1].wait()
+    weights[2].wait()
     values[...] = dot(tokens[...], value_weight[...]).astype(BF)
-    for copy in now:
+    for copy in tiles:
         copy.wait()
     if solo:
-        split_bias(info, slots, bias, rest_bias)
+        split_bias(info, slots, bias, pair_bias)
+    else:
+        pair_bias[...] = jnp.zeros(pair_bias.shape, BF)
 
     def keep(head, top, total):
         tops[head] = top
         totals[head] = total
 
-    out = attend_heads(queries, bias, keys, values, None, keep)
+    out = attend_heads(queries, [bias], keys, values, None, keep)
     for block, piece in enumerate(out):
         mixed[:, block * LANES : (block + 1) * LANES] = piece
-    for copy in later:
-        copy.wait()
-
-
-def attend_rest(queries, key_weight, value_weight, bias, info, former, former_top, former_total, *refs, steps, solo):
+    weights[3].wait()
+    gates[...] = jax.nn.sigmoid(dot(normed, gate_weight[...]).astype(BF).astype(F32))
+
+
+def attend_rest(
+    info, own_far, near_far, queries, key_weight, value_weight, pair_bias, former, former_top, former_total,
+    *refs, steps, solo
+):
     rows_count = len(steps)
     own, near = refs[:rows_count], refs[rows_count : 2 * rows_count]
-    packed, tokens, keys, values = refs[2 * rows_count :]
+    packed, tokens, keys, values, bias, sems = refs[2 * rows_count :]
     heads = bias.shape[0]
     count, wide = queries.shape
+    tiles = []
+    for block in range(bias.shape[2] // (2 * LANES)):
+        targets = [bias.at[:, :, pl.ds((2 * block + half) * LANES, LANES)] for half in range(2)]
+        sources, places = bias_pieces(info, (own_far, near_far), block + 1, targets, own[0].shape[0])
+        tiles += fetches(sources, places, sems, len(tiles))
+    for copy in tiles:
+        copy.start()
     place_keys(info, own, near, tokens, steps, solo)
     keys[...] = dot(tokens[...], key_weight[...]).astype(BF)
     values[...] = dot(tokens[...], value_weight[...]).astype(BF)
+    for copy in tiles:
+        copy.wait()
     lane = lax.broadcasted_iota(jnp.int32, (count, LANES), 1)
     ends = [jnp.zeros((count, LANES), F32), jnp.ones((count, LANES), F32)]
 
@@ -449,7 +444,8 @@
         ends[0] = jnp.where(lane == head, top, ends[0])
         ends[1] = jnp.where(lane == head, total, ends[1])
 
-    out = attend_heads(queries, bias, keys, values, (former, former_top, former_total), keep)
+    biases = [pair_bias, bias] if solo else [bias]
+    out = attend_heads(queries, biases, keys, values, (former, former_top, former_total), keep)
     for block, piece in enumerate(out):
         packed[:, block * LANES : (block + 1) * LANES] = piece.astype(BF)
     logs = ends[0] + jnp.log(ends[1])
@@ -677,6 +673,7 @@
     for step in range(1, pairs):
         piece = lax.dynamic_slice_in_dim(chip_sum, (pair + step) % pairs * share, share, axis=0)
         sums.append(along_pairs(piece, step))
+    sums, bias_near = lax.optimization_barrier((sums, bias_near))
     share_shape = jax.ShapeDtypeStruct((share, wide), BF)
     gain_row = token_gain.reshape(1, -1)
     act, normed = call(
@@ -686,52 +683,48 @@
     group = LANES // share
     solo = group == 2
     split = 1 if solo else group
-    moved_keys = [along_rows(normed, step) for step in range(row_count - 1, 0, -1)]
-    own_keys = [normed] + moved_keys[::-1]
+    own_keys = [normed] + [along_rows(normed, step) for step in range(1, row_count)]
     near_keys = [to_near(x) for x in own_keys[:split]]
     other_acts = [along_pairs(act, step) for step in range(1, pairs)]
     half_shape = jax.ShapeDtypeStruct((half, wide), BF)
     wide_shape = jax.ShapeDtypeStruct((half, wide), F32)
-    act_rows, queries, gates = call(
-        functools.partial(query_tokens, others=len(other_acts)),
-        [half_shape, half_shape, wide_shape],
-        [pltpu.VMEM((wide, wide), BF)] * 2 + [pltpu.SemaphoreType.DMA((2,))],
-        [SMEM, HBM] + [VMEM] * (2 + len(other_acts)),
-        1_000,
-    )(info, stay(token_weight), gain_row, act, *other_acts)
-
     rest = row_count - split
 
     def key_scratch(count):
         return [pltpu.VMEM((2 * count * share, wide), BF)] * 3
 
-    def bias_shape(count):
-        return jax.ShapeDtypeStruct((heads, half, 2 * count * share), BF)
-
     head_shape = jax.ShapeDtypeStruct((heads, half, LANES), F32)
     weight_shape = jax.ShapeDtypeStruct((wide, wide), BF)
-    copies = 2 + 2 * pairs * (row_count // group)
-    bias_scratch = [
-        pltpu.VMEM((heads, half, 2 * split * share), BF),
-        pltpu.VMEM((2, heads, half, LANES), BF),
-        pltpu.SemaphoreType.DMA((copies,)),
-    ]
-    *held, mixed, tops, totals = call(
-        functools.partial(attend_first, steps=list(range(split)), solo=solo),
-        [weight_shape, weight_shape, bias_shape(rest), wide_shape, head_shape, head_shape],
-        key_scratch(split) + bias_scratch,
-        [SMEM, HBM, VMEM, HBM, HBM] + [VMEM] * (2 * split),
+    tile_count = 2 * pairs
+    act_rows, queries, gates, *held, mixed, tops, totals = call(
+        functools.partial(attend_first, others=len(other_acts), steps=list(range(split)), solo=solo),
+        [half_shape, half_shape, wide_shape, weight_shape, weight_shape]
+        + [jax.ShapeDtypeStruct((heads, half, LANES), BF), wide_shape, head_shape, head_shape],
+        [pltpu.VMEM((wide, wide), BF)] * 2
+        + key_scratch(split)
+        + [pltpu.VMEM((heads, half, 2 * split * share), BF), pltpu.VMEM((2, heads, half, LANES), BF)]
+        + [pltpu.SemaphoreType.DMA((4 + tile_count,))],
+        [SMEM, HBM, VMEM, VMEM, HBM, HBM] + [VMEM] * (len(other_acts) + 2 * split),
         1_000,
-    )(info, stay(token_weight), queries, stay(pair_bias), stay(bias_near), *own_keys[:split], *near_keys)
-    rest_keys, mixed = lax.optimization_barrier((own_keys[split:], mixed))
+        24,
+    )(
+        info, stay(token_weight), gain_row, act, stay(pair_bias), stay(bias_near), *other_acts,
+        *own_keys[:split], *near_keys,
+    )
+    rest_steps = sorted(range(split, row_count), key=lambda step: (step >= group, -step))
+    rest_keys, mixed = lax.optimization_barrier(([own_keys[step] for step in rest_steps], mixed))
     rest_near = [to_near(x) for x in rest_keys]
+    blocks = row_count // group - 1
     part = call(
-        functools.partial(attend_rest, steps=list(range(split, row_count)), solo=solo),
+        functools.partial(attend_rest, steps=rest_steps, solo=solo),
         packed_shape,
-        key_scratch(rest),
-        [VMEM] * 4 + [SMEM] + [VMEM] * (3 + 2 * rest),
+        key_scratch(rest)
+        + [pltpu.VMEM((heads, half, 2 * LANES * blocks), BF), pltpu.SemaphoreType.DMA((tile_count * blocks,))],
+        [SMEM, HBM, HBM] + [VMEM] * (7 + 2 * rest),
         2_000_000_000,
-    )(queries, *held, info, mixed, tops, totals, *rest_keys, *rest_near)
+    )(
+        info, stay(pair_bias), stay(bias_near), queries, *held, mixed, tops, totals, *rest_keys, *rest_near,
+    )
 
     near_message, far_message, part = lax.optimization_barrier((near_message, far_message, part))
     parts = [along_pairs(part, step) for step in range(1, pairs)]

time: 60.9 us -> 59.6 us (0.979)
  waiting for transfers between devices: 11.6 us -> 13.4 us
  Pallas kernels: 29.6 us -> 28 us
  starting transfers between devices: 17.5 us -> 16.3 us
    ppermute x3, waiting for transfers between devices: 0.01 us -> 2.23 us  [along_rows(): return lax.ppermute(x, 'row', [(i, i ^ step) for i in range(row_count)])]
    ppermute x9, starting transfers between devices: 6.52 us -> 4.82 us  [to_near(): return lax.ppermute(x, 'col', [(i, i ^ 1) for i in range(col_count)])]
    ppermute x3, starting transfers between devices: 3.34 us -> 5.02 us  [swapped(): return lax.ppermute(x, ('group', 'row', 'col'), pairs_list)]
    pallas_call x3 -> x2, Pallas kernels: 10.7 us -> 9.2 us  [the longest x1 4.84 us: body(): call(functools.partial(attend_first, others=len(other_acts), steps=list(r...]
    ppermute x3, starting transfers between devices: 4.53 us -> 3.36 us  [along_rows(): return lax.ppermute(x, 'row', [(i, i ^ step) for i in range(row_count)])]
  transfers between devices with their start and end apart: 18 -> 18, of which waited for: 8 -> 8; matrix products, arithmetic and copies ran while one was open for 0% -> 0% of each run, Pallas kernels for 31% -> 27%
where the time goes in v6:
time: 59.6 us; the launch traced here: 59 us
  Pallas kernels  28 us (47%)
  starting transfers between devices  16.3 us (27%)
  waiting for transfers between devices  13.4 us (22%)
  local copies, waits for them, and re-layouts  0.92 us (2%)
    pallas_call x1, Pallas kernels, body(): call(functools.partial(first_inner, pieces=pieces), [atom_shape] + edge_s...  6.19 us
    ppermute x3, waiting for transfers between devices, swapped(): return lax.ppermute(x, ('group', 'row', 'col'), pairs_list)  5.63 us
    pallas_call x1, Pallas kernels, body(): call(functools.partial(second_inner, share=share), [atom_shape, atom_shap...  5.15 us
    ppermute x3, starting transfers between devices, swapped(): return lax.ppermute(x, ('group', 'row', 'col'), pairs_list)  5.02 us
    pallas_call x1, Pallas kernels, body(): call(functools.partial(attend_first, others=len(other_acts), steps=list(r...  4.84 us
    ppermute x9, starting transfers between devices, to_near(): return lax.ppermute(x, 'col', [(i, i ^ 1) for i in range(col_count)])  4.82 us
    pallas_call x1, Pallas kernels, body(): call(functools.partial(attend_rest, steps=rest_steps, solo=solo), packed_...  4.36 us
    pallas_call x1, Pallas kernels, body(): call(functools.partial(first_edge, share=share), [atom_shape, packed_shap...  3.67 us
  transfers between devices with their start and end apart: 18, of which 8 were waited for; matrix products, arithmetic and copies ran while one was open for 0% of the time, Pallas kernels for 27%

profile of v6, /device:TPU:1, one launch (start us, length us, event | category | flops | bytes accessed | tf_op | source)
XLA Modules:
  0.0 59.0 jit_solution(6267019266589203458)
XLA Ops:
  0.0 0.7 %constant_dynamic-slice_fusion.2 = (bf16[64,128]{1,0:T(8,128)(2,1)S(1)}, bf16[64,128]{1,0:T(8,128)(2,1)S(1)}) fusion(bf16[2048,128]{1,0:T(8,128)(2,1)} %acts.1, s32[]{:T(128)S(6)} %select_n.41, s32[]{:T(128)S(6)} %select_n.40), kind=kLoop, calls=%fused_computation.4 | loop fusion | bytes 65544 | tf_op jit(solution)/shard_map/dynamic_slice | solution.py:616
  0.7 2.6 %collective-permute-start.1 = (bf16[64,128]{1,0:T(8,128)(2,1)S(1)}, bf16[64,128]{1,0:T(8,128)(2,1)S(1)}, u32[]{:S(2)}, u32[]{:S(2)}) collective-permute-start(bf16[64,128]{1,0:T(8,128)(2,1)S(1)} %get-tuple-element.87), channel_id=1, source_target_pairs={{0,16},{1,2},{2,1},{3,4},{4,3},{5,6},{6,5},{7,8},{8,7},{9,10},{10,... | collective-permute-start | bytes 49160 | tf_op jit(solution)/shard_map/ppermute | solution.py:590
  3.3 0.4 collective-permute-start
  3.8 0.1 stack.23.info
  3.9 0.0 copy-start.10
  3.9 0.0 copy-start.11
  3.9 0.0 copy-start.12
  3.9 6.2 %shard_map.154 = (bf16[2048,128]{1,0:T(8,128)(2,1)S(1)}, bf16[128,128]{1,0:T(8,128)(2,1)S(1)}, f32[256,128]{1,0:T(8,128)S(1)}, f32[256,128]{1,0:T(8,128)S(1)}, bf16[4,128,128]{2,1,0:T(8,128)(2,1)S(1)}) custom-call(s32[5]{0:T(128)S(1)} %stack.23.info, bf16[2048,128]{1,0:T(8,128)(2,1)} %acts.1, f32[1,128]{1,0:T(1,128)} %bitcast.12, bf16[128,384]{1,0:T(8,128)(2,1)} %qkv.3, ...), custom_call_target="tpu_custom_call" | custom-call | flops 1500000000 | bytes 1000 | tf_op jit(solution)/shard_map/pallas_call | solution.py:645
  10.1 0.0 collective-permute-done.near
  10.2 0.0 copy-start.13
  10.2 0.0 copy-start.14
  10.2 3.7 %shard_map.155 = (bf16[2048,128]{1,0:T(8,128)(2,1)S(1)}, bf16[128,896]{1,0:T(8,128)(2,1)S(1)}, bf16[128,896]{1,0:T(8,128)(2,1)S(1)}, bf16[80,128]{1,0:T(8,128)(2,1)S(1)}, bf16[80,128]{1,0:T(8,128)(2,1)S(1)}) custom-call(s32[5]{0:T(128)S(1)} %stack.23.info, s32[64]{0:T(128)S(1)} %copy-done.6, s32[1,2048]{1,0:T(1,128)S(1)} %bitcast.10, ...), custom_call_target="tpu_custom_call" | custom-call | flops 2000000000 | bytes 1000 | tf_op jit(solution)/shard_map/pallas_call | solution.py:657
  13.9 0.1 collective-permute-start.2
  14.0 1.4 %collective-permute-done.2 = bf16[128,896]{1,0:T(8,128)(2,1)S(1)} collective-permute-done((bf16[128,896]{1,0:T(8,128)(2,1)S(1)}, bf16[128,896]{1,0:T(8,128)(2,1)S(1)}, u32[]{:S(2)}, u32[]{:S(2)}) %collective-permute-start.2) | collective-permute-done | bytes 229408 | tf_op jit(solution)/shard_map/ppermute | solution.py:579
  15.4 0.1 add_convert_fusion
  15.5 0.2 collective-permute-start.4
  15.7 1.3 %collective-permute-start.3 = (bf16[64,896]{1,0:T(8,128)(2,1)S(1)}, bf16[64,896]{1,0:T(8,128)(2,1)S(1)}, u32[]{:S(2)}, u32[]{:S(2)}) collective-permute-start(bf16[64,896]{1,0:T(8,128)(2,1)S(1)} %get-tuple-element.89), channel_id=1, source_target_pairs={{0,2},{1,3},{2,0},{3,1},{4,6},{5,7},{6,4},{7,5},{8,10},{9,11},{10,... | collective-permute-start | bytes 344072 | tf_op jit(solution)/shard_map/ppermute | solution.py:608
  17.0 3.1 %collective-permute-done.3.refs_1_ = bf16[64,896]{1,0:T(8,128)(2,1)S(1)} collective-permute-done((bf16[64,896]{1,0:T(8,128)(2,1)S(1)}, bf16[64,896]{1,0:T(8,128)(2,1)S(1)}, u32[]{:S(2)}, u32[]{:S(2)}) %collective-permute-start.3) | collective-permute-done | bytes 114720 | tf_op jit(solution)/shard_map/ppermute | solution.py:608
  20.2 0.0 collective-permute-done.4.near_far
  20.2 0.3 shard_map.156
  20.5 1.5 %collective-permute-start.5 = (bf16[64,768]{1,0:T(8,128)(2,1)S(1)}, bf16[64,768]{1,0:T(8,128)(2,1)S(1)}, u32[]{:S(2)}, u32[]{:S(2)}) collective-permute-start(bf16[64,768]{1,0:T(8,128)(2,1)S(1)} %get-tuple-element.58.own_act), channel_id=1, source_target_pairs={{0,2},{1,3},{2,0},{3,1},{4,6},{5,7},{6,4},{7,5},{8,10},{9,11},{10,... | collective-permute-start | bytes 294920 | tf_op jit(solution)/shard_map/ppermute | solution.py:608
  22.1 1.2 %collective-permute-start.6 = (bf16[64,768]{1,0:T(8,128)(2,1)S(1)}, bf16[64,768]{1,0:T(8,128)(2,1)S(1)}, u32[]{:S(2)}, u32[]{:S(2)}) collective-permute-start(bf16[64,768]{1,0:T(8,128)(2,1)S(1)} %get-tuple-element.60.refs_1_), channel_id=1, source_target_pairs={{0,1},{1,0},{2,3},{3,2},{4,5},{5,4},{6,7},{7,6},{8,9},{9,8},{10,11... | collective-permute-start | bytes 294920 | tf_op jit(solution)/shard_map/ppermute | solution.py:579
  23.3 2.3 %collective-permute-start.9 = (bf16[64,768]{1,0:T(8,128)(2,1)S(1)}, bf16[64,768]{1,0:T(8,128)(2,1)S(1)}, u32[]{:S(2)}, u32[]{:S(2)}) collective-permute-start(bf16[64,768]{1,0:T(8,128)(2,1)S(1)} %get-tuple-element.60.refs_1_), channel_id=1, source_target_pairs={{0,8},{4,12},{8,0},{12,4},{1,9},{5,13},{9,1},{13,5},{2,10},{6,14},... | collective-permute-start | bytes 294920 | tf_op jit(solution)/shard_map/ppermute | solution.py:613
  25.6 1.1 %collective-permute-start.8 = (bf16[64,768]{1,0:T(8,128)(2,1)S(1)}, bf16[64,768]{1,0:T(8,128)(2,1)S(1)}, u32[]{:S(2)}, u32[]{:S(2)}) collective-permute-start(bf16[64,768]{1,0:T(8,128)(2,1)S(1)} %get-tuple-element.60.refs_1_), channel_id=1, source_target_pairs={{0,12},{4,8},{8,4},{12,0},{1,13},{5,9},{9,5},{13,1},{2,14},{6,10},... | collective-permute-start | bytes 294920 | tf_op jit(solution)/shard_map/ppermute | solution.py:613
  26.7 0.0 collective-permute-start.7
  26.7 4.8 %shard_map.157 = (bf16[128,768]{1,0:T(8,128)(2,1)S(1)}, bf16[128,768]{1,0:T(8,128)(2,1)S(1)}, f32[128,768]{1,0:T(8,128)S(1)}, bf16[768,768]{1,0:T(8,128)(2,1)S(1...) custom-call(s32[5]{0:T(128)S(1)} %stack.23.info, ...), custom_call_target="tpu_custom_call" | custom-call | flops 1000 | bytes 1000 | tf_op jit(solution)/shard_map/pallas_call | solution.py:699
  31.5 1.3 %collective-permute-done.9.refs_2_ = bf16[64,768]{1,0:T(8,128)(2,1)S(1)} collective-permute-done((bf16[64,768]{1,0:T(8,128)(2,1)S(1)}, bf16[64,768]{1,0:T(8,128)(2,1)S(1)}, u32[]{:S(2)}, u32[]{:S(2)}) %collective-permute-start.9) | collective-permute-done | bytes 98336 | tf_op jit(solution)/shard_map/ppermute | solution.py:613
  32.9 0.9 %collective-permute-done.7.refs_0_ = bf16[64,768]{1,0:T(8,128)(2,1)S(1)} collective-permute-done((bf16[64,768]{1,0:T(8,128)(2,1)S(1)}, bf16[64,768]{1,0:T(8,128)(2,1)S(1)}, u32[]{:S(2)}, u32[]{:S(2)}) %collective-permute-start.7) | collective-permute-done | bytes 98336 | tf_op jit(solution)/shard_map/ppermute | solution.py:613
  33.7 1.2 %collective-permute-start.10 = (bf16[64,768]{1,0:T(8,128)(2,1)S(1)}, bf16[64,768]{1,0:T(8,128)(2,1)S(1)}, u32[]{:S(2)}, u32[]{:S(2)}) collective-permute-start(bf16[64,768]{1,0:T(8,128)(2,1)S(1)} %collective-permute-done.7.refs_0_), channel_id=1, source_target_pairs={{0,1},{1,0},{2,3},{3,2},{4,5},{5,4},{6,7},{7,6},{8,9},{9,8},{10,11... | collective-permute-start | bytes 294920 | tf_op jit(solution)/shard_map/ppermute | solution.py:579
  35.0 0.0 collective-permute-start.11
  35.0 0.5 collective-permute-start.12
  35.5 0.4 collective-permute-done.10.refs_3_
  35.9 0.4 collective-permute-done.11.refs_4_
  36.3 0.2 collective-permute-done.12.refs_5_
  36.4 4.4 %shard_map.158.refs_0_ = bf16[128,896]{1,0:T(8,128)(2,1)S(1)} custom-call(s32[5]{0:T(128)S(1)} %stack.23.info, bf16[16,256,256]{2,1,0:T(8,128)(2,1)} %own_far.3, bf16[16,256,256]{2,1,0:T(8,128)(2,1)} %collective-permute-done.4.near_far, bf16[128,768]{1,0:T(8,128)(2,1)S(1)} %get-tuple-element.65.queries, bf16[768,768]{1,0:T(8,128)(2,1)S(1)} %get-tuple-element.66.key_weight, ...), custom_call_target="tpu_custom_call" | custom-call | flops 2000000000 | bytes 1000 | tf_op jit(solution)/shard_map/pallas_call | solution.py:718
  40.8 0.0 copy-start
  40.8 0.0 copy-start.3
  40.8 0.0 copy-start.7
  40.8 0.3 collective-permute-start.15
  41.2 0.6 %collective-permute-start.13 = (bf16[80,128]{1,0:T(8,128)(2,1)S(1)}, bf16[80,128]{1,0:T(8,128)(2,1)S(1)}, u32[]{:S(2)}, u32[]{:S(2)}) collective-permute-start(bf16[80,128]{1,0:T(8,128)(2,1)S(1)} %get-tuple-element.77), channel_id=1, source_target_pairs={{0,1},{1,0},{2,3},{3,2},{4,5},{5,4},{6,7},{7,6},{8,9},{9,8},{10,11... | collective-permute-start | bytes 61448 | tf_op jit(solution)/shard_map/ppermute | solution.py:579
  41.8 1.1 %collective-permute-start.14 = (bf16[80,128]{1,0:T(8,128)(2,1)S(1)}, bf16[80,128]{1,0:T(8,128)(2,1)S(1)}, u32[]{:S(2)}, u32[]{:S(2)}) collective-permute-start(bf16[80,128]{1,0:T(8,128)(2,1)S(1)} %get-tuple-element.78), channel_id=1, source_target_pairs={{0,16},{1,2},{2,1},{3,4},{4,3},{5,6},{6,5},{7,8},{8,7},{9,10},{10,... | collective-permute-start | bytes 61448 | tf_op jit(solution)/shard_map/ppermute | solution.py:590
  42.9 5.6 %collective-permute-done.14.far = bf16[80,128]{1,0:T(8,128)(2,1)S(1)} collective-permute-done((bf16[80,128]{1,0:T(8,128)(2,1)S(1)}, bf16[80,128]{1,0:T(8,128)(2,1)S(1)}, u32[]{:S(2)}, u32[]{:S(2)}) %collective-permute-start.14) | collective-permute-done | bytes 20512 | tf_op jit(solution)/shard_map/ppermute | solution.py:590
  48.5 0.9 %shard_map.159.own_back = bf16[128,128]{1,0:T(8,128)(2,1)S(1)} custom-call(bf16[128,768]{1,0:T(8,128)(2,1)S(1)} %get-tuple-element.61.act, f32[128,768]{1,0:T(8,128)S(1)} %get-tuple-element.62.gates, bf16[768,768]{1,0:T(8,128)(2,1)S(1)} %copy-done.1, bf16[768,128]{1,0:T(8,128)(2,1)S(1)} %copy-done.2, bf16[128,896]{1,0:T(8,128)(2,1)S(1)} %shard_map.158.refs_0_, ...), custom_call_target="tpu_custom_call" | custom-call | flops 200000000 | bytes 1000 | tf_op jit(solution)/shard_map/pallas_call | solution.py:735
  49.5 0.5 collective-permute-start.16
  49.9 1.3 %collective-permute-start.17 = (bf16[64,128]{1,0:T(8,128)(2,1)S(1)}, bf16[64,128]{1,0:T(8,128)(2,1)S(1)}, u32[]{:S(2)}, u32[]{:S(2)}) collective-permute-start(bf16[64,128]{1,0:T(8,128)(2,1)S(1)} %slice_select_fusion), channel_id=1, source_target_pairs={{0,16},{1,4},{2,18},{3,6},{4,1},{5,8},{6,3},{7,10},{8,5},{9,12},{1... | collective-permute-start | bytes 49160 | tf_op jit(solution)/shard_map/ppermute | solution.py:590
  51.3 0.0 copy-start.4
  51.3 5.2 %shard_map.160 = (bf16[2048,128]{1,0:T(8,128)(2,1)S(1)}, bf16[2048,128]{1,0:T(8,128)(2,1)S(1)}, bf16[128,128]{1,0:T(8,128)(2,1)S(1)}, f32[256,128]{1,0:T(8,128)S(1)}, f32[256,128]{1,0:T(8,128)S(1)}) custom-call(s32[5]{0:T(128)S(1)} %stack.23.info, s32[64]{0:T(128)S(1)} %copy-done.6, s32[1,2048]{1,0:T(1,128)S(1)} %bitcast.11, ...), custom_call_target="tpu_custom_call" | custom-call | flops 1500000000 | bytes 1000 | tf_op jit(solution)/shard_map/pallas_call | solution.py:754
  56.5 2.6 %shard_map.161 = bf16[2048,128]{1,0:T(8,128)(2,1)} custom-call(s32[5]{0:T(128)S(1)} %stack.23.info, s32[64]{0:T(128)S(1)} %copy-done.6, bf16[2048,128]{1,0:T(8,128)(2,1)S(1)} %get-tuple-element.80.atoms2, bf16[80,128]{1,0:T(8,128)(2,1)S(1)} %collective-permute-done.13.near, bf16[80,128]{1,0:T(8,128)(2,1)S(1)} %collective-permute-done.14.far, ...), custom_call_target="tpu_custom_call" | custom-call | flops 300000000 | bytes 1000 | tf_op jit(solution)/shard_map/pallas_call | solution.py:762
  (32 shorter events, 0.1 us)
Async XLA Ops:
  0.7 9.4 %collective-permute-start.1 = (bf16[64,128]{1,0:T(8,128)(2,1)S(1)}, bf16[64,128]{1,0:T(8,128)(2,1)S(1)}, u32[]{:S(2)}, u32[]{:S(2)}) collective-permute-start(bf16[64,128]{1,0:T(8,128)(2,1)S(1)} %get-tuple-element.87), channel_id=1, source_target_pairs={{0,16},{1,2},{2,1},{3,4},{4,3},{5,6},{6,5},{7,8},{8,7},{9,10},{10,... | collective-permute-start | bytes 49160 | tf_op jit(solution)/shard_map/ppermute | solution.py:590
  3.3 6.8 %collective-permute-start = (bf16[64,128]{1,0:T(8,128)(2,1)S(1)}, bf16[64,128]{1,0:T(8,128)(2,1)S(1)}, u32[]{:S(2)}, u32[]{:S(2)}) collective-permute-start(bf16[64,128]{1,0:T(8,128)(2,1)S(1)} %get-tuple-element.88), channel_id=1, source_target_pairs={{0,1},{1,0},{2,3},{3,2},{4,5},{5,4},{6,7},{7,6},{8,9},{9,8},{10,11... | collective-permute-start | bytes 49160 | tf_op jit(solution)/shard_map/ppermute | solution.py:579
  3.8 6.3 %copy-start.5 = (bf16[2048,128]{1,0:T(8,128)(2,1)S(1)}, bf16[2048,128]{1,0:T(8,128)(2,1)}, u32[]{:S(2)}) copy-start(bf16[2048,128]{1,0:T(8,128)(2,1)} %acts.1) | copy-start | bytes 1572868
  3.9 6.3 %copy-start.6 = (s32[64]{0:T(128)S(1)}, s32[64]{0:T(128)}, u32[]{:S(2)}) copy-start(s32[64]{0:T(128)} %offsets.5) | copy-start | bytes 772
  3.9 6.3 %copy-start.8 = (bf16[128,768]{1,0:T(8,128)(2,1)S(1)}, bf16[128,768]{1,0:T(8,128)(2,1)}, u32[]{:S(2)}) copy-start(bf16[128,768]{1,0:T(8,128)(2,1)} %up.1) | copy-start | bytes 589828
  3.9 6.3 %copy-start.9 = (bf16[128,384]{1,0:T(8,128)(2,1)S(1)}, bf16[128,384]{1,0:T(8,128)(2,1)}, u32[]{:S(2)}) copy-start(bf16[128,384]{1,0:T(8,128)(2,1)} %qkv.3) | copy-start | bytes 294916
  3.9 6.3 %copy-start.10 = (bf16[128,128]{1,0:T(8,128)(2,1)S(1)}, bf16[128,128]{1,0:T(8,128)(2,1)}, u32[]{:S(2)}) copy-start(bf16[128,128]{1,0:T(8,128)(2,1)} %out_weight.2) | copy-start | bytes 98308
  3.9 6.3 %copy-start.11 = (s32[2048]{0:T(1024)S(1)}, s32[2048]{0:T(1024)}, u32[]{:S(2)}) copy-start(s32[2048]{0:T(1024)} %param.25) | copy-start | bytes 24580
  3.9 6.3 %copy-start.12 = (f32[128]{0:T(128)S(1)}, f32[128]{0:T(128)}, u32[]{:S(2)}) copy-start(f32[128]{0:T(128)} %param.17) | copy-start | bytes 1540
  10.2 5.3 %copy-start.13 = (bf16[16,256,256]{2,1,0:T(8,128)(2,1)S(1)}, bf16[16,256,256]{2,1,0:T(8,128)(2,1)}, u32[]{:S(2)}) copy-start(bf16[16,256,256]{2,1,0:T(8,128)(2,1)} %own_far.3) | copy-start | bytes 6291460
  10.2 6.8 %copy-start.14 = (f32[768]{0:T(1024)S(1)}, f32[768]{0:T(1024)}, u32[]{:S(2)}) copy-start(f32[768]{0:T(1024)} %param.27) | copy-start | bytes 9220
  13.9 1.6 %collective-permute-start.2 = (bf16[128,896]{1,0:T(8,128)(2,1)S(1)}, bf16[128,896]{1,0:T(8,128)(2,1)S(1)}, u32[]{:S(2)}, u32[]{:S(2)}) collective-permute-start(bf16[128,896]{1,0:T(8,128)(2,1)S(1)} %get-tuple-element.53), channel_id=1, source_target_pairs={{0,1},{1,0},{2,3},{3,2},{4,5},{5,4},{6,7},{7,6},{8,9},{9,8},{10,11... | collective-permute-start | bytes 688136 | tf_op jit(solution)/shard_map/ppermute | solution.py:579
  15.5 4.7 %collective-permute-start.4 = (bf16[16,256,256]{2,1,0:T(8,128)(2,1)S(1)}, bf16[16,256,256]{2,1,0:T(8,128)(2,1)}, u32[]{:S(2)}, u32[]{:S(2)}) collective-permute-start(bf16[16,256,256]{2,1,0:T(8,128)(2,1)S(1)} %copy-done.13), channel_id=1, source_target_pairs={{0,1},{1,0},{2,3},{3,2},{4,5},{5,4},{6,7},{7,6},{8,9},{9,8},{10,11... | collective-permute-start | bytes 6291464 | tf_op jit(solution)/shard_map/ppermute | solution.py:579
  15.7 4.4 %collective-permute-start.3 = (bf16[64,896]{1,0:T(8,128)(2,1)S(1)}, bf16[64,896]{1,0:T(8,128)(2,1)S(1)}, u32[]{:S(2)}, u32[]{:S(2)}) collective-permute-start(bf16[64,896]{1,0:T(8,128)(2,1)S(1)} %get-tuple-element.89), channel_id=1, source_target_pairs={{0,2},{1,3},{2,0},{3,1},{4,6},{5,7},{6,4},{7,5},{8,10},{9,11},{10,... | collective-permute-start | bytes 344072 | tf_op jit(solution)/shard_map/ppermute | solution.py:608
  20.5 6.1 %collective-permute-start.5 = (bf16[64,768]{1,0:T(8,128)(2,1)S(1)}, bf16[64,768]{1,0:T(8,128)(2,1)S(1)}, u32[]{:S(2)}, u32[]{:S(2)}) collective-permute-start(bf16[64,768]{1,0:T(8,128)(2,1)S(1)} %get-tuple-element.58.own_act), channel_id=1, source_target_pairs={{0,2},{1,3},{2,0},{3,1},{4,6},{5,7},{6,4},{7,5},{8,10},{9,11},{10,... | collective-permute-start | bytes 294920 | tf_op jit(solution)/shard_map/ppermute | solution.py:608
  22.1 4.6 %collective-permute-start.6 = (bf16[64,768]{1,0:T(8,128)(2,1)S(1)}, bf16[64,768]{1,0:T(8,128)(2,1)S(1)}, u32[]{:S(2)}, u32[]{:S(2)}) collective-permute-start(bf16[64,768]{1,0:T(8,128)(2,1)S(1)} %get-tuple-element.60.refs_1_), channel_id=1, source_target_pairs={{0,1},{1,0},{2,3},{3,2},{4,5},{5,4},{6,7},{7,6},{8,9},{9,8},{10,11... | collective-permute-start | bytes 294920 | tf_op jit(solution)/shard_map/ppermute | solution.py:579
  23.3 9.6 %collective-permute-start.9 = (bf16[64,768]{1,0:T(8,128)(2,1)S(1)}, bf16[64,768]{1,0:T(8,128)(2,1)S(1)}, u32[]{:S(2)}, u32[]{:S(2)}) collective-permute-start(bf16[64,768]{1,0:T(8,128)(2,1)S(1)} %get-tuple-element.60.refs_1_), channel_id=1, source_target_pairs={{0,8},{4,12},{8,0},{12,4},{1,9},{5,13},{9,1},{13,5},{2,10},{6,14},... | collective-permute-start | bytes 294920 | tf_op jit(solution)/shard_map/ppermute | solution.py:613
  25.6 7.3 %collective-permute-start.8 = (bf16[64,768]{1,0:T(8,128)(2,1)S(1)}, bf16[64,768]{1,0:T(8,128)(2,1)S(1)}, u32[]{:S(2)}, u32[]{:S(2)}) collective-permute-start(bf16[64,768]{1,0:T(8,128)(2,1)S(1)} %get-tuple-element.60.refs_1_), channel_id=1, source_target_pairs={{0,12},{4,8},{8,4},{12,0},{1,13},{5,9},{9,5},{13,1},{2,14},{6,10},... | collective-permute-start | bytes 294920 | tf_op jit(solution)/shard_map/ppermute | solution.py:613
  26.7 7.1 %collective-permute-start.7 = (bf16[64,768]{1,0:T(8,128)(2,1)S(1)}, bf16[64,768]{1,0:T(8,128)(2,1)S(1)}, u32[]{:S(2)}, u32[]{:S(2)}) collective-permute-start(bf16[64,768]{1,0:T(8,128)(2,1)S(1)} %get-tuple-element.60.refs_1_), channel_id=1, source_target_pairs={{0,4},{4,0},{8,12},{12,8},{1,5},{5,1},{9,13},{13,9},{2,6},{6,2},{1... | collective-permute-start | bytes 294920 | tf_op jit(solution)/shard_map/ppermute | solution.py:613
  33.7 2.2 %collective-permute-start.10 = (bf16[64,768]{1,0:T(8,128)(2,1)S(1)}, bf16[64,768]{1,0:T(8,128)(2,1)S(1)}, u32[]{:S(2)}, u32[]{:S(2)}) collective-permute-start(bf16[64,768]{1,0:T(8,128)(2,1)S(1)} %collective-permute-done.7.refs_0_), channel_id=1, source_target_pairs={{0,1},{1,0},{2,3},{3,2},{4,5},{5,4},{6,7},{7,6},{8,9},{9,8},{10,11... | collective-permute-start | bytes 294920 | tf_op jit(solution)/shard_map/ppermute | solution.py:579
  35.0 1.3 %collective-permute-start.11 = (bf16[64,768]{1,0:T(8,128)(2,1)S(1)}, bf16[64,768]{1,0:T(8,128)(2,1)S(1)}, u32[]{:S(2)}, u32[]{:S(2)}) collective-permute-start(bf16[64,768]{1,0:T(8,128)(2,1)S(1)} %collective-permute-done.8.refs_1_), channel_id=1, source_target_pairs={{0,1},{1,0},{2,3},{3,2},{4,5},{5,4},{6,7},{7,6},{8,9},{9,8},{10,11... | collective-permute-start | bytes 294920 | tf_op jit(solution)/shard_map/ppermute | solution.py:579
  35.0 1.5 %collective-permute-start.12 = (bf16[64,768]{1,0:T(8,128)(2,1)S(1)}, bf16[64,768]{1,0:T(8,128)(2,1)S(1)}, u32[]{:S(2)}, u32[]{:S(2)}) collective-permute-start(bf16[64,768]{1,0:T(8,128)(2,1)S(1)} %collective-permute-done.9.refs_2_), channel_id=1, source_target_pairs={{0,1},{1,0},{2,3},{3,2},{4,5},{5,4},{6,7},{7,6},{8,9},{9,8},{10,11... | collective-permute-start | bytes 294920 | tf_op jit(solution)/shard_map/ppermute | solution.py:579
  36.4 12.1 %copy-start.1 = (bf16[768,768]{1,0:T(8,128)(2,1)S(1)}, bf16[768,768]{1,0:T(8,128)(2,1)}, u32[]{:S(2)}) copy-start(bf16[768,768]{1,0:T(8,128)(2,1)} %token_out.1) | copy-start | bytes 3538948
  36.4 12.1 %copy-start.2 = (bf16[768,128]{1,0:T(8,128)(2,1)S(1)}, bf16[768,128]{1,0:T(8,128)(2,1)}, u32[]{:S(2)}) copy-start(bf16[768,128]{1,0:T(8,128)(2,1)} %down.1) | copy-start | bytes 589828
  40.8 10.4 %copy-start = (bf16[4,2048,128]{2,1,0:T(8,128)(2,1)S(1)}, bf16[4,2048,128]{2,1,0:T(8,128)(2,1)}, u32[]{:S(2)}) copy-start(bf16[4,2048,128]{2,1,0:T(8,128)(2,1)} %bias.3) | copy-start | bytes 6291460
  40.8 10.4 %copy-start.3 = (bf16[128,384]{1,0:T(8,128)(2,1)S(1)}, bf16[128,384]{1,0:T(8,128)(2,1)}, u32[]{:S(2)}) copy-start(bf16[128,384]{1,0:T(8,128)(2,1)} %qkv.5) | copy-start | bytes 294916
  40.8 10.4 %copy-start.7 = (f32[128]{0:T(128)S(1)}, f32[128]{0:T(128)}, u32[]{:S(2)}) copy-start(f32[128]{0:T(128)} %param.20) | copy-start | bytes 1540
  40.8 7.7 %collective-permute-start.15 = (bf16[128,896]{1,0:T(8,128)(2,1)S(1)}, bf16[128,896]{1,0:T(8,128)(2,1)S(1)}, u32[]{:S(2)}, u32[]{:S(2)}) collective-permute-start(bf16[128,896]{1,0:T(8,128)(2,1)S(1)} %shard_map.158.refs_0_), channel_id=1, source_target_pairs={{0,2},{1,3},{2,0},{3,1},{4,6},{5,7},{6,4},{7,5},{8,10},{9,11},{10,... | collective-permute-start | bytes 688136 | tf_op jit(solution)/shard_map/ppermute | solution.py:608
  41.2 1.8 %collective-permute-start.13 = (bf16[80,128]{1,0:T(8,128)(2,1)S(1)}, bf16[80,128]{1,0:T(8,128)(2,1)S(1)}, u32[]{:S(2)}, u32[]{:S(2)}) collective-permute-start(bf16[80,128]{1,0:T(8,128)(2,1)S(1)} %get-tuple-element.77), channel_id=1, source_target_pairs={{0,1},{1,0},{2,3},{3,2},{4,5},{5,4},{6,7},{7,6},{8,9},{9,8},{10,11... | collective-permute-start | bytes 61448 | tf_op jit(solution)/shard_map/ppermute | solution.py:579
  41.8 6.7 %collective-permute-start.14 = (bf16[80,128]{1,0:T(8,128)(2,1)S(1)}, bf16[80,128]{1,0:T(8,128)(2,1)S(1)}, u32[]{:S(2)}, u32[]{:S(2)}) collective-permute-start(bf16[80,128]{1,0:T(8,128)(2,1)S(1)} %get-tuple-element.78), channel_id=1, source_target_pairs={{0,16},{1,2},{2,1},{3,4},{4,3},{5,6},{6,5},{7,8},{8,7},{9,10},{10,... | collective-permute-start | bytes 61448 | tf_op jit(solution)/shard_map/ppermute | solution.py:590
  49.5 1.8 %collective-permute-start.16 = (bf16[128,128]{1,0:T(8,128)(2,1)S(1)}, bf16[128,128]{1,0:T(8,128)(2,1)S(1)}, u32[]{:S(2)}, u32[]{:S(2)}) collective-permute-start(bf16[128,128]{1,0:T(8,128)(2,1)S(1)} %shard_map.159.own_back), channel_id=1, source_target_pairs={{0,1},{1,0},{2,3},{3,2},{4,5},{5,4},{6,7},{7,6},{8,9},{9,8},{10,11... | collective-permute-start | bytes 98312 | tf_op jit(solution)/shard_map/ppermute | solution.py:579
  49.9 6.5 %collective-permute-start.17 = (bf16[64,128]{1,0:T(8,128)(2,1)S(1)}, bf16[64,128]{1,0:T(8,128)(2,1)S(1)}, u32[]{:S(2)}, u32[]{:S(2)}) collective-permute-start(bf16[64,128]{1,0:T(8,128)(2,1)S(1)} %slice_select_fusion), channel_id=1, source_target_pairs={{0,16},{1,4},{2,18},{3,6},{4,1},{5,8},{6,3},{7,10},{8,5},{9,12},{1... | collective-permute-start | bytes 49160 | tf_op jit(solution)/shard_map/ppermute | solution.py:590
  51.3 5.2 %copy-start.4 = (bf16[128,128]{1,0:T(8,128)(2,1)S(1)}, bf16[128,128]{1,0:T(8,128)(2,1)}, u32[]{:S(2)}) copy-start(bf16[128,128]{1,0:T(8,128)(2,1)} %out_weight.3) | copy-start | bytes 98308

commit v7 on v6

--- a/solution.py
+++ b/solution.py
@@ -79,15 +79,18 @@
             out = jnp.where(lane_head == head, stack[head * block : (head + 1) * block], out)
         return out
 
+    yield
     scores = []
     for query_at, _, key_at in places:
         spread = jnp.concatenate([q[pl.ds(query_at, block), :]] * heads, axis=0) * own_head
         scores.append(dot_nt(spread, k[pl.ds(key_at, span), :].astype(BF)))
+    yield
     raised = []
     for (_, bias_at, _), score in zip(places, scores):
         tile = bias[:, pl.ds(bias_at, block), :].reshape(stacked, span).astype(F32)
         score = score * scale + tile
         raised.append(jnp.exp(score - jnp.max(score, axis=-1, keepdims=True)).astype(BF))
+    yield
     for (query_at, _, key_at), weights in zip(places, raised):
         values = jnp.concatenate([v[pl.ds(key_at, span), :].astype(BF), ones], axis=1)
         out = dot(weights, values)
@@ -121,7 +124,8 @@
             window = edge + step * group + member
             at = pl.multiple_of(window * block, block)
             places.append((at, at, offsets[window]))
-        attend_windows(places, bias, q, k, v, mixed)
+        for _ in attend_windows(places, bias, q, k, v, mixed):
+            pass
         return carry
 
     lax.fori_loop(0, (windows - 2 * edge) // group, one_group, 0)
@@ -142,6 +146,7 @@
         target[RIM : 3 * RIM, :] = source[: 2 * RIM, :]
         target[3 * RIM : 5 * RIM, :] = source[2 * RIM :, :]
     normed = norm_rows(jnp.concatenate([near, far], axis=0), gain).astype(BF)
+    yield
     packed = dot(normed, qkv[:, channels:]).astype(BF).astype(F32)
     near_at = pl.multiple_of(jnp.where(side == 0, 5 * RIM, 0), RIM)
     far_at = pl.multiple_of(5 * RIM - near_at, RIM)
@@ -155,7 +160,7 @@
         window = windows - edge + member
         at = RIM + member * block
         places.append((at, at, offsets[window] - (rows - 4 * RIM)))
-    attend_windows(places, bias, edge_q, k, v, mixed)
+    yield from attend_windows(places, bias, edge_q, k, v, mixed)
 
 
 def fetches(sources, targets, sems, first=0):
@@ -215,15 +220,28 @@
 ):
     side = info[0]
     rows = acts.shape[0]
-    close_inner(acts, mixed, out_weight, atoms)
-    edge_windows(
+    edges = edge_windows(
         starts_from(offsets, info[4] - RIM), bias, gain[...], qkv[...], near[...].astype(F32), far[...].astype(F32), side,
         edge_q, edge_k, edge_v, k, v, edge_mixed,
     )
-    close_edge(acts, edge_mixed, out_weight, atoms)
     step = 256
     tokens = 2 * send.shape[0]
     half = tokens // 2
+    wide = up.shape[1]
+    next(edges)
+    close_inner(acts, mixed, out_weight, atoms)
+    member = one_hot(token_of(tokens, share, 1 - side) + info[1] * tokens, ids[...])
+    next(edges)
+    inner = slice(step, rows - step)
+    inner_atoms = atoms[inner, :]
+    partial_sums = []
+    for at in range(0, wide, step):
+        feat = jnp.maximum(dot(inner_atoms, up[:, at : at + step]), 0.0).astype(BF)
+        partial_sums.append(dot(member[:, inner], feat))
+        next(edges, None)
+    for _ in edges:
+        pass
+    close_edge(acts, edge_mixed, out_weight, atoms)
     head_ids = ids[:, :RIM]
     tail_ids = ids[:, rows - RIM :]
     for message, last in ((near_message, 1 - side), (far_message, side)):
@@ -232,12 +250,11 @@
         sent = head_ids + last * (tail_ids - head_ids)
         coded = jnp.concatenate([sent >> 6, sent & 63], axis=1).astype(F32)
         message[RIM:, :] = jnp.broadcast_to(coded, (16, 2 * RIM)).astype(BF)
-    member = one_hot(token_of(tokens, share, 1 - side) + info[1] * tokens, ids[...])
-    wide = up.shape[1]
-    atom_rows = atoms[...]
-    for at in range(0, wide, step):
-        feat = jnp.maximum(dot(atom_rows, up[:, at : at + step]), 0.0).astype(BF)
-        sums = dot(member, feat).astype(BF)
+    outer_atoms = jnp.concatenate([atoms[:step, :], atoms[rows - step :, :]], axis=0)
+    outer_member = jnp.concatenate([member[:, :step], member[:, rows - step :]], axis=1)
+    for at, partial_sum in zip(range(0, wide, step), partial_sums):
+        feat = jnp.maximum(dot(outer_atoms, up[:, at : at + step]), 0.0).astype(BF)
+        sums = (partial_sum + dot(outer_member, feat)).astype(BF)
         send[:, at : at + step] = sums[:half]
         keep[:, at : at + step] = sums[half:]
     count = dot(member, jnp.ones((rows, LANES), BF))
@@ -249,13 +266,13 @@
     keep[:, wide:] = pieces[half:]
 
 
-def close_inner(acts, mixed, out_weight, out):
+def close_inner(acts, mixed, out_weight, out, part=0, parts=1):
     rows = acts.shape[0]
     step = 256
-    for at in range(0, rows, step):
+    for at in range(rows // parts * part, rows // parts * (part + 1), step):
         first, last = max(at, RIM), min(at + step, rows - RIM)
-        part = acts[first:last, :].astype(F32) + dot(mixed[first:last, :], out_weight[...])
-        out[first:last, :] = part.astype(BF)
+        moved = acts[first:last, :].astype(F32) + dot(mixed[first:last, :], out_weight[...])
+        out[first:last, :] = moved.astype(BF)
 
 
 def close_edge(acts, mixed, out_weight, out):
@@ -372,8 +389,8 @@
     rows_count = len(steps)
     other_acts, refs = refs[:others], refs[others:]
     own, near, refs = refs[:rows_count], refs[rows_count : 2 * rows_count], refs[2 * rows_count :]
-    act, queries, gates, key_weight, value_weight, pair_bias, mixed, tops, totals = refs[:9]
-    query_weight, gate_weight, tokens, keys, values, bias, slots, sems = refs[9:]
+    act, queries, gates, key_weight, value_weight, pair_bias, rest_bias, mixed, tops, totals = refs[:10]
+    query_weight, gate_weight, tokens, keys, values, bias, slots, sems = refs[10:]
     share, wide = own[0].shape
     weights = fetches(
         [weight_far.at[:, pl.ds(part * wide, wide)] for part in range(4)],
@@ -382,7 +399,12 @@
     )
     targets = (slots.at[0], slots.at[1]) if solo else [bias.at[:, :, pl.ds(at, LANES)] for at in (0, LANES)]
     tiles = fetches(*bias_pieces(info, (own_far, near_far), 0, targets, share), sems, 4)
-    for copy in weights[:3] + tiles + weights[3:]:
+    later = []
+    for block in range(rest_bias.shape[2] // (2 * LANES)):
+        targets = [rest_bias.at[:, :, pl.ds((2 * block + half) * LANES, LANES)] for half in range(2)]
+        sources, places = bias_pieces(info, (own_far, near_far), block + 1, targets, share)
+        later += fetches(sources, places, sems, 4 + len(tiles) + len(later))
+    for copy in weights[:3] + tiles + weights[3:] + later:
         copy.start()
     pairs = others + 1
     place = info[2]
@@ -414,29 +436,21 @@
         mixed[:, block * LANES : (block + 1) * LANES] = piece
     weights[3].wait()
     gates[...] = jax.nn.sigmoid(dot(normed, gate_weight[...]).astype(BF).astype(F32))
+    for copy in later:
+        copy.wait()
 
 
 def attend_rest(
-    info, own_far, near_far, queries, key_weight, value_weight, pair_bias, former, former_top, former_total,
-    *refs, steps, solo
+    info, queries, key_weight, value_weight, pair_bias, bias, former, former_top, former_total, *refs, steps, solo
 ):
     rows_count = len(steps)
     own, near = refs[:rows_count], refs[rows_count : 2 * rows_count]
-    packed, tokens, keys, values, bias, sems = refs[2 * rows_count :]
+    packed, tokens, keys, values = refs[2 * rows_count :]
     heads = bias.shape[0]
     count, wide = queries.shape
-    tiles = []
-    for block in range(bias.shape[2] // (2 * LANES)):
-        targets = [bias.at[:, :, pl.ds((2 * block + half) * LANES, LANES)] for half in range(2)]
-        sources, places = bias_pieces(info, (own_far, near_far), block + 1, targets, own[0].shape[0])
-        tiles += fetches(sources, places, sems, len(tiles))
-    for copy in tiles:
-        copy.start()
     place_keys(info, own, near, tokens, steps, solo)
     keys[...] = dot(tokens[...], key_weight[...]).astype(BF)
     values[...] = dot(tokens[...], value_weight[...]).astype(BF)
-    for copy in tiles:
-        copy.wait()
     lane = lax.broadcasted_iota(jnp.int32, (count, LANES), 1)
     ends = [jnp.zeros((count, LANES), F32), jnp.ones((count, LANES), F32)]
 
@@ -456,10 +470,9 @@
     packed[:, wide:] = (first + pltpu.roll(second, heads, 1) + pltpu.roll(rest, 2 * heads, 1)).astype(BF)
 
 
-def finish_tokens(act, gates, token_out, down, *refs, parts_count):
+def finish_tokens(act, gates, token_out, down, *refs, parts_count, heads):
     parts, back = refs[:parts_count], refs[parts_count]
     count, wide = act.shape
-    heads = 16
     size = wide // heads
     logs = []
     for part in parts:
@@ -513,7 +526,6 @@
     mixed, edge_q, edge_k, edge_v, result, k, v, edge_mixed, ends, *, share, columns
 ):
     side, column = info[0], info[3]
-    close_inner(atoms2, mixed, out_weight, result)
     ends[:, :RIM, :] = bias[:, :RIM, :]
     ends[:, RIM:, :] = bias[:, bias.shape[1] - RIM :, :]
     tokens = 2 * own_back.shape[0]
@@ -535,10 +547,16 @@
         + dot_tn(one_hot(table_ids, far_token), table)
         + dot_tn(one_hot(beyond, far_token), far_back[...])
     )
-    edge_windows(
+    edges = edge_windows(
         starts_from(offsets, info[4] - RIM), ends, gain[...], qkv[...], near_rows.astype(BF).astype(F32), far_rows.astype(BF).astype(F32), side,
         edge_q, edge_k, edge_v, k, v, edge_mixed,
     )
+    parts = 4
+    for part in range(parts):
+        next(edges)
+        close_inner(atoms2, mixed, out_weight, result, part, parts)
+    for _ in edges:
+        pass
     close_edge(atoms2, edge_mixed, out_weight, result)
 
 
@@ -667,13 +685,18 @@
     )
 
     chip_sum = (keep.astype(F32) + to_near(send).astype(F32)).astype(BF)
-    chip_sum, near_bias = lax.optimization_barrier((chip_sum, pair_bias))
+    chip_sum, near_bias, near_message, far_message = lax.optimization_barrier(
+        (chip_sum, pair_bias, near_message, far_message)
+    )
     bias_near = to_near(near_bias)
     sums = [lax.dynamic_slice_in_dim(chip_sum, pair * share, share, axis=0)]
     for step in range(1, pairs):
         piece = lax.dynamic_slice_in_dim(chip_sum, (pair + step) % pairs * share, share, axis=0)
         sums.append(along_pairs(piece, step))
-    sums, bias_near = lax.optimization_barrier((sums, bias_near))
+    near_message, far_message = to_near(near_message), to_far(far_message)
+    sums, bias_near, near_message, far_message = lax.optimization_barrier(
+        (sums, bias_near, near_message, far_message)
+    )
     share_shape = jax.ShapeDtypeStruct((share, wide), BF)
     gain_row = token_gain.reshape(1, -1)
     act, normed = call(
@@ -696,14 +719,16 @@
     head_shape = jax.ShapeDtypeStruct((heads, half, LANES), F32)
     weight_shape = jax.ShapeDtypeStruct((wide, wide), BF)
     tile_count = 2 * pairs
+    blocks = row_count // group - 1
     act_rows, queries, gates, *held, mixed, tops, totals = call(
         functools.partial(attend_first, others=len(other_acts), steps=list(range(split)), solo=solo),
         [half_shape, half_shape, wide_shape, weight_shape, weight_shape]
-        + [jax.ShapeDtypeStruct((heads, half, LANES), BF), wide_shape, head_shape, head_shape],
+        + [jax.ShapeDtypeStruct((heads, half, LANES), BF), jax.ShapeDtypeStruct((heads, half, 2 * LANES * blocks), BF)]
+        + [wide_shape, head_shape, head_shape],
         [pltpu.VMEM((wide, wide), BF)] * 2
         + key_scratch(split)
         + [pltpu.VMEM((heads, half, 2 * split * share), BF), pltpu.VMEM((2, heads, half, LANES), BF)]
-        + [pltpu.SemaphoreType.DMA((4 + tile_count,))],
+        + [pltpu.SemaphoreType.DMA((4 + tile_count * (blocks + 1),))],
         [SMEM, HBM, VMEM, VMEM, HBM, HBM] + [VMEM] * (len(other_acts) + 2 * split),
         1_000,
         24,
@@ -711,29 +736,20 @@
         info, stay(token_weight), gain_row, act, stay(pair_bias), stay(bias_near), *other_acts,
         *own_keys[:split], *near_keys,
     )
-    rest_steps = sorted(range(split, row_count), key=lambda step: (step >= group, -step))
+    rest_steps = sorted(range(split, row_count), key=lambda step: (step < group, step))
     rest_keys, mixed = lax.optimization_barrier(([own_keys[step] for step in rest_steps], mixed))
     rest_near = [to_near(x) for x in rest_keys]
-    blocks = row_count // group - 1
     part = call(
         functools.partial(attend_rest, steps=rest_steps, solo=solo),
         packed_shape,
-        key_scratch(rest)
-        + [pltpu.VMEM((heads, half, 2 * LANES * blocks), BF), pltpu.SemaphoreType.DMA((tile_count * blocks,))],
-        [SMEM, HBM, HBM] + [VMEM] * (7 + 2 * rest),
+        key_scratch(rest),
+        [SMEM] + [VMEM] * (8 + 2 * rest),
         2_000_000_000,
-    )(
-        info, stay(pair_bias), stay(bias_near), queries, *held, mixed, tops, totals, *rest_keys, *rest_near,
-    )
-
-    near_message, far_message, part = lax.optimization_barrier((near_message, far_message, part))
-    parts = [along_pairs(part, step) for step in range(1, pairs)]
-    near_message, far_message, parts = lax.optimization_barrier(
-        (to_near(near_message), to_far(far_message), parts)
-    )
-    parts = [part] + parts
+    )(info, queries, *held, mixed, tops, totals, *rest_keys, *rest_near)
+
+    parts = [part] + [along_pairs(part, step) for step in range(1, pairs)]
     own_back = call(
-        functools.partial(finish_tokens, parts_count=pairs),
+        functools.partial(finish_tokens, parts_count=pairs, heads=heads),
         jax.ShapeDtypeStruct((half, channels), BF),
         [],
         [VMEM] * (4 + pairs),

time: 59.6 us -> 59 us (0.990)
  starting transfers between devices: 16.3 us -> 15.5 us
  waiting for transfers between devices: 13.4 us -> 14 us
    ppermute x3, waiting for transfers between devices: 5.63 us -> 1.44 us  [swapped(): return lax.ppermute(x, ('group', 'row', 'col'), pairs_list)]
    ppermute x3, waiting for transfers between devices: 3.13 us -> 6.56 us  [along_pairs(): lax.ppermute(x, 'col', [(2 * i + k, 2 * ((i + step) % pairs) + k) for i i...]
    ppermute x9, waiting for transfers between devices: 2.4 us -> 3.93 us  [to_near(): return lax.ppermute(x, 'col', [(i, i ^ 1) for i in range(col_count)])]
    ppermute x3, starting transfers between devices: 5.02 us -> 3.89 us  [swapped(): return lax.ppermute(x, ('group', 'row', 'col'), pairs_list)]
    ppermute x9, starting transfers between devices: 4.82 us -> 5.77 us  [to_near(): return lax.ppermute(x, 'col', [(i, i ^ 1) for i in range(col_count)])]
    ppermute x3, starting transfers between devices: 3.14 us -> 2.4 us  [along_pairs(): lax.ppermute(x, 'col', [(2 * i + k, 2 * ((i + step) % pairs) + k) for i i...]
  transfers between devices with their start and end apart: 18 -> 18, of which waited for: 8 -> 9; matrix products, arithmetic and copies ran while one was open for 0% -> 0% of each run, Pallas kernels for 27% -> 28%
where the time goes in v7:
time: 59 us; the launch traced here: 58.3 us
  Pallas kernels  27.5 us (47%)
  starting transfers between devices  15.5 us (26%)
  waiting for transfers between devices  14 us (24%)
  local copies, waits for them, and re-layouts  0.92 us (2%)
    ppermute x3, waiting for transfers between devices, along_pairs(): lax.ppermute(x, 'col', [(2 * i + k, 2 * ((i + step) % pairs) + k) for i i...  6.56 us
    pallas_call x1, Pallas kernels, body(): call(functools.partial(first_inner, pieces=pieces), [atom_shape] + edge_s...  6.19 us
    ppermute x9, starting transfers between devices, to_near(): return lax.ppermute(x, 'col', [(i, i ^ 1) for i in range(col_count)])  5.77 us
    pallas_call x1, Pallas kernels, body(): call(functools.partial(second_inner, share=share), [atom_shape, atom_shap...  5.17 us
    pallas_call x1, Pallas kernels, body(): call(functools.partial(attend_first, others=len(other_acts), steps=list(r...  4.87 us
    pallas_call x1, Pallas kernels, body(): call(functools.partial(attend_rest, steps=rest_steps, solo=solo), packed_...  4.08 us
    ppermute x9, waiting for transfers between devices, to_near(): return lax.ppermute(x, 'col', [(i, i ^ 1) for i in range(col_count)])  3.93 us
    ppermute x3, starting transfers between devices, swapped(): return lax.ppermute(x, ('group', 'row', 'col'), pairs_list)  3.89 us
  transfers between devices with their start and end apart: 18, of which 9 were waited for; matrix products, arithmetic and copies ran while one was open for 0% of the time, Pallas kernels for 28%

profile of v7, /device:TPU:1, one launch (start us, length us, event | category | flops | bytes accessed | tf_op | source)
XLA Modules:
  0.0 58.3 jit_solution(14183189896349431295)
XLA Ops:
  0.0 0.7 %constant_dynamic-slice_fusion.2 = (bf16[64,128]{1,0:T(8,128)(2,1)S(1)}, bf16[64,128]{1,0:T(8,128)(2,1)S(1)}) fusion(bf16[2048,128]{1,0:T(8,128)(2,1)} %acts.1, s32[]{:T(128)S(6)} %select_n.41, s32[]{:T(128)S(6)} %select_n.40), kind=kLoop, calls=%fused_computation.4 | loop fusion | bytes 65544 | tf_op jit(solution)/shard_map/dynamic_slice | solution.py:634
  0.7 0.1 collective-permute-start
  0.8 2.5 %collective-permute-start.1 = (bf16[64,128]{1,0:T(8,128)(2,1)S(1)}, bf16[64,128]{1,0:T(8,128)(2,1)S(1)}, u32[]{:S(2)}, u32[]{:S(2)}) collective-permute-start(bf16[64,128]{1,0:T(8,128)(2,1)S(1)} %get-tuple-element.85), channel_id=1, source_target_pairs={{0,16},{1,2},{2,1},{3,4},{4,3},{5,6},{6,5},{7,8},{8,7},{9,10},{10,... | collective-permute-start | bytes 49160 | tf_op jit(solution)/shard_map/ppermute | solution.py:608
  3.3 0.1 stack.23.info
  3.4 0.0 copy-start.10
  3.5 0.0 copy-start.11
  3.5 0.0 copy-start.12
  3.5 6.2 %shard_map.154 = (bf16[2048,128]{1,0:T(8,128)(2,1)S(1)}, bf16[128,128]{1,0:T(8,128)(2,1)S(1)}, f32[256,128]{1,0:T(8,128)S(1)}, f32[256,128]{1,0:T(8,128)S(1)}, bf16[4,128,128]{2,1,0:T(8,128)(2,1)S(1)}) custom-call(s32[5]{0:T(128)S(1)} %stack.23.info, bf16[2048,128]{1,0:T(8,128)(2,1)} %acts.1, f32[1,128]{1,0:T(1,128)} %bitcast.12, bf16[128,384]{1,0:T(8,128)(2,1)} %qkv.3, ...), custom_call_target="tpu_custom_call" | custom-call | flops 1500000000 | bytes 1000 | tf_op jit(solution)/shard_map/pallas_call | solution.py:663
  9.7 0.0 collective-permute-done.near
  9.8 0.0 copy-start.13
  9.8 0.0 copy-start.14
  9.8 3.4 %shard_map.155 = (bf16[2048,128]{1,0:T(8,128)(2,1)S(1)}, bf16[128,896]{1,0:T(8,128)(2,1)S(1)}, bf16[128,896]{1,0:T(8,128)(2,1)S(1)}, bf16[80,128]{1,0:T(8,128)(2,1)S(1)}, bf16[80,128]{1,0:T(8,128)(2,1)S(1)}) custom-call(s32[5]{0:T(128)S(1)} %stack.23.info, s32[64]{0:T(128)S(1)} %copy-done.6, s32[1,2048]{1,0:T(1,128)S(1)} %bitcast.10, ...), custom_call_target="tpu_custom_call" | custom-call | flops 2000000000 | bytes 1000 | tf_op jit(solution)/shard_map/pallas_call | solution.py:675
  13.2 0.5 collective-permute-start.2
  13.7 1.1 %collective-permute-done.2 = bf16[128,896]{1,0:T(8,128)(2,1)S(1)} collective-permute-done((bf16[128,896]{1,0:T(8,128)(2,1)S(1)}, bf16[128,896]{1,0:T(8,128)(2,1)S(1)}, u32[]{:S(2)}, u32[]{:S(2)}) %collective-permute-start.2) | collective-permute-done | bytes 229408 | tf_op jit(solution)/shard_map/ppermute | solution.py:597
  14.8 0.1 add_convert_fusion
  14.9 0.4 collective-permute-start.4
  15.3 1.1 %collective-permute-start.3 = (bf16[64,896]{1,0:T(8,128)(2,1)S(1)}, bf16[64,896]{1,0:T(8,128)(2,1)S(1)}, u32[]{:S(2)}, u32[]{:S(2)}) collective-permute-start(bf16[64,896]{1,0:T(8,128)(2,1)S(1)} %get-tuple-element.87), channel_id=1, source_target_pairs={{0,2},{1,3},{2,0},{3,1},{4,6},{5,7},{6,4},{7,5},{8,10},{9,11},{10,... | collective-permute-start | bytes 344072 | tf_op jit(solution)/shard_map/ppermute | solution.py:626
  16.4 0.7 %collective-permute-start.5 = (bf16[80,128]{1,0:T(8,128)(2,1)S(1)}, bf16[80,128]{1,0:T(8,128)(2,1)S(1)}, u32[]{:S(2)}, u32[]{:S(2)}) collective-permute-start(bf16[80,128]{1,0:T(8,128)(2,1)S(1)} %get-tuple-element.57), channel_id=1, source_target_pairs={{0,1},{1,0},{2,3},{3,2},{4,5},{5,4},{6,7},{7,6},{8,9},{9,8},{10,11... | collective-permute-start | bytes 61448 | tf_op jit(solution)/shard_map/ppermute | solution.py:597
  17.0 0.2 collective-permute-start.6
  17.2 1.9 %collective-permute-done.5.near = bf16[80,128]{1,0:T(8,128)(2,1)S(1)} collective-permute-done((bf16[80,128]{1,0:T(8,128)(2,1)S(1)}, bf16[80,128]{1,0:T(8,128)(2,1)S(1)}, u32[]{:S(2)}, u32[]{:S(2)}) %collective-permute-start.5) | collective-permute-done | bytes 20512 | tf_op jit(solution)/shard_map/ppermute | solution.py:597
  19.1 1.4 %collective-permute-done.6.far = bf16[80,128]{1,0:T(8,128)(2,1)S(1)} collective-permute-done((bf16[80,128]{1,0:T(8,128)(2,1)S(1)}, bf16[80,128]{1,0:T(8,128)(2,1)S(1)}, u32[]{:S(2)}, u32[]{:S(2)}) %collective-permute-start.6) | collective-permute-done | bytes 20512 | tf_op jit(solution)/shard_map/ppermute | solution.py:608
  20.6 0.3 shard_map.156
  20.9 1.0 %collective-permute-start.7 = (bf16[64,768]{1,0:T(8,128)(2,1)S(1)}, bf16[64,768]{1,0:T(8,128)(2,1)S(1)}, u32[]{:S(2)}, u32[]{:S(2)}) collective-permute-start(bf16[64,768]{1,0:T(8,128)(2,1)S(1)} %get-tuple-element.61.own_act), channel_id=1, source_target_pairs={{0,2},{1,3},{2,0},{3,1},{4,6},{5,7},{6,4},{7,5},{8,10},{9,11},{10,... | collective-permute-start | bytes 294920 | tf_op jit(solution)/shard_map/ppermute | solution.py:626
  21.9 1.2 %collective-permute-start.8 = (bf16[64,768]{1,0:T(8,128)(2,1)S(1)}, bf16[64,768]{1,0:T(8,128)(2,1)S(1)}, u32[]{:S(2)}, u32[]{:S(2)}) collective-permute-start(bf16[64,768]{1,0:T(8,128)(2,1)S(1)} %get-tuple-element.63.refs_1_), channel_id=1, source_target_pairs={{0,1},{1,0},{2,3},{3,2},{4,5},{5,4},{6,7},{7,6},{8,9},{9,8},{10,11... | collective-permute-start | bytes 294920 | tf_op jit(solution)/shard_map/ppermute | solution.py:597
  23.1 2.3 %collective-permute-start.9 = (bf16[64,768]{1,0:T(8,128)(2,1)S(1)}, bf16[64,768]{1,0:T(8,128)(2,1)S(1)}, u32[]{:S(2)}, u32[]{:S(2)}) collective-permute-start(bf16[64,768]{1,0:T(8,128)(2,1)S(1)} %get-tuple-element.63.refs_1_), channel_id=1, source_target_pairs={{0,8},{4,12},{8,0},{12,4},{1,9},{5,13},{9,1},{13,5},{2,10},{6,14},... | collective-permute-start | bytes 294920 | tf_op jit(solution)/shard_map/ppermute | solution.py:631
  25.4 1.1 %collective-permute-start.10 = (bf16[64,768]{1,0:T(8,128)(2,1)S(1)}, bf16[64,768]{1,0:T(8,128)(2,1)S(1)}, u32[]{:S(2)}, u32[]{:S(2)}) collective-permute-start(bf16[64,768]{1,0:T(8,128)(2,1)S(1)} %get-tuple-element.63.refs_1_), channel_id=1, source_target_pairs={{0,12},{4,8},{8,4},{12,0},{1,13},{5,9},{9,5},{13,1},{2,14},{6,10},... | collective-permute-start | bytes 294920 | tf_op jit(solution)/shard_map/ppermute | solution.py:631
  26.4 0.1 collective-permute-start.11
  26.5 4.9 %shard_map.157 = (bf16[128,768]{1,0:T(8,128)(2,1)S(1)}, bf16[128,768]{1,0:T(8,128)(2,1)S(1)}, f32[128,768]{1,0:T(8,128)S(1)}, bf16[768,768]{1,0:T(8,128)(2,1)S(1...) custom-call(s32[5]{0:T(128)S(1)} %stack.23.info, ...), custom_call_target="tpu_custom_call" | custom-call | flops 1000 | bytes 1000 | tf_op jit(solution)/shard_map/pallas_call | solution.py:723
  31.4 1.2 %collective-permute-done.9.refs_0_ = bf16[64,768]{1,0:T(8,128)(2,1)S(1)} collective-permute-done((bf16[64,768]{1,0:T(8,128)(2,1)S(1)}, bf16[64,768]{1,0:T(8,128)(2,1)S(1)}, u32[]{:S(2)}, u32[]{:S(2)}) %collective-permute-start.9) | collective-permute-done | bytes 98336 | tf_op jit(solution)/shard_map/ppermute | solution.py:631
  32.6 0.9 %collective-permute-done.11.refs_2_ = bf16[64,768]{1,0:T(8,128)(2,1)S(1)} collective-permute-done((bf16[64,768]{1,0:T(8,128)(2,1)S(1)}, bf16[64,768]{1,0:T(8,128)(2,1)S(1)}, u32[]{:S(2)}, u32[]{:S(2)}) %collective-permute-start.11) | collective-permute-done | bytes 98336 | tf_op jit(solution)/shard_map/ppermute | solution.py:631
  33.5 1.2 %collective-permute-start.12 = (bf16[64,768]{1,0:T(8,128)(2,1)S(1)}, bf16[64,768]{1,0:T(8,128)(2,1)S(1)}, u32[]{:S(2)}, u32[]{:S(2)}) collective-permute-start(bf16[64,768]{1,0:T(8,128)(2,1)S(1)} %collective-permute-done.9.refs_0_), channel_id=1, source_target_pairs={{0,1},{1,0},{2,3},{3,2},{4,5},{5,4},{6,7},{7,6},{8,9},{9,8},{10,11... | collective-permute-start | bytes 294920 | tf_op jit(solution)/shard_map/ppermute | solution.py:597
  34.8 0.0 collective-permute-start.13
  34.8 0.5 collective-permute-start.14
  35.3 0.4 collective-permute-done.12.refs_3_
  35.7 0.4 collective-permute-done.13.refs_4_
  36.1 0.2 collective-permute-done.14.refs_5_
  36.2 4.1 %shard_map.158.refs_0_ = bf16[128,896]{1,0:T(8,128)(2,1)S(1)} custom-call(s32[5]{0:T(128)S(1)} %stack.23.info, bf16[128,768]{1,0:T(8,128)(2,1)S(1)} %get-tuple-element.66.queries, bf16[768,768]{1,0:T(8,128)(2,1)S(1)} %get-tuple-element.67.key_weight, bf16[768,768]{1,0:T(8,128)(2,1)S(1)} %get-tuple-element.68.value_weight, ...), custom_call_target="tpu_custom_call" | custom-call | flops 2000000000 | bytes 1000 | tf_op jit(solution)/shard_map/pallas_call | solution.py:742
  40.3 0.0 copy-start
  40.3 0.0 copy-start.3
  40.3 0.0 copy-start.7
  40.3 0.3 collective-permute-start.15
  40.7 6.6 %collective-permute-done.15.refs_1_ = bf16[128,896]{1,0:T(8,128)(2,1)S(1)} collective-permute-done((bf16[128,896]{1,0:T(8,128)(2,1)S(1)}, bf16[128,896]{1,0:T(8,128)(2,1)S(1)}, u32[]{:S(2)}, u32[]{:S(2)}) %collective-permute-start.15) | collective-permute-done | bytes 229408 | tf_op jit(solution)/shard_map/ppermute | solution.py:626
  47.3 0.9 %shard_map.159.own_back = bf16[128,128]{1,0:T(8,128)(2,1)S(1)} custom-call(bf16[128,768]{1,0:T(8,128)(2,1)S(1)} %get-tuple-element.64.act, f32[128,768]{1,0:T(8,128)S(1)} %get-tuple-element.65.gates, bf16[768,768]{1,0:T(8,128)(2,1)S(1)} %copy-done.1, bf16[768,128]{1,0:T(8,128)(2,1)S(1)} %copy-done.2, bf16[128,896]{1,0:T(8,128)(2,1)S(1)} %shard_map.158.refs_0_, ...), custom_call_target="tpu_custom_call" | custom-call | flops 200000000 | bytes 1000 | tf_op jit(solution)/shard_map/pallas_call | solution.py:751
  48.2 1.2 %collective-permute-start.16 = (bf16[128,128]{1,0:T(8,128)(2,1)S(1)}, bf16[128,128]{1,0:T(8,128)(2,1)S(1)}, u32[]{:S(2)}, u32[]{:S(2)}) collective-permute-start(bf16[128,128]{1,0:T(8,128)(2,1)S(1)} %shard_map.159.own_back), channel_id=1, source_target_pairs={{0,1},{1,0},{2,3},{3,2},{4,5},{5,4},{6,7},{7,6},{8,9},{9,8},{10,11... | collective-permute-start | bytes 98312 | tf_op jit(solution)/shard_map/ppermute | solution.py:597
  49.4 1.1 %collective-permute-start.17 = (bf16[64,128]{1,0:T(8,128)(2,1)S(1)}, bf16[64,128]{1,0:T(8,128)(2,1)S(1)}, u32[]{:S(2)}, u32[]{:S(2)}) collective-permute-start(bf16[64,128]{1,0:T(8,128)(2,1)S(1)} %slice_select_fusion), channel_id=1, source_target_pairs={{0,16},{1,4},{2,18},{3,6},{4,1},{5,8},{6,3},{7,10},{8,5},{9,12},{1... | collective-permute-start | bytes 49160 | tf_op jit(solution)/shard_map/ppermute | solution.py:608
  50.6 0.0 copy-start.4
  50.6 5.2 %shard_map.160 = (bf16[2048,128]{1,0:T(8,128)(2,1)S(1)}, bf16[2048,128]{1,0:T(8,128)(2,1)S(1)}, bf16[128,128]{1,0:T(8,128)(2,1)S(1)}, f32[256,128]{1,0:T(8,128)S(1)}, f32[256,128]{1,0:T(8,128)S(1)}) custom-call(s32[5]{0:T(128)S(1)} %stack.23.info, s32[64]{0:T(128)S(1)} %copy-done.6, s32[1,2048]{1,0:T(1,128)S(1)} %bitcast.11, ...), custom_call_target="tpu_custom_call" | custom-call | flops 1500000000 | bytes 1000 | tf_op jit(solution)/shard_map/pallas_call | solution.py:770
  55.8 2.5 %shard_map.161 = bf16[2048,128]{1,0:T(8,128)(2,1)} custom-call(s32[5]{0:T(128)S(1)} %stack.23.info, s32[64]{0:T(128)S(1)} %copy-done.6, bf16[2048,128]{1,0:T(8,128)(2,1)S(1)} %get-tuple-element.78.atoms2, bf16[80,128]{1,0:T(8,128)(2,1)S(1)} %collective-permute-done.5.near, bf16[80,128]{1,0:T(8,128)(2,1)S(1)} %collective-permute-done.6.far, ...), custom_call_target="tpu_custom_call" | custom-call | flops 300000000 | bytes 1000 | tf_op jit(solution)/shard_map/pallas_call | solution.py:778
  (32 shorter events, 0.1 us)
Async XLA Ops:
  0.7 8.9 %collective-permute-start = (bf16[64,128]{1,0:T(8,128)(2,1)S(1)}, bf16[64,128]{1,0:T(8,128)(2,1)S(1)}, u32[]{:S(2)}, u32[]{:S(2)}) collective-permute-start(bf16[64,128]{1,0:T(8,128)(2,1)S(1)} %get-tuple-element.86), channel_id=1, source_target_pairs={{0,1},{1,0},{2,3},{3,2},{4,5},{5,4},{6,7},{7,6},{8,9},{9,8},{10,11... | collective-permute-start | bytes 49160 | tf_op jit(solution)/shard_map/ppermute | solution.py:597
  0.8 8.9 %collective-permute-start.1 = (bf16[64,128]{1,0:T(8,128)(2,1)S(1)}, bf16[64,128]{1,0:T(8,128)(2,1)S(1)}, u32[]{:S(2)}, u32[]{:S(2)}) collective-permute-start(bf16[64,128]{1,0:T(8,128)(2,1)S(1)} %get-tuple-element.85), channel_id=1, source_target_pairs={{0,16},{1,2},{2,1},{3,4},{4,3},{5,6},{6,5},{7,8},{8,7},{9,10},{10,... | collective-permute-start | bytes 49160 | tf_op jit(solution)/shard_map/ppermute | solution.py:608
  3.4 6.3 %copy-start.5 = (bf16[2048,128]{1,0:T(8,128)(2,1)S(1)}, bf16[2048,128]{1,0:T(8,128)(2,1)}, u32[]{:S(2)}) copy-start(bf16[2048,128]{1,0:T(8,128)(2,1)} %acts.1) | copy-start | bytes 1572868
  3.4 6.3 %copy-start.6 = (s32[64]{0:T(128)S(1)}, s32[64]{0:T(128)}, u32[]{:S(2)}) copy-start(s32[64]{0:T(128)} %offsets.5) | copy-start | bytes 772
  3.4 6.3 %copy-start.8 = (bf16[128,768]{1,0:T(8,128)(2,1)S(1)}, bf16[128,768]{1,0:T(8,128)(2,1)}, u32[]{:S(2)}) copy-start(bf16[128,768]{1,0:T(8,128)(2,1)} %up.1) | copy-start | bytes 589828
  3.4 6.3 %copy-start.9 = (bf16[128,384]{1,0:T(8,128)(2,1)S(1)}, bf16[128,384]{1,0:T(8,128)(2,1)}, u32[]{:S(2)}) copy-start(bf16[128,384]{1,0:T(8,128)(2,1)} %qkv.3) | copy-start | bytes 294916
  3.4 6.3 %copy-start.10 = (bf16[128,128]{1,0:T(8,128)(2,1)S(1)}, bf16[128,128]{1,0:T(8,128)(2,1)}, u32[]{:S(2)}) copy-start(bf16[128,128]{1,0:T(8,128)(2,1)} %out_weight.2) | copy-start | bytes 98308
  3.5 6.3 %copy-start.11 = (s32[2048]{0:T(1024)S(1)}, s32[2048]{0:T(1024)}, u32[]{:S(2)}) copy-start(s32[2048]{0:T(1024)} %param.25) | copy-start | bytes 24580
  3.5 6.3 %copy-start.12 = (f32[128]{0:T(128)S(1)}, f32[128]{0:T(128)}, u32[]{:S(2)}) copy-start(f32[128]{0:T(128)} %param.17) | copy-start | bytes 1540
  9.8 5.1 %copy-start.13 = (bf16[16,256,256]{2,1,0:T(8,128)(2,1)S(1)}, bf16[16,256,256]{2,1,0:T(8,128)(2,1)}, u32[]{:S(2)}) copy-start(bf16[16,256,256]{2,1,0:T(8,128)(2,1)} %own_far.1) | copy-start | bytes 6291460
  9.8 7.5 %copy-start.14 = (f32[768]{0:T(1024)S(1)}, f32[768]{0:T(1024)}, u32[]{:S(2)}) copy-start(f32[768]{0:T(1024)} %param.27) | copy-start | bytes 9220
  13.2 1.6 %collective-permute-start.2 = (bf16[128,896]{1,0:T(8,128)(2,1)S(1)}, bf16[128,896]{1,0:T(8,128)(2,1)S(1)}, u32[]{:S(2)}, u32[]{:S(2)}) collective-permute-start(bf16[128,896]{1,0:T(8,128)(2,1)S(1)} %get-tuple-element.52), channel_id=1, source_target_pairs={{0,1},{1,0},{2,3},{3,2},{4,5},{5,4},{6,7},{7,6},{8,9},{9,8},{10,11... | collective-permute-start | bytes 688136 | tf_op jit(solution)/shard_map/ppermute | solution.py:597
  14.9 5.7 %collective-permute-start.4 = (bf16[16,256,256]{2,1,0:T(8,128)(2,1)S(1)}, bf16[16,256,256]{2,1,0:T(8,128)(2,1)}, u32[]{:S(2)}, u32[]{:S(2)}) collective-permute-start(bf16[16,256,256]{2,1,0:T(8,128)(2,1)S(1)} %copy-done.13), channel_id=1, source_target_pairs={{0,1},{1,0},{2,3},{3,2},{4,5},{5,4},{6,7},{7,6},{8,9},{9,8},{10,11... | collective-permute-start | bytes 6291464 | tf_op jit(solution)/shard_map/ppermute | solution.py:597
  15.3 5.2 %collective-permute-start.3 = (bf16[64,896]{1,0:T(8,128)(2,1)S(1)}, bf16[64,896]{1,0:T(8,128)(2,1)S(1)}, u32[]{:S(2)}, u32[]{:S(2)}) collective-permute-start(bf16[64,896]{1,0:T(8,128)(2,1)S(1)} %get-tuple-element.87), channel_id=1, source_target_pairs={{0,2},{1,3},{2,0},{3,1},{4,6},{5,7},{6,4},{7,5},{8,10},{9,11},{10,... | collective-permute-start | bytes 344072 | tf_op jit(solution)/shard_map/ppermute | solution.py:626
  16.4 2.7 %collective-permute-start.5 = (bf16[80,128]{1,0:T(8,128)(2,1)S(1)}, bf16[80,128]{1,0:T(8,128)(2,1)S(1)}, u32[]{:S(2)}, u32[]{:S(2)}) collective-permute-start(bf16[80,128]{1,0:T(8,128)(2,1)S(1)} %get-tuple-element.57), channel_id=1, source_target_pairs={{0,1},{1,0},{2,3},{3,2},{4,5},{5,4},{6,7},{7,6},{8,9},{9,8},{10,11... | collective-permute-start | bytes 61448 | tf_op jit(solution)/shard_map/ppermute | solution.py:597
  17.0 3.5 %collective-permute-start.6 = (bf16[80,128]{1,0:T(8,128)(2,1)S(1)}, bf16[80,128]{1,0:T(8,128)(2,1)S(1)}, u32[]{:S(2)}, u32[]{:S(2)}) collective-permute-start(bf16[80,128]{1,0:T(8,128)(2,1)S(1)} %get-tuple-element.58), channel_id=1, source_target_pairs={{0,16},{1,2},{2,1},{3,4},{4,3},{5,6},{6,5},{7,8},{8,7},{9,10},{10,... | collective-permute-start | bytes 61448 | tf_op jit(solution)/shard_map/ppermute | solution.py:608
  20.9 5.6 %collective-permute-start.7 = (bf16[64,768]{1,0:T(8,128)(2,1)S(1)}, bf16[64,768]{1,0:T(8,128)(2,1)S(1)}, u32[]{:S(2)}, u32[]{:S(2)}) collective-permute-start(bf16[64,768]{1,0:T(8,128)(2,1)S(1)} %get-tuple-element.61.own_act), channel_id=1, source_target_pairs={{0,2},{1,3},{2,0},{3,1},{4,6},{5,7},{6,4},{7,5},{8,10},{9,11},{10,... | collective-permute-start | bytes 294920 | tf_op jit(solution)/shard_map/ppermute | solution.py:626
  21.9 4.6 %collective-permute-start.8 = (bf16[64,768]{1,0:T(8,128)(2,1)S(1)}, bf16[64,768]{1,0:T(8,128)(2,1)S(1)}, u32[]{:S(2)}, u32[]{:S(2)}) collective-permute-start(bf16[64,768]{1,0:T(8,128)(2,1)S(1)} %get-tuple-element.63.refs_1_), channel_id=1, source_target_pairs={{0,1},{1,0},{2,3},{3,2},{4,5},{5,4},{6,7},{7,6},{8,9},{9,8},{10,11... | collective-permute-start | bytes 294920 | tf_op jit(solution)/shard_map/ppermute | solution.py:597
  23.1 9.5 %collective-permute-start.9 = (bf16[64,768]{1,0:T(8,128)(2,1)S(1)}, bf16[64,768]{1,0:T(8,128)(2,1)S(1)}, u32[]{:S(2)}, u32[]{:S(2)}) collective-permute-start(bf16[64,768]{1,0:T(8,128)(2,1)S(1)} %get-tuple-element.63.refs_1_), channel_id=1, source_target_pairs={{0,8},{4,12},{8,0},{12,4},{1,9},{5,13},{9,1},{13,5},{2,10},{6,14},... | collective-permute-start | bytes 294920 | tf_op jit(solution)/shard_map/ppermute | solution.py:631
  25.4 7.3 %collective-permute-start.10 = (bf16[64,768]{1,0:T(8,128)(2,1)S(1)}, bf16[64,768]{1,0:T(8,128)(2,1)S(1)}, u32[]{:S(2)}, u32[]{:S(2)}) collective-permute-start(bf16[64,768]{1,0:T(8,128)(2,1)S(1)} %get-tuple-element.63.refs_1_), channel_id=1, source_target_pairs={{0,12},{4,8},{8,4},{12,0},{1,13},{5,9},{9,5},{13,1},{2,14},{6,10},... | collective-permute-start | bytes 294920 | tf_op jit(solution)/shard_map/ppermute | solution.py:631
  26.4 7.1 %collective-permute-start.11 = (bf16[64,768]{1,0:T(8,128)(2,1)S(1)}, bf16[64,768]{1,0:T(8,128)(2,1)S(1)}, u32[]{:S(2)}, u32[]{:S(2)}) collective-permute-start(bf16[64,768]{1,0:T(8,128)(2,1)S(1)} %get-tuple-element.63.refs_1_), channel_id=1, source_target_pairs={{0,4},{4,0},{8,12},{12,8},{1,5},{5,1},{9,13},{13,9},{2,6},{6,2},{1... | collective-permute-start | bytes 294920 | tf_op jit(solution)/shard_map/ppermute | solution.py:631
  33.5 2.2 %collective-permute-start.12 = (bf16[64,768]{1,0:T(8,128)(2,1)S(1)}, bf16[64,768]{1,0:T(8,128)(2,1)S(1)}, u32[]{:S(2)}, u32[]{:S(2)}) collective-permute-start(bf16[64,768]{1,0:T(8,128)(2,1)S(1)} %collective-permute-done.9.refs_0_), channel_id=1, source_target_pairs={{0,1},{1,0},{2,3},{3,2},{4,5},{5,4},{6,7},{7,6},{8,9},{9,8},{10,11... | collective-permute-start | bytes 294920 | tf_op jit(solution)/shard_map/ppermute | solution.py:597
  34.8 1.3 %collective-permute-start.13 = (bf16[64,768]{1,0:T(8,128)(2,1)S(1)}, bf16[64,768]{1,0:T(8,128)(2,1)S(1)}, u32[]{:S(2)}, u32[]{:S(2)}) collective-permute-start(bf16[64,768]{1,0:T(8,128)(2,1)S(1)} %collective-permute-done.10.refs_1_), channel_id=1, source_target_pairs={{0,1},{1,0},{2,3},{3,2},{4,5},{5,4},{6,7},{7,6},{8,9},{9,8},{10,11... | collective-permute-start | bytes 294920 | tf_op jit(solution)/shard_map/ppermute | solution.py:597
  34.8 1.5 %collective-permute-start.14 = (bf16[64,768]{1,0:T(8,128)(2,1)S(1)}, bf16[64,768]{1,0:T(8,128)(2,1)S(1)}, u32[]{:S(2)}, u32[]{:S(2)}) collective-permute-start(bf16[64,768]{1,0:T(8,128)(2,1)S(1)} %collective-permute-done.11.refs_2_), channel_id=1, source_target_pairs={{0,1},{1,0},{2,3},{3,2},{4,5},{5,4},{6,7},{7,6},{8,9},{9,8},{10,11... | collective-permute-start | bytes 294920 | tf_op jit(solution)/shard_map/ppermute | solution.py:597
  36.2 11.0 %copy-start.1 = (bf16[768,768]{1,0:T(8,128)(2,1)S(1)}, bf16[768,768]{1,0:T(8,128)(2,1)}, u32[]{:S(2)}) copy-start(bf16[768,768]{1,0:T(8,128)(2,1)} %token_out.1) | copy-start | bytes 3538948
  36.2 11.0 %copy-start.2 = (bf16[768,128]{1,0:T(8,128)(2,1)S(1)}, bf16[768,128]{1,0:T(8,128)(2,1)}, u32[]{:S(2)}) copy-start(bf16[768,128]{1,0:T(8,128)(2,1)} %down.1) | copy-start | bytes 589828
  40.3 10.2 %copy-start = (bf16[4,2048,128]{2,1,0:T(8,128)(2,1)S(1)}, bf16[4,2048,128]{2,1,0:T(8,128)(2,1)}, u32[]{:S(2)}) copy-start(bf16[4,2048,128]{2,1,0:T(8,128)(2,1)} %bias.3) | copy-start | bytes 6291460
  40.3 10.2 %copy-start.3 = (bf16[128,384]{1,0:T(8,128)(2,1)S(1)}, bf16[128,384]{1,0:T(8,128)(2,1)}, u32[]{:S(2)}) copy-start(bf16[128,384]{1,0:T(8,128)(2,1)} %qkv.5) | copy-start | bytes 294916
  40.3 10.2 %copy-start.7 = (f32[128]{0:T(128)S(1)}, f32[128]{0:T(128)}, u32[]{:S(2)}) copy-start(f32[128]{0:T(128)} %param.20) | copy-start | bytes 1540
  40.3 6.9 %collective-permute-start.15 = (bf16[128,896]{1,0:T(8,128)(2,1)S(1)}, bf16[128,896]{1,0:T(8,128)(2,1)S(1)}, u32[]{:S(2)}, u32[]{:S(2)}) collective-permute-start(bf16[128,896]{1,0:T(8,128)(2,1)S(1)} %shard_map.158.refs_0_), channel_id=1, source_target_pairs={{0,2},{1,3},{2,0},{3,1},{4,6},{5,7},{6,4},{7,5},{8,10},{9,11},{10,... | collective-permute-start | bytes 688136 | tf_op jit(solution)/shard_map/ppermute | solution.py:626
  48.2 2.4 %collective-permute-start.16 = (bf16[128,128]{1,0:T(8,128)(2,1)S(1)}, bf16[128,128]{1,0:T(8,128)(2,1)S(1)}, u32[]{:S(2)}, u32[]{:S(2)}) collective-permute-start(bf16[128,128]{1,0:T(8,128)(2,1)S(1)} %shard_map.159.own_back), channel_id=1, source_target_pairs={{0,1},{1,0},{2,3},{3,2},{4,5},{5,4},{6,7},{7,6},{8,9},{9,8},{10,11... | collective-permute-start | bytes 98312 | tf_op jit(solution)/shard_map/ppermute | solution.py:597
  49.4 6.3 %collective-permute-start.17 = (bf16[64,128]{1,0:T(8,128)(2,1)S(1)}, bf16[64,128]{1,0:T(8,128)(2,1)S(1)}, u32[]{:S(2)}, u32[]{:S(2)}) collective-permute-start(bf16[64,128]{1,0:T(8,128)(2,1)S(1)} %slice_select_fusion), channel_id=1, source_target_pairs={{0,16},{1,4},{2,18},{3,6},{4,1},{5,8},{6,3},{7,10},{8,5},{9,12},{1... | collective-permute-start | bytes 49160 | tf_op jit(solution)/shard_map/ppermute | solution.py:608
  50.6 5.2 %copy-start.4 = (bf16[128,128]{1,0:T(8,128)(2,1)S(1)}, bf16[128,128]{1,0:T(8,128)(2,1)}, u32[]{:S(2)}) copy-start(bf16[128,128]{1,0:T(8,128)(2,1)} %out_weight.3) | copy-start | bytes 98308

commit v8 on v7

--- a/solution.py
+++ b/solution.py
@@ -441,16 +441,23 @@
 
 
 def attend_rest(
-    info, queries, key_weight, value_weight, pair_bias, bias, former, former_top, former_total, *refs, steps, solo
+    info, queries, key_weight, value_weight, pair_bias, rest_bias, former, former_top, former_total, *refs,
+    steps, solo, part, parts
 ):
-    rows_count = len(steps)
-    own, near = refs[:rows_count], refs[rows_count : 2 * rows_count]
-    packed, tokens, keys, values = refs[2 * rows_count :]
-    heads = bias.shape[0]
-    count, wide = queries.shape
-    place_keys(info, own, near, tokens, steps, solo)
-    keys[...] = dot(tokens[...], key_weight[...]).astype(BF)
-    values[...] = dot(tokens[...], value_weight[...]).astype(BF)
+    if part == 0:
+        rows_count = len(steps)
+        own, near = refs[:rows_count], refs[rows_count : 2 * rows_count]
+        packed, tokens, keys, values = refs[2 * rows_count :]
+        place_keys(info, own, near, tokens, steps, solo)
+    else:
+        tokens, packed, keys, values = refs
+    heads = rest_bias.shape[0] // parts
+    count = queries.shape[0]
+    wide = keys.shape[1]
+    some_heads = pl.ds(part * heads, heads)
+    some = pl.ds(part * wide, wide)
+    keys[...] = dot(tokens[...], key_weight[:, some]).astype(BF)
+    values[...] = dot(tokens[...], value_weight[:, some]).astype(BF)
     lane = lax.broadcasted_iota(jnp.int32, (count, LANES), 1)
     ends = [jnp.zeros((count, LANES), F32), jnp.ones((count, LANES), F32)]
 
@@ -458,8 +465,9 @@
         ends[0] = jnp.where(lane == head, top, ends[0])
         ends[1] = jnp.where(lane == head, total, ends[1])
 
-    biases = [pair_bias, bias] if solo else [bias]
-    out = attend_heads(queries, biases, keys, values, (former, former_top, former_total), keep)
+    biases = [ref.at[some_heads] for ref in ((pair_bias, rest_bias) if solo else (rest_bias,))]
+    previous = (former.at[:, some], former_top.at[some_heads], former_total.at[some_heads])
+    out = attend_heads(queries.at[:, some], biases, keys, values, previous, keep)
     for block, piece in enumerate(out):
         packed[:, block * LANES : (block + 1) * LANES] = piece.astype(BF)
     logs = ends[0] + jnp.log(ends[1])
@@ -470,31 +478,34 @@
     packed[:, wide:] = (first + pltpu.roll(second, heads, 1) + pltpu.roll(rest, 2 * heads, 1)).astype(BF)
 
 
-def finish_tokens(act, gates, token_out, down, *refs, parts_count, heads):
-    parts, back = refs[:parts_count], refs[parts_count]
-    count, wide = act.shape
-    size = wide // heads
+def finish_part(so_far, gates, token_out, *refs, heads, size, part):
+    parts, refs = refs[:-2], refs[-2:]
+    count = so_far.shape[0]
+    some = heads * size
+    head = lax.broadcasted_iota(jnp.int32, (LANES, some), 0)
+    feature = lax.broadcasted_iota(jnp.int32, (LANES, some), 1)
+    expand = jnp.where((feature >= head * size) & (feature < (head + 1) * size), 1.0, 0.0).astype(BF)
     logs = []
-    for part in parts:
-        packed = part[:, wide:].astype(F32)
-        logs.append(
-            packed + pltpu.roll(packed, LANES - heads, 1) + pltpu.roll(packed, LANES - 2 * heads, 1)
-        )
+    for piece in parts:
+        packed = piece[:, some:].astype(F32)
+        logs.append(packed + pltpu.roll(packed, LANES - heads, 1) + pltpu.roll(packed, LANES - 2 * heads, 1))
     top = functools.reduce(jnp.maximum, logs)
     weights = [jnp.exp(log - top) for log in logs]
     total = functools.reduce(jnp.add, weights)
-    head = lax.broadcasted_iota(jnp.int32, (LANES, wide), 0)
-    feature = lax.broadcasted_iota(jnp.int32, (LANES, wide), 1)
-    expand = jnp.where((feature >= head * size) & (feature < (head + 1) * size), 1.0, 0.0).astype(BF)
-    mixed = jnp.zeros((count, wide), F32)
-    for part, weight in zip(parts, weights):
+    mixed = jnp.zeros((count, some), F32)
+    for piece, weight in zip(parts, weights):
         factor = weight / total
         coarse = factor.astype(BF)
         fine = (factor - coarse.astype(F32)).astype(BF)
-        mixed = mixed + (dot(coarse, expand) + dot(fine, expand)) * part[:, :wide].astype(F32)
-    gated = (mixed * gates[...]).astype(BF)
-    result = (act[...].astype(F32) + dot(gated, token_out[...])).astype(BF)
-    back[...] = dot(result, down[...]).astype(BF)
+        mixed = mixed + (dot(coarse, expand) + dot(fine, expand)) * piece[:, :some].astype(F32)
+    place = slice(part * some, (part + 1) * some)
+    gated = (mixed * gates[:, place]).astype(BF)
+    result = so_far[...].astype(F32) + dot(gated, token_out[place, :])
+    down, out = refs
+    if part == 0:
+        out[...] = result
+    else:
+        out[...] = dot(result.astype(BF), down[...]).astype(BF)
 
 
 def second_inner(
@@ -739,22 +750,39 @@
     rest_steps = sorted(range(split, row_count), key=lambda step: (step < group, step))
     rest_keys, mixed = lax.optimization_barrier(([own_keys[step] for step in rest_steps], mixed))
     rest_near = [to_near(x) for x in rest_keys]
-    part = call(
-        functools.partial(attend_rest, steps=rest_steps, solo=solo),
-        packed_shape,
-        key_scratch(rest),
+    halves = 2
+    some = wide // halves
+    key_rows = jax.ShapeDtypeStruct((2 * rest * share, wide), BF)
+    rest_scratch = [pltpu.VMEM((2 * rest * share, some), BF)] * 2
+    part_shape = jax.ShapeDtypeStruct((half, some + LANES), BF)
+    rest_args = [info, queries, *held, mixed, tops, totals]
+    early_part, key_rows = call(
+        functools.partial(attend_rest, steps=rest_steps, solo=solo, part=0, parts=halves),
+        [part_shape, key_rows],
+        rest_scratch,
         [SMEM] + [VMEM] * (8 + 2 * rest),
         2_000_000_000,
-    )(info, queries, *held, mixed, tops, totals, *rest_keys, *rest_near)
-
-    parts = [part] + [along_pairs(part, step) for step in range(1, pairs)]
-    own_back = call(
-        functools.partial(finish_tokens, parts_count=pairs, heads=heads),
-        jax.ShapeDtypeStruct((half, channels), BF),
-        [],
-        [VMEM] * (4 + pairs),
-        200_000_000,
-    )(act_rows, gates, token_out, down_weight, *parts)
+    )(*rest_args, *rest_keys, *rest_near)
+    late_part = call(
+        functools.partial(attend_rest, steps=rest_steps, solo=solo, part=1, parts=halves),
+        part_shape,
+        rest_scratch,
+        [SMEM] + [VMEM] * 9,
+        2_000_000_000,
+    )(*rest_args, key_rows)
+    early_parts = [along_pairs(early_part, step) for step in range(1, pairs)]
+    late_parts = [along_pairs(late_part, step) for step in range(1, pairs)]
+    def finish(so_far, part, pieces, out):
+        return call(
+            functools.partial(finish_part, heads=heads // halves, size=wide // heads, part=part),
+            out,
+            [],
+            [VMEM] * (4 + pairs),
+            200_000_000,
+        )(so_far, gates, token_out, *pieces, down_weight)
+
+    result = finish(act_rows, 0, [early_part] + early_parts, wide_shape)
+    own_back = finish(result, 1, [late_part] + late_parts, jax.ShapeDtypeStruct((half, channels), BF))
 
     near_back = to_near(own_back)
     if share >= RIM:

time: 59 us -> 57.9 us (0.981)
  waiting for transfers between devices: 14 us -> 10.1 us
  starting transfers between devices: 15.5 us -> 17.2 us
  Pallas kernels: 27.5 us -> 28.7 us
    ppermute x3 -> x4, waiting for transfers between devices: 6.56 us -> 2.68 us  [along_pairs(): lax.ppermute(x, 'col', [(2 * i + k, 2 * ((i + step) % pairs) + k) for i i...]
    pallas_call x2 -> x4, Pallas kernels: 5 us -> 6.26 us  [the longest x1 2.48 us: body(): call(functools.partial(attend_rest, steps=rest_steps, solo=solo, part=0,...]
    ppermute x3 -> x4, starting transfers between devices: 2.4 us -> 3.6 us  [along_pairs(): lax.ppermute(x, 'col', [(2 * i + k, 2 * ((i + step) % pairs) + k) for i i...]
  transfers between devices with their start and end apart: 18 -> 19, of which waited for: 9 -> 10; matrix products, arithmetic and copies ran while one was open for 0% -> 0% of each run, Pallas kernels for 28% -> 34%
where the time goes in v8:
time: 57.9 us; the launch traced here: 57.3 us
  Pallas kernels  28.7 us (50%)
  starting transfers between devices  17.2 us (30%)
  waiting for transfers between devices  10.1 us (17%)
  local copies, waits for them, and re-layouts  0.92 us (2%)
    pallas_call x1, Pallas kernels, body(): call(functools.partial(first_inner, pieces=pieces), [atom_shape] + edge_s...  6.17 us
    ppermute x9, starting transfers between devices, to_near(): return lax.ppermute(x, 'col', [(i, i ^ 1) for i in range(col_count)])  6.08 us
    pallas_call x1, Pallas kernels, body(): call(functools.partial(second_inner, share=share), [atom_shape, atom_shap...  5.15 us
    pallas_call x1, Pallas kernels, body(): call(functools.partial(attend_first, others=len(other_acts), steps=list(r...  4.87 us
    ppermute x3, starting transfers between devices, swapped(): return lax.ppermute(x, ('group', 'row', 'col'), pairs_list)  4.05 us
    ppermute x9, waiting for transfers between devices, to_near(): return lax.ppermute(x, 'col', [(i, i ^ 1) for i in range(col_count)])  3.93 us
    ppermute x4, starting transfers between devices, along_pairs(): lax.ppermute(x, 'col', [(2 * i + k, 2 * ((i + step) % pairs) + k) for i i...  3.6 us
    ppermute x3, starting transfers between devices, along_rows(): return lax.ppermute(x, 'row', [(i, i ^ step) for i in range(row_count)])  3.49 us
  transfers between devices with their start and end apart: 19, of which 10 were waited for; matrix products, arithmetic and copies ran while one was open for 0% of the time, Pallas kernels for 34%

profile of v8, /device:TPU:1, one launch (start us, length us, event | category | flops | bytes accessed | tf_op | source)
XLA Modules:
  0.0 57.3 jit_solution(3202296847910991531)
XLA Ops:
  0.0 0.7 %constant_dynamic-slice_fusion.2 = (bf16[64,128]{1,0:T(8,128)(2,1)S(1)}, bf16[64,128]{1,0:T(8,128)(2,1)S(1)}) fusion(bf16[2048,128]{1,0:T(8,128)(2,1)} %acts.1, s32[]{:T(128)S(6)} %select_n.41, s32[]{:T(128)S(6)} %select_n.40), kind=kLoop, calls=%fused_computation.4 | loop fusion | bytes 65544 | tf_op jit(solution)/shard_map/dynamic_slice | solution.py:645
  0.7 0.1 collective-permute-start
  0.8 2.5 %collective-permute-start.1 = (bf16[64,128]{1,0:T(8,128)(2,1)S(1)}, bf16[64,128]{1,0:T(8,128)(2,1)S(1)}, u32[]{:S(2)}, u32[]{:S(2)}) collective-permute-start(bf16[64,128]{1,0:T(8,128)(2,1)S(1)} %get-tuple-element.89), channel_id=1, source_target_pairs={{0,16},{1,2},{2,1},{3,4},{4,3},{5,6},{6,5},{7,8},{8,7},{9,10},{10,... | collective-permute-start | bytes 49160 | tf_op jit(solution)/shard_map/ppermute | solution.py:619
  3.3 0.1 stack.23.info
  3.4 0.0 copy-start.10
  3.5 0.0 copy-start.11
  3.5 0.0 copy-start.12
  3.5 6.2 %shard_map.154 = (bf16[2048,128]{1,0:T(8,128)(2,1)S(1)}, bf16[128,128]{1,0:T(8,128)(2,1)S(1)}, f32[256,128]{1,0:T(8,128)S(1)}, f32[256,128]{1,0:T(8,128)S(1)}, bf16[4,128,128]{2,1,0:T(8,128)(2,1)S(1)}) custom-call(s32[5]{0:T(128)S(1)} %stack.23.info, bf16[2048,128]{1,0:T(8,128)(2,1)} %acts.1, f32[1,128]{1,0:T(1,128)} %bitcast.12, bf16[128,384]{1,0:T(8,128)(2,1)} %qkv.3, ...), custom_call_target="tpu_custom_call" | custom-call | flops 1500000000 | bytes 1000 | tf_op jit(solution)/shard_map/pallas_call | solution.py:674
  9.8 0.0 copy-start.13
  9.8 0.0 copy-start.14
  9.8 3.4 %shard_map.155 = (bf16[2048,128]{1,0:T(8,128)(2,1)S(1)}, bf16[128,896]{1,0:T(8,128)(2,1)S(1)}, bf16[128,896]{1,0:T(8,128)(2,1)S(1)}, bf16[80,128]{1,0:T(8,128)(2,1)S(1)}, bf16[80,128]{1,0:T(8,128)(2,1)S(1)}) custom-call(s32[5]{0:T(128)S(1)} %stack.23.info, s32[64]{0:T(128)S(1)} %copy-done.6, s32[1,2048]{1,0:T(1,128)S(1)} %bitcast.10, ...), custom_call_target="tpu_custom_call" | custom-call | flops 2000000000 | bytes 1000 | tf_op jit(solution)/shard_map/pallas_call | solution.py:686
  13.2 0.5 collective-permute-start.2
  13.7 1.1 %collective-permute-done.2 = bf16[128,896]{1,0:T(8,128)(2,1)S(1)} collective-permute-done((bf16[128,896]{1,0:T(8,128)(2,1)S(1)}, bf16[128,896]{1,0:T(8,128)(2,1)S(1)}, u32[]{:S(2)}, u32[]{:S(2)}) %collective-permute-start.2) | collective-permute-done | bytes 229408 | tf_op jit(solution)/shard_map/ppermute | solution.py:608
  14.8 0.1 add_convert_fusion
  14.9 0.4 collective-permute-start.4
  15.3 1.0 %collective-permute-start.3 = (bf16[64,896]{1,0:T(8,128)(2,1)S(1)}, bf16[64,896]{1,0:T(8,128)(2,1)S(1)}, u32[]{:S(2)}, u32[]{:S(2)}) collective-permute-start(bf16[64,896]{1,0:T(8,128)(2,1)S(1)} %get-tuple-element.91), channel_id=1, source_target_pairs={{0,2},{1,3},{2,0},{3,1},{4,6},{5,7},{6,4},{7,5},{8,10},{9,11},{10,... | collective-permute-start | bytes 344072 | tf_op jit(solution)/shard_map/ppermute | solution.py:637
  16.3 0.7 %collective-permute-start.5 = (bf16[80,128]{1,0:T(8,128)(2,1)S(1)}, bf16[80,128]{1,0:T(8,128)(2,1)S(1)}, u32[]{:S(2)}, u32[]{:S(2)}) collective-permute-start(bf16[80,128]{1,0:T(8,128)(2,1)S(1)} %get-tuple-element.59), channel_id=1, source_target_pairs={{0,1},{1,0},{2,3},{3,2},{4,5},{5,4},{6,7},{7,6},{8,9},{9,8},{10,11... | collective-permute-start | bytes 61448 | tf_op jit(solution)/shard_map/ppermute | solution.py:608
  17.0 0.3 collective-permute-start.6
  17.3 1.9 %collective-permute-done.5.near = bf16[80,128]{1,0:T(8,128)(2,1)S(1)} collective-permute-done((bf16[80,128]{1,0:T(8,128)(2,1)S(1)}, bf16[80,128]{1,0:T(8,128)(2,1)S(1)}, u32[]{:S(2)}, u32[]{:S(2)}) %collective-permute-start.5) | collective-permute-done | bytes 20512 | tf_op jit(solution)/shard_map/ppermute | solution.py:608
  19.1 1.4 %collective-permute-done.6.far = bf16[80,128]{1,0:T(8,128)(2,1)S(1)} collective-permute-done((bf16[80,128]{1,0:T(8,128)(2,1)S(1)}, bf16[80,128]{1,0:T(8,128)(2,1)S(1)}, u32[]{:S(2)}, u32[]{:S(2)}) %collective-permute-start.6) | collective-permute-done | bytes 20512 | tf_op jit(solution)/shard_map/ppermute | solution.py:619
  20.6 0.3 shard_map.156
  20.9 1.0 %collective-permute-start.7 = (bf16[64,768]{1,0:T(8,128)(2,1)S(1)}, bf16[64,768]{1,0:T(8,128)(2,1)S(1)}, u32[]{:S(2)}, u32[]{:S(2)}) collective-permute-start(bf16[64,768]{1,0:T(8,128)(2,1)S(1)} %get-tuple-element.63.own_act), channel_id=1, source_target_pairs={{0,2},{1,3},{2,0},{3,1},{4,6},{5,7},{6,4},{7,5},{8,10},{9,11},{10,... | collective-permute-start | bytes 294920 | tf_op jit(solution)/shard_map/ppermute | solution.py:637
  21.9 1.1 %collective-permute-start.8 = (bf16[64,768]{1,0:T(8,128)(2,1)S(1)}, bf16[64,768]{1,0:T(8,128)(2,1)S(1)}, u32[]{:S(2)}, u32[]{:S(2)}) collective-permute-start(bf16[64,768]{1,0:T(8,128)(2,1)S(1)} %get-tuple-element.65.refs_1_), channel_id=1, source_target_pairs={{0,1},{1,0},{2,3},{3,2},{4,5},{5,4},{6,7},{7,6},{8,9},{9,8},{10,11... | collective-permute-start | bytes 294920 | tf_op jit(solution)/shard_map/ppermute | solution.py:608
  23.0 2.4 %collective-permute-start.9 = (bf16[64,768]{1,0:T(8,128)(2,1)S(1)}, bf16[64,768]{1,0:T(8,128)(2,1)S(1)}, u32[]{:S(2)}, u32[]{:S(2)}) collective-permute-start(bf16[64,768]{1,0:T(8,128)(2,1)S(1)} %get-tuple-element.65.refs_1_), channel_id=1, source_target_pairs={{0,8},{4,12},{8,0},{12,4},{1,9},{5,13},{9,1},{13,5},{2,10},{6,14},... | collective-permute-start | bytes 294920 | tf_op jit(solution)/shard_map/ppermute | solution.py:642
  25.4 1.1 %collective-permute-start.10 = (bf16[64,768]{1,0:T(8,128)(2,1)S(1)}, bf16[64,768]{1,0:T(8,128)(2,1)S(1)}, u32[]{:S(2)}, u32[]{:S(2)}) collective-permute-start(bf16[64,768]{1,0:T(8,128)(2,1)S(1)} %get-tuple-element.65.refs_1_), channel_id=1, source_target_pairs={{0,12},{4,8},{8,4},{12,0},{1,13},{5,9},{9,5},{13,1},{2,14},{6,10},... | collective-permute-start | bytes 294920 | tf_op jit(solution)/shard_map/ppermute | solution.py:642
  26.4 0.1 collective-permute-start.11
  26.5 4.9 %shard_map.157 = (bf16[128,768]{1,0:T(8,128)(2,1)S(1)}, bf16[128,768]{1,0:T(8,128)(2,1)S(1)}, f32[128,768]{1,0:T(8,128)S(1)}, bf16[768,768]{1,0:T(8,128)(2,1)S(1...) custom-call(s32[5]{0:T(128)S(1)} %stack.23.info, ...), custom_call_target="tpu_custom_call" | custom-call | flops 1000 | bytes 1000 | tf_op jit(solution)/shard_map/pallas_call | solution.py:734
  31.4 1.1 %collective-permute-done.9.refs_0_ = bf16[64,768]{1,0:T(8,128)(2,1)S(1)} collective-permute-done((bf16[64,768]{1,0:T(8,128)(2,1)S(1)}, bf16[64,768]{1,0:T(8,128)(2,1)S(1)}, u32[]{:S(2)}, u32[]{:S(2)}) %collective-permute-start.9) | collective-permute-done | bytes 98336 | tf_op jit(solution)/shard_map/ppermute | solution.py:642
  32.5 1.0 %collective-permute-done.11.refs_2_ = bf16[64,768]{1,0:T(8,128)(2,1)S(1)} collective-permute-done((bf16[64,768]{1,0:T(8,128)(2,1)S(1)}, bf16[64,768]{1,0:T(8,128)(2,1)S(1)}, u32[]{:S(2)}, u32[]{:S(2)}) %collective-permute-start.11) | collective-permute-done | bytes 98336 | tf_op jit(solution)/shard_map/ppermute | solution.py:642
  33.5 1.2 %collective-permute-start.12 = (bf16[64,768]{1,0:T(8,128)(2,1)S(1)}, bf16[64,768]{1,0:T(8,128)(2,1)S(1)}, u32[]{:S(2)}, u32[]{:S(2)}) collective-permute-start(bf16[64,768]{1,0:T(8,128)(2,1)S(1)} %collective-permute-done.9.refs_0_), channel_id=1, source_target_pairs={{0,1},{1,0},{2,3},{3,2},{4,5},{5,4},{6,7},{7,6},{8,9},{9,8},{10,11... | collective-permute-start | bytes 294920 | tf_op jit(solution)/shard_map/ppermute | solution.py:608
  34.7 0.5 collective-permute-start.14
  35.2 0.4 collective-permute-done.12.refs_3_
  35.7 0.4 collective-permute-done.13.refs_4_
  36.0 0.2 collective-permute-done.14.refs_5_
  36.2 2.5 %shard_map.158 = (bf16[128,512]{1,0:T(8,128)(2,1)S(1)}, bf16[384,768]{1,0:T(8,128)(2,1)S(1)}) custom-call(s32[5]{0:T(128)S(1)} %stack.23.info, bf16[128,768]{1,0:T(8,128)(2,1)S(1)} %get-tuple-element.68.queries, bf16[768,768]{1,0:T(8,128)(2,1)S(1)} %get-tuple-element.69.key_weight, bf16[768,768]{1,0:T(8,128)(2,1)S(1)} %get-tuple-element.70.value_weight, ...), custom_call_target="tpu_custom_call" | custom-call | flops 2000000000 | bytes 1000 | tf_op jit(solution)/shard_map/pallas_call | solution.py:759
  38.7 0.4 collective-permute-start.15
  39.1 2.5 %shard_map.160.refs_0_ = bf16[128,512]{1,0:T(8,128)(2,1)S(1)} custom-call(s32[5]{0:T(128)S(1)} %stack.23.info, bf16[128,768]{1,0:T(8,128)(2,1)S(1)} %get-tuple-element.68.queries, bf16[768,768]{1,0:T(8,128)(2,1)S(1)} %get-tuple-element.69.key_weight, bf16[768,768]{1,0:T(8,128)(2,1)S(1)} %get-tuple-element.70.value_weight, ...), custom_call_target="tpu_custom_call" | custom-call | flops 2000000000 | bytes 1000 | tf_op jit(solution)/shard_map/pallas_call | solution.py:766
  41.6 1.2 %collective-permute-start.16 = (bf16[128,512]{1,0:T(8,128)(2,1)S(1)}, bf16[128,512]{1,0:T(8,128)(2,1)S(1)}, u32[]{:S(2)}, u32[]{:S(2)}) collective-permute-start(bf16[128,512]{1,0:T(8,128)(2,1)S(1)} %shard_map.160.refs_0_), channel_id=1, source_target_pairs={{0,2},{1,3},{2,0},{3,1},{4,6},{5,7},{6,4},{7,5},{8,10},{9,11},{10,... | collective-permute-start | bytes 393224 | tf_op jit(solution)/shard_map/ppermute | solution.py:637
  42.8 0.7 %collective-permute-done.15.refs_1_ = bf16[128,512]{1,0:T(8,128)(2,1)S(1)} collective-permute-done((bf16[128,512]{1,0:T(8,128)(2,1)S(1)}, bf16[128,512]{1,0:T(8,128)(2,1)S(1)}, u32[]{:S(2)}, u32[]{:S(2)}) %collective-permute-start.15) | collective-permute-done | bytes 131104 | tf_op jit(solution)/shard_map/ppermute | solution.py:637
  43.5 0.0 copy-start.7
  43.5 0.6 %shard_map.159.so_far = f32[128,768]{1,0:T(8,128)S(1)} custom-call(bf16[128,768]{1,0:T(8,128)(2,1)S(1)} %get-tuple-element.66.so_far, f32[128,768]{1,0:T(8,128)S(1)} %get-tuple-element.67.gates, bf16[768,768]{1,0:T(8,128)(2,1)S(1)} %copy-done, bf16[128,512]{1,0:T(8,128)(2,1)S(1)} %get-tuple-element.80.refs_0_, ...), custom_call_target="tpu_custom_call" | custom-call | flops 200000000 | bytes 1000 | tf_op jit(solution)/shard_map/pallas_call | solution.py:776
  44.1 2.0 %collective-permute-done.16.refs_1_ = bf16[128,512]{1,0:T(8,128)(2,1)S(1)} collective-permute-done((bf16[128,512]{1,0:T(8,128)(2,1)S(1)}, bf16[128,512]{1,0:T(8,128)(2,1)S(1)}, u32[]{:S(2)}, u32[]{:S(2)}) %collective-permute-start.16) | collective-permute-done | bytes 131104 | tf_op jit(solution)/shard_map/ppermute | solution.py:637
  46.0 0.7 %shard_map.161.own_back = bf16[128,128]{1,0:T(8,128)(2,1)S(1)} custom-call(f32[128,768]{1,0:T(8,128)S(1)} %shard_map.159.so_far, f32[128,768]{1,0:T(8,128)S(1)} %get-tuple-element.67.gates, bf16[768,768]{1,0:T(8,128)(2,1)S(1)} %copy-done, bf16[128,512]{1,0:T(8,128)(2,1)S(1)} %shard_map.160.refs_0_, bf16[128,512]{1,0:T(8,128)(2,1)S(1)} %collective-permute-done.16.refs_1_, ...), custom_call_target="tpu_custom_call" | custom-call | flops 200000000 | bytes 1000 | tf_op jit(solution)/shard_map/pallas_call | solution.py:776
  46.8 1.6 %collective-permute-start.17 = (bf16[128,128]{1,0:T(8,128)(2,1)S(1)}, bf16[128,128]{1,0:T(8,128)(2,1)S(1)}, u32[]{:S(2)}, u32[]{:S(2)}) collective-permute-start(bf16[128,128]{1,0:T(8,128)(2,1)S(1)} %shard_map.161.own_back), channel_id=1, source_target_pairs={{0,1},{1,0},{2,3},{3,2},{4,5},{5,4},{6,7},{7,6},{8,9},{9,8},{10,11... | collective-permute-start | bytes 98312 | tf_op jit(solution)/shard_map/ppermute | solution.py:608
  48.3 1.2 %collective-permute-start.18 = (bf16[64,128]{1,0:T(8,128)(2,1)S(1)}, bf16[64,128]{1,0:T(8,128)(2,1)S(1)}, u32[]{:S(2)}, u32[]{:S(2)}) collective-permute-start(bf16[64,128]{1,0:T(8,128)(2,1)S(1)} %slice_select_fusion), channel_id=1, source_target_pairs={{0,16},{1,4},{2,18},{3,6},{4,1},{5,8},{6,3},{7,10},{8,5},{9,12},{1... | collective-permute-start | bytes 49160 | tf_op jit(solution)/shard_map/ppermute | solution.py:619
  49.6 0.0 copy-start.4
  49.6 5.2 %shard_map.162 = (bf16[2048,128]{1,0:T(8,128)(2,1)S(1)}, bf16[2048,128]{1,0:T(8,128)(2,1)S(1)}, bf16[128,128]{1,0:T(8,128)(2,1)S(1)}, f32[256,128]{1,0:T(8,128)S(1)}, f32[256,128]{1,0:T(8,128)S(1)}) custom-call(s32[5]{0:T(128)S(1)} %stack.23.info, s32[64]{0:T(128)S(1)} %copy-done.6, s32[1,2048]{1,0:T(1,128)S(1)} %bitcast.11, ...), custom_call_target="tpu_custom_call" | custom-call | flops 1500000000 | bytes 1000 | tf_op jit(solution)/shard_map/pallas_call | solution.py:798
  54.8 2.5 %shard_map.163 = bf16[2048,128]{1,0:T(8,128)(2,1)} custom-call(s32[5]{0:T(128)S(1)} %stack.23.info, s32[64]{0:T(128)S(1)} %copy-done.6, bf16[2048,128]{1,0:T(8,128)(2,1)S(1)} %get-tuple-element.82.atoms2, bf16[80,128]{1,0:T(8,128)(2,1)S(1)} %collective-permute-done.5.near, bf16[80,128]{1,0:T(8,128)(2,1)S(1)} %collective-permute-done.6.far, ...), custom_call_target="tpu_custom_call" | custom-call | flops 300000000 | bytes 1000 | tf_op jit(solution)/shard_map/pallas_call | solution.py:806
  (36 shorter events, 0.1 us)
Async XLA Ops:
  0.7 8.9 %collective-permute-start = (bf16[64,128]{1,0:T(8,128)(2,1)S(1)}, bf16[64,128]{1,0:T(8,128)(2,1)S(1)}, u32[]{:S(2)}, u32[]{:S(2)}) collective-permute-start(bf16[64,128]{1,0:T(8,128)(2,1)S(1)} %get-tuple-element.90), channel_id=1, source_target_pairs={{0,1},{1,0},{2,3},{3,2},{4,5},{5,4},{6,7},{7,6},{8,9},{9,8},{10,11... | collective-permute-start | bytes 49160 | tf_op jit(solution)/shard_map/ppermute | solution.py:608
  0.8 8.9 %collective-permute-start.1 = (bf16[64,128]{1,0:T(8,128)(2,1)S(1)}, bf16[64,128]{1,0:T(8,128)(2,1)S(1)}, u32[]{:S(2)}, u32[]{:S(2)}) collective-permute-start(bf16[64,128]{1,0:T(8,128)(2,1)S(1)} %get-tuple-element.89), channel_id=1, source_target_pairs={{0,16},{1,2},{2,1},{3,4},{4,3},{5,6},{6,5},{7,8},{8,7},{9,10},{10,... | collective-permute-start | bytes 49160 | tf_op jit(solution)/shard_map/ppermute | solution.py:619
  3.4 6.3 %copy-start.5 = (bf16[2048,128]{1,0:T(8,128)(2,1)S(1)}, bf16[2048,128]{1,0:T(8,128)(2,1)}, u32[]{:S(2)}) copy-start(bf16[2048,128]{1,0:T(8,128)(2,1)} %acts.1) | copy-start | bytes 1572868
  3.4 6.3 %copy-start.6 = (s32[64]{0:T(128)S(1)}, s32[64]{0:T(128)}, u32[]{:S(2)}) copy-start(s32[64]{0:T(128)} %offsets.5) | copy-start | bytes 772
  3.4 6.3 %copy-start.8 = (bf16[128,768]{1,0:T(8,128)(2,1)S(1)}, bf16[128,768]{1,0:T(8,128)(2,1)}, u32[]{:S(2)}) copy-start(bf16[128,768]{1,0:T(8,128)(2,1)} %up.1) | copy-start | bytes 589828
  3.4 6.3 %copy-start.9 = (bf16[128,384]{1,0:T(8,128)(2,1)S(1)}, bf16[128,384]{1,0:T(8,128)(2,1)}, u32[]{:S(2)}) copy-start(bf16[128,384]{1,0:T(8,128)(2,1)} %qkv.3) | copy-start | bytes 294916
  3.4 6.3 %copy-start.10 = (bf16[128,128]{1,0:T(8,128)(2,1)S(1)}, bf16[128,128]{1,0:T(8,128)(2,1)}, u32[]{:S(2)}) copy-start(bf16[128,128]{1,0:T(8,128)(2,1)} %out_weight.2) | copy-start | bytes 98308
  3.5 6.3 %copy-start.11 = (s32[2048]{0:T(1024)S(1)}, s32[2048]{0:T(1024)}, u32[]{:S(2)}) copy-start(s32[2048]{0:T(1024)} %param.25) | copy-start | bytes 24580
  3.5 6.3 %copy-start.12 = (f32[128]{0:T(128)S(1)}, f32[128]{0:T(128)}, u32[]{:S(2)}) copy-start(f32[128]{0:T(128)} %param.17) | copy-start | bytes 1540
  9.8 5.1 %copy-start.13 = (bf16[16,256,256]{2,1,0:T(8,128)(2,1)S(1)}, bf16[16,256,256]{2,1,0:T(8,128)(2,1)}, u32[]{:S(2)}) copy-start(bf16[16,256,256]{2,1,0:T(8,128)(2,1)} %own_far.1) | copy-start | bytes 6291460
  9.8 7.5 %copy-start.14 = (f32[768]{0:T(1024)S(1)}, f32[768]{0:T(1024)}, u32[]{:S(2)}) copy-start(f32[768]{0:T(1024)} %param.27) | copy-start | bytes 9220
  13.2 1.6 %collective-permute-start.2 = (bf16[128,896]{1,0:T(8,128)(2,1)S(1)}, bf16[128,896]{1,0:T(8,128)(2,1)S(1)}, u32[]{:S(2)}, u32[]{:S(2)}) collective-permute-start(bf16[128,896]{1,0:T(8,128)(2,1)S(1)} %get-tuple-element.54), channel_id=1, source_target_pairs={{0,1},{1,0},{2,3},{3,2},{4,5},{5,4},{6,7},{7,6},{8,9},{9,8},{10,11... | collective-permute-start | bytes 688136 | tf_op jit(solution)/shard_map/ppermute | solution.py:608
  14.9 5.7 %collective-permute-start.4 = (bf16[16,256,256]{2,1,0:T(8,128)(2,1)S(1)}, bf16[16,256,256]{2,1,0:T(8,128)(2,1)}, u32[]{:S(2)}, u32[]{:S(2)}) collective-permute-start(bf16[16,256,256]{2,1,0:T(8,128)(2,1)S(1)} %copy-done.13), channel_id=1, source_target_pairs={{0,1},{1,0},{2,3},{3,2},{4,5},{5,4},{6,7},{7,6},{8,9},{9,8},{10,11... | collective-permute-start | bytes 6291464 | tf_op jit(solution)/shard_map/ppermute | solution.py:608
  15.3 5.2 %collective-permute-start.3 = (bf16[64,896]{1,0:T(8,128)(2,1)S(1)}, bf16[64,896]{1,0:T(8,128)(2,1)S(1)}, u32[]{:S(2)}, u32[]{:S(2)}) collective-permute-start(bf16[64,896]{1,0:T(8,128)(2,1)S(1)} %get-tuple-element.91), channel_id=1, source_target_pairs={{0,2},{1,3},{2,0},{3,1},{4,6},{5,7},{6,4},{7,5},{8,10},{9,11},{10,... | collective-permute-start | bytes 344072 | tf_op jit(solution)/shard_map/ppermute | solution.py:637
  16.3 2.8 %collective-permute-start.5 = (bf16[80,128]{1,0:T(8,128)(2,1)S(1)}, bf16[80,128]{1,0:T(8,128)(2,1)S(1)}, u32[]{:S(2)}, u32[]{:S(2)}) collective-permute-start(bf16[80,128]{1,0:T(8,128)(2,1)S(1)} %get-tuple-element.59), channel_id=1, source_target_pairs={{0,1},{1,0},{2,3},{3,2},{4,5},{5,4},{6,7},{7,6},{8,9},{9,8},{10,11... | collective-permute-start | bytes 61448 | tf_op jit(solution)/shard_map/ppermute | solution.py:608
  17.0 3.6 %collective-permute-start.6 = (bf16[80,128]{1,0:T(8,128)(2,1)S(1)}, bf16[80,128]{1,0:T(8,128)(2,1)S(1)}, u32[]{:S(2)}, u32[]{:S(2)}) collective-permute-start(bf16[80,128]{1,0:T(8,128)(2,1)S(1)} %get-tuple-element.60), channel_id=1, source_target_pairs={{0,16},{1,2},{2,1},{3,4},{4,3},{5,6},{6,5},{7,8},{8,7},{9,10},{10,... | collective-permute-start | bytes 61448 | tf_op jit(solution)/shard_map/ppermute | solution.py:619
  20.9 5.6 %collective-permute-start.7 = (bf16[64,768]{1,0:T(8,128)(2,1)S(1)}, bf16[64,768]{1,0:T(8,128)(2,1)S(1)}, u32[]{:S(2)}, u32[]{:S(2)}) collective-permute-start(bf16[64,768]{1,0:T(8,128)(2,1)S(1)} %get-tuple-element.63.own_act), channel_id=1, source_target_pairs={{0,2},{1,3},{2,0},{3,1},{4,6},{5,7},{6,4},{7,5},{8,10},{9,11},{10,... | collective-permute-start | bytes 294920 | tf_op jit(solution)/shard_map/ppermute | solution.py:637
  21.9 4.6 %collective-permute-start.8 = (bf16[64,768]{1,0:T(8,128)(2,1)S(1)}, bf16[64,768]{1,0:T(8,128)(2,1)S(1)}, u32[]{:S(2)}, u32[]{:S(2)}) collective-permute-start(bf16[64,768]{1,0:T(8,128)(2,1)S(1)} %get-tuple-element.65.refs_1_), channel_id=1, source_target_pairs={{0,1},{1,0},{2,3},{3,2},{4,5},{5,4},{6,7},{7,6},{8,9},{9,8},{10,11... | collective-permute-start | bytes 294920 | tf_op jit(solution)/shard_map/ppermute | solution.py:608
  23.0 9.5 %collective-permute-start.9 = (bf16[64,768]{1,0:T(8,128)(2,1)S(1)}, bf16[64,768]{1,0:T(8,128)(2,1)S(1)}, u32[]{:S(2)}, u32[]{:S(2)}) collective-permute-start(bf16[64,768]{1,0:T(8,128)(2,1)S(1)} %get-tuple-element.65.refs_1_), channel_id=1, source_target_pairs={{0,8},{4,12},{8,0},{12,4},{1,9},{5,13},{9,1},{13,5},{2,10},{6,14},... | collective-permute-start | bytes 294920 | tf_op jit(solution)/shard_map/ppermute | solution.py:642
  25.4 7.1 %collective-permute-start.10 = (bf16[64,768]{1,0:T(8,128)(2,1)S(1)}, bf16[64,768]{1,0:T(8,128)(2,1)S(1)}, u32[]{:S(2)}, u32[]{:S(2)}) collective-permute-start(bf16[64,768]{1,0:T(8,128)(2,1)S(1)} %get-tuple-element.65.refs_1_), channel_id=1, source_target_pairs={{0,12},{4,8},{8,4},{12,0},{1,13},{5,9},{9,5},{13,1},{2,14},{6,10},... | collective-permute-start | bytes 294920 | tf_op jit(solution)/shard_map/ppermute | solution.py:642
  26.4 7.0 %collective-permute-start.11 = (bf16[64,768]{1,0:T(8,128)(2,1)S(1)}, bf16[64,768]{1,0:T(8,128)(2,1)S(1)}, u32[]{:S(2)}, u32[]{:S(2)}) collective-permute-start(bf16[64,768]{1,0:T(8,128)(2,1)S(1)} %get-tuple-element.65.refs_1_), channel_id=1, source_target_pairs={{0,4},{4,0},{8,12},{12,8},{1,5},{5,1},{9,13},{13,9},{2,6},{6,2},{1... | collective-permute-start | bytes 294920 | tf_op jit(solution)/shard_map/ppermute | solution.py:642
  33.5 2.2 %collective-permute-start.12 = (bf16[64,768]{1,0:T(8,128)(2,1)S(1)}, bf16[64,768]{1,0:T(8,128)(2,1)S(1)}, u32[]{:S(2)}, u32[]{:S(2)}) collective-permute-start(bf16[64,768]{1,0:T(8,128)(2,1)S(1)} %collective-permute-done.9.refs_0_), channel_id=1, source_target_pairs={{0,1},{1,0},{2,3},{3,2},{4,5},{5,4},{6,7},{7,6},{8,9},{9,8},{10,11... | collective-permute-start | bytes 294920 | tf_op jit(solution)/shard_map/ppermute | solution.py:608
  34.7 1.3 %collective-permute-start.13 = (bf16[64,768]{1,0:T(8,128)(2,1)S(1)}, bf16[64,768]{1,0:T(8,128)(2,1)S(1)}, u32[]{:S(2)}, u32[]{:S(2)}) collective-permute-start(bf16[64,768]{1,0:T(8,128)(2,1)S(1)} %collective-permute-done.10.refs_1_), channel_id=1, source_target_pairs={{0,1},{1,0},{2,3},{3,2},{4,5},{5,4},{6,7},{7,6},{8,9},{9,8},{10,11... | collective-permute-start | bytes 294920 | tf_op jit(solution)/shard_map/ppermute | solution.py:608
  34.7 1.5 %collective-permute-start.14 = (bf16[64,768]{1,0:T(8,128)(2,1)S(1)}, bf16[64,768]{1,0:T(8,128)(2,1)S(1)}, u32[]{:S(2)}, u32[]{:S(2)}) collective-permute-start(bf16[64,768]{1,0:T(8,128)(2,1)S(1)} %collective-permute-done.11.refs_2_), channel_id=1, source_target_pairs={{0,1},{1,0},{2,3},{3,2},{4,5},{5,4},{6,7},{7,6},{8,9},{9,8},{10,11... | collective-permute-start | bytes 294920 | tf_op jit(solution)/shard_map/ppermute | solution.py:608
  38.7 4.8 %collective-permute-start.15 = (bf16[128,512]{1,0:T(8,128)(2,1)S(1)}, bf16[128,512]{1,0:T(8,128)(2,1)S(1)}, u32[]{:S(2)}, u32[]{:S(2)}) collective-permute-start(bf16[128,512]{1,0:T(8,128)(2,1)S(1)} %get-tuple-element.80.refs_0_), channel_id=1, source_target_pairs={{0,2},{1,3},{2,0},{3,1},{4,6},{5,7},{6,4},{7,5},{8,10},{9,11},{10,... | collective-permute-start | bytes 393224 | tf_op jit(solution)/shard_map/ppermute | solution.py:637
  39.1 4.4 %copy-start = (bf16[768,768]{1,0:T(8,128)(2,1)S(1)}, bf16[768,768]{1,0:T(8,128)(2,1)}, u32[]{:S(2)}) copy-start(bf16[768,768]{1,0:T(8,128)(2,1)} %token_out.3) | copy-start | bytes 3538948
  39.1 4.4 %copy-start.2 = (bf16[768,128]{1,0:T(8,128)(2,1)S(1)}, bf16[768,128]{1,0:T(8,128)(2,1)}, u32[]{:S(2)}) copy-start(bf16[768,128]{1,0:T(8,128)(2,1)} %refs_2_.3) | copy-start | bytes 589828
  41.6 4.5 %collective-permute-start.16 = (bf16[128,512]{1,0:T(8,128)(2,1)S(1)}, bf16[128,512]{1,0:T(8,128)(2,1)S(1)}, u32[]{:S(2)}, u32[]{:S(2)}) collective-permute-start(bf16[128,512]{1,0:T(8,128)(2,1)S(1)} %shard_map.160.refs_0_), channel_id=1, source_target_pairs={{0,2},{1,3},{2,0},{3,1},{4,6},{5,7},{6,4},{7,5},{8,10},{9,11},{10,... | collective-permute-start | bytes 393224 | tf_op jit(solution)/shard_map/ppermute | solution.py:637
  43.5 6.1 %copy-start.1 = (bf16[4,2048,128]{2,1,0:T(8,128)(2,1)S(1)}, bf16[4,2048,128]{2,1,0:T(8,128)(2,1)}, u32[]{:S(2)}) copy-start(bf16[4,2048,128]{2,1,0:T(8,128)(2,1)} %bias.3) | copy-start | bytes 6291460
  43.5 6.1 %copy-start.3 = (bf16[128,384]{1,0:T(8,128)(2,1)S(1)}, bf16[128,384]{1,0:T(8,128)(2,1)}, u32[]{:S(2)}) copy-start(bf16[128,384]{1,0:T(8,128)(2,1)} %qkv.5) | copy-start | bytes 294916
  43.5 6.1 %copy-start.7 = (f32[128]{0:T(128)S(1)}, f32[128]{0:T(128)}, u32[]{:S(2)}) copy-start(f32[128]{0:T(128)} %param.20) | copy-start | bytes 1540
  46.8 2.8 %collective-permute-start.17 = (bf16[128,128]{1,0:T(8,128)(2,1)S(1)}, bf16[128,128]{1,0:T(8,128)(2,1)S(1)}, u32[]{:S(2)}, u32[]{:S(2)}) collective-permute-start(bf16[128,128]{1,0:T(8,128)(2,1)S(1)} %shard_map.161.own_back), channel_id=1, source_target_pairs={{0,1},{1,0},{2,3},{3,2},{4,5},{5,4},{6,7},{7,6},{8,9},{9,8},{10,11... | collective-permute-start | bytes 98312 | tf_op jit(solution)/shard_map/ppermute | solution.py:608
  48.3 6.4 %collective-permute-start.18 = (bf16[64,128]{1,0:T(8,128)(2,1)S(1)}, bf16[64,128]{1,0:T(8,128)(2,1)S(1)}, u32[]{:S(2)}, u32[]{:S(2)}) collective-permute-start(bf16[64,128]{1,0:T(8,128)(2,1)S(1)} %slice_select_fusion), channel_id=1, source_target_pairs={{0,16},{1,4},{2,18},{3,6},{4,1},{5,8},{6,3},{7,10},{8,5},{9,12},{1... | collective-permute-start | bytes 49160 | tf_op jit(solution)/shard_map/ppermute | solution.py:619
  49.6 5.2 %copy-start.4 = (bf16[128,128]{1,0:T(8,128)(2,1)S(1)}, bf16[128,128]{1,0:T(8,128)(2,1)}, u32[]{:S(2)}) copy-start(bf16[128,128]{1,0:T(8,128)(2,1)} %out_weight.3) | copy-start | bytes 98308

commit v9 on v8

--- a/solution.py
+++ b/solution.py
@@ -106,7 +106,7 @@
 
 
 def window_group(windows, edge):
-    return next(size for size in (15, 12, 10, 6, 5, 4, 3, 2, 1) if (windows - 2 * edge) % size == 0)
+    return next(size for size in (30, 20, 15, 12, 10, 6, 5, 4, 3, 2, 1) if (windows - 2 * edge) % size == 0)
 
 
 def inner_windows(offsets, bias, q, k, v, mixed, edge_q, edge_k, edge_v, ready=None):
@@ -344,7 +344,7 @@
     span = keys.shape[0] // LANES
     lane = lax.broadcasted_iota(jnp.int32, (count, LANES), 1)
     out = [None] * (wide // LANES)
-    together = 4
+    together = 8
     for start in range(0, heads, together):
         members = []
         for head in range(start, start + together):

time: 57.9 us -> 57.4 us (level)
  Pallas kernels: 28.7 us -> 28 us
  transfers between devices with their start and end apart: 19 -> 19, of which waited for: 10 -> 10; matrix products, arithmetic and copies ran while one was open for 0% -> 0% of each run, Pallas kernels for 34% -> 33%
where the time goes in v9:
time: 57.4 us; the launch traced here: 56.8 us
  Pallas kernels  28 us (49%)
  starting transfers between devices  17 us (30%)
  waiting for transfers between devices  10.6 us (18%)
  local copies, waits for them, and re-layouts  0.92 us (2%)
    pallas_call x1, Pallas kernels, body(): call(functools.partial(first_inner, pieces=pieces), [atom_shape] + edge_s...  6.12 us
    ppermute x9, starting transfers between devices, to_near(): return lax.ppermute(x, 'col', [(i, i ^ 1) for i in range(col_count)])  6.05 us
    pallas_call x1, Pallas kernels, body(): call(functools.partial(second_inner, share=share), [atom_shape, atom_shap...  4.89 us
    pallas_call x1, Pallas kernels, body(): call(functools.partial(attend_first, others=len(other_acts), steps=list(r...  4.61 us
    ppermute x9, waiting for transfers between devices, to_near(): return lax.ppermute(x, 'col', [(i, i ^ 1) for i in range(col_count)])  3.93 us
    ppermute x3, starting transfers between devices, swapped(): return lax.ppermute(x, ('group', 'row', 'col'), pairs_list)  3.89 us
    ppermute x4, starting transfers between devices, along_pairs(): lax.ppermute(x, 'col', [(2 * i + k, 2 * ((i + step) % pairs) + k) for i i...  3.69 us
    ppermute x3, starting transfers between devices, along_rows(): return lax.ppermute(x, 'row', [(i, i ^ step) for i in range(row_count)])  3.41 us
  transfers between devices with their start and end apart: 19, of which 10 were waited for; matrix products, arithmetic and copies ran while one was open for 0% of the time, Pallas kernels for 33%

profile of v9, /device:TPU:1, one launch (start us, length us, event | category | flops | bytes accessed | tf_op | source)
XLA Modules:
  0.0 56.8 jit_solution(17775242150573947669)
XLA Ops:
  0.0 0.7 %constant_dynamic-slice_fusion.2 = (bf16[64,128]{1,0:T(8,128)(2,1)S(1)}, bf16[64,128]{1,0:T(8,128)(2,1)S(1)}) fusion(bf16[2048,128]{1,0:T(8,128)(2,1)} %acts.1, s32[]{:T(128)S(6)} %select_n.41, s32[]{:T(128)S(6)} %select_n.40), kind=kLoop, calls=%fused_computation.4 | loop fusion | bytes 65544 | tf_op jit(solution)/shard_map/dynamic_slice | solution.py:645
  0.7 0.1 collective-permute-start
  0.8 2.5 %collective-permute-start.1 = (bf16[64,128]{1,0:T(8,128)(2,1)S(1)}, bf16[64,128]{1,0:T(8,128)(2,1)S(1)}, u32[]{:S(2)}, u32[]{:S(2)}) collective-permute-start(bf16[64,128]{1,0:T(8,128)(2,1)S(1)} %get-tuple-element.89), channel_id=1, source_target_pairs={{0,16},{1,2},{2,1},{3,4},{4,3},{5,6},{6,5},{7,8},{8,7},{9,10},{10,... | collective-permute-start | bytes 49160 | tf_op jit(solution)/shard_map/ppermute | solution.py:619
  3.3 0.1 stack.23.info
  3.4 0.0 copy-start.10
  3.5 0.0 copy-start.11
  3.5 0.0 copy-start.12
  3.5 6.1 %shard_map.154 = (bf16[2048,128]{1,0:T(8,128)(2,1)S(1)}, bf16[128,128]{1,0:T(8,128)(2,1)S(1)}, f32[256,128]{1,0:T(8,128)S(1)}, f32[256,128]{1,0:T(8,128)S(1)}, bf16[4,128,128]{2,1,0:T(8,128)(2,1)S(1)}) custom-call(s32[5]{0:T(128)S(1)} %stack.23.info, bf16[2048,128]{1,0:T(8,128)(2,1)} %acts.1, f32[1,128]{1,0:T(1,128)} %bitcast.12, bf16[128,384]{1,0:T(8,128)(2,1)} %qkv.3, ...), custom_call_target="tpu_custom_call" | custom-call | flops 1500000000 | bytes 1000 | tf_op jit(solution)/shard_map/pallas_call | solution.py:674
  9.7 0.0 copy-start.13
  9.7 0.0 copy-start.14
  9.7 3.4 %shard_map.155 = (bf16[2048,128]{1,0:T(8,128)(2,1)S(1)}, bf16[128,896]{1,0:T(8,128)(2,1)S(1)}, bf16[128,896]{1,0:T(8,128)(2,1)S(1)}, bf16[80,128]{1,0:T(8,128)(2,1)S(1)}, bf16[80,128]{1,0:T(8,128)(2,1)S(1)}) custom-call(s32[5]{0:T(128)S(1)} %stack.23.info, s32[64]{0:T(128)S(1)} %copy-done.6, s32[1,2048]{1,0:T(1,128)S(1)} %bitcast.10, ...), custom_call_target="tpu_custom_call" | custom-call | flops 2000000000 | bytes 1000 | tf_op jit(solution)/shard_map/pallas_call | solution.py:686
  13.1 0.5 collective-permute-start.2
  13.6 1.1 %collective-permute-done.2 = bf16[128,896]{1,0:T(8,128)(2,1)S(1)} collective-permute-done((bf16[128,896]{1,0:T(8,128)(2,1)S(1)}, bf16[128,896]{1,0:T(8,128)(2,1)S(1)}, u32[]{:S(2)}, u32[]{:S(2)}) %collective-permute-start.2) | collective-permute-done | bytes 229408 | tf_op jit(solution)/shard_map/ppermute | solution.py:608
  14.7 0.1 add_convert_fusion
  14.8 0.4 collective-permute-start.4
  15.2 1.1 %collective-permute-start.3 = (bf16[64,896]{1,0:T(8,128)(2,1)S(1)}, bf16[64,896]{1,0:T(8,128)(2,1)S(1)}, u32[]{:S(2)}, u32[]{:S(2)}) collective-permute-start(bf16[64,896]{1,0:T(8,128)(2,1)S(1)} %get-tuple-element.91), channel_id=1, source_target_pairs={{0,2},{1,3},{2,0},{3,1},{4,6},{5,7},{6,4},{7,5},{8,10},{9,11},{10,... | collective-permute-start | bytes 344072 | tf_op jit(solution)/shard_map/ppermute | solution.py:637
  16.3 0.7 %collective-permute-start.5 = (bf16[80,128]{1,0:T(8,128)(2,1)S(1)}, bf16[80,128]{1,0:T(8,128)(2,1)S(1)}, u32[]{:S(2)}, u32[]{:S(2)}) collective-permute-start(bf16[80,128]{1,0:T(8,128)(2,1)S(1)} %get-tuple-element.59), channel_id=1, source_target_pairs={{0,1},{1,0},{2,3},{3,2},{4,5},{5,4},{6,7},{7,6},{8,9},{9,8},{10,11... | collective-permute-start | bytes 61448 | tf_op jit(solution)/shard_map/ppermute | solution.py:608
  17.0 0.2 collective-permute-start.6
  17.2 1.9 %collective-permute-done.5.near = bf16[80,128]{1,0:T(8,128)(2,1)S(1)} collective-permute-done((bf16[80,128]{1,0:T(8,128)(2,1)S(1)}, bf16[80,128]{1,0:T(8,128)(2,1)S(1)}, u32[]{:S(2)}, u32[]{:S(2)}) %collective-permute-start.5) | collective-permute-done | bytes 20512 | tf_op jit(solution)/shard_map/ppermute | solution.py:608
  19.0 1.4 %collective-permute-done.6.far = bf16[80,128]{1,0:T(8,128)(2,1)S(1)} collective-permute-done((bf16[80,128]{1,0:T(8,128)(2,1)S(1)}, bf16[80,128]{1,0:T(8,128)(2,1)S(1)}, u32[]{:S(2)}, u32[]{:S(2)}) %collective-permute-start.6) | collective-permute-done | bytes 20512 | tf_op jit(solution)/shard_map/ppermute | solution.py:619
  20.5 0.3 shard_map.156
  20.8 1.0 %collective-permute-start.7 = (bf16[64,768]{1,0:T(8,128)(2,1)S(1)}, bf16[64,768]{1,0:T(8,128)(2,1)S(1)}, u32[]{:S(2)}, u32[]{:S(2)}) collective-permute-start(bf16[64,768]{1,0:T(8,128)(2,1)S(1)} %get-tuple-element.63.own_act), channel_id=1, source_target_pairs={{0,2},{1,3},{2,0},{3,1},{4,6},{5,7},{6,4},{7,5},{8,10},{9,11},{10,... | collective-permute-start | bytes 294920 | tf_op jit(solution)/shard_map/ppermute | solution.py:637
  21.8 1.2 %collective-permute-start.8 = (bf16[64,768]{1,0:T(8,128)(2,1)S(1)}, bf16[64,768]{1,0:T(8,128)(2,1)S(1)}, u32[]{:S(2)}, u32[]{:S(2)}) collective-permute-start(bf16[64,768]{1,0:T(8,128)(2,1)S(1)} %get-tuple-element.65.refs_1_), channel_id=1, source_target_pairs={{0,1},{1,0},{2,3},{3,2},{4,5},{5,4},{6,7},{7,6},{8,9},{9,8},{10,11... | collective-permute-start | bytes 294920 | tf_op jit(solution)/shard_map/ppermute | solution.py:608
  23.0 2.3 %collective-permute-start.9 = (bf16[64,768]{1,0:T(8,128)(2,1)S(1)}, bf16[64,768]{1,0:T(8,128)(2,1)S(1)}, u32[]{:S(2)}, u32[]{:S(2)}) collective-permute-start(bf16[64,768]{1,0:T(8,128)(2,1)S(1)} %get-tuple-element.65.refs_1_), channel_id=1, source_target_pairs={{0,8},{4,12},{8,0},{12,4},{1,9},{5,13},{9,1},{13,5},{2,10},{6,14},... | collective-permute-start | bytes 294920 | tf_op jit(solution)/shard_map/ppermute | solution.py:642
  25.3 1.0 %collective-permute-start.10 = (bf16[64,768]{1,0:T(8,128)(2,1)S(1)}, bf16[64,768]{1,0:T(8,128)(2,1)S(1)}, u32[]{:S(2)}, u32[]{:S(2)}) collective-permute-start(bf16[64,768]{1,0:T(8,128)(2,1)S(1)} %get-tuple-element.65.refs_1_), channel_id=1, source_target_pairs={{0,12},{4,8},{8,4},{12,0},{1,13},{5,9},{9,5},{13,1},{2,14},{6,10},... | collective-permute-start | bytes 294920 | tf_op jit(solution)/shard_map/ppermute | solution.py:642
  26.3 0.1 collective-permute-start.11
  26.4 4.6 %shard_map.157 = (bf16[128,768]{1,0:T(8,128)(2,1)S(1)}, bf16[128,768]{1,0:T(8,128)(2,1)S(1)}, f32[128,768]{1,0:T(8,128)S(1)}, bf16[768,768]{1,0:T(8,128)(2,1)S(1...) custom-call(s32[5]{0:T(128)S(1)} %stack.23.info, ...), custom_call_target="tpu_custom_call" | custom-call | flops 1000 | bytes 1000 | tf_op jit(solution)/shard_map/pallas_call | solution.py:734
  31.1 1.5 %collective-permute-done.9.refs_0_ = bf16[64,768]{1,0:T(8,128)(2,1)S(1)} collective-permute-done((bf16[64,768]{1,0:T(8,128)(2,1)S(1)}, bf16[64,768]{1,0:T(8,128)(2,1)S(1)}, u32[]{:S(2)}, u32[]{:S(2)}) %collective-permute-start.9) | collective-permute-done | bytes 98336 | tf_op jit(solution)/shard_map/ppermute | solution.py:642
  32.6 0.9 %collective-permute-done.11.refs_2_ = bf16[64,768]{1,0:T(8,128)(2,1)S(1)} collective-permute-done((bf16[64,768]{1,0:T(8,128)(2,1)S(1)}, bf16[64,768]{1,0:T(8,128)(2,1)S(1)}, u32[]{:S(2)}, u32[]{:S(2)}) %collective-permute-start.11) | collective-permute-done | bytes 98336 | tf_op jit(solution)/shard_map/ppermute | solution.py:642
  33.5 1.2 %collective-permute-start.12 = (bf16[64,768]{1,0:T(8,128)(2,1)S(1)}, bf16[64,768]{1,0:T(8,128)(2,1)S(1)}, u32[]{:S(2)}, u32[]{:S(2)}) collective-permute-start(bf16[64,768]{1,0:T(8,128)(2,1)S(1)} %collective-permute-done.9.refs_0_), channel_id=1, source_target_pairs={{0,1},{1,0},{2,3},{3,2},{4,5},{5,4},{6,7},{7,6},{8,9},{9,8},{10,11... | collective-permute-start | bytes 294920 | tf_op jit(solution)/shard_map/ppermute | solution.py:608
  34.7 0.5 collective-permute-start.14
  35.2 0.4 collective-permute-done.12.refs_3_
  35.7 0.4 collective-permute-done.13.refs_4_
  36.0 0.2 collective-permute-done.14.refs_5_
  36.2 2.4 %shard_map.158 = (bf16[128,512]{1,0:T(8,128)(2,1)S(1)}, bf16[384,768]{1,0:T(8,128)(2,1)S(1)}) custom-call(s32[5]{0:T(128)S(1)} %stack.23.info, bf16[128,768]{1,0:T(8,128)(2,1)S(1)} %get-tuple-element.68.queries, bf16[768,768]{1,0:T(8,128)(2,1)S(1)} %get-tuple-element.69.key_weight, bf16[768,768]{1,0:T(8,128)(2,1)S(1)} %get-tuple-element.70.value_weight, ...), custom_call_target="tpu_custom_call" | custom-call | flops 2000000000 | bytes 1000 | tf_op jit(solution)/shard_map/pallas_call | solution.py:759
  38.6 0.3 collective-permute-start.15
  38.9 2.4 %shard_map.160.refs_0_ = bf16[128,512]{1,0:T(8,128)(2,1)S(1)} custom-call(s32[5]{0:T(128)S(1)} %stack.23.info, bf16[128,768]{1,0:T(8,128)(2,1)S(1)} %get-tuple-element.68.queries, bf16[768,768]{1,0:T(8,128)(2,1)S(1)} %get-tuple-element.69.key_weight, bf16[768,768]{1,0:T(8,128)(2,1)S(1)} %get-tuple-element.70.value_weight, ...), custom_call_target="tpu_custom_call" | custom-call | flops 2000000000 | bytes 1000 | tf_op jit(solution)/shard_map/pallas_call | solution.py:766
  41.3 1.2 %collective-permute-start.16 = (bf16[128,512]{1,0:T(8,128)(2,1)S(1)}, bf16[128,512]{1,0:T(8,128)(2,1)S(1)}, u32[]{:S(2)}, u32[]{:S(2)}) collective-permute-start(bf16[128,512]{1,0:T(8,128)(2,1)S(1)} %shard_map.160.refs_0_), channel_id=1, source_target_pairs={{0,2},{1,3},{2,0},{3,1},{4,6},{5,7},{6,4},{7,5},{8,10},{9,11},{10,... | collective-permute-start | bytes 393224 | tf_op jit(solution)/shard_map/ppermute | solution.py:637
  42.5 0.8 %collective-permute-done.15.refs_1_ = bf16[128,512]{1,0:T(8,128)(2,1)S(1)} collective-permute-done((bf16[128,512]{1,0:T(8,128)(2,1)S(1)}, bf16[128,512]{1,0:T(8,128)(2,1)S(1)}, u32[]{:S(2)}, u32[]{:S(2)}) %collective-permute-start.15) | collective-permute-done | bytes 131104 | tf_op jit(solution)/shard_map/ppermute | solution.py:637
  43.4 0.0 copy-start.7
  43.4 0.6 %shard_map.159.so_far = f32[128,768]{1,0:T(8,128)S(1)} custom-call(bf16[128,768]{1,0:T(8,128)(2,1)S(1)} %get-tuple-element.66.so_far, f32[128,768]{1,0:T(8,128)S(1)} %get-tuple-element.67.gates, bf16[768,768]{1,0:T(8,128)(2,1)S(1)} %copy-done, bf16[128,512]{1,0:T(8,128)(2,1)S(1)} %get-tuple-element.80.refs_0_, ...), custom_call_target="tpu_custom_call" | custom-call | flops 200000000 | bytes 1000 | tf_op jit(solution)/shard_map/pallas_call | solution.py:776
  44.0 2.0 %collective-permute-done.16.refs_1_ = bf16[128,512]{1,0:T(8,128)(2,1)S(1)} collective-permute-done((bf16[128,512]{1,0:T(8,128)(2,1)S(1)}, bf16[128,512]{1,0:T(8,128)(2,1)S(1)}, u32[]{:S(2)}, u32[]{:S(2)}) %collective-permute-start.16) | collective-permute-done | bytes 131104 | tf_op jit(solution)/shard_map/ppermute | solution.py:637
  45.9 0.7 %shard_map.161.own_back = bf16[128,128]{1,0:T(8,128)(2,1)S(1)} custom-call(f32[128,768]{1,0:T(8,128)S(1)} %shard_map.159.so_far, f32[128,768]{1,0:T(8,128)S(1)} %get-tuple-element.67.gates, bf16[768,768]{1,0:T(8,128)(2,1)S(1)} %copy-done, bf16[128,512]{1,0:T(8,128)(2,1)S(1)} %shard_map.160.refs_0_, bf16[128,512]{1,0:T(8,128)(2,1)S(1)} %collective-permute-done.16.refs_1_, ...), custom_call_target="tpu_custom_call" | custom-call | flops 200000000 | bytes 1000 | tf_op jit(solution)/shard_map/pallas_call | solution.py:776
  46.6 1.5 %collective-permute-start.17 = (bf16[128,128]{1,0:T(8,128)(2,1)S(1)}, bf16[128,128]{1,0:T(8,128)(2,1)S(1)}, u32[]{:S(2)}, u32[]{:S(2)}) collective-permute-start(bf16[128,128]{1,0:T(8,128)(2,1)S(1)} %shard_map.161.own_back), channel_id=1, source_target_pairs={{0,1},{1,0},{2,3},{3,2},{4,5},{5,4},{6,7},{7,6},{8,9},{9,8},{10,11... | collective-permute-start | bytes 98312 | tf_op jit(solution)/shard_map/ppermute | solution.py:608
  48.2 1.2 %collective-permute-start.18 = (bf16[64,128]{1,0:T(8,128)(2,1)S(1)}, bf16[64,128]{1,0:T(8,128)(2,1)S(1)}, u32[]{:S(2)}, u32[]{:S(2)}) collective-permute-start(bf16[64,128]{1,0:T(8,128)(2,1)S(1)} %slice_select_fusion), channel_id=1, source_target_pairs={{0,16},{1,4},{2,18},{3,6},{4,1},{5,8},{6,3},{7,10},{8,5},{9,12},{1... | collective-permute-start | bytes 49160 | tf_op jit(solution)/shard_map/ppermute | solution.py:619
  49.3 0.0 copy-start.4
  49.3 4.9 %shard_map.162 = (bf16[2048,128]{1,0:T(8,128)(2,1)S(1)}, bf16[2048,128]{1,0:T(8,128)(2,1)S(1)}, bf16[128,128]{1,0:T(8,128)(2,1)S(1)}, f32[256,128]{1,0:T(8,128)S(1)}, f32[256,128]{1,0:T(8,128)S(1)}) custom-call(s32[5]{0:T(128)S(1)} %stack.23.info, s32[64]{0:T(128)S(1)} %copy-done.6, s32[1,2048]{1,0:T(1,128)S(1)} %bitcast.11, ...), custom_call_target="tpu_custom_call" | custom-call | flops 1500000000 | bytes 1000 | tf_op jit(solution)/shard_map/pallas_call | solution.py:798
  54.2 2.5 %shard_map.163 = bf16[2048,128]{1,0:T(8,128)(2,1)} custom-call(s32[5]{0:T(128)S(1)} %stack.23.info, s32[64]{0:T(128)S(1)} %copy-done.6, bf16[2048,128]{1,0:T(8,128)(2,1)S(1)} %get-tuple-element.82.atoms2, bf16[80,128]{1,0:T(8,128)(2,1)S(1)} %collective-permute-done.5.near, bf16[80,128]{1,0:T(8,128)(2,1)S(1)} %collective-permute-done.6.far, ...), custom_call_target="tpu_custom_call" | custom-call | flops 300000000 | bytes 1000 | tf_op jit(solution)/shard_map/pallas_call | solution.py:806
  (36 shorter events, 0.1 us)
Async XLA Ops:
  0.7 8.9 %collective-permute-start = (bf16[64,128]{1,0:T(8,128)(2,1)S(1)}, bf16[64,128]{1,0:T(8,128)(2,1)S(1)}, u32[]{:S(2)}, u32[]{:S(2)}) collective-permute-start(bf16[64,128]{1,0:T(8,128)(2,1)S(1)} %get-tuple-element.90), channel_id=1, source_target_pairs={{0,1},{1,0},{2,3},{3,2},{4,5},{5,4},{6,7},{7,6},{8,9},{9,8},{10,11... | collective-permute-start | bytes 49160 | tf_op jit(solution)/shard_map/ppermute | solution.py:608
  0.8 8.8 %collective-permute-start.1 = (bf16[64,128]{1,0:T(8,128)(2,1)S(1)}, bf16[64,128]{1,0:T(8,128)(2,1)S(1)}, u32[]{:S(2)}, u32[]{:S(2)}) collective-permute-start(bf16[64,128]{1,0:T(8,128)(2,1)S(1)} %get-tuple-element.89), channel_id=1, source_target_pairs={{0,16},{1,2},{2,1},{3,4},{4,3},{5,6},{6,5},{7,8},{8,7},{9,10},{10,... | collective-permute-start | bytes 49160 | tf_op jit(solution)/shard_map/ppermute | solution.py:619
  3.4 6.2 %copy-start.5 = (bf16[2048,128]{1,0:T(8,128)(2,1)S(1)}, bf16[2048,128]{1,0:T(8,128)(2,1)}, u32[]{:S(2)}) copy-start(bf16[2048,128]{1,0:T(8,128)(2,1)} %acts.1) | copy-start | bytes 1572868
  3.4 6.2 %copy-start.6 = (s32[64]{0:T(128)S(1)}, s32[64]{0:T(128)}, u32[]{:S(2)}) copy-start(s32[64]{0:T(128)} %offsets.5) | copy-start | bytes 772
  3.4 6.2 %copy-start.8 = (bf16[128,768]{1,0:T(8,128)(2,1)S(1)}, bf16[128,768]{1,0:T(8,128)(2,1)}, u32[]{:S(2)}) copy-start(bf16[128,768]{1,0:T(8,128)(2,1)} %up.1) | copy-start | bytes 589828
  3.4 6.2 %copy-start.9 = (bf16[128,384]{1,0:T(8,128)(2,1)S(1)}, bf16[128,384]{1,0:T(8,128)(2,1)}, u32[]{:S(2)}) copy-start(bf16[128,384]{1,0:T(8,128)(2,1)} %qkv.3) | copy-start | bytes 294916
  3.4 6.2 %copy-start.10 = (bf16[128,128]{1,0:T(8,128)(2,1)S(1)}, bf16[128,128]{1,0:T(8,128)(2,1)}, u32[]{:S(2)}) copy-start(bf16[128,128]{1,0:T(8,128)(2,1)} %out_weight.2) | copy-start | bytes 98308
  3.5 6.2 %copy-start.11 = (s32[2048]{0:T(1024)S(1)}, s32[2048]{0:T(1024)}, u32[]{:S(2)}) copy-start(s32[2048]{0:T(1024)} %param.25) | copy-start | bytes 24580
  3.5 6.2 %copy-start.12 = (f32[128]{0:T(128)S(1)}, f32[128]{0:T(128)}, u32[]{:S(2)}) copy-start(f32[128]{0:T(128)} %param.17) | copy-start | bytes 1540
  9.7 5.1 %copy-start.13 = (bf16[16,256,256]{2,1,0:T(8,128)(2,1)S(1)}, bf16[16,256,256]{2,1,0:T(8,128)(2,1)}, u32[]{:S(2)}) copy-start(bf16[16,256,256]{2,1,0:T(8,128)(2,1)} %own_far.1) | copy-start | bytes 6291460
  9.7 7.5 %copy-start.14 = (f32[768]{0:T(1024)S(1)}, f32[768]{0:T(1024)}, u32[]{:S(2)}) copy-start(f32[768]{0:T(1024)} %param.27) | copy-start | bytes 9220
  13.1 1.6 %collective-permute-start.2 = (bf16[128,896]{1,0:T(8,128)(2,1)S(1)}, bf16[128,896]{1,0:T(8,128)(2,1)S(1)}, u32[]{:S(2)}, u32[]{:S(2)}) collective-permute-start(bf16[128,896]{1,0:T(8,128)(2,1)S(1)} %get-tuple-element.54), channel_id=1, source_target_pairs={{0,1},{1,0},{2,3},{3,2},{4,5},{5,4},{6,7},{7,6},{8,9},{9,8},{10,11... | collective-permute-start | bytes 688136 | tf_op jit(solution)/shard_map/ppermute | solution.py:608
  14.8 5.7 %collective-permute-start.4 = (bf16[16,256,256]{2,1,0:T(8,128)(2,1)S(1)}, bf16[16,256,256]{2,1,0:T(8,128)(2,1)}, u32[]{:S(2)}, u32[]{:S(2)}) collective-permute-start(bf16[16,256,256]{2,1,0:T(8,128)(2,1)S(1)} %copy-done.13), channel_id=1, source_target_pairs={{0,1},{1,0},{2,3},{3,2},{4,5},{5,4},{6,7},{7,6},{8,9},{9,8},{10,11... | collective-permute-start | bytes 6291464 | tf_op jit(solution)/shard_map/ppermute | solution.py:608
  15.2 5.2 %collective-permute-start.3 = (bf16[64,896]{1,0:T(8,128)(2,1)S(1)}, bf16[64,896]{1,0:T(8,128)(2,1)S(1)}, u32[]{:S(2)}, u32[]{:S(2)}) collective-permute-start(bf16[64,896]{1,0:T(8,128)(2,1)S(1)} %get-tuple-element.91), channel_id=1, source_target_pairs={{0,2},{1,3},{2,0},{3,1},{4,6},{5,7},{6,4},{7,5},{8,10},{9,11},{10,... | collective-permute-start | bytes 344072 | tf_op jit(solution)/shard_map/ppermute | solution.py:637
  16.3 2.7 %collective-permute-start.5 = (bf16[80,128]{1,0:T(8,128)(2,1)S(1)}, bf16[80,128]{1,0:T(8,128)(2,1)S(1)}, u32[]{:S(2)}, u32[]{:S(2)}) collective-permute-start(bf16[80,128]{1,0:T(8,128)(2,1)S(1)} %get-tuple-element.59), channel_id=1, source_target_pairs={{0,1},{1,0},{2,3},{3,2},{4,5},{5,4},{6,7},{7,6},{8,9},{9,8},{10,11... | collective-permute-start | bytes 61448 | tf_op jit(solution)/shard_map/ppermute | solution.py:608
  17.0 3.5 %collective-permute-start.6 = (bf16[80,128]{1,0:T(8,128)(2,1)S(1)}, bf16[80,128]{1,0:T(8,128)(2,1)S(1)}, u32[]{:S(2)}, u32[]{:S(2)}) collective-permute-start(bf16[80,128]{1,0:T(8,128)(2,1)S(1)} %get-tuple-element.60), channel_id=1, source_target_pairs={{0,16},{1,2},{2,1},{3,4},{4,3},{5,6},{6,5},{7,8},{8,7},{9,10},{10,... | collective-permute-start | bytes 61448 | tf_op jit(solution)/shard_map/ppermute | solution.py:619
  20.8 5.6 %collective-permute-start.7 = (bf16[64,768]{1,0:T(8,128)(2,1)S(1)}, bf16[64,768]{1,0:T(8,128)(2,1)S(1)}, u32[]{:S(2)}, u32[]{:S(2)}) collective-permute-start(bf16[64,768]{1,0:T(8,128)(2,1)S(1)} %get-tuple-element.63.own_act), channel_id=1, source_target_pairs={{0,2},{1,3},{2,0},{3,1},{4,6},{5,7},{6,4},{7,5},{8,10},{9,11},{10,... | collective-permute-start | bytes 294920 | tf_op jit(solution)/shard_map/ppermute | solution.py:637
  21.8 4.6 %collective-permute-start.8 = (bf16[64,768]{1,0:T(8,128)(2,1)S(1)}, bf16[64,768]{1,0:T(8,128)(2,1)S(1)}, u32[]{:S(2)}, u32[]{:S(2)}) collective-permute-start(bf16[64,768]{1,0:T(8,128)(2,1)S(1)} %get-tuple-element.65.refs_1_), channel_id=1, source_target_pairs={{0,1},{1,0},{2,3},{3,2},{4,5},{5,4},{6,7},{7,6},{8,9},{9,8},{10,11... | collective-permute-start | bytes 294920 | tf_op jit(solution)/shard_map/ppermute | solution.py:608
  23.0 9.5 %collective-permute-start.9 = (bf16[64,768]{1,0:T(8,128)(2,1)S(1)}, bf16[64,768]{1,0:T(8,128)(2,1)S(1)}, u32[]{:S(2)}, u32[]{:S(2)}) collective-permute-start(bf16[64,768]{1,0:T(8,128)(2,1)S(1)} %get-tuple-element.65.refs_1_), channel_id=1, source_target_pairs={{0,8},{4,12},{8,0},{12,4},{1,9},{5,13},{9,1},{13,5},{2,10},{6,14},... | collective-permute-start | bytes 294920 | tf_op jit(solution)/shard_map/ppermute | solution.py:642
  25.3 7.2 %collective-permute-start.10 = (bf16[64,768]{1,0:T(8,128)(2,1)S(1)}, bf16[64,768]{1,0:T(8,128)(2,1)S(1)}, u32[]{:S(2)}, u32[]{:S(2)}) collective-permute-start(bf16[64,768]{1,0:T(8,128)(2,1)S(1)} %get-tuple-element.65.refs_1_), channel_id=1, source_target_pairs={{0,12},{4,8},{8,4},{12,0},{1,13},{5,9},{9,5},{13,1},{2,14},{6,10},... | collective-permute-start | bytes 294920 | tf_op jit(solution)/shard_map/ppermute | solution.py:642
  26.3 7.1 %collective-permute-start.11 = (bf16[64,768]{1,0:T(8,128)(2,1)S(1)}, bf16[64,768]{1,0:T(8,128)(2,1)S(1)}, u32[]{:S(2)}, u32[]{:S(2)}) collective-permute-start(bf16[64,768]{1,0:T(8,128)(2,1)S(1)} %get-tuple-element.65.refs_1_), channel_id=1, source_target_pairs={{0,4},{4,0},{8,12},{12,8},{1,5},{5,1},{9,13},{13,9},{2,6},{6,2},{1... | collective-permute-start | bytes 294920 | tf_op jit(solution)/shard_map/ppermute | solution.py:642
  33.5 2.2 %collective-permute-start.12 = (bf16[64,768]{1,0:T(8,128)(2,1)S(1)}, bf16[64,768]{1,0:T(8,128)(2,1)S(1)}, u32[]{:S(2)}, u32[]{:S(2)}) collective-permute-start(bf16[64,768]{1,0:T(8,128)(2,1)S(1)} %collective-permute-done.9.refs_0_), channel_id=1, source_target_pairs={{0,1},{1,0},{2,3},{3,2},{4,5},{5,4},{6,7},{7,6},{8,9},{9,8},{10,11... | collective-permute-start | bytes 294920 | tf_op jit(solution)/shard_map/ppermute | solution.py:608
  34.7 1.3 %collective-permute-start.13 = (bf16[64,768]{1,0:T(8,128)(2,1)S(1)}, bf16[64,768]{1,0:T(8,128)(2,1)S(1)}, u32[]{:S(2)}, u32[]{:S(2)}) collective-permute-start(bf16[64,768]{1,0:T(8,128)(2,1)S(1)} %collective-permute-done.10.refs_1_), channel_id=1, source_target_pairs={{0,1},{1,0},{2,3},{3,2},{4,5},{5,4},{6,7},{7,6},{8,9},{9,8},{10,11... | collective-permute-start | bytes 294920 | tf_op jit(solution)/shard_map/ppermute | solution.py:608
  34.7 1.5 %collective-permute-start.14 = (bf16[64,768]{1,0:T(8,128)(2,1)S(1)}, bf16[64,768]{1,0:T(8,128)(2,1)S(1)}, u32[]{:S(2)}, u32[]{:S(2)}) collective-permute-start(bf16[64,768]{1,0:T(8,128)(2,1)S(1)} %collective-permute-done.11.refs_2_), channel_id=1, source_target_pairs={{0,1},{1,0},{2,3},{3,2},{4,5},{5,4},{6,7},{7,6},{8,9},{9,8},{10,11... | collective-permute-start | bytes 294920 | tf_op jit(solution)/shard_map/ppermute | solution.py:608
  38.6 4.8 %collective-permute-start.15 = (bf16[128,512]{1,0:T(8,128)(2,1)S(1)}, bf16[128,512]{1,0:T(8,128)(2,1)S(1)}, u32[]{:S(2)}, u32[]{:S(2)}) collective-permute-start(bf16[128,512]{1,0:T(8,128)(2,1)S(1)} %get-tuple-element.80.refs_0_), channel_id=1, source_target_pairs={{0,2},{1,3},{2,0},{3,1},{4,6},{5,7},{6,4},{7,5},{8,10},{9,11},{10,... | collective-permute-start | bytes 393224 | tf_op jit(solution)/shard_map/ppermute | solution.py:637
  38.9 4.5 %copy-start = (bf16[768,768]{1,0:T(8,128)(2,1)S(1)}, bf16[768,768]{1,0:T(8,128)(2,1)}, u32[]{:S(2)}) copy-start(bf16[768,768]{1,0:T(8,128)(2,1)} %token_out.3) | copy-start | bytes 3538948
  38.9 4.5 %copy-start.2 = (bf16[768,128]{1,0:T(8,128)(2,1)S(1)}, bf16[768,128]{1,0:T(8,128)(2,1)}, u32[]{:S(2)}) copy-start(bf16[768,128]{1,0:T(8,128)(2,1)} %refs_2_.3) | copy-start | bytes 589828
  41.3 4.6 %collective-permute-start.16 = (bf16[128,512]{1,0:T(8,128)(2,1)S(1)}, bf16[128,512]{1,0:T(8,128)(2,1)S(1)}, u32[]{:S(2)}, u32[]{:S(2)}) collective-permute-start(bf16[128,512]{1,0:T(8,128)(2,1)S(1)} %shard_map.160.refs_0_), channel_id=1, source_target_pairs={{0,2},{1,3},{2,0},{3,1},{4,6},{5,7},{6,4},{7,5},{8,10},{9,11},{10,... | collective-permute-start | bytes 393224 | tf_op jit(solution)/shard_map/ppermute | solution.py:637
  43.4 5.9 %copy-start.1 = (bf16[4,2048,128]{2,1,0:T(8,128)(2,1)S(1)}, bf16[4,2048,128]{2,1,0:T(8,128)(2,1)}, u32[]{:S(2)}) copy-start(bf16[4,2048,128]{2,1,0:T(8,128)(2,1)} %bias.3) | copy-start | bytes 6291460
  43.4 5.9 %copy-start.3 = (bf16[128,384]{1,0:T(8,128)(2,1)S(1)}, bf16[128,384]{1,0:T(8,128)(2,1)}, u32[]{:S(2)}) copy-start(bf16[128,384]{1,0:T(8,128)(2,1)} %qkv.5) | copy-start | bytes 294916
  43.4 5.9 %copy-start.7 = (f32[128]{0:T(128)S(1)}, f32[128]{0:T(128)}, u32[]{:S(2)}) copy-start(f32[128]{0:T(128)} %param.20) | copy-start | bytes 1540
  46.6 2.7 %collective-permute-start.17 = (bf16[128,128]{1,0:T(8,128)(2,1)S(1)}, bf16[128,128]{1,0:T(8,128)(2,1)S(1)}, u32[]{:S(2)}, u32[]{:S(2)}) collective-permute-start(bf16[128,128]{1,0:T(8,128)(2,1)S(1)} %shard_map.161.own_back), channel_id=1, source_target_pairs={{0,1},{1,0},{2,3},{3,2},{4,5},{5,4},{6,7},{7,6},{8,9},{9,8},{10,11... | collective-permute-start | bytes 98312 | tf_op jit(solution)/shard_map/ppermute | solution.py:608
  48.2 6.1 %collective-permute-start.18 = (bf16[64,128]{1,0:T(8,128)(2,1)S(1)}, bf16[64,128]{1,0:T(8,128)(2,1)S(1)}, u32[]{:S(2)}, u32[]{:S(2)}) collective-permute-start(bf16[64,128]{1,0:T(8,128)(2,1)S(1)} %slice_select_fusion), channel_id=1, source_target_pairs={{0,16},{1,4},{2,18},{3,6},{4,1},{5,8},{6,3},{7,10},{8,5},{9,12},{1... | collective-permute-start | bytes 49160 | tf_op jit(solution)/shard_map/ppermute | solution.py:619
  49.3 4.9 %copy-start.4 = (bf16[128,128]{1,0:T(8,128)(2,1)S(1)}, bf16[128,128]{1,0:T(8,128)(2,1)}, u32[]{:S(2)}) copy-start(bf16[128,128]{1,0:T(8,128)(2,1)} %out_weight.3) | copy-start | bytes 98308
